TPU v7x, 32 devices: a whole 2x2x4 slice. The times are simulated.
32 devices in a mesh: dp: 8 (over y, x, core), fsdp: 4 (over z).
Axes of the slice: x: 2, y: 2, z: 4, core: 2. Of those that a mesh axis runs over, the one named last changes fastest.
Arguments:
- inputs: bfloat16 [32, 128, 1024], P(('dp', 'fsdp')), may hold values from -6 to 6
- cotangent: bfloat16 [32, 128, 1024], P(('dp', 'fsdp')), may hold values from -6 to 6
- segment_ids: int32 [32, 128], P(('dp', 'fsdp')), may hold values from 0 to 2, never falling along the last dimension, each value on 1 to 80 neighbouring positions
- section_ids: int32 [32], P(('dp', 'fsdp')), may hold values from 0 to 7
- w_big: bfloat16 [2, 1024, 8192], P(None, ('dp', 'fsdp')), may hold values from -0.9375 to 0.9375
- w_down: bfloat16 [2, 4096, 1024], P(None, ('dp', 'fsdp')), may hold values from -0.09375 to 0.09375
- norm_table: bfloat16 [9, 4096], P(None, ('dp', 'fsdp')), may hold values from -1.5 to 1.6
- m_big: float32 [2, 1024, 8192], P(None, ('dp', 'fsdp')), may hold values from -48 to 48
- m_down: float32 [2, 4096, 1024], P(None, ('dp', 'fsdp')), may hold values from -48 to 48
- m_table: float32 [9, 4096], P(None, ('dp', 'fsdp')), may hold values from -48 to 48
- v_big: float32 [2, 1024, 8192], P(None, ('dp', 'fsdp')), may hold values from 64 to 16384
- v_down: float32 [2, 4096, 1024], P(None, ('dp', 'fsdp')), may hold values from 64 to 16384
- v_table: float32 [9, 4096], P(None, ('dp', 'fsdp')), may hold values from 64 to 16384
Outputs:
- out_act: bfloat16 [32, 128, 1024], P(('dp', 'fsdp'))
- grad_input: bfloat16 [32, 128, 1024], P(('dp', 'fsdp'))
- grad_big: float32 [2, 1024, 8192], P(None, ('dp', 'fsdp'))
- grad_down: float32 [2, 4096, 1024], P(None, ('dp', 'fsdp'))
- grad_table: float32 [9, 4096], P(None, ('dp', 'fsdp'))
- new_m_big: float32 [2, 1024, 8192], P(None, ('dp', 'fsdp'))
- new_m_down: float32 [2, 4096, 1024], P(None, ('dp', 'fsdp'))
- new_m_table: float32 [9, 4096], P(None, ('dp', 'fsdp'))
- step_big: float32 [2, 1024, 8192], P(None, ('dp', 'fsdp'))
- step_down: float32 [2, 4096, 1024], P(None, ('dp', 'fsdp'))
- step_table: float32 [9, 4096], P(None, ('dp', 'fsdp'))
Inputs may be any that keep to these rules, and one draw needn't show every extreme that they name: `segment_ids`: in each row the numbers never fall, every one of the 3 utterances has 1 to 80 frames, and one has exactly 80.
All inputs are finite; a program needn't handle non-finite values.
Results may differ from a plain program's by a relative error of at most 0.015.
Values may be sent and summed in bfloat16 or wider, within the bound.
No kernel may reach another device: no remote copies, remote signals or barrier semaphores. Data moves between devices by JAX's collectives and lax.ppermute only.
A program may use at most 384 MiB of HBM per device.

v0:
```python
from functools import partial

import jax
import jax.numpy as jnp
from jax import lax
from jax.sharding import PartitionSpec as P

HEADS = 16


beta_one = 0.9
beta_two = 0.999
first_fix = 1.0 - 0.9**10
second_fix = 1.0 - 0.999**10


def contract_rows(left, right):
    return lax.dot_general(
        left, right, (((0,), (0,)), ((), ())), preferred_element_type=jnp.float32
    )


def times_transposed(left, right):
    return lax.dot_general(
        left, right, (((1,), (1,)), ((), ())), preferred_element_type=jnp.float32
    )


def layer_norm(hidden):
    centred = hidden - jnp.mean(hidden, axis=-1, keepdims=True)
    return centred * lax.rsqrt(jnp.mean(centred * centred, axis=-1, keepdims=True) + 1e-05)


def normalize(hidden, gain_rows, select, which):
    model_width = hidden.shape[-1]
    picked = jnp.dot(select, gain_rows, precision=lax.Precision.HIGHEST)
    offset = 2 * which * model_width
    scale_part = picked[:, offset : offset + model_width][:, None, :]
    shift_part = picked[:, offset + model_width : offset + 2 * model_width][:, None, :]
    return layer_norm(hidden) * scale_part + shift_part


def segment_mask(segment_ids, causal):
    allowed = segment_ids[:, :, None] == segment_ids[:, None, :]
    if causal:
        position = jnp.arange(segment_ids.shape[1])
        allowed = allowed & (position[:, None] >= position[None, :])
    return allowed


def masked_scores(queries, key_vecs, allowed):
    score_scale = queries.shape[-1] ** (-0.5)
    scores = (
        jnp.einsum("rqhe,rkhe->rhqk", queries, key_vecs, preferred_element_type=jnp.float32)
        * score_scale
    )
    return jnp.where(allowed[:, None], scores, -1e30)


def fetch_forward(w_big, w_down, table_part, layer_index):
    return (
        lax.all_gather(w_big[layer_index], ("dp", "fsdp"), axis=0, tiled=True),
        lax.all_gather(w_down[layer_index], ("dp", "fsdp"), axis=0, tiled=True),
        lax.all_gather(table_part, ("dp", "fsdp"), axis=1, tiled=True),
    )


def forward_layer(hidden, gathered, select, segment_ids, causal):
    w_rows, w_lower, gain_rows = gathered
    row_count, row_length, model_width = hidden.shape
    tokens = row_count * row_length
    head_size = model_width // HEADS
    normed_one = (
        normalize(hidden, gain_rows, select, 0).astype(jnp.bfloat16).reshape(tokens, model_width)
    )
    projected = jnp.dot(
        normed_one, w_rows[:, : 3 * model_width], preferred_element_type=jnp.float32
    ).astype(jnp.bfloat16)
    queries = projected[:, :model_width].reshape(row_count, row_length, HEADS, head_size)
    key_vecs = projected[:, model_width : 2 * model_width].reshape(
        row_count, row_length, HEADS, head_size
    )
    values = projected[:, 2 * model_width :].reshape(row_count, row_length, HEADS, head_size)
    scores = masked_scores(queries, key_vecs, segment_mask(segment_ids, causal))
    row_top = jnp.max(scores, axis=-1, keepdims=True)
    exponent = jnp.exp(scores - row_top)
    row_total = jnp.sum(exponent, axis=-1, keepdims=True)
    shares = exponent / row_total
    log_total = row_top + jnp.log(row_total)
    mixed = jnp.einsum(
        "rhqk,rkhe->rqhe", shares.astype(jnp.bfloat16), values, preferred_element_type=jnp.float32
    )
    mixed = mixed.astype(jnp.bfloat16).reshape(tokens, model_width)
    attended = hidden.reshape(tokens, model_width) + jnp.dot(
        mixed, w_rows[:, 3 * model_width : 4 * model_width], preferred_element_type=jnp.float32
    )
    normed_two = normalize(
        attended.reshape(row_count, row_length, model_width), gain_rows, select, 1
    )
    normed_two = normed_two.astype(jnp.bfloat16).reshape(tokens, model_width)
    pre_active = jnp.dot(
        normed_two, w_rows[:, 4 * model_width :], preferred_element_type=jnp.float32
    )
    active = jax.nn.gelu(pre_active).astype(jnp.bfloat16)
    output = attended + jnp.dot(active, w_lower, preferred_element_type=jnp.float32)
    stored = (
        hidden,
        attended,
        normed_one,
        queries,
        key_vecs,
        values,
        log_total,
        mixed,
        normed_two,
        pre_active,
        active,
    )
    return (output.reshape(row_count, row_length, model_width), stored)


def backward_layer(grad_out, gathered, select, segment_ids, causal, stored):
    (
        hidden,
        attended,
        normed_one,
        queries,
        key_vecs,
        values,
        log_total,
        mixed,
        normed_two,
        pre_active,
        active,
    ) = stored
    w_rows, w_lower, gain_rows = gathered
    row_count, row_length, model_width = hidden.shape
    tokens = row_count * row_length
    grad_flat = grad_out.reshape(tokens, model_width)
    grad_branch = grad_flat.astype(jnp.bfloat16)
    grad_lower = contract_rows(active, grad_branch)
    grad_active = times_transposed(grad_branch, w_lower)
    unused_value, gelu_back = jax.vjp(jax.nn.gelu, pre_active)
    grad_pre = gelu_back(grad_active)[0].astype(jnp.bfloat16)
    grad_up = contract_rows(normed_two, grad_pre)
    grad_normed_two = times_transposed(grad_pre, w_rows[:, 4 * model_width :])
    unused_two, norm_back = jax.vjp(
        partial(normalize, select=select, which=1),
        attended.reshape(row_count, row_length, model_width),
        gain_rows,
    )
    grad_attended_part, grad_gain_two = norm_back(
        grad_normed_two.reshape(row_count, row_length, model_width)
    )
    grad_attended = grad_flat + grad_attended_part.reshape(tokens, model_width)
    grad_mix_in = grad_attended.astype(jnp.bfloat16)
    grad_out_proj = contract_rows(mixed, grad_mix_in)
    grad_mixed = times_transposed(grad_mix_in, w_rows[:, 3 * model_width : 4 * model_width]).astype(
        jnp.bfloat16
    )
    grad_mixed = grad_mixed.reshape(queries.shape)
    scores = masked_scores(queries, key_vecs, segment_mask(segment_ids, causal))
    shares = jnp.exp(scores - log_total)
    grad_shares = jnp.einsum(
        "rqhe,rkhe->rhqk", grad_mixed, values, preferred_element_type=jnp.float32
    )
    grad_values = jnp.einsum(
        "rhqk,rqhe->rkhe",
        shares.astype(jnp.bfloat16),
        grad_mixed,
        preferred_element_type=jnp.float32,
    ).astype(jnp.bfloat16)
    share_dot = jnp.sum(shares * grad_shares, axis=-1, keepdims=True)
    grad_scores = (shares * (grad_shares - share_dot)).astype(jnp.bfloat16)
    score_scale = queries.shape[-1] ** (-0.5)
    grad_queries = (
        jnp.einsum("rhqk,rkhe->rqhe", grad_scores, key_vecs, preferred_element_type=jnp.float32)
        * score_scale
    ).astype(jnp.bfloat16)
    grad_keys = (
        jnp.einsum("rhqk,rqhe->rkhe", grad_scores, queries, preferred_element_type=jnp.float32)
        * score_scale
    ).astype(jnp.bfloat16)
    grad_projected = jnp.concatenate(
        [
            grad_queries.reshape(tokens, model_width),
            grad_keys.reshape(tokens, model_width),
            grad_values.reshape(tokens, model_width),
        ],
        axis=1,
    )
    grad_qkv = contract_rows(normed_one, grad_projected)
    grad_normed_one = times_transposed(grad_projected, w_rows[:, : 3 * model_width])
    unused_one, norm_back_one = jax.vjp(
        partial(normalize, select=select, which=0), hidden, gain_rows
    )
    grad_hidden_part, grad_gain_one = norm_back_one(
        grad_normed_one.reshape(row_count, row_length, model_width)
    )
    grad_hidden = grad_attended.reshape(row_count, row_length, model_width) + grad_hidden_part
    grad_gains = jnp.transpose(grad_gain_one + grad_gain_two)
    return (grad_hidden, (grad_qkv, grad_out_proj, grad_up, grad_lower, grad_gains))


def reduce_gradients(layer_grads):
    result = (
        lax.psum_scatter(layer_grads[0], ("dp", "fsdp"), scatter_dimension=0, tiled=True),
        lax.psum_scatter(layer_grads[1], ("dp", "fsdp"), scatter_dimension=0, tiled=True),
        lax.psum_scatter(layer_grads[2], ("dp", "fsdp"), scatter_dimension=0, tiled=True),
        lax.psum_scatter(layer_grads[3], ("dp", "fsdp"), scatter_dimension=0, tiled=True),
        lax.psum_scatter(
            layer_grads[4].astype(jnp.float32), ("dp", "fsdp"), scatter_dimension=0, tiled=True
        ),
    )
    grad_qkv, grad_out_proj, grad_up, grad_lower, grad_gains = result
    return (
        jnp.concatenate([grad_qkv, grad_out_proj, grad_up], axis=1),
        grad_lower,
        jnp.transpose(grad_gains),
    )


def adam_update(moment, square, gradient):
    moment = beta_one * moment + (1.0 - beta_one) * gradient
    square = beta_two * square + (1.0 - beta_two) * gradient * gradient
    update = moment / first_fix / (jnp.sqrt(square / second_fix) + 1e-08)
    return (moment, update)


def body(
    inputs,
    cotangent,
    segment_ids,
    section_ids,
    w_big,
    w_down,
    norm_table,
    m_big,
    m_down,
    m_table,
    v_big,
    v_down,
    v_table,
):
    row_count = inputs.shape[0]
    section_count = norm_table.shape[0] - 1
    select_first = jnp.ones((row_count, 1), jnp.float32)
    select_second = (section_ids[:, None] == jnp.arange(section_count)[None, :]).astype(jnp.float32)
    selects = (select_first, select_second)
    table_parts = (norm_table[0:1], norm_table[1:])
    hidden = inputs.astype(jnp.float32)
    gathered_all = []
    stored_all = []
    for layer_index in range(2):
        gathered = fetch_forward(w_big, w_down, table_parts[layer_index], layer_index)
        hidden, stored = forward_layer(
            hidden, gathered, selects[layer_index], segment_ids, layer_index == 0
        )
        gathered_all.append(gathered)
        stored_all.append(stored)
    out_act = hidden.astype(jnp.bfloat16)
    grad_hidden = cotangent.astype(jnp.float32)
    reduced = [None, None]
    for layer_index in (1, 0):
        gathered = (
            lax.all_gather(w_big[layer_index], ("dp", "fsdp"), axis=0, tiled=True),
            lax.all_gather(w_down[layer_index], ("dp", "fsdp"), axis=0, tiled=True),
            lax.all_gather(table_parts[layer_index], ("dp", "fsdp"), axis=1, tiled=True),
        )
        grad_hidden, layer_grads = backward_layer(
            grad_hidden,
            gathered,
            selects[layer_index],
            segment_ids,
            layer_index == 0,
            stored_all[layer_index],
        )
        reduced[layer_index] = reduce_gradients(layer_grads)
    grad_big = jnp.stack([reduced[0][0], reduced[1][0]])
    grad_down = jnp.stack([reduced[0][1], reduced[1][1]])
    grad_table = jnp.concatenate([reduced[0][2], reduced[1][2]], axis=0)
    new_m_big, step_big = adam_update(m_big, v_big, grad_big)
    new_m_down, step_down = adam_update(m_down, v_down, grad_down)
    new_m_table, step_table = adam_update(m_table, v_table, grad_table)
    return (
        out_act,
        grad_hidden.astype(jnp.bfloat16),
        grad_big,
        grad_down,
        grad_table,
        new_m_big,
        new_m_down,
        new_m_table,
        step_big,
        step_down,
        step_table,
    )


def solution(mesh):
    placed = (
        P(("dp", "fsdp"), None, None),
        P(("dp", "fsdp"), None, None),
        P(("dp", "fsdp"), None),
        P(("dp", "fsdp")),
        P(None, ("dp", "fsdp"), None),
        P(None, ("dp", "fsdp"), None),
        P(None, ("dp", "fsdp")),
        P(None, ("dp", "fsdp"), None),
        P(None, ("dp", "fsdp"), None),
        P(None, ("dp", "fsdp")),
        P(None, ("dp", "fsdp"), None),
        P(None, ("dp", "fsdp"), None),
        P(None, ("dp", "fsdp")),
    )
    return jax.shard_map(
        body,
        mesh=mesh,
        in_specs=placed,
        out_specs=(
            P(("dp", "fsdp"), None, None),
            P(("dp", "fsdp"), None, None),
            P(None, ("dp", "fsdp"), None),
            P(None, ("dp", "fsdp"), None),
            P(None, ("dp", "fsdp")),
            P(None, ("dp", "fsdp"), None),
            P(None, ("dp", "fsdp"), None),
            P(None, ("dp", "fsdp")),
            P(None, ("dp", "fsdp"), None),
            P(None, ("dp", "fsdp"), None),
            P(None, ("dp", "fsdp")),
        ),
        check_vma=False,
    )
```

profile of v0, /device:TPU:0, one launch (start us, length us, event | category | flops | bytes accessed | tf_op | source)
XLA Modules:
  0.0 2823.7 jit_solution(2275475026468577287)
XLA Ops:
  7.3 2.3 fusion.168
  12.5 69.7 %all_gather.24 = bf16[1,4096]{1,0:T(2,128)(2,1)S(1)} all-gather(bf16[1,128]{1,0:T(2,128)(2,1)S(1)} %slice.92), channel_id=1, replica_groups=mesh['dp'=8,'fsdp'=4] {'dp','fsdp'}, dimensions={1}, use_global_device_ids=true | all-gather | bytes 8448 | tf_op jit(solution)/shard_map/all_gather | solution.py:64
  82.2 65.2 %all_gather.27 = bf16[8,4096]{1,0:T(8,128)(2,1)S(1)} all-gather(bf16[8,128]{1,0:T(8,128)(2,1)S(1)} %slice.105), channel_id=1, replica_groups=mesh['dp'=8,'fsdp'=4] {'dp','fsdp'}, dimensions={1}, use_global_device_ids=true | all-gather | bytes 67584 | tf_op jit(solution)/shard_map/all_gather | solution.py:64
  148.1 3.9 fusion.24
  153.5 2.2 fusion.175
  156.0 6.3 fusion.14
  162.2 47.2 %all-gather.11.cloned.1.call-done = bf16[1,4096,1024]{2,1,0:T(8,128)(2,1)} async-done(((bf16[1,128,1024]{2,1,0:T(8,128)(2,1)}), bf16[1,4096,1024]{2,1,0:T(8,128)(2,1)}) %all-gather.11.cloned.1.call-update) | async-done | bytes 8388624 | tf_op jit(solution)/shard_map/all_gather | solution.py:63
  209.4 5.6 fusion.176
  215.3 111.2 %all-gather.13.cloned.1.call-done = bf16[1,1024,8192]{2,1,0:T(8,128)(2,1)} async-done(((bf16[1,32,8192]{2,1,0:T(8,128)(2,1)}), bf16[1,1024,8192]{2,1,0:T(8,128)(2,1)}) %all-gather.13.cloned.1.call-update) | async-done | bytes 16777232 | tf_op jit(solution)/shard_map/all_gather | solution.py:62
  326.5 3.8 fusion.27
  333.6 2.1 fusion.178
  336.0 6.2 fusion.10
  342.1 63.3 %all-gather.15.cloned.1.call-done = bf16[1,4096,1024]{2,1,0:T(8,128)(2,1)} async-done(((bf16[1,128,1024]{2,1,0:T(8,128)(2,1)}), bf16[1,4096,1024]{2,1,0:T(8,128)(2,1)}) %all-gather.15.cloned.1.call-update) | async-done | bytes 8388624 | tf_op jit(solution)/shard_map/all_gather | solution.py:63
  405.4 8.1 fusion.43
  413.5 6.8 multiply_reduce_fusion.2
  421.4 3.2 fusion.85
  424.6 1.8 copy.72
  426.3 1.4 convolution_convert_fusion.1
  427.8 1.5 multiply_reduce_fusion.1
  430.6 5.5 multiply_reduce_fusion.3
  437.7 7.1 fusion.36
  444.9 3.2 multiply_reduce_fusion.4
  449.3 1.5 fusion.82
  450.9 1.8 copy.76
  454.1 1.5 multiply_reduce_fusion
  456.8 5.2 fusion.113
  462.4 2.0 copy.88
  465.3 9.7 fusion.135
  476.0 9.7 fusion.127
  486.8 2.6 fusion.132
  490.4 7.4 fusion.120
  497.8 9.4 fusion.163
  508.4 2.9 fusion.124
  512.4 6.4 fusion.121
  520.0 8.2 fusion.164
  529.2 6.4 fusion.88
  535.6 65.7 %reduce-scatter.31.cloned.1.call-done = f32[128,1]{1,0:T(8,128)} async-done(((f32[4096,1]{1,0:T(8,128)}), f32[128,1]{1,0:T(8,128)}) %reduce-scatter.31.cloned.1.call-update) | async-done | bytes 528
  602.2 132.8 %reduce-scatter.29.cloned.1.call-done = f32[128,8]{0,1:T(8,128)} async-done(((f32[4096,8]{0,1:T(8,128)}), f32[128,8]{0,1:T(8,128)}) %reduce-scatter.29.cloned.1.call-update) | async-done | bytes 4112 | tf_op jit(solution)/shard_map/reduce_scatter | solution.py:211
  736.3 361.9 %reduce-scatter.25.cloned.1.call-done = f32[128,1024]{1,0:T(8,128)} async-done(((f32[4096,1024]{1,0:T(8,128)}), f32[128,1024]{1,0:T(8,128)}) %reduce-scatter.25.cloned.1.call-update) | async-done | bytes 524304 | tf_op jit(solution)/shard_map/reduce_scatter | solution.py:210
  1098.3 364.5 %reduce-scatter.27.cloned.1.call-done = f32[128,1024]{1,0:T(8,128)} async-done(((f32[4096,1024]{1,0:T(8,128)}), f32[128,1024]{1,0:T(8,128)}) %reduce-scatter.27.cloned.1.call-update) | async-done | bytes 524304 | tf_op jit(solution)/shard_map/reduce_scatter | solution.py:210
  1462.7 3.2 fusion.95
  1466.0 144.8 %reduce-scatter.15.cloned.1.call-done = f32[32,1024]{1,0:T(8,128)} async-done(((f32[1024,1024]{1,0:T(8,128)}), f32[32,1024]{1,0:T(8,128)}) %reduce-scatter.15.cloned.1.call-update) | async-done | bytes 131088 | tf_op jit(solution)/shard_map/reduce_scatter | solution.py:208
  1610.8 160.2 %reduce-scatter.13.cloned.1.call-done = f32[32,3072]{1,0:T(8,128)} async-done(((f32[1024,3072]{1,0:T(8,128)}), f32[32,3072]{1,0:T(8,128)}) %reduce-scatter.13.cloned.1.call-update) | async-done | bytes 393232 | tf_op jit(solution)/shard_map/reduce_scatter | solution.py:207
  1771.0 365.7 %reduce-scatter.17.cloned.1.call-done = f32[32,4096]{1,0:T(8,128)} async-done(((f32[1024,4096]{1,0:T(8,128)}), f32[32,4096]{1,0:T(8,128)}) %reduce-scatter.17.cloned.1.call-update) | async-done | bytes 524304 | tf_op jit(solution)/shard_map/reduce_scatter | solution.py:209
  2138.0 146.8 %reduce-scatter.21.cloned.1.call-done = f32[32,1024]{1,0:T(8,128)} async-done(((f32[1024,1024]{1,0:T(8,128)}), f32[32,1024]{1,0:T(8,128)}) %reduce-scatter.21.cloned.1.call-update) | async-done | bytes 131088 | tf_op jit(solution)/shard_map/reduce_scatter | solution.py:208
  2284.8 161.2 %reduce-scatter.19.cloned.1.call-done = f32[32,3072]{1,0:T(8,128)} async-done(((f32[1024,3072]{1,0:T(8,128)}), f32[32,3072]{1,0:T(8,128)}) %reduce-scatter.19.cloned.1.call-update) | async-done | bytes 393232 | tf_op jit(solution)/shard_map/reduce_scatter | solution.py:207
  2446.0 365.5 %reduce-scatter.23.cloned.1.call-done = f32[32,4096]{1,0:T(8,128)} async-done(((f32[1024,4096]{1,0:T(8,128)}), f32[32,4096]{1,0:T(8,128)}) %reduce-scatter.23.cloned.1.call-update) | async-done | bytes 524304 | tf_op jit(solution)/shard_map/reduce_scatter | solution.py:209
  2813.4 3.3 fusion.48
  (202 shorter events, 29.9 us)
Async XLA Ops:
  7.2 2.4 copy-start.43
  7.2 4.7 copy-start.47
  7.2 140.2 %copy-start = (bf16[1,128,1024]{2,1,0:T(8,128)(2,1)S(1)}, bf16[1,128,1024]{2,1,0:T(8,128)(2,1)}, u32[]{:S(2)}) copy-start(bf16[1,128,1024]{2,1,0:T(8,128)(2,1)} %param.13) | copy-start | bytes 786436
  7.2 140.9 %all-gather.9.cloned.1.call-start = ((), (), s32[]{:S(2)}) async-start(), calls=%async_computation.19 | async-start | bytes 17301504 | tf_op jit(solution)/shard_map/all_gather | solution.py:62
  9.5 138.4 %copy-start.46 = (s32[1,128]{1,0:T(1,128)S(1)}, s32[1,128]{1,0:T(1,128)}, u32[]{:S(2)}) copy-start(s32[1,128]{1,0:T(1,128)} %param.15) | copy-start | bytes 1540
  9.6 199.8 %all-gather.11.cloned.1.call-start = ((), (), s32[]{:S(2)}) async-start(), calls=%async_computation.20 | async-start | bytes 8650752 | tf_op jit(solution)/shard_map/all_gather | solution.py:63
  10.5 316.0 %all-gather.13.cloned.1.call-start = ((), (), s32[]{:S(2)}) async-start(), calls=%async_computation.21 | async-start | bytes 17301504 | tf_op jit(solution)/shard_map/all_gather | solution.py:62
  11.2 394.2 %all-gather.15.cloned.1.call-start = ((), (), s32[]{:S(2)}) async-start(), calls=%async_computation.22 | async-start | bytes 8650752 | tf_op jit(solution)/shard_map/all_gather | solution.py:63
  11.8 589.5 %reduce-scatter.31.cloned.1.call-start = ((), (), s32[]{:S(2)}) async-start(), calls=%async_computation.23 | async-start | bytes 2162688
  152.2 1.2 copy-start.13
  153.5 8.8 copy-start.39
  155.7 53.7 %copy-start.1 = (f32[128,1024]{1,0:T(8,128)}, f32[128,1024]{1,0:T(8,128)S(1)}, u32[]{:S(2)}) copy-start(f32[128,1024]{1,0:T(8,128)S(1)} %get-tuple-element.60) | copy-start | bytes 1572868
  330.6 2.3 copy-start.17
  330.7 2.1 copy-start.19
  413.5 6.8 copy-start.23
  413.5 7.9 copy-start.9
  427.8 2.8 copy-start.28
  427.8 1.8 copy-start.20
  429.3 15.5 slice-start
  430.3 5.8 copy-start.30
  430.5 5.6 copy-start.32
  430.6 5.9 copy-start.6
  430.6 5.9 copy-start.10
  430.6 14.2 slice-start.1
  436.1 1.6 copy-start.8
  437.7 7.1 copy-start.2
  437.7 7.1 slice-start.2
  437.7 7.1 slice-start.3
  444.9 3.2 copy-start.25
  454.1 2.8 copy-start.34
  454.1 1.8 copy-start.16
  456.8 5.2 copy-start.36
  464.4 270.6 %reduce-scatter.29.cloned.1.call-start = ((), (), s32[]{:S(2)}) async-start(), calls=%async_computation.18 | async-start | bytes 135168 | tf_op jit(solution)/shard_map/reduce_scatter | solution.py:211
  465.3 633.0 %reduce-scatter.25.cloned.1.call-start = ((), (), s32[]{:S(2)}) async-start(), calls=%async_computation.16 | async-start | bytes 17301504 | tf_op jit(solution)/shard_map/reduce_scatter | solution.py:210
  475.0 987.7 %reduce-scatter.27.cloned.1.call-start = ((), (), s32[]{:S(2)}) async-start(), calls=%async_computation.17 | async-start | bytes 17301504 | tf_op jit(solution)/shard_map/reduce_scatter | solution.py:210
  485.7 1125.1 %reduce-scatter.15.cloned.1.call-start = ((), (), s32[]{:S(2)}) async-start(), calls=%async_computation.11 | async-start | bytes 4325376 | tf_op jit(solution)/shard_map/reduce_scatter | solution.py:208
  489.4 1281.6 %reduce-scatter.13.cloned.1.call-start = ((), (), s32[]{:S(2)}) async-start(), calls=%async_computation.10 | async-start | bytes 12976128 | tf_op jit(solution)/shard_map/reduce_scatter | solution.py:207
  497.8 1639.0 %reduce-scatter.17.cloned.1.call-start = ((), (), s32[]{:S(2)}) async-start(), calls=%async_computation.12 | async-start | bytes 17301504 | tf_op jit(solution)/shard_map/reduce_scatter | solution.py:209
  507.2 1777.6 %reduce-scatter.21.cloned.1.call-start = ((), (), s32[]{:S(2)}) async-start(), calls=%async_computation.14 | async-start | bytes 4325376 | tf_op jit(solution)/shard_map/reduce_scatter | solution.py:208
  511.3 1934.7 %reduce-scatter.19.cloned.1.call-start = ((), (), s32[]{:S(2)}) async-start(), calls=%async_computation.13 | async-start | bytes 12976128 | tf_op jit(solution)/shard_map/reduce_scatter | solution.py:207
  518.8 1.2 copy-start.24
  518.8 2292.7 %reduce-scatter.23.cloned.1.call-start = ((), (), s32[]{:S(2)}) async-start(), calls=%async_computation.15 | async-start | bytes 17301504 | tf_op jit(solution)/shard_map/reduce_scatter | solution.py:209
  529.2 205.8 %copy-start.44 = (f32[9,128]{1,0:T(8,128)S(1)}, f32[9,128]{1,0:T(8,128)}, u32[]{:S(2)}) copy-start(f32[9,128]{1,0:T(8,128)} %param.25) | copy-start | bytes 13828
  529.2 205.8 %copy-start.45 = (f32[9,128]{1,0:T(8,128)S(1)}, f32[9,128]{1,0:T(8,128)}, u32[]{:S(2)}) copy-start(f32[9,128]{1,0:T(8,128)} %param.22) | copy-start | bytes 13828
  529.2 933.5 %copy-start.37 = (f32[2,128,1024]{2,1,0:T(8,128)S(1)}, f32[2,128,1024]{2,1,0:T(8,128)}, u32[]{:S(2)}) copy-start(f32[2,128,1024]{2,1,0:T(8,128)} %param.24) | copy-start | bytes 3145732
  529.2 933.5 %copy-start.38 = (f32[2,128,1024]{2,1,0:T(8,128)S(1)}, f32[2,128,1024]{2,1,0:T(8,128)}, u32[]{:S(2)}) copy-start(f32[2,128,1024]{2,1,0:T(8,128)} %param.21) | copy-start | bytes 3145732
  1466.0 1346.9 %copy-start.21 = (f32[2,32,8192]{2,1,0:T(8,128)S(1)}, f32[2,32,8192]{2,1,0:T(8,128)}, u32[]{:S(2)}) copy-start(f32[2,32,8192]{2,1,0:T(8,128)} %param.23) | copy-start | bytes 6291460
  2811.5 1.9 copy-start.22
  (18 other events, 17.5 us)
Sparse Core Ops, SparseCore 0:
  11.6 118.3 all-gather.8
  133.5 75.8 all-gather.10
  213.0 113.4 all-gather.12
  329.8 75.5 all-gather.14
  464.5 136.7 reduce-scatter.30
  603.5 131.4 reduce-scatter.28
  737.3 360.9 reduce-scatter.24
  1100.6 362.1 reduce-scatter.26
  1465.0 145.7 reduce-scatter.14
  1616.7 154.3 reduce-scatter.12
  1773.4 363.2 reduce-scatter.16
  2139.0 145.7 reduce-scatter.20
  2291.9 154.1 reduce-scatter.18
  2448.2 363.2 reduce-scatter.22
where the time goes:
time: 2830 us; the launch traced here: 2820 us
  waiting for transfers between devices  2490 us (88%)
  matrix products  142 us (5%)
  blocking collectives  135 us (5%)
    reduce_scatter x2, waiting for transfers between devices, reduce_gradients(): lax.psum_scatter(layer_grads[2], ('dp', 'fsdp'), scatter_dimension=0, til...  731 us
    reduce_scatter x2, waiting for transfers between devices, reduce_gradients(): lax.psum_scatter(layer_grads[3], ('dp', 'fsdp'), scatter_dimension=0, til...  726 us
    reduce_scatter x2, waiting for transfers between devices, reduce_gradients(): lax.psum_scatter(layer_grads[0], ('dp', 'fsdp'), scatter_dimension=0, til...  321 us
    reduce_scatter x2, waiting for transfers between devices, reduce_gradients(): lax.psum_scatter(layer_grads[1], ('dp', 'fsdp'), scatter_dimension=0, til...  292 us
    all_gather x2, blocking collectives, fetch_forward(): lax.all_gather(table_part, ('dp', 'fsdp'), axis=1, tiled=True)  135 us
    reduce_scatter x1, waiting for transfers between devices, reduce_gradients(): lax.psum_scatter(layer_grads[4].astype(jnp.float32), ('dp', 'fsdp'), scat...  133 us
    all_gather x2, waiting for transfers between devices, fetch_forward(): lax.all_gather(w_big[layer_index], ('dp', 'fsdp'), axis=0, tiled=True)  111 us
    all_gather x2, waiting for transfers between devices, fetch_forward(): lax.all_gather(w_down[layer_index], ('dp', 'fsdp'), axis=0, tiled=True)  110 us
  transfers between devices with their start and end apart: 14, of which 13 were waited for; matrix products, arithmetic and copies ran while one was open for 4% of the time, Pallas kernels for 0%

commit v1 on v0

v1 whole, which is shorter than its diff:
```python
from functools import partial

import jax
import jax.numpy as jnp
from jax import lax
from jax.sharding import PartitionSpec as P

HEADS = 16

beta_one = 0.9
beta_two = 0.999
first_fix = 1.0 - 0.9**10
second_fix = 1.0 - 0.999**10

f32 = jnp.float32
bf16 = jnp.bfloat16

CORE = ("dp", 1)
SIDE = ("dp", 2)


def masks(size):
    return [1 << k for k in reversed(range(size.bit_length() - 1))]


class Slice:
    def __init__(self, dp, fsdp):
        self.dp, self.fsdp = dp, fsdp
        self.high = [("dp", m) for m in masks(dp) if m > 2]
        self.deep = [("fsdp", m) for m in masks(fsdp)]
        self.order = self.high + [SIDE, CORE] + self.deep
        self.size = {"dp": dp, "fsdp": fsdp}

    def flip(self, value, bit):
        axis, mask = bit
        return lax.ppermute(value, axis, [(i, i ^ mask) for i in range(self.size[axis])])

    def place(self, bit, have):
        return sum(self.order.index(b) < self.order.index(bit) for b in have)


def mine(bit):
    axis, mask = bit
    return (lax.axis_index(axis) // mask) % 2


def merge(own, other, bit, pos):
    side = mine(bit)
    return jnp.where(side == 0, jnp.stack([own, other], pos), jnp.stack([other, own], pos))


def gather(sl, value, bits, have=()):
    have = list(have)
    for bit in bits:
        value = merge(value, sl.flip(value, bit), bit, sl.place(bit, have))
        have.append(bit)
    return value


def split(value, bit, pos):
    side = mine(bit)
    keep = lax.dynamic_index_in_dim(value, side, pos, keepdims=False)
    send = lax.dynamic_index_in_dim(value, 1 - side, pos, keepdims=False)
    return keep, send


def scatter(sl, value, bits, have):
    have, kind = list(have), value.dtype
    for n, bit in enumerate(bits):
        keep, send = split(value, bit, sl.place(bit, have))
        have.remove(bit)
        value = keep.astype(f32) + sl.flip(send, bit).astype(f32)
        if n < len(bits) - 1:
            value = value.astype(kind)
    return value


def dot(left, right):
    return jnp.dot(left, right, preferred_element_type=f32)


def contract_rows(left, right):
    return lax.dot_general(left, right, (((0,), (0,)), ((), ())), preferred_element_type=f32)


def times_transposed(left, right):
    return lax.dot_general(left, right, (((1,), (1,)), ((), ())), preferred_element_type=f32)


def norm(hidden):
    centred = hidden - jnp.mean(hidden, axis=-1, keepdims=True)
    scale = lax.rsqrt(jnp.mean(centred * centred, axis=-1, keepdims=True) + 1e-05)
    return centred * scale, scale


def norm_back(hidden, grad, gain):
    normed, scale = norm(hidden)
    e = grad * gain
    part = scale * (
        e
        - jnp.mean(e, axis=-1, keepdims=True)
        - normed * jnp.mean(e * normed, axis=-1, keepdims=True)
    )
    return part, jnp.sum(grad * normed, axis=0), jnp.sum(grad, axis=0)


def rows_of_pair(sl, value):
    return jnp.concatenate([value, sl.flip(value, CORE)], 0)


def rows_of_four(sl, value):
    two = jnp.concatenate([value, sl.flip(value, SIDE)], 0)
    return jnp.concatenate([two, sl.flip(two, CORE)], 0)


def sum_pair(sl, value):
    n = value.shape[0] // 2
    return value[:n] + sl.flip(value[n:], CORE)


def sum_four(sl, value):
    two = sum_pair(sl, value)
    n = two.shape[0] // 2
    return two[:n] + sl.flip(two[n:].astype(bf16), SIDE).astype(f32)


def allowed_of(segments, causal):
    allowed = segments[:, :, None] == segments[:, None, :]
    if causal:
        position = jnp.arange(segments.shape[1])
        allowed = allowed & (position[:, None] >= position[None, :])
    return allowed


def probs_of(q, k, allowed):
    scores = jnp.einsum("rqhe,rkhe->rhqk", q, k, preferred_element_type=f32) * (
        q.shape[-1] ** -0.5
    )
    scores = jnp.where(allowed[:, None], scores, -1e30)
    exponent = jnp.exp(scores - jnp.max(scores, axis=-1, keepdims=True))
    return exponent / jnp.sum(exponent, axis=-1, keepdims=True)


def heads_of(projected, length):
    tokens, width = projected.shape
    parts = projected.reshape(tokens // length, length, 3, HEADS // 2, width // 3 // (HEADS // 2))
    return parts[:, :, 0], parts[:, :, 1], parts[:, :, 2]


def attend(projected, allowed):
    q, k, v = heads_of(projected, allowed.shape[1])
    probs = probs_of(q, k, allowed)
    mixed = jnp.einsum("rhqk,rkhe->rqhe", probs.astype(bf16), v, preferred_element_type=f32)
    return mixed.astype(bf16).reshape(projected.shape[0], -1)


def attend_back(projected, allowed, d_mixed):
    q, k, v = heads_of(projected, allowed.shape[1])
    d_mixed = d_mixed.reshape(q.shape)
    probs = probs_of(q, k, allowed)
    d_probs = jnp.einsum("rqhe,rkhe->rhqk", d_mixed, v, preferred_element_type=f32)
    d_v = jnp.einsum("rhqk,rqhe->rkhe", probs.astype(bf16), d_mixed, preferred_element_type=f32)
    d_scores = probs * (d_probs - jnp.sum(probs * d_probs, axis=-1, keepdims=True))
    d_scores = d_scores.astype(bf16)
    size = q.shape[-1] ** -0.5
    d_q = jnp.einsum("rhqk,rkhe->rqhe", d_scores, k, preferred_element_type=f32) * size
    d_k = jnp.einsum("rhqk,rqhe->rkhe", d_scores, q, preferred_element_type=f32) * size
    out = jnp.stack([d_q, d_k, d_v], 2).astype(bf16)
    return out.reshape(projected.shape)


def forward(sl, hidden, weights, gains, allowed):
    w_qkv, w_out, w_up, w_down = weights
    first = (norm(hidden)[0] * gains[0] + gains[1]).astype(bf16)
    first = rows_of_pair(sl, first)
    projected = dot(first, w_qkv).astype(bf16)
    mixed = attend(projected, allowed)
    attended = hidden + sum_pair(sl, dot(mixed, w_out))
    second = (norm(attended)[0] * gains[2] + gains[3]).astype(bf16)
    second = rows_of_four(sl, second)
    pre = dot(second, w_up)
    active = jax.nn.gelu(pre).astype(bf16)
    output = attended + sum_four(sl, dot(active, w_down))
    return output, (hidden, first, projected, mixed, attended, second, pre, active)


def backward(sl, d_out, weights, gains, allowed, stored):
    w_qkv, w_out, w_up, w_down = weights
    hidden, first, projected, mixed, attended, second, pre, active = stored
    d_branch = rows_of_four(sl, d_out.astype(bf16))
    g_down = contract_rows(active, d_branch).astype(bf16)
    d_active = times_transposed(d_branch, w_down)
    d_pre = jax.vjp(jax.nn.gelu, pre)[1](d_active)[0].astype(bf16)
    g_up = contract_rows(second, d_pre).astype(bf16)
    d_second = sum_four(sl, times_transposed(d_pre, w_up))
    part, d_gain2, d_shift2 = norm_back(attended, d_second, gains[2])
    d_attended = d_out + part
    d_mix_in = rows_of_pair(sl, d_attended.astype(bf16))
    g_out = contract_rows(mixed, d_mix_in).astype(bf16)
    d_mixed = times_transposed(d_mix_in, w_out).astype(bf16)
    d_projected = attend_back(projected, allowed, d_mixed)
    g_qkv = contract_rows(first, d_projected).astype(bf16)
    d_first = sum_pair(sl, times_transposed(d_projected, w_qkv))
    part, d_gain1, d_shift1 = norm_back(hidden, d_first, gains[0])
    g_table = jnp.concatenate([d_gain1, d_shift1, d_gain2, d_shift2])
    return d_attended + part, (g_qkv, g_out, g_up, g_down, g_table)


def adam_update(moment, square, gradient):
    moment = beta_one * moment + (1.0 - beta_one) * gradient
    square = beta_two * square + (1.0 - beta_two) * gradient * gradient
    update = moment / first_fix / (jnp.sqrt(square / second_fix) + 1e-08)
    return (moment, update)


def body(
    dp,
    fsdp,
    inputs,
    cotangent,
    segment_ids,
    section_ids,
    w_big,
    w_down,
    norm_table,
    m_big,
    m_down,
    m_table,
    v_big,
    v_down,
    v_table,
):
    sl = Slice(dp, fsdp)
    width = inputs.shape[-1]
    rows = w_big.shape[1]
    feeds = w_down.shape[1]
    feed = w_big.shape[2] - 4 * width
    high = dp // 4
    two = 2 * [2]

    qkv = w_big[:, :, : 3 * width].reshape(2, rows, 3, 2 * high, 2, fsdp * rows)
    up = w_big[:, :, 4 * width :].reshape(2, rows, high, 2, 2, fsdp * feeds)
    qkv_keep, qkv_send = split(qkv, CORE, 4)
    up_keep, up_send = split(up, CORE, 4)
    half = 3 * width // 2

    def side_by_side(a, b):
        return jnp.concatenate([a.reshape(2, rows, half), b.reshape(2, rows, feed // 2)], 2)

    pair = merge(
        side_by_side(qkv_keep, up_keep),
        sl.flip(side_by_side(qkv_send, up_send), CORE),
        CORE,
        1,
    )
    out_proj = w_big[:, :, 3 * width : 4 * width].reshape(2, rows, 2, width // 2)
    attn_own = jnp.concatenate([pair[..., :half], jnp.swapaxes(out_proj, 1, 2)], -1)
    up_pair = pair[..., half:].reshape(2, 2, rows, high, 2, fsdp * feeds)
    up_keep, up_send = split(up_pair, SIDE, 4)
    up_own = merge(up_keep, sl.flip(up_send, SIDE), SIDE, 1).reshape(2, *two, rows, feed // 4)

    table = gather(sl, norm_table, [CORE] + sl.deep + sl.high + [SIDE])
    table = table.reshape(dp * fsdp, *norm_table.shape)
    table = jnp.swapaxes(table, 0, 1).reshape(norm_table.shape[0], 4, width).astype(f32)
    section = section_ids[0]
    gains_all = (table[0], lax.dynamic_index_in_dim(table, 1 + section, 0, keepdims=False))

    attn_orders = (sl.deep + sl.high + [SIDE], sl.high + sl.deep + [SIDE])
    feed_order = sl.deep + sl.high

    def fetch(layer):
        attn = gather(sl, attn_own[layer], attn_orders[layer], [CORE])
        attn = attn.reshape(2 * high, 2, fsdp * rows, 2 * width)
        w_qkv = attn[..., :half].reshape(width, half)
        w_out = jnp.swapaxes(attn[..., half:], 1, 2).reshape(width // 2, width)
        w_up = gather(sl, up_own[layer], feed_order, [SIDE, CORE]).reshape(width, feed // 4)
        w_dn = gather(sl, w_down[layer], feed_order).reshape(feed // 4, width)
        return w_qkv, w_out, w_up, w_dn

    weights = [fetch(0), fetch(1)]
    segments = rows_of_pair(sl, segment_ids.astype(f32))
    hidden = inputs[0].astype(f32)
    stored = [None, None]
    allowed = [allowed_of(segments, layer == 0) for layer in range(2)]
    for layer in range(2):
        hidden, stored[layer] = forward(
            sl, hidden, weights[layer], gains_all[layer], allowed[layer]
        )
    out_act = hidden.astype(bf16)
    grad = cotangent[0].astype(f32)
    big, down, tables = [None, None], [None, None], [None, None]
    bits = sl.high + [SIDE]
    for layer in (1, 0):
        grad, (g_qkv, g_out, g_up, g_down, g_table) = backward(
            sl, grad, weights[layer], gains_all[layer], allowed[layer], stored[layer]
        )
        nh, nz = len(sl.high), len(sl.deep)
        feed_back = feed_order[::-1]
        attn_back = attn_orders[layer][::-1]
        g_down = g_down.reshape(*(nh + nz) * [2], feeds, width)
        down[layer] = scatter(sl, g_down, feed_back, feed_order)
        g_up = g_up.reshape(*(nh + 2 + nz) * [2], rows, feed // 4)
        g_up = scatter(sl, g_up, feed_back, sl.order)
        g_up = g_up.reshape(*two, rows, high, fsdp * feeds)
        keep, send = split(g_up, SIDE, 0)
        g_up = merge(keep, sl.flip(send, SIDE), SIDE, 3)
        keep, send = split(g_up, CORE, 0)
        g_up = merge(keep, sl.flip(send, CORE), CORE, 3).reshape(rows, feed)
        g_out = g_out.reshape(*(nh + 1 + nz) * [2], rows, width)
        g_out = scatter(sl, g_out, attn_back, attn_back)
        g_qkv = g_qkv.reshape(*(nh + 2 + nz) * [2], rows, half)
        g_qkv = scatter(sl, g_qkv, attn_back, sl.order)
        g_qkv = g_qkv.reshape(2, rows, 3, 2 * high, fsdp * rows)
        keep, send = split(g_qkv, CORE, 0)
        g_qkv = merge(keep, sl.flip(send, CORE), CORE, 3).reshape(rows, 3 * width)
        big[layer] = jnp.concatenate([g_qkv, g_out, g_up], 1)
        if layer == 0:
            g_table = g_table[None]
        else:
            count = norm_table.shape[0] - 1
            g_table = jnp.where((jnp.arange(count) == section)[:, None], g_table[None], 0.0)
        g_table = jnp.swapaxes(g_table.reshape(-1, dp * fsdp, norm_table.shape[1]), 0, 1)
        g_table = g_table.reshape(*(nh + 2 + nz) * [2], *g_table.shape[1:])
        tables[layer] = scatter(sl, g_table, [CORE] + attn_back, sl.order)
    grad_big = jnp.stack(big)
    grad_down = jnp.stack(down)
    grad_table = jnp.concatenate(tables, 0)
    new_m_big, step_big = adam_update(m_big, v_big, grad_big)
    new_m_down, step_down = adam_update(m_down, v_down, grad_down)
    new_m_table, step_table = adam_update(m_table, v_table, grad_table)
    return (
        out_act[None],
        grad.astype(bf16)[None],
        grad_big,
        grad_down,
        grad_table,
        new_m_big,
        new_m_down,
        new_m_table,
        step_big,
        step_down,
        step_table,
    )


def solution(mesh):
    both = ("dp", "fsdp")
    rows, middle, last = P(both, None, None), P(None, both, None), P(None, both)
    return jax.shard_map(
        partial(body, mesh.shape["dp"], mesh.shape["fsdp"]),
        mesh=mesh,
        in_specs=(rows, rows, P(both, None), P(both), middle, middle, last)
        + 2 * (middle, middle, last),
        out_specs=(rows, rows) + 3 * (middle, middle, last),
        check_vma=False,
    )
```

time: 2830 us -> 712 us (0.25)
  waiting for transfers between devices: 2490 us -> 362 us
  blocking collectives: 135 us -> 0 us
  starting transfers between devices: 1.04 us -> 97 us
  matrix products: 142 us -> 48.2 us
  other arithmetic: 15.7 us -> 99.5 us
  local copies, waits for them, and re-layouts: 21.8 us -> 90 us
    reduce_scatter x9 -> x0, waiting for transfers between devices: 2200 us -> none  [the longest x2 731 us: reduce_gradients(): lax.psum_scatter(layer_grads[2], ('dp', 'fsdp'), scatter_dimension=0, til...]
    ppermute x0 -> x96, waiting for transfers between devices: none -> 362 us  [flip(): lax.ppermute(value, axis, [(i, i ^ mask) for i in range(self.size[axis])])]
    all_gather x4 -> x0, waiting for transfers between devices: 222 us -> none  [the longest x2 111 us: fetch_forward(): lax.all_gather(w_big[layer_index], ('dp', 'fsdp'), axis=0, tiled=True)]
    all_gather x2 -> x0, blocking collectives: 135 us -> none  [fetch_forward(): lax.all_gather(table_part, ('dp', 'fsdp'), axis=1, tiled=True)]
    ppermute x0 -> x96, starting transfers between devices: none -> 97 us  [flip(): lax.ppermute(value, axis, [(i, i ^ mask) for i in range(self.size[axis])])]
    unnamed x15 -> x0, waiting for transfers between devices: 67.1 us -> none
    select_n x0 -> x53, other arithmetic: none -> 42.9 us  [the longest x52 42.9 us: merge(): jnp.where(side == 0, jnp.stack([own, other], pos), jnp.stack([other, own]...]
    dot_general x8, matrix products: 56.3 us -> 14.3 us  [contract_rows(): lax.dot_general(left, right, (((0,), (0,)), ((), ())), preferred_element_...]
  transfers between devices with their start and end apart: 14 -> 96, of which waited for: 13 -> 40; matrix products, arithmetic and copies ran while one was open for 4% -> 29% of each run, Pallas kernels for 0% -> 0%
where the time goes in v1:
time: 712 us; the launch traced here: 701 us
  waiting for transfers between devices  362 us (51%)
  other arithmetic  99.5 us (14%)
  starting transfers between devices  97 us (14%)
  local copies, waits for them, and re-layouts  90 us (13%)
  matrix products  48.2 us (7%)
    ppermute x96, waiting for transfers between devices, flip(): lax.ppermute(value, axis, [(i, i ^ mask) for i in range(self.size[axis])])  362 us
    ppermute x96, starting transfers between devices, flip(): lax.ppermute(value, axis, [(i, i ^ mask) for i in range(self.size[axis])])  97 us
    select_n x52, other arithmetic, merge(): jnp.where(side == 0, jnp.stack([own, other], pos), jnp.stack([other, own]...  42.9 us
    unnamed x260, local copies, waits for them, and re-layouts  24.7 us
    convert_element_type x20, other arithmetic, scatter(): value = value.astype(kind)  16.1 us
    dot_general x8, matrix products, contract_rows(): lax.dot_general(left, right, (((0,), (0,)), ((), ())), preferred_element_...  14.3 us
    dot_general x8, matrix products, times_transposed(): lax.dot_general(left, right, (((1,), (1,)), ((), ())), preferred_element_...  14.3 us
  transfers between devices with their start and end apart: 96, of which 40 were waited for; matrix products, arithmetic and copies ran while one was open for 29% of the time, Pallas kernels for 0%

profile of v1, /device:TPU:0, one launch (start us, length us, event | category | flops | bytes accessed | tf_op | source)
XLA Modules:
  0.0 701.5 jit_solution(16037063213084259527)
XLA Ops:
  2.1 3.6 dynamic-slice_reduce_fusion.1
  6.2 2.4 dynamic-slice_reduce_fusion.3
  11.7 3.7 collective-permute-start.19
  17.0 3.0 collective-permute-start.1
  20.0 19.7 %collective-permute-done.1 = bf16[2,9,128]{2,1,0:T(8,128)(2,1)S(1)} collective-permute-done((bf16[2,9,128]{2,1,0:T(8,128)(2,1)S(1)}, bf16[2,9,128]{2,1,0:T(8,128)(2,1)S(1)}, u32[]{:S(2)}, u32[]{:S(2)}) %collective-permute-start.1) | collective-permute-done | bytes 4640 | tf_op jit(solution)/shard_map/ppermute | solution.py:36
  40.5 3.0 collective-permute-done.2
  49.1 2.7 collective-permute-done.4
  64.3 7.4 %collective-permute-done.7 = bf16[2,32,2048]{2,1,0:T(8,128)(2,1)S(1)} collective-permute-done((bf16[2,32,2048]{2,1,0:T(8,128)(2,1)}, bf16[2,32,2048]{2,1,0:T(8,128)(2,1)S(1)}, u32[]{:S(2)}, u32[]{:S(2)}) %collective-permute-start.7) | collective-permute-done | bytes 262176 | tf_op jit(solution)/shard_map/ppermute | solution.py:36
  76.0 13.5 %collective-permute-done.8 = bf16[2,2,32,2048]{3,2,0,1:T(8,128)(2,1)S(1)} collective-permute-done((bf16[2,2,32,2048]{3,2,0,1:T(8,128)(2,1)S(1)}, bf16[2,2,32,2048]{3,2,0,1:T(8,128)(2,1)S(1)}, u32[]{:S(2)}, u32[]{:S(2)}) %collective-permute-start.8) | collective-permute-done | bytes 524320 | tf_op jit(solution)/shard_map/ppermute | solution.py:36
  95.8 19.9 %collective-permute-done.9 = bf16[2,2,2,32,2048]{4,3,0,1,2:T(8,128)(2,1)} collective-permute-done((bf16[2,2,2,32,2048]{4,3,0,1,2:T(8,128)(2,1)}, bf16[2,2,2,32,2048]{4,3,0,1,2:T(8,128)(2,1)}, u32[]{:S(2)}, u32[]{:S(2)}) %collective-permute-start.9) | collective-permute-done | bytes 1048608 | tf_op jit(solution)/shard_map/ppermute | solution.py:36
  115.7 3.2 maximum_select_fusion.2
  135.2 30.3 %collective-permute-done.10 = bf16[2,2,2,2,32,2048]{5,4,0,1,2,3:T(8,128)(2,1)} collective-permute-done((bf16[2,2,2,2,32,2048]{5,4,0,1,2,3:T(8,128)(2,1)}, bf16[2,2,2,2,32,2048]{5,4,0,1,2,3:T(8,128)(2,1)}, u32[]{:S(2)}, u32[]{:S(2)}) %collective-permute-start.10) | collective-permute-done | bytes 2097184 | tf_op jit(solution)/shard_map/ppermute | solution.py:36
  165.7 2.8 maximum_select_fusion
  171.9 2.9 convolution_convert_fusion.3
  174.7 2.6 reshape.2163
  195.6 6.2 collective-permute-done.13
  205.3 9.4 %collective-permute-done.27 = bf16[2,2,2,32,2048]{4,3,0,1,2:T(8,128)(2,1)S(1)} collective-permute-done((bf16[2,2,2,32,2048]{4,3,0,1,2:T(8,128)(2,1)S(1)}, bf16[2,2,2,32,2048]{4,3,0,1,2:T(8,128)(2,1)S(1)}, u32[]{:S(2)}, u32[]{:S(2)}) %collective-permute-start.27) | collective-permute-done | bytes 1048608 | tf_op jit(solution)/shard_map/ppermute | solution.py:36
  224.3 2.9 collective-permute-start.32
  233.4 6.5 collective-permute-done.32
  244.6 20.7 %collective-permute-done.28 = bf16[2,2,2,2,32,2048]{5,4,0,1,2,3:T(8,128)(2,1)} collective-permute-done((bf16[2,2,2,2,32,2048]{5,4,0,1,2,3:T(8,128)(2,1)}, bf16[2,2,2,2,32,2048]{5,4,0,1,2,3:T(8,128)(2,1)}, u32[]{:S(2)}, u32[]{:S(2)}) %collective-permute-start.28) | collective-permute-done | bytes 2097184 | tf_op jit(solution)/shard_map/ppermute | solution.py:36
  265.3 2.9 maximum_select_fusion.1
  275.2 2.8 reshape.2164
  299.6 4.6 collective-permute-done.30
  305.8 11.6 %collective-permute-done.37 = bf16[2,2,128,1024]{3,2,0,1:T(8,128)(2,1)S(1)} collective-permute-done((bf16[2,2,128,1024]{3,2,0,1:T(8,128)(2,1)S(1)}, bf16[2,2,128,1024]{3,2,0,1:T(8,128)(2,1)S(1)}, u32[]{:S(2)}, u32[]{:S(2)}) %collective-permute-start.37) | collective-permute-done | bytes 1048608 | tf_op jit(solution)/shard_map/ppermute | solution.py:36
  317.9 21.0 %collective-permute-done.34 = bf16[2,2,2,2,32,1024]{5,4,1,0,2,3:T(8,128)(2,1)S(1)} collective-permute-done((bf16[2,2,2,2,32,1024]{5,4,1,0,2,3:T(8,128)(2,1)S(1)}, bf16[2,2,2,2,32,1024]{5,4,1,0,2,3:T(8,128)(2,1)S(1)}, u32[]{:S(2)}, u32[]{:S(2)}) %collective-permute-start.34) | collective-permute-done | bytes 1048608 | tf_op jit(solution)/shard_map/ppermute | solution.py:36
  340.8 3.5 fusion.17
  351.5 4.0 convolution_convert_fusion.4
  358.0 6.9 collective-permute-done.43
  365.2 4.0 collective-permute-done.39
  371.4 3.5 collective-permute-done.75
  390.9 2.8 collective-permute-start.77
  400.0 31.3 %collective-permute-done.92 = f32[2,2,2,8,128]{4,3,0,1,2:T(8,128)S(1)} collective-permute-done((f32[2,2,2,8,128]{4,3,0,1,2:T(8,128)S(1)}, f32[2,2,2,8,128]{4,3,0,1,2:T(8,128)S(1)}, u32[]{:S(2)}, u32[]{:S(2)}) %collective-permute-start.92) | collective-permute-done | bytes 32800 | tf_op jit(solution)/shard_map/ppermute | solution.py:36
  437.3 2.4 collective-permute-done.94
  444.2 5.2 fusion.10
  455.3 2.5 convolution_convert_fusion.5
  465.7 14.1 %collective-permute-done.61 = bf16[2,2,2,2,32,1024]{5,4,1,0,2,3:T(8,128)(2,1)S(1)} collective-permute-done((bf16[2,2,2,2,32,1024]{5,4,1,0,2,3:T(8,128)(2,1)S(1)}, bf16[2,2,2,2,32,1024]{5,4,1,0,2,3:T(8,128)(2,1)S(1)}, u32[]{:S(2)}, u32[]{:S(2)}) %collective-permute-start.61) | collective-permute-done | bytes 1048608 | tf_op jit(solution)/shard_map/ppermute | solution.py:36
  483.4 18.9 %collective-permute-done.83 = bf16[2,2,128,1024]{3,2,0,1:T(8,128)(2,1)S(1)} collective-permute-done((bf16[2,2,128,1024]{3,2,0,1:T(8,128)(2,1)S(1)}, bf16[2,2,128,1024]{3,2,0,1:T(8,128)(2,1)S(1)}, u32[]{:S(2)}, u32[]{:S(2)}) %collective-permute-start.83) | collective-permute-done | bytes 1048608 | tf_op jit(solution)/shard_map/ppermute | solution.py:36
  504.7 18.6 %collective-permute-done.80 = bf16[2,2,128,1024]{3,2,0,1:T(8,128)(2,1)S(1)} collective-permute-done((bf16[2,2,128,1024]{3,2,0,1:T(8,128)(2,1)S(1)}, bf16[2,2,128,1024]{3,2,0,1:T(8,128)(2,1)S(1)}, u32[]{:S(2)}, u32[]{:S(2)}) %collective-permute-start.80) | collective-permute-done | bytes 1048608 | tf_op jit(solution)/shard_map/ppermute | solution.py:36
  575.1 9.1 %collective-permute-done.85 = bf16[128,1024]{1,0:T(8,128)(2,1)} collective-permute-done((bf16[128,1024]{1,0:T(8,128)(2,1)}, bf16[128,1024]{1,0:T(8,128)(2,1)}, u32[]{:S(2)}, u32[]{:S(2)}) %collective-permute-start.85) | collective-permute-done | bytes 262176 | tf_op jit(solution)/shard_map/ppermute | solution.py:36
  586.7 2.6 collective-permute-done.82
  594.0 31.4 %collective-permute-done.78 = f32[2,32,2,512]{3,1,2,0:T(8,128)S(1)} collective-permute-done((f32[2,32,2,512]{3,1,2,0:T(8,128)S(1)}, f32[2,32,2,512]{3,1,2,0:T(8,128)S(1)}, u32[]{:S(2)}, u32[]{:S(2)}) %collective-permute-start.78) | collective-permute-done | bytes 262176 | tf_op jit(solution)/shard_map/ppermute | solution.py:36
  636.1 3.1 collective-permute-done.88
  642.9 2.7 collective-permute-start.90
  649.2 2.6 collective-permute-start.73
  661.0 11.8 %collective-permute-done.53 = bf16[2,2,2,32,1536]{4,3,2,1,0:T(8,128)(2,1)} collective-permute-done((bf16[2,2,2,32,1536]{4,3,2,1,0:T(8,128)(2,1)}, bf16[2,2,2,32,1536]{4,3,2,1,0:T(8,128)(2,1)}, u32[]{:S(2)}, u32[]{:S(2)}) %collective-permute-start.53) | collective-permute-done | bytes 786464 | tf_op jit(solution)/shard_map/ppermute | solution.py:36
  676.3 8.2 %collective-permute-done.54 = bf16[2,2,32,1536]{3,2,1,0:T(8,128)(2,1)S(1)} collective-permute-done((bf16[2,2,32,1536]{3,2,1,0:T(8,128)(2,1)S(1)}, bf16[2,2,32,1536]{3,2,1,0:T(8,128)(2,1)S(1)}, u32[]{:S(2)}, u32[]{:S(2)}) %collective-permute-start.54) | collective-permute-done | bytes 393248 | tf_op jit(solution)/shard_map/ppermute | solution.py:36
  686.6 5.5 collective-permute-done.55
  696.4 4.9 fusion.22
  (736 shorter events, 288.4 us)
Async XLA Ops:
  9.6 43.5 %collective-permute-start.6 = (bf16[2,32,3584]{2,1,0:T(8,128)(2,1)}, bf16[2,32,3584]{2,1,0:T(8,128)(2,1)S(1)}, u32[]{:S(2)}, u32[]{:S(2)}) collective-permute-start(bf16[2,32,3584]{2,1,0:T(8,128)(2,1)} %pad_maximum_fusion.20), channel_id=1, source_target_pairs={{0,4},{4,0},{8,12},{12,8},{16,20},{20,16},{24,28},{28,24},{1,5},{5... | collective-permute-start | bytes 1376264 | tf_op jit(solution)/shard_map/ppermute | solution.py:36
  11.7 46.5 %collective-permute-start.19 = (bf16[128,1024]{1,0:T(8,128)(2,1)}, bf16[128,1024]{1,0:T(8,128)(2,1)S(1)}, u32[]{:S(2)}, u32[]{:S(2)}) collective-permute-start(bf16[128,1024]{1,0:T(8,128)(2,1)} %get-tuple-element.89), channel_id=1, source_target_pairs={{0,2},{1,3},{2,0},{3,1},{4,6},{5,7},{6,4},{7,5},{8,10},{9,11},{10,... | collective-permute-start | bytes 786440 | tf_op jit(solution)/shard_map/ppermute | solution.py:36
  15.3 211.9 %collective-permute-start.35 = (bf16[128,1024]{1,0:T(8,128)(2,1)}, bf16[128,1024]{1,0:T(8,128)(2,1)}, u32[]{:S(2)}, u32[]{:S(2)}) collective-permute-start(bf16[128,1024]{1,0:T(8,128)(2,1)} %get-tuple-element.90), channel_id=1, source_target_pairs={{0,2},{1,3},{2,0},{3,1},{4,6},{5,7},{6,4},{7,5},{8,10},{9,11},{10,... | collective-permute-start | bytes 786440 | tf_op jit(solution)/shard_map/ppermute | solution.py:36
  17.0 22.6 %collective-permute-start.1 = (bf16[2,9,128]{2,1,0:T(8,128)(2,1)S(1)}, bf16[2,9,128]{2,1,0:T(8,128)(2,1)S(1)}, u32[]{:S(2)}, u32[]{:S(2)}) collective-permute-start(bf16[2,9,128]{2,1,0:T(8,128)(2,1)S(1)} %maximum_select_fusion.44), channel_id=1, source_target_pairs={{0,2},{1,3},{2,0},{3,1},{4,6},{5,7},{6,4},{7,5},{8,10},{9,11},{10,... | collective-permute-start | bytes 13832 | tf_op jit(solution)/shard_map/ppermute | solution.py:36
  53.1 118.8 %collective-permute-start.5 = (bf16[128,1024]{1,0:T(8,128)(2,1)}, bf16[128,1024]{1,0:T(8,128)(2,1)}, u32[]{:S(2)}, u32[]{:S(2)}) collective-permute-start(bf16[128,1024]{1,0:T(8,128)(2,1)} %fusion.74), channel_id=1, source_target_pairs={{0,4},{4,0},{8,12},{12,8},{16,20},{20,16},{24,28},{28,24},{1,5},{5... | collective-permute-start | bytes 786440 | tf_op jit(solution)/shard_map/ppermute | solution.py:36
  59.1 62.7 %collective-permute-start.20 = (bf16[2,128,1024]{2,1,0:T(8,128)(2,1)}, bf16[2,128,1024]{2,1,0:T(8,128)(2,1)}, u32[]{:S(2)}, u32[]{:S(2)}) collective-permute-start(bf16[2,128,1024]{2,1,0:T(8,128)(2,1)} %maximum_select_fusion.23), channel_id=1, source_target_pairs={{0,1},{1,0},{2,3},{3,2},{4,5},{5,4},{6,7},{7,6},{8,9},{9,8},{10,11... | collective-permute-start | bytes 1572872 | tf_op jit(solution)/shard_map/ppermute | solution.py:36
  74.3 19.9 %collective-permute-start.25 = (bf16[2,32,2048]{2,1,0:T(8,128)(2,1)S(1)}, bf16[2,32,2048]{2,1,0:T(8,128)(2,1)S(1)}, u32[]{:S(2)}, u32[]{:S(2)}) collective-permute-start(bf16[2,32,2048]{2,1,0:T(8,128)(2,1)S(1)} %bitcast.668), channel_id=1, source_target_pairs={{0,16},{4,20},{8,24},{12,28},{16,0},{20,4},{24,8},{28,12},{1,17},{... | collective-permute-start | bytes 786440 | tf_op jit(solution)/shard_map/ppermute | solution.py:36
  90.6 25.1 %collective-permute-start.9 = (bf16[2,2,2,32,2048]{4,3,0,1,2:T(8,128)(2,1)}, bf16[2,2,2,32,2048]{4,3,0,1,2:T(8,128)(2,1)}, u32[]{:S(2)}, u32[]{:S(2)}) collective-permute-start(bf16[2,2,2,32,2048]{4,3,0,1,2:T(8,128)(2,1)} %maximum_select_fusion.9), channel_id=1, source_target_pairs={{0,16},{4,20},{8,24},{12,28},{16,0},{20,4},{24,8},{28,12},{1,17},{... | collective-permute-start | bytes 3145736 | tf_op jit(solution)/shard_map/ppermute | solution.py:36
  94.2 33.4 %collective-permute-start.16 = (bf16[2,2,32,1024]{3,2,1,0:T(8,128)(2,1)}, bf16[2,2,32,1024]{3,2,1,0:T(8,128)(2,1)}, u32[]{:S(2)}, u32[]{:S(2)}) collective-permute-start(bf16[2,2,32,1024]{3,2,1,0:T(8,128)(2,1)} %squeeze.293), channel_id=1, source_target_pairs={{0,2},{1,3},{2,0},{3,1},{4,6},{5,7},{6,4},{7,5},{8,10},{9,11},{10,... | collective-permute-start | bytes 786440 | tf_op jit(solution)/shard_map/ppermute | solution.py:36
  118.9 46.7 %collective-permute-start.10 = (bf16[2,2,2,2,32,2048]{5,4,0,1,2,3:T(8,128)(2,1)}, bf16[2,2,2,2,32,2048]{5,4,0,1,2,3:T(8,128)(2,1)}, u32[]{:S(2)}, u32[]{:S(2)}) collective-permute-start(bf16[2,2,2,2,32,2048]{5,4,0,1,2,3:T(8,128)(2,1)} %maximum_select_fusion.2), channel_id=1, source_target_pairs={{0,8},{4,12},{8,0},{12,4},{16,24},{20,28},{24,16},{28,20},{1,9},{5... | collective-permute-start | bytes 6291464 | tf_op jit(solution)/shard_map/ppermute | solution.py:36
  121.7 67.1 %collective-permute-start.26 = (bf16[2,2,32,2048]{3,2,0,1:T(8,128)(2,1)}, bf16[2,2,32,2048]{3,2,0,1:T(8,128)(2,1)S(1)}, u32[]{:S(2)}, u32[]{:S(2)}) collective-permute-start(bf16[2,2,32,2048]{3,2,0,1:T(8,128)(2,1)} %maximum_select_fusion.25), channel_id=1, source_target_pairs={{0,2},{1,3},{2,0},{3,1},{4,6},{5,7},{6,4},{7,5},{8,10},{9,11},{10,... | collective-permute-start | bytes 1572872 | tf_op jit(solution)/shard_map/ppermute | solution.py:36
  127.5 75.8 %collective-permute-start.21 = (bf16[2,2,128,1024]{3,2,1,0:T(8,128)(2,1)}, bf16[2,2,128,1024]{3,2,1,0:T(8,128)(2,1)}, u32[]{:S(2)}, u32[]{:S(2)}) collective-permute-start(bf16[2,2,128,1024]{3,2,1,0:T(8,128)(2,1)} %maximum_select_fusion.12), channel_id=1, source_target_pairs={{0,16},{4,20},{8,24},{12,28},{16,0},{20,4},{24,8},{28,12},{1,17},{... | collective-permute-start | bytes 3145736 | tf_op jit(solution)/shard_map/ppermute | solution.py:36
  165.6 25.4 %collective-permute-start.17 = (bf16[2,2,2,32,1024]{4,3,1,0,2:T(8,128)(2,1)}, bf16[2,2,2,32,1024]{4,3,1,0,2:T(8,128)(2,1)S(1)}, u32[]{:S(2)}, u32[]{:S(2)}) collective-permute-start(bf16[2,2,2,32,1024]{4,3,1,0,2:T(8,128)(2,1)} %maximum_select_fusion.22), channel_id=1, source_target_pairs={{0,1},{1,0},{2,3},{3,2},{4,5},{5,4},{6,7},{7,6},{8,9},{9,8},{10,11... | collective-permute-start | bytes 1572872 | tf_op jit(solution)/shard_map/ppermute | solution.py:36
  189.1 25.7 %collective-permute-start.27 = (bf16[2,2,2,32,2048]{4,3,0,1,2:T(8,128)(2,1)S(1)}, bf16[2,2,2,32,2048]{4,3,0,1,2:T(8,128)(2,1)S(1)}, u32[]{:S(2)}, u32[]{:S(2)}) collective-permute-start(bf16[2,2,2,32,2048]{4,3,0,1,2:T(8,128)(2,1)S(1)} %maximum_select_fusion.14), channel_id=1, source_target_pairs={{0,1},{1,0},{2,3},{3,2},{4,5},{5,4},{6,7},{7,6},{8,9},{9,8},{10,11... | collective-permute-start | bytes 3145736 | tf_op jit(solution)/shard_map/ppermute | solution.py:36
  191.4 26.5 %collective-permute-start.18 = (bf16[2,2,2,2,32,1024]{5,4,1,0,3,2:T(8,128)(2,1)S(1)}, bf16[2,2,2,2,32,1024]{5,4,1,0,3,2:T(8,128)(2,1)S(1)}, u32[]{:S(2)}, u32[]{:S(2)}) collective-permute-start(bf16[2,2,2,2,32,1024]{5,4,1,0,3,2:T(8,128)(2,1)S(1)} %maximum_select_fusion.11), channel_id=1, source_target_pairs={{0,16},{4,20},{8,24},{12,28},{16,0},{20,4},{24,8},{28,12},{1,17},{... | collective-permute-start | bytes 3145736 | tf_op jit(solution)/shard_map/ppermute | solution.py:36
  201.8 27.6 %collective-permute-start.40 = (bf16[128,1024]{1,0:T(8,128)(2,1)}, bf16[128,1024]{1,0:T(8,128)(2,1)}, u32[]{:S(2)}, u32[]{:S(2)}) collective-permute-start(bf16[128,1024]{1,0:T(8,128)(2,1)} %bitcast.116), channel_id=1, source_target_pairs={{0,8},{4,12},{8,0},{12,4},{16,24},{20,28},{24,16},{28,20},{1,9},{5... | collective-permute-start | bytes 786440 | tf_op jit(solution)/shard_map/ppermute | solution.py:36
  216.4 48.8 %collective-permute-start.28 = (bf16[2,2,2,2,32,2048]{5,4,0,1,2,3:T(8,128)(2,1)}, bf16[2,2,2,2,32,2048]{5,4,0,1,2,3:T(8,128)(2,1)}, u32[]{:S(2)}, u32[]{:S(2)}) collective-permute-start(bf16[2,2,2,2,32,2048]{5,4,0,1,2,3:T(8,128)(2,1)} %maximum_select_fusion.6), channel_id=1, source_target_pairs={{0,8},{4,12},{8,0},{12,4},{16,24},{20,28},{24,16},{28,20},{1,9},{5... | collective-permute-start | bytes 6291464 | tf_op jit(solution)/shard_map/ppermute | solution.py:36
  229.1 60.4 %collective-permute-start.36 = (bf16[2,128,1024]{2,1,0:T(8,128)(2,1)}, bf16[2,128,1024]{2,1,0:T(8,128)(2,1)}, u32[]{:S(2)}, u32[]{:S(2)}) collective-permute-start(bf16[2,128,1024]{2,1,0:T(8,128)(2,1)} %maximum_select_fusion.29), channel_id=1, source_target_pairs={{0,1},{1,0},{2,3},{3,2},{4,5},{5,4},{6,7},{7,6},{8,9},{9,8},{10,11... | collective-permute-start | bytes 1572872 | tf_op jit(solution)/shard_map/ppermute | solution.py:36
  231.3 109.6 %collective-permute-start.41 = (bf16[256,1024]{1,0:T(8,128)(2,1)}, bf16[256,1024]{1,0:T(8,128)(2,1)}, u32[]{:S(2)}, u32[]{:S(2)}) collective-permute-start(bf16[256,1024]{1,0:T(8,128)(2,1)} %pad_maximum_fusion.16), channel_id=1, source_target_pairs={{0,4},{4,0},{8,12},{12,8},{16,20},{20,16},{24,28},{28,24},{1,5},{5... | collective-permute-start | bytes 1572872 | tf_op jit(solution)/shard_map/ppermute | solution.py:36
  240.7 52.3 %collective-permute-start.33 = (bf16[2,2,2,32,1024]{4,3,1,0,2:T(8,128)(2,1)}, bf16[2,2,2,32,1024]{4,3,1,0,2:T(8,128)(2,1)}, u32[]{:S(2)}, u32[]{:S(2)}) collective-permute-start(bf16[2,2,2,32,1024]{4,3,1,0,2:T(8,128)(2,1)} %maximum_select_fusion.27), channel_id=1, source_target_pairs={{0,1},{1,0},{2,3},{3,2},{4,5},{5,4},{6,7},{7,6},{8,9},{9,8},{10,11... | collective-permute-start | bytes 1572872 | tf_op jit(solution)/shard_map/ppermute | solution.py:36
  243.9 25.6 %collective-permute-start.23 = (bf16[128,1024]{1,0:T(8,128)(2,1)S(1)}, bf16[128,1024]{1,0:T(8,128)(2,1)S(1)}, u32[]{:S(2)}, u32[]{:S(2)}) collective-permute-start(bf16[128,1024]{1,0:T(8,128)(2,1)S(1)} %slice.360), channel_id=1, source_target_pairs={{0,8},{4,12},{8,0},{12,4},{16,24},{20,28},{24,16},{28,20},{1,9},{5... | collective-permute-start | bytes 786440 | tf_op jit(solution)/shard_map/ppermute | solution.py:36
  291.3 26.1 %collective-permute-start.37 = (bf16[2,2,128,1024]{3,2,0,1:T(8,128)(2,1)S(1)}, bf16[2,2,128,1024]{3,2,0,1:T(8,128)(2,1)S(1)}, u32[]{:S(2)}, u32[]{:S(2)}) collective-permute-start(bf16[2,2,128,1024]{3,2,0,1:T(8,128)(2,1)S(1)} %maximum_select_fusion.18), channel_id=1, source_target_pairs={{0,16},{4,20},{8,24},{12,28},{16,0},{20,4},{24,8},{28,12},{1,17},{... | collective-permute-start | bytes 3145736 | tf_op jit(solution)/shard_map/ppermute | solution.py:36
  294.5 44.5 %collective-permute-start.34 = (bf16[2,2,2,2,32,1024]{5,4,1,0,2,3:T(8,128)(2,1)S(1)}, bf16[2,2,2,2,32,1024]{5,4,1,0,2,3:T(8,128)(2,1)S(1)}, u32[]{:S(2)}, u32[]{:S(2)}) collective-permute-start(bf16[2,2,2,2,32,1024]{5,4,1,0,2,3:T(8,128)(2,1)S(1)} %maximum_select_fusion.16), channel_id=1, source_target_pairs={{0,16},{4,20},{8,24},{12,28},{16,0},{20,4},{24,8},{28,12},{1,17},{... | collective-permute-start | bytes 3145736 | tf_op jit(solution)/shard_map/ppermute | solution.py:36
  304.3 35.2 %collective-permute-start.31 = (bf16[256,1024]{1,0:T(8,128)(2,1)S(1)}, bf16[256,1024]{1,0:T(8,128)(2,1)S(1)}, u32[]{:S(2)}, u32[]{:S(2)}) collective-permute-start(bf16[256,1024]{1,0:T(8,128)(2,1)S(1)} %pad_maximum_fusion.15), channel_id=1, source_target_pairs={{0,4},{4,0},{8,12},{12,8},{16,20},{20,16},{24,28},{28,24},{1,5},{5... | collective-permute-start | bytes 1572872 | tf_op jit(solution)/shard_map/ppermute | solution.py:36
  349.7 25.1 %collective-permute-start.75 = (bf16[2,2,2,2,32,1024]{5,4,1,0,2,3:T(8,128)(2,1)S(1)}, bf16[2,2,2,2,32,1024]{5,4,1,0,2,3:T(8,128)(2,1)S(1)}, u32[]{:S(2)}, u32[]{:S(2)}) collective-permute-start(bf16[2,2,2,2,32,1024]{5,4,1,0,2,3:T(8,128)(2,1)S(1)} %bitcast.734), channel_id=1, source_target_pairs={{0,16},{4,20},{8,24},{12,28},{16,0},{20,4},{24,8},{28,12},{1,17},{... | collective-permute-start | bytes 3145736 | tf_op jit(solution)/shard_map/ppermute | solution.py:36
  390.9 51.2 %collective-permute-start.77 = (bf16[2,2,32,1024]{3,2,1,0:T(8,128)(2,1)S(1)}, bf16[2,2,32,1024]{3,2,1,0:T(8,128)(2,1)S(1)}, u32[]{:S(2)}, u32[]{:S(2)}) collective-permute-start(bf16[2,2,32,1024]{3,2,1,0:T(8,128)(2,1)S(1)} %dynamic-slice_bitcast_fusion.14), channel_id=1, source_target_pairs={{0,2},{1,3},{2,0},{3,1},{4,6},{5,7},{6,4},{7,5},{8,10},{9,11},{10,... | collective-permute-start | bytes 786440 | tf_op jit(solution)/shard_map/ppermute | solution.py:36
  396.1 61.7 %collective-permute-start.66 = (bf16[2,2,2,2,32,1536]{5,4,3,2,1,0:T(8,128)(2,1)}, bf16[2,2,2,2,32,1536]{5,4,3,2,1,0:T(8,128)(2,1)}, u32[]{:S(2)}, u32[]{:S(2)}) collective-permute-start(bf16[2,2,2,2,32,1536]{5,4,3,2,1,0:T(8,128)(2,1)} %dynamic-slice_bitcast_fusion), channel_id=1, source_target_pairs={{0,8},{4,12},{8,0},{12,4},{16,24},{20,28},{24,16},{28,20},{1,9},{5... | collective-permute-start | bytes 4718600 | tf_op jit(solution)/shard_map/ppermute | solution.py:36
  399.4 31.9 %collective-permute-start.92 = (f32[2,2,2,8,128]{4,3,0,1,2:T(8,128)S(1)}, f32[2,2,2,8,128]{4,3,0,1,2:T(8,128)S(1)}, u32[]{:S(2)}, u32[]{:S(2)}) collective-permute-start(f32[2,2,2,8,128]{4,3,0,1,2:T(8,128)S(1)} %dynamic-slice_bitcast_fusion.29), channel_id=1, source_target_pairs={{0,8},{4,12},{8,0},{12,4},{16,24},{20,28},{24,16},{28,20},{1,9},{5... | collective-permute-start | bytes 98312 | tf_op jit(solution)/shard_map/ppermute | solution.py:36
  453.7 26.2 %collective-permute-start.61 = (bf16[2,2,2,2,32,1024]{5,4,1,0,2,3:T(8,128)(2,1)S(1)}, bf16[2,2,2,2,32,1024]{5,4,1,0,2,3:T(8,128)(2,1)S(1)}, u32[]{:S(2)}, u32[]{:S(2)}) collective-permute-start(bf16[2,2,2,2,32,1024]{5,4,1,0,2,3:T(8,128)(2,1)S(1)} %bitcast.736), channel_id=1, source_target_pairs={{0,16},{4,20},{8,24},{12,28},{16,0},{20,4},{24,8},{28,12},{1,17},{... | collective-permute-start | bytes 3145736 | tf_op jit(solution)/shard_map/ppermute | solution.py:36
  460.0 22.3 %collective-permute-start.67 = (bf16[2,2,2,32,1536]{4,3,2,1,0:T(8,128)(2,1)S(1)}, bf16[2,2,2,32,1536]{4,3,2,1,0:T(8,128)(2,1)S(1)}, u32[]{:S(2)}, u32[]{:S(2)}) collective-permute-start(bf16[2,2,2,32,1536]{4,3,2,1,0:T(8,128)(2,1)S(1)} %dynamic-slice_bitcast_fusion.2), channel_id=1, source_target_pairs={{0,1},{1,0},{2,3},{3,2},{4,5},{5,4},{6,7},{7,6},{8,9},{9,8},{10,11... | collective-permute-start | bytes 2359304 | tf_op jit(solution)/shard_map/ppermute | solution.py:36
  461.8 40.5 %collective-permute-start.83 = (bf16[2,2,128,1024]{3,2,0,1:T(8,128)(2,1)S(1)}, bf16[2,2,128,1024]{3,2,0,1:T(8,128)(2,1)S(1)}, u32[]{:S(2)}, u32[]{:S(2)}) collective-permute-start(bf16[2,2,128,1024]{3,2,0,1:T(8,128)(2,1)S(1)} %bitcast.737), channel_id=1, source_target_pairs={{0,16},{4,20},{8,24},{12,28},{16,0},{20,4},{24,8},{28,12},{1,17},{... | collective-permute-start | bytes 3145736 | tf_op jit(solution)/shard_map/ppermute | solution.py:36
  463.1 60.1 %collective-permute-start.80 = (bf16[2,2,128,1024]{3,2,0,1:T(8,128)(2,1)S(1)}, bf16[2,2,128,1024]{3,2,0,1:T(8,128)(2,1)S(1)}, u32[]{:S(2)}, u32[]{:S(2)}) collective-permute-start(bf16[2,2,128,1024]{3,2,0,1:T(8,128)(2,1)S(1)} %bitcast.735), channel_id=1, source_target_pairs={{0,16},{4,20},{8,24},{12,28},{16,0},{20,4},{24,8},{28,12},{1,17},{... | collective-permute-start | bytes 3145736 | tf_op jit(solution)/shard_map/ppermute | solution.py:36
  464.2 61.5 %collective-permute-start.49 = (bf16[128,1024]{1,0:T(8,128)(2,1)S(1)}, bf16[128,1024]{1,0:T(8,128)(2,1)S(1)}, u32[]{:S(2)}, u32[]{:S(2)}) collective-permute-start(bf16[128,1024]{1,0:T(8,128)(2,1)S(1)} %slice.357), channel_id=1, source_target_pairs={{0,8},{4,12},{8,0},{12,4},{16,24},{20,28},{24,16},{28,20},{1,9},{5... | collective-permute-start | bytes 786440 | tf_op jit(solution)/shard_map/ppermute | solution.py:36
  481.2 57.3 %collective-permute-start.62 = (bf16[2,2,2,32,1024]{4,3,1,0,2:T(8,128)(2,1)}, bf16[2,2,2,32,1024]{4,3,1,0,2:T(8,128)(2,1)}, u32[]{:S(2)}, u32[]{:S(2)}) collective-permute-start(bf16[2,2,2,32,1024]{4,3,1,0,2:T(8,128)(2,1)} %dynamic-slice_bitcast_fusion.7), channel_id=1, source_target_pairs={{0,1},{1,0},{2,3},{3,2},{4,5},{5,4},{6,7},{7,6},{8,9},{9,8},{10,11... | collective-permute-start | bytes 1572872 | tf_op jit(solution)/shard_map/ppermute | solution.py:36
  482.6 44.6 %collective-permute-start.68 = (bf16[2,2,32,1536]{3,2,1,0:T(8,128)(2,1)S(1)}, bf16[2,2,32,1536]{3,2,1,0:T(8,128)(2,1)S(1)}, u32[]{:S(2)}, u32[]{:S(2)}) collective-permute-start(bf16[2,2,32,1536]{3,2,1,0:T(8,128)(2,1)S(1)} %dynamic-slice_bitcast_fusion.8), channel_id=1, source_target_pairs={{0,2},{1,3},{2,0},{3,1},{4,6},{5,7},{6,4},{7,5},{8,10},{9,11},{10,... | collective-permute-start | bytes 1179656 | tf_op jit(solution)/shard_map/ppermute | solution.py:36
  503.6 43.4 %collective-permute-start.84 = (bf16[2,128,1024]{2,1,0:T(8,128)(2,1)}, bf16[2,128,1024]{2,1,0:T(8,128)(2,1)}, u32[]{:S(2)}, u32[]{:S(2)}) collective-permute-start(bf16[2,128,1024]{2,1,0:T(8,128)(2,1)} %dynamic-slice_bitcast_fusion.4), channel_id=1, source_target_pairs={{0,1},{1,0},{2,3},{3,2},{4,5},{5,4},{6,7},{7,6},{8,9},{9,8},{10,11... | collective-permute-start | bytes 1572872 | tf_op jit(solution)/shard_map/ppermute | solution.py:36
  524.7 27.3 %collective-permute-start.81 = (bf16[2,128,1024]{2,1,0:T(8,128)(2,1)}, bf16[2,128,1024]{2,1,0:T(8,128)(2,1)}, u32[]{:S(2)}, u32[]{:S(2)}) collective-permute-start(bf16[2,128,1024]{2,1,0:T(8,128)(2,1)} %dynamic-slice_bitcast_fusion.5), channel_id=1, source_target_pairs={{0,1},{1,0},{2,3},{3,2},{4,5},{5,4},{6,7},{7,6},{8,9},{9,8},{10,11... | collective-permute-start | bytes 1572872 | tf_op jit(solution)/shard_map/ppermute | solution.py:36
  528.7 25.8 %collective-permute-start.69 = (bf16[2,32,1536]{2,1,0:T(8,128)(2,1)}, bf16[2,32,1536]{2,1,0:T(8,128)(2,1)}, u32[]{:S(2)}, u32[]{:S(2)}) collective-permute-start(bf16[2,32,1536]{2,1,0:T(8,128)(2,1)} %dynamic-slice_bitcast_fusion.21), channel_id=1, source_target_pairs={{0,16},{4,20},{8,24},{12,28},{16,0},{20,4},{24,8},{28,12},{1,17},{... | collective-permute-start | bytes 589832 | tf_op jit(solution)/shard_map/ppermute | solution.py:36
  538.3 88.8 %collective-permute-start.51 = (f32[128,1024]{1,0:T(8,128)}, f32[128,1024]{1,0:T(8,128)}, u32[]{:S(2)}, u32[]{:S(2)}) collective-permute-start(f32[128,1024]{1,0:T(8,128)} %slice.284), channel_id=1, source_target_pairs={{0,4},{4,0},{8,12},{12,8},{16,20},{20,16},{24,28},{28,24},{1,5},{5... | collective-permute-start | bytes 1572872 | tf_op jit(solution)/shard_map/ppermute | solution.py:36
  540.7 27.5 %collective-permute-start.63 = (bf16[2,2,32,1024]{3,2,1,0:T(8,128)(2,1)}, bf16[2,2,32,1024]{3,2,1,0:T(8,128)(2,1)}, u32[]{:S(2)}, u32[]{:S(2)}) collective-permute-start(bf16[2,2,32,1024]{3,2,1,0:T(8,128)(2,1)} %dynamic-slice_bitcast_fusion.18), channel_id=1, source_target_pairs={{0,2},{1,3},{2,0},{3,1},{4,6},{5,7},{6,4},{7,5},{8,10},{9,11},{10,... | collective-permute-start | bytes 786440 | tf_op jit(solution)/shard_map/ppermute | solution.py:36
  547.1 82.5 %collective-permute-start.71 = (bf16[2,2,2,32,1024]{4,3,0,1,2:T(8,128)(2,1)}, bf16[2,2,2,32,1024]{4,3,0,1,2:T(8,128)(2,1)}, u32[]{:S(2)}, u32[]{:S(2)}) collective-permute-start(bf16[2,2,2,32,1024]{4,3,0,1,2:T(8,128)(2,1)} %bitcast.647), channel_id=1, source_target_pairs={{0,8},{4,12},{8,0},{12,4},{16,24},{20,28},{24,16},{28,20},{1,9},{5... | collective-permute-start | bytes 1572872 | tf_op jit(solution)/shard_map/ppermute | solution.py:36
  552.0 87.2 %collective-permute-start.57 = (bf16[2,2,2,32,1024]{4,3,1,2,0:T(8,128)(2,1)}, bf16[2,2,2,32,1024]{4,3,1,2,0:T(8,128)(2,1)}, u32[]{:S(2)}, u32[]{:S(2)}) collective-permute-start(bf16[2,2,2,32,1024]{4,3,1,2,0:T(8,128)(2,1)} %bitcast.648), channel_id=1, source_target_pairs={{0,8},{4,12},{8,0},{12,4},{16,24},{20,28},{24,16},{28,20},{1,9},{5... | collective-permute-start | bytes 1572872 | tf_op jit(solution)/shard_map/ppermute | solution.py:36
  562.6 21.6 %collective-permute-start.85 = (bf16[128,1024]{1,0:T(8,128)(2,1)}, bf16[128,1024]{1,0:T(8,128)(2,1)}, u32[]{:S(2)}, u32[]{:S(2)}) collective-permute-start(bf16[128,1024]{1,0:T(8,128)(2,1)} %dynamic-slice_bitcast_fusion.10), channel_id=1, source_target_pairs={{0,2},{1,3},{2,0},{3,1},{4,6},{5,7},{6,4},{7,5},{8,10},{9,11},{10,... | collective-permute-start | bytes 786440 | tf_op jit(solution)/shard_map/ppermute | solution.py:36
  568.1 21.2 %collective-permute-start.82 = (bf16[128,1024]{1,0:T(8,128)(2,1)}, bf16[128,1024]{1,0:T(8,128)(2,1)}, u32[]{:S(2)}, u32[]{:S(2)}) collective-permute-start(bf16[128,1024]{1,0:T(8,128)(2,1)} %dynamic-slice_bitcast_fusion.11), channel_id=1, source_target_pairs={{0,2},{1,3},{2,0},{3,1},{4,6},{5,7},{6,4},{7,5},{8,10},{9,11},{10,... | collective-permute-start | bytes 786440 | tf_op jit(solution)/shard_map/ppermute | solution.py:36
  584.2 67.7 %collective-permute-start.52 = (bf16[2,2,2,2,32,1536]{5,4,3,2,1,0:T(8,128)(2,1)S(1)}, bf16[2,2,2,2,32,1536]{5,4,3,2,1,0:T(8,128)(2,1)S(1)}, u32[]{:S(2)}, u32[]{:S(2)}) collective-permute-start(bf16[2,2,2,2,32,1536]{5,4,3,2,1,0:T(8,128)(2,1)S(1)} %copy-done.63), channel_id=1, source_target_pairs={{0,8},{4,12},{8,0},{12,4},{16,24},{20,28},{24,16},{28,20},{1,9},{5... | collective-permute-start | bytes 4718600 | tf_op jit(solution)/shard_map/ppermute | solution.py:36
  589.4 36.0 %collective-permute-start.78 = (f32[2,32,2,512]{3,1,2,0:T(8,128)S(1)}, f32[2,32,2,512]{3,1,2,0:T(8,128)S(1)}, u32[]{:S(2)}, u32[]{:S(2)}) collective-permute-start(f32[2,32,2,512]{3,1,2,0:T(8,128)S(1)} %bitcast.748), channel_id=1, source_target_pairs={{0,8},{4,12},{8,0},{12,4},{16,24},{20,28},{24,16},{28,20},{1,9},{5... | collective-permute-start | bytes 786440 | tf_op jit(solution)/shard_map/ppermute | solution.py:36
  627.1 24.8 %collective-permute-start.79 = (f32[32,2,2,512]{3,0,2,1:T(8,128)S(1)}, f32[32,2,2,512]{3,0,2,1:T(8,128)S(1)}, u32[]{:S(2)}, u32[]{:S(2)}) collective-permute-start(f32[32,2,2,512]{3,0,2,1:T(8,128)S(1)} %get-tuple-element.81), channel_id=1, source_target_pairs={{0,4},{4,0},{8,12},{12,8},{16,20},{20,16},{24,28},{28,24},{1,5},{5... | collective-permute-start | bytes 786440 | tf_op jit(solution)/shard_map/ppermute | solution.py:36
  654.7 18.1 %collective-permute-start.53 = (bf16[2,2,2,32,1536]{4,3,2,1,0:T(8,128)(2,1)}, bf16[2,2,2,32,1536]{4,3,2,1,0:T(8,128)(2,1)}, u32[]{:S(2)}, u32[]{:S(2)}) collective-permute-start(bf16[2,2,2,32,1536]{4,3,2,1,0:T(8,128)(2,1)} %dynamic-slice_bitcast_fusion.3), channel_id=1, source_target_pairs={{0,16},{4,20},{8,24},{12,28},{16,0},{20,4},{24,8},{28,12},{1,17},{... | collective-permute-start | bytes 2359304 | tf_op jit(solution)/shard_map/ppermute | solution.py:36
  (176 other events, 1478.9 us)

commit v2 on v1

v2 whole, which is shorter than its diff:
```python
import math
from functools import partial

import jax
import jax.numpy as jnp
from jax import lax
from jax.experimental import pallas as pl
from jax.experimental.pallas import tpu as pltpu
from jax.sharding import PartitionSpec as P

HEADS = 16

beta_one = 0.9
beta_two = 0.999
first_fix = 1.0 - 0.9**10
second_fix = 1.0 - 0.999**10

f32 = jnp.float32
bf16 = jnp.bfloat16

VMEM = pl.BlockSpec(memory_space=pltpu.VMEM)
SMEM = pl.BlockSpec(memory_space=pltpu.SMEM)
ANY = pl.BlockSpec(memory_space=pl.ANY)

CORE = ("dp", 1)
SIDE = ("dp", 2)


def masks(size):
    return [1 << k for k in reversed(range(size.bit_length() - 1))]


class Slice:
    def __init__(self, dp, fsdp):
        self.high = [("dp", m) for m in masks(dp) if m > 2]
        self.deep = [("fsdp", m) for m in masks(fsdp)]
        self.size = {"dp": dp, "fsdp": fsdp}

    def flip(self, value, bit):
        axis, mask = bit
        return lax.ppermute(value, axis, [(i, i ^ mask) for i in range(self.size[axis])])


def mine(bit):
    axis, mask = bit
    return (lax.axis_index(axis) // mask) % 2


def call(kernel, outs, operands, specs, scratch=(), flops=0, name=None):
    held = [(v.shape, v.dtype) for v, spec in zip(operands, specs) if spec is VMEM] + list(outs)
    held += [(s.shape, s.dtype) for s in scratch if hasattr(s, "memory_space") and s.memory_space == pltpu.VMEM]
    held = sum(math.prod(shape) * jnp.dtype(kind).itemsize for shape, kind in held)
    return pl.pallas_call(
        kernel,
        out_shape=[jax.ShapeDtypeStruct(shape, kind) for shape, kind in outs],
        in_specs=specs,
        out_specs=[VMEM] * len(outs),
        scratch_shapes=list(scratch),
        compiler_params=pltpu.CompilerParams(vmem_limit_bytes=held + (8 << 20)),
        name=name,
    )(*operands)


def merge(own, other, bit, pos):
    side = mine(bit)
    return jnp.where(side == 0, jnp.stack([own, other], pos), jnp.stack([other, own], pos))


def split(value, bit, pos):
    side = mine(bit)
    keep = lax.dynamic_index_in_dim(value, side, pos, keepdims=False)
    send = lax.dynamic_index_in_dim(value, 1 - side, pos, keepdims=False)
    return keep, send


def interleave_kernel(side, own, other, *outs):
    each = own.shape[0] // len(outs)
    for n, out in enumerate(outs):
        part = pl.ds(n * each, each)
        out[:, pl.ds(side[0], 1)] = own[part][:, None]
        out[:, pl.ds(1 - side[0], 1)] = other[part][:, None]


def interleave(own, other, bit, before, outs=1):
    rows, n = own.shape
    shape = (before, rows // before, n)
    whole = (before // outs, 2, rows // before, n)
    result = call(
        interleave_kernel,
        outs * [(whole, own.dtype)],
        [mine(bit)[None], own.reshape(shape), other.reshape(shape)],
        [SMEM, VMEM, VMEM],
        name="interleave",
    )
    return [part.reshape(-1, n) for part in result]


class Gather:
    def __init__(self, sl, own, lead, top_first=False):
        self.sl, self.value, self.lead, self.top_first = sl, own, lead, top_first
        self.have, self.air, self.quarters = [], None, None
        near = sl.high[:0:-1]
        if top_first:
            self.steps = [sl.high[:1], near + sl.deep[:-1], sl.deep[-1:]]
        else:
            self.steps = [sl.deep[:-1], sl.deep[-1:] + near]
        core = mine(CORE)
        self.place = jnp.stack([jnp.zeros_like(core) if top_first else mine(sl.high[0]), core])

    def before(self, bit):
        order = self.sl.high + self.sl.deep
        count = sum(order.index(b) < order.index(bit) for b in self.have)
        return (1 << count) * (1 if bit in self.sl.high else self.lead)

    def start(self):
        if not self.steps:
            self.air = self.sl.flip(self.value, self.sl.high[0]), self.sl.flip(self.value, CORE)
            return
        *others, self.bit = self.steps.pop(0)
        for bit in others:
            other = self.sl.flip(self.value, bit)
            self.value = interleave(self.value, other, bit, self.before(bit))[0]
            self.have.append(bit)
        self.air = self.sl.flip(self.value, self.bit)

    def land(self):
        air, self.air = self.air, None
        if isinstance(air, tuple):
            self.quarters, self.value = [self.value, *air], None
            return
        last = self.top_first and not self.steps
        halves = interleave(self.value, air, self.bit, self.before(self.bit), 1 + last)
        self.have.append(self.bit)
        if last:
            self.quarters = [*halves, self.sl.flip(halves[0], CORE)]
            self.value = None
        else:
            self.value = halves[0]

    def finish(self):
        self.quarters = [*self.quarters, self.sl.flip(self.quarters[1], CORE)]


def add_low_kernel(one, two, out):
    out[...] = (one[...].astype(f32) + two[...].astype(f32)).astype(bf16)


def add_split_kernel(side, *refs):
    *parts, kept, sent = refs
    for at, out in ((side[0], kept), (1 - side[0], sent)):
        total = parts[0][:, pl.ds(at, 1)].astype(f32)
        for other in parts[1:]:
            total = total + other[:, pl.ds(at, 1)].astype(f32)
        out[...] = total.astype(bf16)[:, 0]


class Scatter:
    def __init__(self, sl, quarters, lead):
        self.sl, self.quarters, self.value, self.lead = sl, quarters, None, lead
        self.have = sl.high[1:] + sl.deep
        self.steps = [sl.high[:1], sl.high[1:] + sl.deep[-1:], sl.deep[-2::-1]]

    def cross(self):
        own, top, core, both = self.quarters
        top_other = self.sl.flip(both, CORE)
        core_other = self.sl.flip(core, CORE)
        (send,) = call(
            add_low_kernel, [(top.shape, bf16)], [top, top_other], [VMEM] * 2, name="add_low"
        )
        self.quarters = [[own, core_other], send]

    def split(self, other, bit):
        parts = [*self.quarters[0], other]
        if bit is None:
            self.value = sum(part.astype(f32) for part in parts)
            self.quarters = None
            return
        order = self.sl.high + self.sl.deep
        before = 1 << sum(order.index(b) < order.index(bit) for b in self.have)
        before = before * (1 if bit in self.sl.high else self.lead)
        self.have.remove(bit)
        rows, n = other.shape
        shape = (before, 2, rows // 2 // before, n)
        half = ((before, rows // 2 // before, n), bf16)
        keep, send = call(
            add_split_kernel,
            [half, half],
            [mine(bit)[None], *(part.reshape(shape) for part in parts)],
            [SMEM] + [VMEM] * len(parts),
            name="add_split",
        )
        self.quarters = [[keep.reshape(-1, n)], send.reshape(-1, n)]

    def start(self):
        bits = self.steps.pop(0)
        for n, bit in enumerate(bits):
            self.air = self.sl.flip(self.quarters[1], bit)
            if n < len(bits) - 1:
                self.split(self.air, bits[n + 1])
        self.next = self.steps[0][0] if self.steps else None

    def land(self):
        other, self.air = self.air, None
        self.split(other, self.next)


class Live:
    def __init__(self, **values):
        self.flows = []
        self.values = values

    def flow(self, made):
        self.flows.append(made)
        return made

    def __getattr__(self, name):
        return self.values[name]

    def put(self, **values):
        self.values.update(values)

    def drop(self, *names):
        for name in names:
            del self.values[name]

    def seal(self, *landing):
        for made in landing:
            made.land()
        kept = (self.values, [(made.value, made.quarters) for made in self.flows])
        self.values, flown = lax.optimization_barrier(kept)
        for made, (made.value, made.quarters) in zip(self.flows, flown):
            pass


def dot(left, right):
    return jnp.dot(left, right, preferred_element_type=f32)


def dot_t(left, right):
    return lax.dot_general(left, right, (((1,), (1,)), ((), ())), preferred_element_type=f32)


def t_dot(left, right):
    return lax.dot_general(left, right, (((0,), (0,)), ((), ())), preferred_element_type=f32)


def fetch(place, quarters, whole, lead, sems):
    width = whole.shape[1]
    block = whole.shape[0] // (4 * lead)
    copies = []
    for n, part in enumerate(quarters):
        top = place[0] if n % 2 == 0 else 1 - place[0]
        core = place[1] if n < 2 else 1 - place[1]
        for a in range(lead):
            at = pl.multiple_of(((top * lead + a) * 2 + core) * block, block)
            source = part.at[pl.ds(a * block, block), pl.ds(0, width)]
            copies.append(
                pltpu.make_async_copy(source, whole.at[pl.ds(at, block)], sems.at[n * lead + a])
            )
    for copy in copies:
        copy.start()
    return copies


def norm(hidden):
    centred = hidden - jnp.mean(hidden, axis=-1, keepdims=True)
    scale = lax.rsqrt(jnp.mean(centred * centred, axis=-1, keepdims=True) + 1e-05)
    return centred * scale, scale


def norm_kernel(which, base, gains, out):
    rows = base.shape[0] // 2
    for r in range(2):
        block = pl.ds(r * rows, rows)
        g = gains[r, pl.ds(2 * which, 1)]
        b = gains[r, pl.ds(2 * which + 1, 1)]
        out[block] = (norm(base[block])[0] * g + b).astype(bf16)


def add_norm_kernel(which, base, keep, other, gains, total, out):
    rows = base.shape[0] // 2
    for r in range(2):
        block = pl.ds(r * rows, rows)
        back = pl.ds((1 - r) * rows, rows)
        value = base[block] + (keep[block] + other[back].astype(f32))
        total[block] = value
        g = gains[r, pl.ds(2 * which, 1)]
        b = gains[r, pl.ds(2 * which + 1, 1)]
        out[block] = (norm(value)[0] * g + b).astype(bf16)


def norm_back_kernel(which, d_out, keep, other, hidden, gains, total, low, d_gain, d_shift):
    rows = d_out.shape[0] // 2
    for r in range(2):
        block = pl.ds(r * rows, rows)
        back = pl.ds((1 - r) * rows, rows)
        grad = keep[block] + other[back].astype(f32)
        normed, scale = norm(hidden[block])
        if r == 0:
            d_gain[...] = jnp.sum(grad * normed, axis=0, keepdims=True)
            d_shift[...] = jnp.sum(grad, axis=0, keepdims=True)
        e = grad * gains[r, pl.ds(2 * which, 1)]
        part = e - jnp.mean(e, axis=-1, keepdims=True)
        part = part - normed * jnp.mean(e * normed, axis=-1, keepdims=True)
        value = d_out[block] + scale * part
        total[block] = value
        low[block] = value.astype(bf16)


def score(q, k, allowed, size):
    scores = jnp.where(allowed, dot_t(q, k) * size, -1e30)
    exponent = jnp.exp(scores - jnp.max(scores, axis=-1, keepdims=True))
    return exponent / jnp.sum(exponent, axis=-1, keepdims=True)


def lanes_of(which, shape):
    lane = lax.broadcasted_iota(jnp.int32, shape, 1)
    return (lane < shape[1] // 2) if which == 0 else (lane >= shape[1] // 2)


def out_block(weight, k, block, at):
    count = weight.shape[0] // (2 * block)
    wide = weight.shape[1] - at
    return jnp.concatenate([weight[pl.ds((2 * h + k) * block, block), pl.ds(at, wide)] for h in range(count)], 0)


def attend_kernel(size, lead, block, place, f, q0, q1, q2, q3, allow, qkv, mixed, keep, low, weight, sems):
    for copy in fetch(place, (q0, q1, q2, q3), weight, lead, sems):
        copy.wait()
    length = allow.shape[-1]
    third = qkv.shape[1] // 3
    for n in range(3):
        cols = pl.ds(n * third, third)
        qkv[:, cols] = dot(f[...], weight[:, cols]).astype(bf16)

    def one_row(r, carry):
        at = pl.ds(pl.multiple_of(r * length, length), length)
        allowed = allow[r] > 0
        for p in range(third // 128):
            q = qkv[at, pl.ds(p * 128, 128)]
            k = qkv[at, pl.ds(third + p * 128, 128)]
            v = qkv[at, pl.ds(2 * third + p * 128, 128)]
            parts = []
            for h in range(2):
                probs = score(jnp.where(lanes_of(h, q.shape), q, 0), k, allowed, size)
                parts.append(dot(probs.astype(bf16), v))
            mixed[at, pl.ds(p * 128, 128)] = jnp.where(
                lanes_of(0, q.shape), parts[0], parts[1]
            ).astype(bf16)
        return carry

    lax.fori_loop(0, f.shape[0] // length, one_row, 0)
    for k in range(2):
        cols = pl.ds(k * third, third)
        value = dot(mixed[...], out_block(weight, k, block, 3 * third))
        keep[:, cols] = value
        low[:, cols] = value.astype(bf16)


def attend_back_kernel(size, lead, block, place, d, q0, q1, q2, q3, allow, qkv, d_qkv, keep, low, weight, d_mixed, sems):
    for copy in fetch(place, (q0, q1, q2, q3), weight, lead, sems):
        copy.wait()
    length = allow.shape[-1]
    third = qkv.shape[1] // 3
    value = dot_t(d[:, pl.ds(0, third)], out_block(weight, 0, block, 3 * third))
    value = value + dot_t(d[:, pl.ds(third, third)], out_block(weight, 1, block, 3 * third))
    d_mixed[...] = value.astype(bf16)

    def one_row(r, carry):
        at = pl.ds(pl.multiple_of(r * length, length), length)
        allowed = allow[r] > 0
        for p in range(third // 128):
            q = qkv[at, pl.ds(p * 128, 128)]
            k = qkv[at, pl.ds(third + p * 128, 128)]
            v = qkv[at, pl.ds(2 * third + p * 128, 128)]
            dm = d_mixed[at, pl.ds(p * 128, 128)]
            d_q, d_k, d_v = [], [], []
            for h in range(2):
                pick = lanes_of(h, q.shape)
                probs = score(jnp.where(pick, q, 0), k, allowed, size)
                d_probs = dot_t(jnp.where(pick, dm, 0), v)
                d_v.append(t_dot(probs.astype(bf16), dm))
                inner = jnp.sum(probs * d_probs, axis=-1, keepdims=True)
                d_scores = (probs * (d_probs - inner)).astype(bf16)
                d_q.append(dot(d_scores, k))
                d_k.append(t_dot(d_scores, q))
            pick = lanes_of(0, q.shape)
            for n, (parts, scale) in enumerate(((d_q, size), (d_k, size), (d_v, 1.0))):
                value = jnp.where(pick, parts[0], parts[1]) * scale
                d_qkv[at, pl.ds(n * third + p * 128, 128)] = value.astype(bf16)
        return carry

    lax.fori_loop(0, d.shape[0] // length, one_row, 0)
    for n in range(keep.shape[1] // 256):
        cols = pl.ds(n * 256, 256)
        value = dot_t(d_qkv[...], weight[cols, pl.ds(0, 3 * third)])
        keep[:, cols] = value
        low[:, cols] = value.astype(bf16)


def up_kernel(lead, place, f, q0, q1, q2, q3, pre, active, weight, sems):
    for copy in fetch(place, (q0, q1, q2, q3), weight, lead, sems):
        copy.wait()
    for n in range(pre.shape[1] // 256):
        cols = pl.ds(n * 256, 256)
        value = dot(f[...], weight[:, cols])
        pre[:, cols] = value
        active[:, cols] = jax.nn.gelu(value).astype(bf16)


def down_kernel(lead, place, active, q0, q1, q2, q3, keep, low, weight, sems):
    for copy in fetch(place, (q0, q1, q2, q3), weight, lead, sems):
        copy.wait()
    for n in range(keep.shape[1] // 256):
        cols = pl.ds(n * 256, 256)
        value = dot(active[...], weight[:, cols])
        keep[:, cols] = value
        low[:, cols] = value.astype(bf16)


def gelu_slope(x):
    c = 0.7978845608028654
    t = jnp.tanh(c * (x + 0.044715 * (x * x * x)))
    return 0.5 * (1.0 + t) + 0.5 * x * (1.0 - t * t) * (c * (1.0 + 3 * 0.044715 * (x * x)))


def feed_back_kernel(lead, up_place, dn_place, d, pre, u0, u1, u2, u3, n0, n1, n2, n3, d_pre, keep, low, w_up, w_dn, up_sems, dn_sems):
    dn_copies = fetch(dn_place, (n0, n1, n2, n3), w_dn, lead // 2, dn_sems)
    up_copies = fetch(up_place, (u0, u1, u2, u3), w_up, lead, up_sems)
    for copy in dn_copies:
        copy.wait()
    for n in range(pre.shape[1] // 256):
        cols = pl.ds(n * 256, 256)
        d_pre[:, cols] = (gelu_slope(pre[:, cols]) * dot_t(d[...], w_dn[cols])).astype(bf16)
    for copy in up_copies:
        copy.wait()
    for n in range(keep.shape[1] // 256):
        cols = pl.ds(n * 256, 256)
        value = dot_t(d_pre[...], w_up[cols])
        keep[:, cols] = value
        low[:, cols] = value.astype(bf16)


def columns_of(place, value, lead):
    block = value.shape[1] // (4 * lead)
    parts = []
    for n in range(4):
        top = place[0] if n % 2 == 0 else 1 - place[0]
        core = place[1] if n < 2 else 1 - place[1]
        starts = [((top * lead + a) * 2 + core) * block for a in range(lead)]
        if block % 128 == 0:
            starts = [pl.multiple_of(at, 128) for at in starts]
        parts.append(jnp.concatenate([value[:, pl.ds(at, block)] for at in starts], 1))
    return parts


def weight_grad_kernel(lead, aligned, place, left, right, *outs):
    place = place if aligned else (0, 0)
    for part, out in zip(columns_of(place, left, lead), outs):
        out[...] = t_dot(part, right[...]).astype(bf16)


def attend_grad_kernel(lead, aligned, place, left, mixed, d_qkv, d, *outs):
    width = d_qkv.shape[1]
    third = width // 3
    place = place if aligned else (0, 0)
    block = left.shape[1] // (4 * lead)
    lefts, inners = columns_of(place, left, lead), columns_of(place, mixed, lead // 2)
    for part, inner, out in zip(lefts, inners, outs):
        out[:, pl.ds(0, width)] = t_dot(part, d_qkv[...]).astype(bf16)
        value = t_dot(inner, d[...]).astype(bf16)
        for h in range(inner.shape[1] // block):
            for k in range(2):
                out[pl.ds((2 * h + k) * block, block), pl.ds(width, third)] = value[
                    h * block : (h + 1) * block, k * third : (k + 1) * third
                ]


def turn(sl, value, lead):
    tokens, width = value.shape
    value = value.reshape(tokens, 2, lead, 2, width // (4 * lead))
    value = jnp.stack(split(value, sl.high[0], 1), 1)
    return jnp.stack(split(value, CORE, 3), 3).reshape(tokens, width)


def finish_kernel(span, chunk, side, keep, other, out, m, v, *refs):
    grad, new_m, step = refs[-3:]
    third = out.shape[-1]
    part = 3 * third
    rows = keep.shape[0]
    for source, x in ((keep, side[0]), (other, 1 - side[0])):
        for first, base, width, total in ((0, 0, span, part), (part, 8 * third, chunk, keep.shape[1] - part)):
            for n in range(total // width):
                at = pl.multiple_of(base + (2 * n + x) * width, 128)
                grad[0, :, pl.ds(at, width)] = source[:, pl.ds(first + n * width, width)]
    for k in range(2):
        grad[0, :, pl.ds((6 + k) * third, third)] = out[k]
    for n in range(grad.shape[2] // 1024):
        cols = pl.ds(n * 1024, 1024)
        new_m[0, :, cols], step[0, :, cols] = adam_update(m[0, :, cols], v[0, :, cols], grad[0, :, cols])


def finish_down_kernel(value, m, v, *refs):
    grad, new_m, step = refs[-3:]
    grad[0] = value[...]
    new_m[0], step[0] = adam_update(m[0], v[0], value[...])


def update(kernel, layer, shape, parts, specs, moments, before, name):
    one = pl.BlockSpec((1, *shape[1:]), lambda i: (layer, 0, 0))
    count = len(parts) + 2
    return pl.pallas_call(
        kernel,
        grid=(1,),
        out_shape=[jax.ShapeDtypeStruct(shape, f32)] * 3,
        in_specs=[*specs, one, one, *len(before) * [ANY]],
        out_specs=[one] * 3,
        input_output_aliases={count + n: n for n in range(len(before))},
        compiler_params=pltpu.CompilerParams(vmem_limit_bytes=20 << 20),
        name=name,
    )(*parts, *moments, *before)


def adam_update(moment, square, gradient):
    moment = beta_one * moment + (1.0 - beta_one) * gradient
    square = beta_two * square + (1.0 - beta_two) * gradient * gradient
    update = moment / first_fix / (jnp.sqrt(square / second_fix) + 1e-08)
    return (moment, update)


def dma(count):
    return pltpu.SemaphoreType.DMA((count,))


def body(
    dp,
    fsdp,
    inputs,
    cotangent,
    segment_ids,
    section_ids,
    w_big,
    w_down,
    norm_table,
    m_big,
    m_down,
    m_table,
    v_big,
    v_down,
    v_table,
):
    sl = Slice(dp, fsdp)
    length, width = inputs.shape[1:]
    rows = w_big.shape[1]
    feeds = w_down.shape[1]
    feed = w_big.shape[2] - 4 * width
    high = dp // 4
    lead = high
    half, part = width // 2, 3 * width // 2
    block = fsdp * rows
    count = norm_table.shape[0]
    size = (width // HEADS) ** -0.5
    two_f, two_b = ((2 * length, width), f32), ((2 * length, width), bf16)
    wide_b = ((2 * length, feed // 2), bf16)
    quarter = ((width // 4, 2 * width), bf16)
    gain_row = ((1, width), f32)
    place = jnp.stack([mine(sl.high[0]), mine(CORE)])
    w_attn = pltpu.VMEM((width, 2 * width), bf16)
    w_upper = pltpu.VMEM((width, feed // 2), bf16)
    w_lower = pltpu.VMEM((feed // 2, width), bf16)

    qkv = w_big[:, :, : 3 * width].reshape(2, rows, 3, high, 2, 2 * block)
    up = w_big[:, :, 4 * width :].reshape(2, rows, high, 2, 2 * fsdp * feeds)
    qkv_keep, qkv_send = [v.reshape(2, rows, part) for v in split(qkv, SIDE, 4)]
    up_keep, up_send = [v.reshape(2, rows, feed // 2) for v in split(up, SIDE, 3)]
    table_part = norm_table.reshape(-1)
    table_part = jnp.pad(table_part, (0, rows * 128 - table_part.shape[0])).reshape(rows, 128)
    out_proj = w_big[:, :, 3 * width : 4 * width].reshape(2, rows, 2, half)
    out_proj = jnp.swapaxes(out_proj, 1, 2)
    extra = jnp.zeros((16, width), bf16)
    extra = extra.at[0, :length].set(segment_ids[0].astype(bf16))
    extra = extra.at[1, 0].set(section_ids[0].astype(bf16))

    live = Live()
    downs = [live.flow(Gather(sl, w_down[n], 1)) for n in range(2)]

    send = jnp.concatenate([qkv_send[0], table_part], -1)
    keep = jnp.concatenate([qkv_keep[0], table_part], -1)
    own = merge(keep, sl.flip(send, SIDE), SIDE, 0)
    own = jnp.concatenate([own[..., :part], out_proj[0], own[..., part:]], -1)
    attns = [live.flow(Gather(sl, own.reshape(2 * rows, -1), 2))]
    live.put(
        up_keep=up_keep,
        up_send=up_send,
        next_keep=jnp.concatenate([qkv_keep[1], up_keep[1]], -1),
        next_send=jnp.concatenate([qkv_send[1], up_send[1]], -1),
        pack=jnp.concatenate([inputs[0], cotangent[0], extra], 0),
    )
    live.seal()

    attns[0].start()
    other = sl.flip(live.up_send[0], SIDE)
    own = merge(live.up_keep[0], other, SIDE, 0).reshape(2 * rows, -1)
    ups = [live.flow(Gather(sl, own, 2))]
    live.drop("up_keep", "up_send")
    live.seal(attns[0])

    attns[0].start()
    ups[0].start()
    own = merge(live.next_keep, sl.flip(live.next_send, SIDE), SIDE, 0)
    live.put(next=own)
    live.drop("next_keep", "next_send")
    live.seal(attns[0], ups[0])

    attns[0].start()
    ups[0].start()
    downs[0].start()
    packed = jnp.stack([live.pack, sl.flip(live.pack, SIDE)])
    extras = packed[:, 2 * length :]
    segments = extras[:, 0, :length].astype(f32)
    same = segments[:, :, None] == segments[:, None, :]
    position = jnp.arange(length)
    live.put(
        hidden=packed[:, :length].reshape(2 * length, width).astype(f32),
        d_low=packed[:, length : 2 * length].reshape(2 * length, width),
        sections=extras[:, 1, 0].astype(jnp.int32),
        allows=[
            (same & (position[:, None] >= position[None, :])).astype(f32),
            same.astype(f32),
        ],
    )
    live.drop("pack")
    own = jnp.concatenate([live.next[..., :part], out_proj[1]], -1)
    attns.append(live.flow(Gather(sl, own.reshape(2 * rows, -1), 2)))
    ups.append(live.flow(Gather(sl, live.next[..., part:].reshape(2 * rows, -1), 2)))
    live.drop("next")
    live.seal(attns[0], ups[0], downs[0])

    def gains_of(quarters, sections):
        wide = norm_table.shape[1]
        parts = jnp.stack([q[:, 2 * width :] for q in quarters])
        parts = parts.reshape(4, lead // 2, 2, fsdp, rows, 128)
        if wide == 128:
            parts = parts[..., :count, :]
        else:
            parts = parts.reshape(4, lead // 2, 2, fsdp, rows * 128)[..., : count * wide]
            parts = parts.reshape(4, lead // 2, 2, fsdp, count, wide)
        pick = jnp.concatenate([jnp.zeros((2,), jnp.int32), 1 + sections])
        pick = (pick[:, None] == jnp.arange(count)[None, :]).astype(bf16)
        picked = jnp.einsum("sr,qhxdrj->qshxdj", pick, parts, preferred_element_type=f32)
        own, top, core, both = picked
        both = merge(merge(own, core, CORE, 3), merge(top, both, CORE, 3), sl.high[0], 1)
        both = both.reshape(2, 2, 4, width)
        return [both[0], both[1]]

    def attend(layer):
        sems = dma(4 * lead)
        qkv, mixed, keep, low = call(
            partial(attend_kernel, size, lead, 2 * block),
            [((2 * length, part), bf16), ((2 * length, half), bf16), two_f, two_b],
            [attns[layer].place, live.first, *attns[layer].quarters, live.allows[layer]],
            [SMEM, VMEM, ANY, ANY, ANY, ANY, VMEM],
            [w_attn, sems],
            name="attend",
        )
        live.put(**{f"attn{layer}": (live.hidden, live.first, qkv, mixed)})
        live.put(keep=keep, other=sl.flip(low, SIDE))

    def add_norm(which, layer, base):
        return call(
            partial(add_norm_kernel, which),
            [two_f, two_b],
            [base, live.keep, live.other, live.gains[layer]],
            [VMEM] * 4,
            name="add_norm",
        )

    def feed_up(layer):
        attended, second = add_norm(1, layer, live.hidden)
        pre, active = call(
            partial(up_kernel, lead),
            [(wide_b[0], f32), wide_b],
            [ups[layer].place, second, *ups[layer].quarters],
            [SMEM, VMEM, ANY, ANY, ANY, ANY],
            [w_upper, dma(4 * lead)],
            name="up",
        )
        live.put(**{f"feed{layer}": (attended, second, pre, active)})

    def feed_down(layer):
        keep, low = call(
            partial(down_kernel, lead // 2),
            [two_f, two_b],
            [downs[layer].place, live.values[f"feed{layer}"][3], *downs[layer].quarters],
            [SMEM, VMEM, ANY, ANY, ANY, ANY],
            [w_lower, dma(2 * lead)],
            name="down",
        )
        return keep, sl.flip(low, SIDE)

    def feed_back(layer):
        pre = live.values[f"feed{layer}"][2]
        d_pre, keep, low = call(
            partial(feed_back_kernel, lead),
            [wide_b, two_f, two_b],
            [
                ups[layer].place,
                downs[layer].place,
                live.d_low,
                pre,
                *ups[layer].quarters,
                *downs[layer].quarters,
            ],
            [SMEM, SMEM, VMEM, VMEM] + [ANY] * 8,
            [w_upper, w_lower, dma(4 * lead), dma(2 * lead)],
            name="feed_back",
        )
        live.put(d_pre=d_pre, keep=keep, other=sl.flip(low, SIDE))

    def down_grad(layer):
        aligned = feed // 4 // lead % 128 == 0
        active = live.values[f"feed{layer}"][3]
        parts = call(
            partial(weight_grad_kernel, lead // 2, aligned),
            [((feed // 8, width), bf16)] * 4,
            [place, active if aligned else turn(sl, active, lead // 2), live.d_low],
            [SMEM, VMEM, VMEM],
            name="down_grad",
        )
        return live.flow(Scatter(sl, parts, 1))

    def up_grad(layer):
        aligned = block % 128 == 0
        second = live.values[f"feed{layer}"][1]
        parts = call(
            partial(weight_grad_kernel, lead, aligned),
            [quarter] * 4,
            [place, second if aligned else turn(sl, second, lead), live.d_pre],
            [SMEM, VMEM, VMEM],
            name="up_grad",
        )
        return live.flow(Scatter(sl, parts, 2))

    def norm_back(which, layer, hidden):
        grad, d_low, d_gain, d_shift = call(
            partial(norm_back_kernel, which),
            [two_f, two_b, gain_row, gain_row],
            [live.grad, live.keep, live.other, hidden, live.gains[layer]],
            [VMEM] * 5,
            name="norm_back",
        )
        live.put(grad=grad, d_low=d_low)
        live.put(**{f"gains{layer}{which}": jnp.concatenate([d_gain, d_shift], 1)})

    def attend_back(layer):
        norm_back(1, layer, live.values[f"feed{layer}"][0])
        d_qkv, keep, low = call(
            partial(attend_back_kernel, size, lead, 2 * block),
            [((2 * length, part), bf16), two_f, two_b],
            [
                attns[layer].place,
                live.d_low,
                *attns[layer].quarters,
                live.allows[layer],
                live.values[f"attn{layer}"][2],
            ],
            [SMEM, VMEM, ANY, ANY, ANY, ANY, VMEM, VMEM],
            [w_attn, pltpu.VMEM((2 * length, half), bf16), dma(4 * lead)],
            name="attend_back",
        )
        live.put(d_qkv=d_qkv, keep=keep, other=sl.flip(low, SIDE))

    def attend_grad(layer):
        hidden, first, qkv, mixed = live.values[f"attn{layer}"]
        aligned = block % 128 == 0
        if not aligned:
            first, mixed = turn(sl, first, lead), turn(sl, mixed, lead // 2)
        parts = call(
            partial(attend_grad_kernel, lead, aligned),
            [quarter] * 4,
            [place, first, mixed, live.d_qkv, live.d_low],
            [SMEM] + [VMEM] * 4,
            name="attend_grad",
        )
        return live.flow(Scatter(sl, parts, 2))

    def finish(layer, g_attn, g_up, before):
        g_attn = g_attn.value.reshape(2, rows, 2 * width)
        g_up = g_up.value.reshape(2, rows, feed // 2)
        keep, send = split(jnp.concatenate([g_attn[..., :part], g_up], -1), SIDE, 0)
        return update(
            partial(finish_kernel, 2 * block, 2 * fsdp * feeds),
            layer,
            w_big.shape,
            [mine(SIDE)[None], keep, sl.flip(send, SIDE), g_attn[..., part:]],
            [SMEM, VMEM, VMEM, VMEM],
            [m_big, v_big],
            before,
            "finish",
        )

    def finish_down(layer, flow, before):
        return update(
            finish_down_kernel,
            layer,
            w_down.shape,
            [flow.value],
            [VMEM],
            [m_down, v_down],
            before,
            "finish_down",
        )

    def table_grad(layer):
        g_table = jnp.concatenate([live.values[f"gains{layer}0"], live.values[f"gains{layer}1"]], 1)
        if layer == 1:
            hit = jnp.arange(count - 1) == section_ids[0]
            g_table = jnp.where(hit[:, None], g_table, 0.0)
        g_table = g_table.reshape(g_table.shape[0], high, 2, 2, fsdp, norm_table.shape[1])
        g_table = jnp.moveaxis(g_table, 0, 4)
        keep, send = split(g_table, CORE, 2)
        g_table = keep + sl.flip(send, CORE)
        keep, send = split(g_table, SIDE, 1)
        g_table = keep + sl.flip(send, SIDE)
        g_table = g_table.reshape(*(len(sl.high) + len(sl.deep)) * [2], *g_table.shape[-2:])
        for bit in sl.high + sl.deep:
            keep, send = split(g_table, bit, 0)
            g_table = keep + sl.flip(send, bit)
        return g_table

    ups[0].start()
    downs[0].start()
    attns[1].start()
    attns[0].finish()
    live.put(gains=gains_of(attns[0].quarters, live.sections))
    (first,) = call(
        partial(norm_kernel, 0), [two_b], [live.hidden, live.gains[0]], [VMEM] * 2, name="norm"
    )
    live.put(first=first)
    attend(0)
    live.seal(ups[0], downs[0], attns[1])

    downs[0].start()
    attns[1].start()
    ups[1].start()
    ups[0].finish()
    feed_up(0)
    live.seal(downs[0], attns[1], ups[1])

    attns[1].start()
    ups[1].start()
    downs[1].start()
    downs[0].finish()
    keep, other = feed_down(0)
    live.put(keep=keep, other=other)
    live.seal(attns[1], ups[1], downs[1])

    ups[1].start()
    downs[1].start()
    attns[1].finish()
    hidden, first = add_norm(0, 1, live.feed0[0])
    live.put(hidden=hidden, first=first)
    attend(1)
    live.seal(ups[1], downs[1])

    downs[1].start()
    ups[1].finish()
    feed_up(1)
    live.put(grad=live.d_low.astype(f32))
    g_down1 = down_grad(1)
    g_down1.cross()
    live.seal(downs[1])

    g_down1.start()
    downs[1].finish()
    feed_back(1)
    g_up1 = up_grad(1)
    g_up1.cross()
    live.seal(g_down1)

    g_up1.start()
    g_down1.start()
    attend_back(1)
    g_attn1 = attend_grad(1)
    g_attn1.cross()
    live.seal(g_up1, g_down1)

    g_attn1.start()
    g_up1.start()
    g_down1.start()
    norm_back(0, 1, live.attn1[0])
    feed_back(0)
    g_down0, g_up0 = down_grad(0), up_grad(0)
    g_down0.cross()
    g_up0.cross()
    live.seal(g_attn1, g_up1, g_down1)

    g_down0.start()
    g_attn1.start()
    g_up1.start()
    attend_back(0)
    g_attn0 = attend_grad(0)
    g_attn0.cross()
    live.seal(g_down0, g_attn1, g_up1)

    g_up0.start()
    g_down0.start()
    g_attn1.start()
    norm_back(0, 0, live.attn0[0])
    out_keep, out_other = feed_down(1)
    out_act = live.feed1[0][:length] + (out_keep[:length] + out_other[length:].astype(f32))
    live.put(out_act=out_act.astype(bf16), down=finish_down(1, g_down1, []))
    live.seal(g_up0, g_down0, g_attn1)

    g_attn0.start()
    g_up0.start()
    g_down0.start()
    live.put(big=finish(1, g_attn1, g_up1, []), table1=table_grad(1), table0=table_grad(0))
    live.seal(g_attn0, g_up0, g_down0)

    g_attn0.start()
    g_up0.start()
    live.seal(g_attn0, g_up0)

    g_attn0.start()
    live.put(down=finish_down(0, g_down0, live.down))
    live.seal(g_attn0)

    grad_big, new_m_big, step_big = finish(0, g_attn0, g_up0, live.big)
    grad_down, new_m_down, step_down = live.down
    grad_table = jnp.concatenate([live.table0, live.table1], 0)
    new_m_table, step_table = adam_update(m_table, v_table, grad_table)
    return (
        live.out_act[None],
        live.d_low[:length][None],
        grad_big,
        grad_down,
        grad_table,
        new_m_big,
        new_m_down,
        new_m_table,
        step_big,
        step_down,
        step_table,
    )


def solution(mesh):
    both = ("dp", "fsdp")
    rows, middle, last = P(both, None, None), P(None, both, None), P(None, both)
    return jax.shard_map(
        partial(body, mesh.shape["dp"], mesh.shape["fsdp"]),
        mesh=mesh,
        in_specs=(rows, rows, P(both, None), P(both), middle, middle, last)
        + 2 * (middle, middle, last),
        out_specs=(rows, rows) + 3 * (middle, middle, last),
        check_vma=False,
    )
```

time: 712 us -> 490 us (0.69)
  waiting for transfers between devices: 362 us -> 261 us
  Pallas kernels: 0 us -> 92.6 us
  other arithmetic: 99.5 us -> 10.4 us
  local copies, waits for them, and re-layouts: 90 us -> 32.4 us
  matrix products: 48.2 us -> 0.2 us
  starting transfers between devices: 97 us -> 82.1 us
    ppermute x96 -> x84, waiting for transfers between devices: 362 us -> 261 us  [flip(): lax.ppermute(value, axis, [(i, i ^ mask) for i in range(self.size[axis])])]
    pallas_call x0 -> x58, Pallas kernels: none -> 92.6 us  [the longest x54 85.1 us: call(): pl.pallas_call(kernel, out_shape=[jax.ShapeDtypeStruct(shape, kind) for s...]
    dot_general x34 -> x1, matrix products: 47.2 us -> 0.2 us  [gains_of(): jnp.einsum('sr,qhxdrj->qshxdj', pick, parts, preferred_element_type=f32)]
    select_n x52 -> x4, other arithmetic: 42.9 us -> 0.14 us  [merge(): jnp.where(side == 0, jnp.stack([own, other], pos), jnp.stack([other, own]...]
    convert_element_type x33 -> x7, other arithmetic: 22.8 us -> 2.65 us  [the longest x1 0.81 us: body(): extras[:, 1, 0].astype(jnp.int32)]
    ppermute x96 -> x84, starting transfers between devices: 97 us -> 82.1 us  [flip(): lax.ppermute(value, axis, [(i, i ^ mask) for i in range(self.size[axis])])]
    squeeze x32 -> x9, local copies, waits for them, and re-layouts: 14.2 us -> 0.06 us  [split(): send = lax.dynamic_index_in_dim(value, 1 - side, pos, keepdims=False)]
    reshape x18 -> x6, local copies, waits for them, and re-layouts: 14.3 us -> 1.1 us  [the longest x1 0.38 us: body(): up = w_big[:, :, 4 * width:].reshape(2, rows, high, 2, 2 * fsdp * feeds)]
  transfers between devices with their start and end apart: 96 -> 84, of which waited for: 40 -> 43; matrix products, arithmetic and copies ran while one was open for 29% -> 4% of each run, Pallas kernels for 0% -> 17%
where the time goes in v2:
time: 490 us; the launch traced here: 482 us
  waiting for transfers between devices  261 us (53%)
  Pallas kernels  92.6 us (19%)
  starting transfers between devices  82.1 us (17%)
  local copies, waits for them, and re-layouts  32.4 us (7%)
  other arithmetic  10.4 us (2%)
    ppermute x84, waiting for transfers between devices, flip(): lax.ppermute(value, axis, [(i, i ^ mask) for i in range(self.size[axis])])  261 us
    pallas_call x54, Pallas kernels, call(): pl.pallas_call(kernel, out_shape=[jax.ShapeDtypeStruct(shape, kind) for s...  85.1 us
    ppermute x84, starting transfers between devices, flip(): lax.ppermute(value, axis, [(i, i ^ mask) for i in range(self.size[axis])])  82.1 us
    unnamed x138, local copies, waits for them, and re-layouts  18.9 us
  transfers between devices with their start and end apart: 84, of which 43 were waited for; matrix products, arithmetic and copies ran while one was open for 4% of the time, Pallas kernels for 17%

profile of v2, /device:TPU:0, one launch (start us, length us, event | category | flops | bytes accessed | tf_op | source)
XLA Modules:
  0.0 482.1 jit_solution(6946151823757304168)
XLA Ops:
  2.0 2.7 dynamic-slice_reduce_fusion.1
  4.8 3.0 collective-permute-start
  14.4 2.6 collective-permute-start.1
  18.6 10.8 %collective-permute-done.1 = bf16[64,2176]{1,0:T(8,128)(2,1)S(1)} collective-permute-done((bf16[64,2176]{1,0:T(8,128)(2,1)S(1)}, bf16[64,2176]{1,0:T(8,128)(2,1)S(1)}, u32[]{:S(2)}, u32[]{:S(2)}) %collective-permute-start.1) | collective-permute-done | bytes 278560 | tf_op jit(solution)/shard_map/ppermute | solution.py:41
  31.2 3.4 collective-permute-start.5
  36.1 12.5 %collective-permute-done.5 = bf16[64,2048]{1,0:T(8,128)(2,1)S(1)} collective-permute-done((bf16[64,2048]{1,0:T(8,128)(2,1)S(1)}, bf16[64,2048]{1,0:T(8,128)(2,1)S(1)}, u32[]{:S(2)}, u32[]{:S(2)}) %collective-permute-start.5) | collective-permute-done | bytes 262176 | tf_op jit(solution)/shard_map/ppermute | solution.py:41
  50.5 3.4 collective-permute-start.10
  58.7 11.1 %collective-permute-done.7 = bf16[128,1024]{1,0:T(8,128)(2,1)S(1)} collective-permute-done((bf16[128,1024]{1,0:T(8,128)(2,1)S(1)}, bf16[128,1024]{1,0:T(8,128)(2,1)S(1)}, u32[]{:S(2)}, u32[]{:S(2)}) %collective-permute-start.7) | collective-permute-done | bytes 262176 | tf_op jit(solution)/shard_map/ppermute | solution.py:41
  74.4 4.7 collective-permute-done.8.q1
  87.1 10.0 %attend.2 = (bf16[256,1536]{1,0:T(8,128)(2,1)S(1)}, bf16[256,512]{1,0:T(8,128)(2,1)S(1)}, f32[256,1024]{1,0:T(8,128)S(1)}, bf16[256,1024]{1,0:T(8,128)(2,1)}) custom-call(s32[2]{0:T(128)S(1)} %pad_add_fusion.place.up_place.dn_place, bf16[256,1024]{1,0:T(8,128)(2,1)S(1)} %norm.1.f.left, bf16[256,2176]{1,0:T(8,128)(2,1)S(1)} %bitcast.262, ...), custom_call_target="tpu_custom_call" | custom-call | tf_op jit(solution)/shard_map/attend/pallas_call | solution.py:53
  101.3 12.9 %collective-permute-done.16 = bf16[64,2048]{1,0:T(8,128)(2,1)S(1)} collective-permute-done((bf16[64,2048]{1,0:T(8,128)(2,1)S(1)}, bf16[64,2048]{1,0:T(8,128)(2,1)S(1)}, u32[]{:S(2)}, u32[]{:S(2)}) %collective-permute-start.16) | collective-permute-done | bytes 262176 | tf_op jit(solution)/shard_map/ppermute | solution.py:41
  119.7 3.0 collective-permute-start.21
  125.4 12.2 %collective-permute-done.21 = bf16[64,2048]{1,0:T(8,128)(2,1)S(1)} collective-permute-done((bf16[64,2048]{1,0:T(8,128)(2,1)}, bf16[64,2048]{1,0:T(8,128)(2,1)S(1)}, u32[]{:S(2)}, u32[]{:S(2)}) %collective-permute-start.21) | collective-permute-done | bytes 262176 | tf_op jit(solution)/shard_map/ppermute | solution.py:41
  139.8 3.9 up.2
  151.8 12.2 %collective-permute-done.24 = bf16[128,1024]{1,0:T(8,128)(2,1)S(1)} collective-permute-done((bf16[128,1024]{1,0:T(8,128)(2,1)S(1)}, bf16[128,1024]{1,0:T(8,128)(2,1)S(1)}, u32[]{:S(2)}, u32[]{:S(2)}) %collective-permute-start.24) | collective-permute-done | bytes 262176 | tf_op jit(solution)/shard_map/ppermute | solution.py:41
  165.4 4.6 collective-permute-done.25.q1
  172.7 7.7 %attend.3 = (bf16[256,1536]{1,0:T(8,128)(2,1)S(1)}, bf16[256,512]{1,0:T(8,128)(2,1)S(1)}, f32[256,1024]{1,0:T(8,128)S(1)}, bf16[256,1024]{1,0:T(8,128)(2,1)S(1)}) custom-call(s32[2]{0:T(128)S(1)} %pad_add_fusion.place.up_place.dn_place, bf16[256,1024]{1,0:T(8,128)(2,1)S(1)} %get-tuple-element.797.f.left, bf16[256,2048]{1,0:T(8,128)(2,1)S(1)} %bitcast.266, ...), custom_call_target="tpu_custom_call" | custom-call | tf_op jit(solution)/shard_map/attend/pallas_call | solution.py:53
  181.6 3.7 collective-permute-done.30
  185.4 10.2 %collective-permute-done.31.q1.u1 = bf16[256,2048]{1,0:T(8,128)(2,1)S(1)} collective-permute-done((bf16[256,2048]{1,0:T(8,128)(2,1)S(1)}, bf16[256,2048]{1,0:T(8,128)(2,1)S(1)}, u32[]{:S(2)}, u32[]{:S(2)}) %collective-permute-start.31) | collective-permute-done | bytes 1048608 | tf_op jit(solution)/shard_map/ppermute | solution.py:41
  196.1 2.2 collective-permute-done.33.q3.u3
  198.3 3.0 up.3
  206.2 22.7 %collective-permute-done.34.n1.q1 = bf16[512,1024]{1,0:T(8,128)(2,1)S(1)} collective-permute-done((bf16[512,1024]{1,0:T(8,128)(2,1)S(1)}, bf16[512,1024]{1,0:T(8,128)(2,1)S(1)}, u32[]{:S(2)}, u32[]{:S(2)}) %collective-permute-start.34) | collective-permute-done | bytes 1048608 | tf_op jit(solution)/shard_map/ppermute | solution.py:41
  231.6 4.6 feed_back.2
  239.7 14.8 %collective-permute-done.40 = bf16[512,1024]{1,0:T(8,128)(2,1)S(1)} collective-permute-done((bf16[512,1024]{1,0:T(8,128)(2,1)S(1)}, bf16[512,1024]{1,0:T(8,128)(2,1)S(1)}, u32[]{:S(2)}, u32[]{:S(2)}) %collective-permute-start.40) | collective-permute-done | bytes 1048608 | tf_op jit(solution)/shard_map/ppermute | solution.py:41
  256.9 9.3 %attend_back.2 = (bf16[256,1536]{1,0:T(8,128)(2,1)S(1)}, f32[256,1024]{1,0:T(8,128)S(1)}, bf16[256,1024]{1,0:T(8,128)(2,1)S(1)}) custom-call(s32[2]{0:T(128)S(1)} %pad_add_fusion.place.up_place.dn_place, bf16[256,1024]{1,0:T(8,128)(2,1)S(1)} %get-tuple-element.805.d, bf16[256,2048]{1,0:T(8,128)(2,1)S(1)} %bitcast.267, ...), custom_call_target="tpu_custom_call" | custom-call | tf_op jit(solution)/shard_map/attend_back/pallas_call | solution.py:53
  270.9 11.7 %collective-permute-done.44 = bf16[256,1024]{1,0:T(8,128)(2,1)S(1)} collective-permute-done((bf16[256,1024]{1,0:T(8,128)(2,1)S(1)}, bf16[256,1024]{1,0:T(8,128)(2,1)S(1)}, u32[]{:S(2)}, u32[]{:S(2)}) %collective-permute-start.44) | collective-permute-done | bytes 524320 | tf_op jit(solution)/shard_map/ppermute | solution.py:41
  285.5 2.2 collective-permute-start.49
  290.4 4.5 feed_back.3
  298.2 3.0 collective-permute-done.49
  303.0 4.7 collective-permute-done.51
  311.8 8.1 %collective-permute-done.48.other = bf16[256,1024]{1,0:T(8,128)(2,1)S(1)} collective-permute-done((bf16[256,1024]{1,0:T(8,128)(2,1)S(1)}, bf16[256,1024]{1,0:T(8,128)(2,1)S(1)}, u32[]{:S(2)}, u32[]{:S(2)}) %collective-permute-start.48) | collective-permute-done | bytes 524320 | tf_op jit(solution)/shard_map/ppermute | solution.py:41
  322.0 10.7 %attend_back.3 = (bf16[256,1536]{1,0:T(8,128)(2,1)S(1)}, f32[256,1024]{1,0:T(8,128)S(1)}, bf16[256,1024]{1,0:T(8,128)(2,1)S(1)}) custom-call(s32[2]{0:T(128)S(1)} %pad_add_fusion.place.up_place.dn_place, bf16[256,1024]{1,0:T(8,128)(2,1)S(1)} %get-tuple-element.921.d, bf16[256,2176]{1,0:T(8,128)(2,1)S(1)} %bitcast.263, ...), custom_call_target="tpu_custom_call" | custom-call | tf_op jit(solution)/shard_map/attend_back/pallas_call | solution.py:53
  338.5 12.4 %collective-permute-done.57 = bf16[64,2048]{1,0:T(8,128)(2,1)S(1)} collective-permute-done((bf16[64,2048]{1,0:T(8,128)(2,1)S(1)}, bf16[64,2048]{1,0:T(8,128)(2,1)S(1)}, u32[]{:S(2)}, u32[]{:S(2)}) %collective-permute-start.57) | collective-permute-done | bytes 262176 | tf_op jit(solution)/shard_map/ppermute | solution.py:41
  351.8 12.6 %collective-permute-done.58 = bf16[128,2048]{1,0:T(8,128)(2,1)S(1)} collective-permute-done((bf16[128,2048]{1,0:T(8,128)(2,1)S(1)}, bf16[128,2048]{1,0:T(8,128)(2,1)S(1)}, u32[]{:S(2)}, u32[]{:S(2)}) %collective-permute-start.58) | collective-permute-done | bytes 524320 | tf_op jit(solution)/shard_map/ppermute | solution.py:41
  375.3 2.1 down.3
  384.7 9.6 %collective-permute-done.64 = bf16[256,1024]{1,0:T(8,128)(2,1)S(1)} collective-permute-done((bf16[256,1024]{1,0:T(8,128)(2,1)S(1)}, bf16[256,1024]{1,0:T(8,128)(2,1)S(1)}, u32[]{:S(2)}, u32[]{:S(2)}) %collective-permute-start.64) | collective-permute-done | bytes 524320 | tf_op jit(solution)/shard_map/ppermute | solution.py:41
  400.1 2.4 collective-permute-done.68
  403.2 2.9 collective-permute-done.69
  413.4 2.5 collective-permute-start.78
  417.3 10.6 %collective-permute-done.75 = f32[2,8,128]{2,1,0:T(8,128)S(1)} collective-permute-done((f32[2,8,128]{2,1,0:T(8,128)S(1)}, f32[2,8,128]{2,1,0:T(8,128)S(1)}, u32[]{:S(2)}, u32[]{:S(2)}) %collective-permute-start.75) | collective-permute-done | bytes 8224 | tf_op jit(solution)/shard_map/ppermute | solution.py:41
  427.9 3.5 collective-permute-start.71
  436.7 2.4 finish.2
  442.9 6.5 %collective-permute-done.80 = bf16[64,2048]{1,0:T(8,128)(2,1)S(1)} collective-permute-done((bf16[64,2048]{1,0:T(8,128)(2,1)S(1)}, bf16[64,2048]{1,0:T(8,128)(2,1)S(1)}, u32[]{:S(2)}, u32[]{:S(2)}) %collective-permute-start.80) | collective-permute-done | bytes 262176 | tf_op jit(solution)/shard_map/ppermute | solution.py:41
  449.4 6.9 %collective-permute-done.81 = bf16[128,2048]{1,0:T(8,128)(2,1)S(1)} collective-permute-done((bf16[128,2048]{1,0:T(8,128)(2,1)S(1)}, bf16[128,2048]{1,0:T(8,128)(2,1)S(1)}, u32[]{:S(2)}, u32[]{:S(2)}) %collective-permute-start.81) | collective-permute-done | bytes 524320 | tf_op jit(solution)/shard_map/ppermute | solution.py:41
  456.4 2.6 collective-permute-start.82
  460.3 7.7 %collective-permute-done.82 = bf16[64,2048]{1,0:T(8,128)(2,1)S(1)} collective-permute-done((bf16[64,2048]{1,0:T(8,128)(2,1)S(1)}, bf16[64,2048]{1,0:T(8,128)(2,1)S(1)}, u32[]{:S(2)}, u32[]{:S(2)}) %collective-permute-start.82) | collective-permute-done | bytes 262176 | tf_op jit(solution)/shard_map/ppermute | solution.py:41
  470.7 8.7 %collective-permute-done.83.other = f32[32,3584]{1,0:T(8,128)S(1)} collective-permute-done((f32[32,3584]{1,0:T(8,128)S(1)}, f32[32,3584]{1,0:T(8,128)S(1)}, u32[]{:S(2)}, u32[]{:S(2)}) %collective-permute-start.83) | collective-permute-done | bytes 458784 | tf_op jit(solution)/shard_map/ppermute | solution.py:41
  479.4 2.4 finish.3
  (425 shorter events, 147.0 us)
Async XLA Ops:
  30.5 18.8 %collective-permute-start.4 = (bf16[128,2176]{1,0:T(8,128)(2,1)S(1)}, bf16[128,2176]{1,0:T(8,128)(2,1)S(1)}, u32[]{:S(2)}, u32[]{:S(2)}) collective-permute-start(bf16[128,2176]{1,0:T(8,128)(2,1)S(1)} %bitcast.287), channel_id=1, source_target_pairs={{0,1},{1,0},{2,3},{3,2},{4,5},{5,4},{6,7},{7,6},{8,9},{9,8},{10,11... | collective-permute-start | bytes 1671176 | tf_op jit(solution)/shard_map/ppermute | solution.py:41
  31.2 17.4 %collective-permute-start.5 = (bf16[64,2048]{1,0:T(8,128)(2,1)S(1)}, bf16[64,2048]{1,0:T(8,128)(2,1)S(1)}, u32[]{:S(2)}, u32[]{:S(2)}) collective-permute-start(bf16[64,2048]{1,0:T(8,128)(2,1)S(1)} %bitcast.317), channel_id=1, source_target_pairs={{0,2},{1,3},{2,0},{3,1},{4,6},{5,7},{6,4},{7,5},{8,10},{9,11},{10,... | collective-permute-start | bytes 786440 | tf_op jit(solution)/shard_map/ppermute | solution.py:41
  49.4 21.3 %collective-permute-start.6 = (bf16[272,1024]{1,0:T(8,128)(2,1)}, bf16[272,1024]{1,0:T(8,128)(2,1)S(1)}, u32[]{:S(2)}, u32[]{:S(2)}) collective-permute-start(bf16[272,1024]{1,0:T(8,128)(2,1)} %pad_maximum_fusion), channel_id=1, source_target_pairs={{0,8},{4,12},{8,0},{12,4},{16,24},{20,28},{24,16},{28,20},{1,9},{5... | collective-permute-start | bytes 1671176 | tf_op jit(solution)/shard_map/ppermute | solution.py:41
  50.5 20.1 %collective-permute-start.10 = (bf16[128,2048]{1,0:T(8,128)(2,1)S(1)}, bf16[128,2048]{1,0:T(8,128)(2,1)S(1)}, u32[]{:S(2)}, u32[]{:S(2)}) collective-permute-start(bf16[128,2048]{1,0:T(8,128)(2,1)S(1)} %bitcast.297), channel_id=1, source_target_pairs={{0,1},{1,0},{2,3},{3,2},{4,5},{5,4},{6,7},{7,6},{8,9},{9,8},{10,11... | collective-permute-start | bytes 1572872 | tf_op jit(solution)/shard_map/ppermute | solution.py:41
  54.0 25.2 %collective-permute-start.8 = (bf16[256,2176]{1,0:T(8,128)(2,1)S(1)}, bf16[256,2176]{1,0:T(8,128)(2,1)}, u32[]{:S(2)}, u32[]{:S(2)}) collective-permute-start(bf16[256,2176]{1,0:T(8,128)(2,1)S(1)} %bitcast.259), channel_id=1, source_target_pairs={{0,16},{4,20},{8,24},{12,28},{16,0},{20,4},{24,8},{28,12},{1,17},{... | collective-permute-start | bytes 3342344 | tf_op jit(solution)/shard_map/ppermute | solution.py:41
  55.5 23.7 %collective-permute-start.9 = (bf16[256,2176]{1,0:T(8,128)(2,1)S(1)}, bf16[256,2176]{1,0:T(8,128)(2,1)S(1)}, u32[]{:S(2)}, u32[]{:S(2)}) collective-permute-start(bf16[256,2176]{1,0:T(8,128)(2,1)S(1)} %bitcast.260), channel_id=1, source_target_pairs={{0,4},{4,0},{8,12},{12,8},{16,20},{20,16},{24,28},{28,24},{1,5},{5... | collective-permute-start | bytes 3342344 | tf_op jit(solution)/shard_map/ppermute | solution.py:41
  81.1 37.5 %collective-permute-start.14 = (bf16[256,2048]{1,0:T(8,128)(2,1)S(1)}, bf16[256,2048]{1,0:T(8,128)(2,1)}, u32[]{:S(2)}, u32[]{:S(2)}) collective-permute-start(bf16[256,2048]{1,0:T(8,128)(2,1)S(1)} %bitcast.268), channel_id=1, source_target_pairs={{0,16},{4,20},{8,24},{12,28},{16,0},{20,4},{24,8},{28,12},{1,17},{... | collective-permute-start | bytes 3145736 | tf_op jit(solution)/shard_map/ppermute | solution.py:41
  82.6 36.0 %collective-permute-start.15 = (bf16[256,2048]{1,0:T(8,128)(2,1)S(1)}, bf16[256,2048]{1,0:T(8,128)(2,1)}, u32[]{:S(2)}, u32[]{:S(2)}) collective-permute-start(bf16[256,2048]{1,0:T(8,128)(2,1)S(1)} %bitcast.269), channel_id=1, source_target_pairs={{0,4},{4,0},{8,12},{12,8},{16,20},{20,16},{24,28},{28,24},{1,5},{5... | collective-permute-start | bytes 3145736 | tf_op jit(solution)/shard_map/ppermute | solution.py:41
  83.8 31.3 %collective-permute-start.13 = (bf16[256,1024]{1,0:T(8,128)(2,1)}, bf16[256,1024]{1,0:T(8,128)(2,1)}, u32[]{:S(2)}, u32[]{:S(2)}) collective-permute-start(bf16[256,1024]{1,0:T(8,128)(2,1)} %bitcast.289), channel_id=1, source_target_pairs={{0,1},{1,0},{2,3},{3,2},{4,5},{5,4},{6,7},{7,6},{8,9},{9,8},{10,11... | collective-permute-start | bytes 1572872 | tf_op jit(solution)/shard_map/ppermute | solution.py:41
  98.7 19.8 %collective-permute-start.12 = (bf16[256,1024]{1,0:T(8,128)(2,1)}, bf16[256,1024]{1,0:T(8,128)(2,1)}, u32[]{:S(2)}, u32[]{:S(2)}) collective-permute-start(bf16[256,1024]{1,0:T(8,128)(2,1)} %get-tuple-element.585), channel_id=1, source_target_pairs={{0,8},{4,12},{8,0},{12,4},{16,24},{20,28},{24,16},{28,20},{1,9},{5... | collective-permute-start | bytes 1572872 | tf_op jit(solution)/shard_map/ppermute | solution.py:41
  118.6 21.2 %collective-permute-start.17 = (bf16[256,2048]{1,0:T(8,128)(2,1)}, bf16[256,2048]{1,0:T(8,128)(2,1)S(1)}, u32[]{:S(2)}, u32[]{:S(2)}) collective-permute-start(bf16[256,2048]{1,0:T(8,128)(2,1)} %collective-permute-done.14.q1.u1), channel_id=1, source_target_pairs={{0,4},{4,0},{8,12},{12,8},{16,20},{20,16},{24,28},{28,24},{1,5},{5... | collective-permute-start | bytes 3145736 | tf_op jit(solution)/shard_map/ppermute | solution.py:41
  118.6 25.8 %collective-permute-start.18 = (bf16[512,1024]{1,0:T(8,128)(2,1)}, bf16[512,1024]{1,0:T(8,128)(2,1)S(1)}, u32[]{:S(2)}, u32[]{:S(2)}) collective-permute-start(bf16[512,1024]{1,0:T(8,128)(2,1)} %bitcast.280), channel_id=1, source_target_pairs={{0,16},{4,20},{8,24},{12,28},{16,0},{20,4},{24,8},{28,12},{1,17},{... | collective-permute-start | bytes 3145736 | tf_op jit(solution)/shard_map/ppermute | solution.py:41
  119.5 24.9 %collective-permute-start.19 = (bf16[512,1024]{1,0:T(8,128)(2,1)}, bf16[512,1024]{1,0:T(8,128)(2,1)S(1)}, u32[]{:S(2)}, u32[]{:S(2)}) collective-permute-start(bf16[512,1024]{1,0:T(8,128)(2,1)} %bitcast.281), channel_id=1, source_target_pairs={{0,4},{4,0},{8,12},{12,8},{16,20},{20,16},{24,28},{28,24},{1,5},{5... | collective-permute-start | bytes 3145736 | tf_op jit(solution)/shard_map/ppermute | solution.py:41
  119.7 20.0 %collective-permute-start.20 = (bf16[128,2048]{1,0:T(8,128)(2,1)}, bf16[128,2048]{1,0:T(8,128)(2,1)S(1)}, u32[]{:S(2)}, u32[]{:S(2)}) collective-permute-start(bf16[128,2048]{1,0:T(8,128)(2,1)} %bitcast.293), channel_id=1, source_target_pairs={{0,1},{1,0},{2,3},{3,2},{4,5},{5,4},{6,7},{7,6},{8,9},{9,8},{10,11... | collective-permute-start | bytes 1572872 | tf_op jit(solution)/shard_map/ppermute | solution.py:41
  119.7 17.9 %collective-permute-start.21 = (bf16[64,2048]{1,0:T(8,128)(2,1)}, bf16[64,2048]{1,0:T(8,128)(2,1)S(1)}, u32[]{:S(2)}, u32[]{:S(2)}) collective-permute-start(bf16[64,2048]{1,0:T(8,128)(2,1)} %bitcast.318), channel_id=1, source_target_pairs={{0,2},{1,3},{2,0},{3,1},{4,6},{5,7},{6,4},{7,5},{8,10},{9,11},{10,... | collective-permute-start | bytes 786440 | tf_op jit(solution)/shard_map/ppermute | solution.py:41
  144.4 25.6 %collective-permute-start.25 = (bf16[256,2048]{1,0:T(8,128)(2,1)S(1)}, bf16[256,2048]{1,0:T(8,128)(2,1)S(1)}, u32[]{:S(2)}, u32[]{:S(2)}) collective-permute-start(bf16[256,2048]{1,0:T(8,128)(2,1)S(1)} %bitcast.264), channel_id=1, source_target_pairs={{0,16},{4,20},{8,24},{12,28},{16,0},{20,4},{24,8},{28,12},{1,17},{... | collective-permute-start | bytes 3145736 | tf_op jit(solution)/shard_map/ppermute | solution.py:41
  145.3 24.7 %collective-permute-start.26 = (bf16[256,2048]{1,0:T(8,128)(2,1)S(1)}, bf16[256,2048]{1,0:T(8,128)(2,1)S(1)}, u32[]{:S(2)}, u32[]{:S(2)}) collective-permute-start(bf16[256,2048]{1,0:T(8,128)(2,1)S(1)} %bitcast.265), channel_id=1, source_target_pairs={{0,4},{4,0},{8,12},{12,8},{16,20},{20,16},{24,28},{28,24},{1,5},{5... | collective-permute-start | bytes 3145736 | tf_op jit(solution)/shard_map/ppermute | solution.py:41
  145.5 19.8 %collective-permute-start.27 = (bf16[128,2048]{1,0:T(8,128)(2,1)S(1)}, bf16[128,2048]{1,0:T(8,128)(2,1)S(1)}, u32[]{:S(2)}, u32[]{:S(2)}) collective-permute-start(bf16[128,2048]{1,0:T(8,128)(2,1)S(1)} %bitcast.291), channel_id=1, source_target_pairs={{0,1},{1,0},{2,3},{3,2},{4,5},{5,4},{6,7},{7,6},{8,9},{9,8},{10,11... | collective-permute-start | bytes 1572872 | tf_op jit(solution)/shard_map/ppermute | solution.py:41
  149.2 20.8 %collective-permute-start.23 = (bf16[256,1024]{1,0:T(8,128)(2,1)S(1)}, bf16[256,1024]{1,0:T(8,128)(2,1)S(1)}, u32[]{:S(2)}, u32[]{:S(2)}) collective-permute-start(bf16[256,1024]{1,0:T(8,128)(2,1)S(1)} %get-tuple-element.635), channel_id=1, source_target_pairs={{0,8},{4,12},{8,0},{12,4},{16,24},{20,28},{24,16},{28,20},{1,9},{5... | collective-permute-start | bytes 1572872 | tf_op jit(solution)/shard_map/ppermute | solution.py:41
  170.0 25.6 %collective-permute-start.31 = (bf16[256,2048]{1,0:T(8,128)(2,1)S(1)}, bf16[256,2048]{1,0:T(8,128)(2,1)S(1)}, u32[]{:S(2)}, u32[]{:S(2)}) collective-permute-start(bf16[256,2048]{1,0:T(8,128)(2,1)S(1)} %bitcast.272), channel_id=1, source_target_pairs={{0,16},{4,20},{8,24},{12,28},{16,0},{20,4},{24,8},{28,12},{1,17},{... | collective-permute-start | bytes 3145736 | tf_op jit(solution)/shard_map/ppermute | solution.py:41
  170.9 24.7 %collective-permute-start.32 = (bf16[256,2048]{1,0:T(8,128)(2,1)S(1)}, bf16[256,2048]{1,0:T(8,128)(2,1)S(1)}, u32[]{:S(2)}, u32[]{:S(2)}) collective-permute-start(bf16[256,2048]{1,0:T(8,128)(2,1)S(1)} %bitcast.273), channel_id=1, source_target_pairs={{0,4},{4,0},{8,12},{12,8},{16,20},{20,16},{24,28},{28,24},{1,5},{5... | collective-permute-start | bytes 3145736 | tf_op jit(solution)/shard_map/ppermute | solution.py:41
  180.4 15.2 %collective-permute-start.29 = (bf16[256,1024]{1,0:T(8,128)(2,1)S(1)}, bf16[256,1024]{1,0:T(8,128)(2,1)S(1)}, u32[]{:S(2)}, u32[]{:S(2)}) collective-permute-start(bf16[256,1024]{1,0:T(8,128)(2,1)S(1)} %get-tuple-element.670), channel_id=1, source_target_pairs={{0,8},{4,12},{8,0},{12,4},{16,24},{20,28},{24,16},{28,20},{1,9},{5... | collective-permute-start | bytes 1572872 | tf_op jit(solution)/shard_map/ppermute | solution.py:41
  203.4 25.4 %collective-permute-start.34 = (bf16[512,1024]{1,0:T(8,128)(2,1)S(1)}, bf16[512,1024]{1,0:T(8,128)(2,1)S(1)}, u32[]{:S(2)}, u32[]{:S(2)}) collective-permute-start(bf16[512,1024]{1,0:T(8,128)(2,1)S(1)} %bitcast.276), channel_id=1, source_target_pairs={{0,16},{4,20},{8,24},{12,28},{16,0},{20,4},{24,8},{28,12},{1,17},{... | collective-permute-start | bytes 3145736 | tf_op jit(solution)/shard_map/ppermute | solution.py:41
  204.2 24.6 %collective-permute-start.35 = (bf16[512,1024]{1,0:T(8,128)(2,1)S(1)}, bf16[512,1024]{1,0:T(8,128)(2,1)S(1)}, u32[]{:S(2)}, u32[]{:S(2)}) collective-permute-start(bf16[512,1024]{1,0:T(8,128)(2,1)S(1)} %bitcast.277), channel_id=1, source_target_pairs={{0,4},{4,0},{8,12},{12,8},{16,20},{20,16},{24,28},{28,24},{1,5},{5... | collective-permute-start | bytes 3145736 | tf_op jit(solution)/shard_map/ppermute | solution.py:41
  204.3 24.5 %collective-permute-start.36 = (bf16[512,1024]{1,0:T(8,128)(2,1)S(1)}, bf16[512,1024]{1,0:T(8,128)(2,1)S(1)}, u32[]{:S(2)}, u32[]{:S(2)}) collective-permute-start(bf16[512,1024]{1,0:T(8,128)(2,1)S(1)} %get-tuple-element.730), channel_id=1, source_target_pairs={{0,4},{4,0},{8,12},{12,8},{16,20},{20,16},{24,28},{28,24},{1,5},{5... | collective-permute-start | bytes 3145736 | tf_op jit(solution)/shard_map/ppermute | solution.py:41
  228.9 25.6 %collective-permute-start.40 = (bf16[512,1024]{1,0:T(8,128)(2,1)S(1)}, bf16[512,1024]{1,0:T(8,128)(2,1)S(1)}, u32[]{:S(2)}, u32[]{:S(2)}) collective-permute-start(bf16[512,1024]{1,0:T(8,128)(2,1)S(1)} %add_low.6), channel_id=1, source_target_pairs={{0,16},{4,20},{8,24},{12,28},{16,0},{20,4},{24,8},{28,12},{1,17},{... | collective-permute-start | bytes 3145736 | tf_op jit(solution)/shard_map/ppermute | solution.py:41
  238.1 16.8 %collective-permute-start.42 = (bf16[256,2048]{1,0:T(8,128)(2,1)S(1)}, bf16[256,2048]{1,0:T(8,128)(2,1)S(1)}, u32[]{:S(2)}, u32[]{:S(2)}) collective-permute-start(bf16[256,2048]{1,0:T(8,128)(2,1)S(1)} %get-tuple-element.789), channel_id=1, source_target_pairs={{0,4},{4,0},{8,12},{12,8},{16,20},{20,16},{24,28},{28,24},{1,5},{5... | collective-permute-start | bytes 3145736 | tf_op jit(solution)/shard_map/ppermute | solution.py:41
  238.3 16.9 %collective-permute-start.41 = (bf16[256,2048]{1,0:T(8,128)(2,1)S(1)}, bf16[256,2048]{1,0:T(8,128)(2,1)S(1)}, u32[]{:S(2)}, u32[]{:S(2)}) collective-permute-start(bf16[256,2048]{1,0:T(8,128)(2,1)S(1)} %get-tuple-element.787), channel_id=1, source_target_pairs={{0,4},{4,0},{8,12},{12,8},{16,20},{20,16},{24,28},{28,24},{1,5},{5... | collective-permute-start | bytes 3145736 | tf_op jit(solution)/shard_map/ppermute | solution.py:41
  238.7 16.5 %collective-permute-start.39 = (bf16[256,1024]{1,0:T(8,128)(2,1)S(1)}, bf16[256,1024]{1,0:T(8,128)(2,1)S(1)}, u32[]{:S(2)}, u32[]{:S(2)}) collective-permute-start(bf16[256,1024]{1,0:T(8,128)(2,1)S(1)} %get-tuple-element.764), channel_id=1, source_target_pairs={{0,8},{4,12},{8,0},{12,4},{16,24},{20,28},{24,16},{28,20},{1,9},{5... | collective-permute-start | bytes 1572872 | tf_op jit(solution)/shard_map/ppermute | solution.py:41
  255.2 27.5 %collective-permute-start.45 = (bf16[256,2048]{1,0:T(8,128)(2,1)S(1)}, bf16[256,2048]{1,0:T(8,128)(2,1)S(1)}, u32[]{:S(2)}, u32[]{:S(2)}) collective-permute-start(bf16[256,2048]{1,0:T(8,128)(2,1)S(1)} %add_low.7), channel_id=1, source_target_pairs={{0,16},{4,20},{8,24},{12,28},{16,0},{20,4},{24,8},{28,12},{1,17},{... | collective-permute-start | bytes 3145736 | tf_op jit(solution)/shard_map/ppermute | solution.py:41
  268.1 15.3 %collective-permute-start.46 = (bf16[256,2048]{1,0:T(8,128)(2,1)S(1)}, bf16[256,2048]{1,0:T(8,128)(2,1)S(1)}, u32[]{:S(2)}, u32[]{:S(2)}) collective-permute-start(bf16[256,2048]{1,0:T(8,128)(2,1)S(1)} %get-tuple-element.848), channel_id=1, source_target_pairs={{0,4},{4,0},{8,12},{12,8},{16,20},{20,16},{24,28},{28,24},{1,5},{5... | collective-permute-start | bytes 3145736 | tf_op jit(solution)/shard_map/ppermute | solution.py:41
  283.4 24.3 %collective-permute-start.51 = (bf16[256,2048]{1,0:T(8,128)(2,1)S(1)}, bf16[256,2048]{1,0:T(8,128)(2,1)S(1)}, u32[]{:S(2)}, u32[]{:S(2)}) collective-permute-start(bf16[256,2048]{1,0:T(8,128)(2,1)S(1)} %add_low.8), channel_id=1, source_target_pairs={{0,16},{4,20},{8,24},{12,28},{16,0},{20,4},{24,8},{28,12},{1,17},{... | collective-permute-start | bytes 3145736 | tf_op jit(solution)/shard_map/ppermute | solution.py:41
  284.6 18.4 %collective-permute-start.50 = (bf16[128,2048]{1,0:T(8,128)(2,1)S(1)}, bf16[128,2048]{1,0:T(8,128)(2,1)S(1)}, u32[]{:S(2)}, u32[]{:S(2)}) collective-permute-start(bf16[128,2048]{1,0:T(8,128)(2,1)S(1)} %bitcast.354), channel_id=1, source_target_pairs={{0,1},{1,0},{2,3},{3,2},{4,5},{5,4},{6,7},{7,6},{8,9},{9,8},{10,11... | collective-permute-start | bytes 1572872 | tf_op jit(solution)/shard_map/ppermute | solution.py:41
  285.5 15.8 %collective-permute-start.49 = (bf16[128,1024]{1,0:T(8,128)(2,1)S(1)}, bf16[128,1024]{1,0:T(8,128)(2,1)S(1)}, u32[]{:S(2)}, u32[]{:S(2)}) collective-permute-start(bf16[128,1024]{1,0:T(8,128)(2,1)S(1)} %bitcast.358), channel_id=1, source_target_pairs={{0,2},{1,3},{2,0},{3,1},{4,6},{5,7},{6,4},{7,5},{8,10},{9,11},{10,... | collective-permute-start | bytes 786440 | tf_op jit(solution)/shard_map/ppermute | solution.py:41
  290.3 19.9 %collective-permute-start.53 = (bf16[512,1024]{1,0:T(8,128)(2,1)S(1)}, bf16[512,1024]{1,0:T(8,128)(2,1)S(1)}, u32[]{:S(2)}, u32[]{:S(2)}) collective-permute-start(bf16[512,1024]{1,0:T(8,128)(2,1)S(1)} %get-tuple-element.906), channel_id=1, source_target_pairs={{0,4},{4,0},{8,12},{12,8},{16,20},{20,16},{24,28},{28,24},{1,5},{5... | collective-permute-start | bytes 3145736 | tf_op jit(solution)/shard_map/ppermute | solution.py:41
  301.3 18.6 %collective-permute-start.52 = (bf16[512,1024]{1,0:T(8,128)(2,1)S(1)}, bf16[512,1024]{1,0:T(8,128)(2,1)S(1)}, u32[]{:S(2)}, u32[]{:S(2)}) collective-permute-start(bf16[512,1024]{1,0:T(8,128)(2,1)S(1)} %get-tuple-element.904), channel_id=1, source_target_pairs={{0,4},{4,0},{8,12},{12,8},{16,20},{20,16},{24,28},{28,24},{1,5},{5... | collective-permute-start | bytes 3145736 | tf_op jit(solution)/shard_map/ppermute | solution.py:41
  303.0 16.9 %collective-permute-start.54 = (bf16[256,2048]{1,0:T(8,128)(2,1)S(1)}, bf16[256,2048]{1,0:T(8,128)(2,1)S(1)}, u32[]{:S(2)}, u32[]{:S(2)}) collective-permute-start(bf16[256,2048]{1,0:T(8,128)(2,1)S(1)} %get-tuple-element.908), channel_id=1, source_target_pairs={{0,4},{4,0},{8,12},{12,8},{16,20},{20,16},{24,28},{28,24},{1,5},{5... | collective-permute-start | bytes 3145736 | tf_op jit(solution)/shard_map/ppermute | solution.py:41
  319.9 45.3 %collective-permute-start.59 = (bf16[512,1024]{1,0:T(8,128)(2,1)S(1)}, bf16[512,1024]{1,0:T(8,128)(2,1)S(1)}, u32[]{:S(2)}, u32[]{:S(2)}) collective-permute-start(bf16[512,1024]{1,0:T(8,128)(2,1)S(1)} %add_low.9), channel_id=1, source_target_pairs={{0,16},{4,20},{8,24},{12,28},{16,0},{20,4},{24,8},{28,12},{1,17},{... | collective-permute-start | bytes 3145736 | tf_op jit(solution)/shard_map/ppermute | solution.py:41
  335.5 30.1 %collective-permute-start.61 = (bf16[256,2048]{1,0:T(8,128)(2,1)S(1)}, bf16[256,2048]{1,0:T(8,128)(2,1)S(1)}, u32[]{:S(2)}, u32[]{:S(2)}) collective-permute-start(bf16[256,2048]{1,0:T(8,128)(2,1)S(1)} %get-tuple-element.958), channel_id=1, source_target_pairs={{0,4},{4,0},{8,12},{12,8},{16,20},{20,16},{24,28},{28,24},{1,5},{5... | collective-permute-start | bytes 3145736 | tf_op jit(solution)/shard_map/ppermute | solution.py:41
  335.6 32.7 %collective-permute-start.60 = (bf16[256,2048]{1,0:T(8,128)(2,1)S(1)}, bf16[256,2048]{1,0:T(8,128)(2,1)S(1)}, u32[]{:S(2)}, u32[]{:S(2)}) collective-permute-start(bf16[256,2048]{1,0:T(8,128)(2,1)S(1)} %get-tuple-element.956), channel_id=1, source_target_pairs={{0,4},{4,0},{8,12},{12,8},{16,20},{20,16},{24,28},{28,24},{1,5},{5... | collective-permute-start | bytes 3145736 | tf_op jit(solution)/shard_map/ppermute | solution.py:41
  337.4 30.1 %collective-permute-start.56 = (bf16[256,1024]{1,0:T(8,128)(2,1)S(1)}, bf16[256,1024]{1,0:T(8,128)(2,1)S(1)}, u32[]{:S(2)}, u32[]{:S(2)}) collective-permute-start(bf16[256,1024]{1,0:T(8,128)(2,1)S(1)} %get-tuple-element.935), channel_id=1, source_target_pairs={{0,8},{4,12},{8,0},{12,4},{16,24},{20,28},{24,16},{28,20},{1,9},{5... | collective-permute-start | bytes 1572872 | tf_op jit(solution)/shard_map/ppermute | solution.py:41
  370.7 24.6 %collective-permute-start.65 = (bf16[256,2048]{1,0:T(8,128)(2,1)}, bf16[256,2048]{1,0:T(8,128)(2,1)}, u32[]{:S(2)}, u32[]{:S(2)}) collective-permute-start(bf16[256,2048]{1,0:T(8,128)(2,1)} %add_low.10), channel_id=1, source_target_pairs={{0,16},{4,20},{8,24},{12,28},{16,0},{20,4},{24,8},{28,12},{1,17},{... | collective-permute-start | bytes 3145736 | tf_op jit(solution)/shard_map/ppermute | solution.py:41
  377.5 16.9 %collective-permute-start.62 = (bf16[256,1024]{1,0:T(8,128)(2,1)S(1)}, bf16[256,1024]{1,0:T(8,128)(2,1)S(1)}, u32[]{:S(2)}, u32[]{:S(2)}) collective-permute-start(bf16[256,1024]{1,0:T(8,128)(2,1)S(1)} %get-tuple-element.981), channel_id=1, source_target_pairs={{0,8},{4,12},{8,0},{12,4},{16,24},{20,28},{24,16},{28,20},{1,9},{5... | collective-permute-start | bytes 1572872 | tf_op jit(solution)/shard_map/ppermute | solution.py:41
  378.7 15.6 %collective-permute-start.64 = (bf16[256,1024]{1,0:T(8,128)(2,1)S(1)}, bf16[256,1024]{1,0:T(8,128)(2,1)S(1)}, u32[]{:S(2)}, u32[]{:S(2)}) collective-permute-start(bf16[256,1024]{1,0:T(8,128)(2,1)S(1)} %bitcast.352), channel_id=1, source_target_pairs={{0,1},{1,0},{2,3},{3,2},{4,5},{5,4},{6,7},{7,6},{8,9},{9,8},{10,11... | collective-permute-start | bytes 1572872 | tf_op jit(solution)/shard_map/ppermute | solution.py:41
  410.8 25.8 %collective-permute-start.66 = (f32[32,3584]{1,0:T(8,128)S(1)}, f32[32,3584]{1,0:T(8,128)S(1)}, u32[]{:S(2)}, u32[]{:S(2)}) collective-permute-start(f32[32,3584]{1,0:T(8,128)S(1)} %get-tuple-element.1082), channel_id=1, source_target_pairs={{0,8},{4,12},{8,0},{12,4},{16,24},{20,28},{24,16},{28,20},{1,9},{5... | collective-permute-start | bytes 1376264 | tf_op jit(solution)/shard_map/ppermute | solution.py:41
  412.0 24.6 %collective-permute-start.77 = (bf16[128,1024]{1,0:T(8,128)(2,1)S(1)}, bf16[128,1024]{1,0:T(8,128)(2,1)S(1)}, u32[]{:S(2)}, u32[]{:S(2)}) collective-permute-start(bf16[128,1024]{1,0:T(8,128)(2,1)S(1)} %bitcast.357), channel_id=1, source_target_pairs={{0,2},{1,3},{2,0},{3,1},{4,6},{5,7},{6,4},{7,5},{8,10},{9,11},{10,... | collective-permute-start | bytes 786440 | tf_op jit(solution)/shard_map/ppermute | solution.py:41
  413.4 25.6 %collective-permute-start.78 = (bf16[128,2048]{1,0:T(8,128)(2,1)S(1)}, bf16[128,2048]{1,0:T(8,128)(2,1)S(1)}, u32[]{:S(2)}, u32[]{:S(2)}) collective-permute-start(bf16[128,2048]{1,0:T(8,128)(2,1)S(1)} %bitcast.351), channel_id=1, source_target_pairs={{0,1},{1,0},{2,3},{3,2},{4,5},{5,4},{6,7},{7,6},{8,9},{9,8},{10,11... | collective-permute-start | bytes 1572872 | tf_op jit(solution)/shard_map/ppermute | solution.py:41
  415.9 23.3 %collective-permute-start.79 = (bf16[256,2048]{1,0:T(8,128)(2,1)S(1)}, bf16[256,2048]{1,0:T(8,128)(2,1)S(1)}, u32[]{:S(2)}, u32[]{:S(2)}) collective-permute-start(bf16[256,2048]{1,0:T(8,128)(2,1)S(1)} %copy-done.30), channel_id=1, source_target_pairs={{0,16},{4,20},{8,24},{12,28},{16,0},{20,4},{24,8},{28,12},{1,17},{... | collective-permute-start | bytes 3145736 | tf_op jit(solution)/shard_map/ppermute | solution.py:41
  (106 other events, 820.8 us)

commit v3 on v2

v3 whole, which is shorter than its diff:
```python
import itertools
import math
from functools import partial

import jax
import jax.numpy as jnp
from jax import lax
from jax.experimental import pallas as pl
from jax.experimental.pallas import tpu as pltpu
from jax.sharding import PartitionSpec as P

HEADS = 16

beta_one = 0.9
beta_two = 0.999
first_fix = 1.0 - 0.9**10
second_fix = 1.0 - 0.999**10

f32 = jnp.float32
bf16 = jnp.bfloat16

VMEM = pl.BlockSpec(memory_space=pltpu.VMEM)
SMEM = pl.BlockSpec(memory_space=pltpu.SMEM)
ANY = pl.BlockSpec(memory_space=pl.ANY)

CORE = ("dp", 1)
SIDE = ("dp", 2)


def masks(size):
    return [1 << k for k in reversed(range(size.bit_length() - 1))]


class Slice:
    def __init__(self, dp, fsdp):
        self.high = [("dp", m) for m in masks(dp) if m > 2]
        self.deep = [("fsdp", m) for m in masks(fsdp)]
        self.size = {"dp": dp, "fsdp": fsdp}

    def flip(self, value, bit):
        axis, mask = bit
        return lax.ppermute(value, axis, [(i, i ^ mask) for i in range(self.size[axis])])


def mine(bit):
    axis, mask = bit
    return (lax.axis_index(axis) // mask) % 2


def call(kernel, outs, operands, specs, scratch=(), flops=0, name=None):
    held = [(v.shape, v.dtype) for v, spec in zip(operands, specs) if spec is VMEM] + list(outs)
    held += [(s.shape, s.dtype) for s in scratch if hasattr(s, "memory_space") and s.memory_space == pltpu.VMEM]
    held = sum(math.prod(shape) * jnp.dtype(kind).itemsize for shape, kind in held)
    return pl.pallas_call(
        kernel,
        out_shape=[jax.ShapeDtypeStruct(shape, kind) for shape, kind in outs],
        in_specs=specs,
        out_specs=[VMEM] * len(outs),
        scratch_shapes=list(scratch),
        compiler_params=pltpu.CompilerParams(vmem_limit_bytes=held + (8 << 20)),
        name=name,
    )(*operands)


def merge(own, other, bit, pos):
    side = mine(bit)
    return jnp.where(side == 0, jnp.stack([own, other], pos), jnp.stack([other, own], pos))


def split(value, bit, pos):
    side = mine(bit)
    keep = lax.dynamic_index_in_dim(value, side, pos, keepdims=False)
    send = lax.dynamic_index_in_dim(value, 1 - side, pos, keepdims=False)
    return keep, send


def interleave_kernel(side, own, other, *outs):
    each = own.shape[0] // len(outs)
    for n, out in enumerate(outs):
        part = pl.ds(n * each, each)
        out[:, pl.ds(side[0], 1)] = own[part][:, None]
        out[:, pl.ds(1 - side[0], 1)] = other[part][:, None]


def interleave(own, other, bit, before, outs=1):
    rows, n = own.shape
    shape = (before, rows // before, n)
    whole = (before // outs, 2, rows // before, n)
    result = call(
        interleave_kernel,
        outs * [(whole, own.dtype)],
        [mine(bit)[None], own.reshape(shape), other.reshape(shape)],
        [SMEM, VMEM, VMEM],
        name="interleave",
    )
    return [part.reshape(-1, n) for part in result]


def prepare_kernel(side, big, table, first, first_sent, up0, up0_sent, after, after_sent, out, sems):
    width = out.shape[-1] * 2
    span, chunk = first.shape[1] // 6 // 128 * 128, up0.shape[1] // 2
    third = 3 * width
    copies = []
    for layer, qkv, up in ((0, (first, first_sent), (up0, up0_sent)), (1, (after, after_sent), (after, after_sent))):
        for x, target, upper in ((side[0], qkv[0], up[0]), (1 - side[0], qkv[1], up[1])):
            for n in range(third // (2 * span)):
                at = pl.multiple_of((2 * n + x) * span, 128)
                copies.append((big.at[layer, :, pl.ds(at, span)], target.at[:, pl.ds(n * span, span)]))
            base = 0 if layer == 0 else third // 2
            for n in range(2):
                at = pl.multiple_of(4 * width + (2 * n + x) * chunk, 128)
                copies.append((big.at[layer, :, pl.ds(at, chunk)], upper.at[:, pl.ds(base + n * chunk, chunk)]))
        for k in range(2):
            copies.append((big.at[layer, :, pl.ds(third + k * width // 2, width // 2)], out.at[layer, k]))
    for target in (first, first_sent):
        copies.append((table, target.at[:, pl.ds(third // 2, 128)]))
    copies = [pltpu.make_async_copy(a, b, sems.at[n]) for n, (a, b) in enumerate(copies)]
    for copy in copies:
        copy.start()
    for copy in copies:
        copy.wait()


def place_first_kernel(side, keep, other, out, own):
    part = keep.shape[1] - 128
    wide = out.shape[-1]
    for source, x in ((keep, side[0]), (other, 1 - side[0])):
        own[pl.ds(x, 1), :, pl.ds(0, part)] = source[:, pl.ds(0, part)][None]
        own[pl.ds(x, 1), :, pl.ds(part + wide, 128)] = source[:, pl.ds(part, 128)][None]
    own[:, :, pl.ds(part, wide)] = out[...]


def place_next_kernel(side, keep, other, out, own):
    wide = out.shape[-1]
    part = 3 * wide
    for source, x in ((keep, side[0]), (other, 1 - side[0])):
        own[pl.ds(x, 1), :, pl.ds(0, part)] = source[:, pl.ds(0, part)][None]
        own[pl.ds(2 + x, 1)] = source[:, pl.ds(part, part + wide)][None]
    own[pl.ds(0, 2), :, pl.ds(part, wide)] = out[...]


class Gather:
    def __init__(self, sl, own, lead, top_first=False, twins=False):
        self.sl, self.value, self.lead, self.top_first, self.twins = sl, own, lead, top_first, twins
        self.have, self.air, self.quarters = [], None, None
        near = sl.high[:0:-1]
        if top_first:
            self.steps = [sl.high[:1], near + sl.deep[:-1], sl.deep[-1:]]
        else:
            self.steps = [sl.deep[:-1], sl.deep[-1:] + near]
        core = mine(CORE)
        self.place = jnp.stack([jnp.zeros_like(core) if top_first else mine(sl.high[0]), core])

    def before(self, bit):
        order = self.sl.high + self.sl.deep
        count = sum(order.index(b) < order.index(bit) for b in self.have)
        return (1 + self.twins) * (1 << count) * (1 if bit in self.sl.high else self.lead)

    def start(self):
        if not self.steps:
            self.air = self.sl.flip(self.value, self.sl.high[0]), self.sl.flip(self.value, CORE)
            return
        *others, self.bit = self.steps.pop(0)
        for bit in others:
            other = self.sl.flip(self.value, bit)
            self.value = interleave(self.value, other, bit, self.before(bit))[0]
            self.have.append(bit)
        self.air = self.sl.flip(self.value, self.bit)

    def land(self):
        air, self.air = self.air, None
        if isinstance(air, tuple):
            self.quarters, self.value = [self.value, *air], None
            return
        last = (self.top_first or self.twins) and not self.steps
        halves = interleave(self.value, air, self.bit, self.before(self.bit), 1 + last)
        self.have.append(self.bit)
        if last and self.twins:
            self.value = halves
        elif last:
            self.quarters = [*halves, self.sl.flip(halves[0], CORE)]
            self.value = None
        else:
            self.value = halves[0]

    def part(self, n):
        made = Gather(self.sl, self.value[n], self.lead)
        made.steps = []
        return made

    def finish(self):
        self.quarters = [*self.quarters, self.sl.flip(self.quarters[1], CORE)]


def add_low_kernel(one, two, out):
    out[...] = (one[...].astype(f32) + two[...].astype(f32)).astype(bf16)


def add_split_kernel(side, *refs):
    *parts, kept, sent = refs
    for at, out in ((side[0], kept), (1 - side[0], sent)):
        total = parts[0][:, pl.ds(at, 1)].astype(f32)
        for other in parts[1:]:
            total = total + other[:, pl.ds(at, 1)].astype(f32)
        out[...] = total.astype(bf16)[:, 0]


def cross_split_kernel(side, own, own_other, top, top_other, kept, sent):
    for n, (one, two) in enumerate(((own, own_other), (top, top_other))):
        for at, out in ((side[0], kept), (1 - side[0], sent)):
            total = one[:, pl.ds(at, 1)].astype(f32) + two[:, pl.ds(at, 1)].astype(f32)
            out[n] = total.astype(bf16)[:, 0]


class Scatter:
    def __init__(self, sl, quarters, lead, top_last=False):
        self.sl, self.quarters, self.value, self.lead, self.top_last = sl, quarters, None, lead, top_last
        top, near, deep = sl.high[:1], sl.high[1:], sl.deep
        self.have = sl.high + deep
        if top_last:
            self.steps = [deep[-1:], deep[-2::-1] + near, top]
        else:
            self.steps = [top, near + deep[-1:], deep[-2::-1]]

    def before(self, bit):
        order = self.sl.high + self.sl.deep
        count = sum(order.index(b) < order.index(bit) for b in self.have)
        return (1 << count) * (1 if bit in self.sl.high else self.lead)

    def side(self, bit):
        return jnp.zeros((1,), jnp.int32) if bit == self.sl.high[0] else mine(bit)[None]

    def cross(self):
        own, top, core, both = self.quarters
        top_other = self.sl.flip(both, CORE)
        core_other = self.sl.flip(core, CORE)
        rows, n = top.shape
        if not self.top_last:
            (send,) = call(
                add_low_kernel, [(top.shape, bf16)], [top, top_other], [VMEM] * 2, name="add_low"
            )
            self.quarters = [[own, core_other], send]
            return
        bit = self.steps[0][0]
        before = self.before(bit) // 2
        shape = (before, 2, rows // 2 // before, n)
        half = ((2, before, rows // 2 // before, n), bf16)
        keep, send = call(
            cross_split_kernel,
            [half, half],
            [self.side(bit), *(v.reshape(shape) for v in (own, core_other, top, top_other))],
            [SMEM] + [VMEM] * 4,
            name="cross_split",
        )
        self.quarters = [[keep.reshape(-1, n)], send.reshape(-1, n)]

    def split(self, other, bit):
        parts = [*self.quarters[0], other]
        if bit is None:
            self.value = sum(part.astype(f32) for part in parts)
            self.quarters = None
            return
        before = self.before(bit)
        rows, n = other.shape
        shape = (before, 2, rows // 2 // before, n)
        half = ((before, rows // 2 // before, n), bf16)
        keep, send = call(
            add_split_kernel,
            [half, half],
            [self.side(bit), *(part.reshape(shape) for part in parts)],
            [SMEM] + [VMEM] * len(parts),
            name="add_split",
        )
        self.quarters = [[keep.reshape(-1, n)], send.reshape(-1, n)]

    def start(self):
        bits = self.steps.pop(0)
        for n, bit in enumerate(bits):
            self.air = self.sl.flip(self.quarters[1], bit)
            self.have.remove(bit)
            if n < len(bits) - 1:
                self.split(self.air, bits[n + 1])
        self.next = self.steps[0][0] if self.steps else None

    def land(self):
        other, self.air = self.air, None
        self.split(other, self.next)


class Live:
    def __init__(self, **values):
        self.flows = []
        self.values = values

    def flow(self, made):
        self.flows.append(made)
        return made

    def __getattr__(self, name):
        return self.values[name]

    def put(self, **values):
        self.values.update(values)

    def drop(self, *names):
        for name in names:
            del self.values[name]

    def seal(self, *landing):
        kept = (
            self.values,
            [(made.value, made.quarters) for made in self.flows],
            [made.air for made in landing],
        )
        self.values, flown, airs = lax.optimization_barrier(kept)
        for made, (made.value, made.quarters) in zip(self.flows, flown):
            pass
        for made, made.air in zip(landing, airs):
            made.land()


def dot(left, right):
    return jnp.dot(left, right, preferred_element_type=f32)


def dot_t(left, right):
    return lax.dot_general(left, right, (((1,), (1,)), ((), ())), preferred_element_type=f32)


def t_dot(left, right):
    return lax.dot_general(left, right, (((0,), (0,)), ((), ())), preferred_element_type=f32)


def fetch(place, quarters, whole, lead, sems):
    width = whole.shape[1]
    block = whole.shape[0] // (4 * lead)
    copies = []
    for n, part in enumerate(quarters):
        top = place[0] if n % 2 == 0 else 1 - place[0]
        core = place[1] if n < 2 else 1 - place[1]
        for a in range(lead):
            at = pl.multiple_of(((top * lead + a) * 2 + core) * block, block)
            source = part.at[pl.ds(a * block, block), pl.ds(0, width)]
            copies.append(
                pltpu.make_async_copy(source, whole.at[pl.ds(at, block)], sems.at[n * lead + a])
            )
    for copy in copies:
        copy.start()
    return copies


def norm(hidden):
    centred = hidden - jnp.mean(hidden, axis=-1, keepdims=True)
    scale = lax.rsqrt(jnp.mean(centred * centred, axis=-1, keepdims=True) + 1e-05)
    return centred * scale, scale


def put_rows(outs, cols, value):
    rows = value.shape[0] // len(outs)
    for r, out in enumerate(outs):
        out[:, cols] = value[r * rows : (r + 1) * rows].astype(bf16)


def theirs(others, r, rows):
    if len(others) == 2:
        return others[1 - r][...].astype(f32)
    return others[0][pl.ds((1 - r) * rows, rows)].astype(f32)


def gains_at(gains, r, place, width):
    return gains[pl.ds(r, 1), pl.ds(place * width, width)]


def add_norm(which, parts, gains, total, out):
    base, *shares = parts
    rows, width = out.shape[0] // 2, out.shape[1]
    for r in range(2):
        block = pl.ds(r * rows, rows)
        value = base[block]
        if shares:
            value = value + (shares[0][block] + theirs(shares[1:], r, rows))
            total[block] = value
        gain, bias = [gains_at(gains, r, 2 * which + n, width) for n in range(2)]
        out[block] = (norm(value)[0] * gain + bias).astype(bf16)


def norm_back(which, d_out, keep, others, hidden, gains, total, low, d_gain, d_shift):
    rows, width = d_out.shape[0] // 2, d_out.shape[1]
    for r in range(2):
        block = pl.ds(r * rows, rows)
        grad = keep[block] + theirs(others, r, rows)
        normed, scale = norm(hidden[block])
        if r == 0:
            d_gain[...] = jnp.sum(grad * normed, axis=0, keepdims=True)
            d_shift[...] = jnp.sum(grad, axis=0, keepdims=True)
        e = grad * gains_at(gains, r, 2 * which, width)
        part = e - jnp.mean(e, axis=-1, keepdims=True)
        part = part - normed * jnp.mean(e * normed, axis=-1, keepdims=True)
        value = d_out[block] + scale * part
        total[block] = value
        low[block] = value.astype(bf16)


def norm_back_kernel(which, d_out, keep, *refs):
    norm_back(which, d_out, keep, refs[:-6], *refs[-6:])


def gains_kernel(lead, count, rows, place, pick, q0, q1, q2, q3, first, second, held, wide, sems):
    copies = []
    for n, part in enumerate((q0, q1, q2, q3)):
        source = part.at[:, pl.ds(part.shape[1] - 128, 128)]
        copies.append(pltpu.make_async_copy(source, held.at[n], sems.at[n]))
    for copy in copies:
        copy.start()
    for copy in copies:
        copy.wait()
    wide[...] = held[...].astype(f32)
    deep = wide.shape[1] // (lead * rows)
    for n in range(4):
        top = place[0] if n % 2 == 0 else 1 - place[0]
        core = place[1] if n < 2 else 1 - place[1]
        for a in range(lead):
            for z in range(deep):
                cols = pl.multiple_of((((top * lead + a) * 2 + core) * deep + z) * 128, 128)
                base = (a * deep + z) * rows
                for r in range(2):
                    first[pl.ds(r, 1), pl.ds(cols, 128)] = wide[n, pl.ds(base, 1)]
                    second[pl.ds(r, 1), pl.ds(cols, 128)] = wide[n, pl.ds(base + 1 + pick[r], 1)]


def score(q, k, allowed, size):
    scores = jnp.where(allowed, dot_t(q, k) * size, -1e30)
    exponent = jnp.exp(scores - jnp.max(scores, axis=-1, keepdims=True))
    return exponent / jnp.sum(exponent, axis=-1, keepdims=True)


def lanes_of(which, shape):
    lane = lax.broadcasted_iota(jnp.int32, shape, 1)
    return (lane < shape[1] // 2) if which == 0 else (lane >= shape[1] // 2)


def out_block(weight, k, block, at):
    count = weight.shape[0] // (2 * block)
    wide = weight.shape[1] - at
    return jnp.concatenate([weight[pl.ds((2 * h + k) * block, block), pl.ds(at, wide)] for h in range(count)], 0)


def attend_kernel(ways, size, lead, block, place, *refs):
    refs, (weight, sems) = refs[:-2], refs[-2:]
    refs, lows = refs[:-ways], refs[-ways:]
    *parts, gains, q0, q1, q2, q3, allow, total, f, qkv, mixed, keep = refs
    copies = fetch(place, (q0, q1, q2, q3), weight, lead, sems)
    add_norm(0, parts, gains, total, f)
    for copy in copies:
        copy.wait()
    length = allow.shape[-1]
    third = qkv.shape[1] // 3
    for n in range(3):
        cols = pl.ds(n * third, third)
        qkv[:, cols] = dot(f[...], weight[:, cols]).astype(bf16)

    def one_row(r, carry):
        at = pl.ds(pl.multiple_of(r * length, length), length)
        allowed = allow[r] > 0
        for p in range(third // 128):
            q = qkv[at, pl.ds(p * 128, 128)]
            k = qkv[at, pl.ds(third + p * 128, 128)]
            v = qkv[at, pl.ds(2 * third + p * 128, 128)]
            halves = []
            for h in range(2):
                probs = score(jnp.where(lanes_of(h, q.shape), q, 0), k, allowed, size)
                halves.append(dot(probs.astype(bf16), v))
            mixed[at, pl.ds(p * 128, 128)] = jnp.where(
                lanes_of(0, q.shape), halves[0], halves[1]
            ).astype(bf16)
        return carry

    lax.fori_loop(0, f.shape[0] // length, one_row, 0)
    for k in range(2):
        cols = pl.ds(k * third, third)
        value = dot(mixed[...], out_block(weight, k, block, 3 * third))
        keep[:, cols] = value
        put_rows(lows, cols, value)


def attend_back_kernel(ways, size, lead, block, place, d_out, part, *refs):
    refs, (weight, d_mixed, sems) = refs[:-3], refs[-3:]
    refs, lows = refs[:-ways], refs[-ways:]
    *others, attended, gains, q0, q1, q2, q3, allow, qkv, total, d, d_gain, d_shift, d_qkv, keep = refs
    copies = fetch(place, (q0, q1, q2, q3), weight, lead, sems)
    norm_back(1, d_out, part, others, attended, gains, total, d, d_gain, d_shift)
    for copy in copies:
        copy.wait()
    length = allow.shape[-1]
    third = qkv.shape[1] // 3
    value = dot_t(d[:, pl.ds(0, third)], out_block(weight, 0, block, 3 * third))
    value = value + dot_t(d[:, pl.ds(third, third)], out_block(weight, 1, block, 3 * third))
    d_mixed[...] = value.astype(bf16)

    def one_row(r, carry):
        at = pl.ds(pl.multiple_of(r * length, length), length)
        allowed = allow[r] > 0
        for p in range(third // 128):
            q = qkv[at, pl.ds(p * 128, 128)]
            k = qkv[at, pl.ds(third + p * 128, 128)]
            v = qkv[at, pl.ds(2 * third + p * 128, 128)]
            dm = d_mixed[at, pl.ds(p * 128, 128)]
            d_q, d_k, d_v = [], [], []
            for h in range(2):
                pick = lanes_of(h, q.shape)
                probs = score(jnp.where(pick, q, 0), k, allowed, size)
                d_probs = dot_t(jnp.where(pick, dm, 0), v)
                d_v.append(t_dot(probs.astype(bf16), dm))
                inner = jnp.sum(probs * d_probs, axis=-1, keepdims=True)
                d_scores = (probs * (d_probs - inner)).astype(bf16)
                d_q.append(dot(d_scores, k))
                d_k.append(t_dot(d_scores, q))
            pick = lanes_of(0, q.shape)
            for n, (halves, scale) in enumerate(((d_q, size), (d_k, size), (d_v, 1.0))):
                value = jnp.where(pick, halves[0], halves[1]) * scale
                d_qkv[at, pl.ds(n * third + p * 128, 128)] = value.astype(bf16)
        return carry

    lax.fori_loop(0, d.shape[0] // length, one_row, 0)
    for n in range(keep.shape[1] // 256):
        cols = pl.ds(n * 256, 256)
        value = dot_t(d_qkv[...], weight[cols, pl.ds(0, 3 * third)])
        keep[:, cols] = value
        put_rows(lows, cols, value)


def up(f, weight, pre, active):
    for n in range(pre.shape[1] // 256):
        cols = pl.ds(n * 256, 256)
        value = dot(f[...], weight[:, cols])
        pre[:, cols] = value
        active[:, cols] = jax.nn.gelu(value).astype(bf16)


def down(active, weight, keep, lows):
    for n in range(keep.shape[1] // 256):
        cols = pl.ds(n * 256, 256)
        value = dot(active[...], weight[:, cols])
        keep[:, cols] = value
        put_rows(lows, cols, value)


def feed_kernel(ways, lead, up_place, dn_place, *refs):
    refs, (w_up, w_dn, up_sems, dn_sems) = refs[:-4], refs[-4:]
    refs, lows = refs[:-ways], refs[-ways:]
    *parts, gains, u0, u1, u2, u3, n0, n1, n2, n3, total, f, pre, active, keep = refs
    up_copies = fetch(up_place, (u0, u1, u2, u3), w_up, lead, up_sems)
    dn_copies = fetch(dn_place, (n0, n1, n2, n3), w_dn, lead // 2, dn_sems)
    add_norm(1, parts, gains, total, f)
    for copy in up_copies:
        copy.wait()
    up(f, w_up, pre, active)
    for copy in dn_copies:
        copy.wait()
    down(active, w_dn, keep, lows)


def down_kernel(lead, place, active, q0, q1, q2, q3, keep, low, weight, sems):
    for copy in fetch(place, (q0, q1, q2, q3), weight, lead, sems):
        copy.wait()
    down(active, weight, keep, (low,))


def gelu_slope(x):
    c = 0.7978845608028654
    t = jnp.tanh(c * (x + 0.044715 * (x * x * x)))
    return 0.5 * (1.0 + t) + 0.5 * x * (1.0 - t * t) * (c * (1.0 + 3 * 0.044715 * (x * x)))


def feed_back(d, pre, w_up, w_dn, d_pre, keep, lows):
    for n in range(pre.shape[1] // 256):
        cols = pl.ds(n * 256, 256)
        d_pre[:, cols] = (gelu_slope(pre[:, cols]) * dot_t(d[...], w_dn[cols])).astype(bf16)
    for n in range(keep.shape[1] // 256):
        cols = pl.ds(n * 256, 256)
        value = dot_t(d_pre[...], w_up[cols])
        keep[:, cols] = value
        put_rows(lows, cols, value)


def feed_back_kernel(ways, lead, up_place, dn_place, d_out, part, *refs):
    refs, (w_up, w_dn, up_sems, dn_sems) = refs[:-4], refs[-4:]
    refs, lows = refs[:-ways], refs[-ways:]
    *others, hidden, gains, pre, u0, u1, u2, u3, n0, n1, n2, n3, total, d, d_gain, d_shift, d_pre, keep = refs
    copies = fetch(dn_place, (n0, n1, n2, n3), w_dn, lead // 2, dn_sems)
    copies += fetch(up_place, (u0, u1, u2, u3), w_up, lead, up_sems)
    norm_back(0, d_out, part, others, hidden, gains, total, d, d_gain, d_shift)
    for copy in copies:
        copy.wait()
    feed_back(d, pre, w_up, w_dn, d_pre, keep, lows)


def feed_turn_kernel(ways, lead, up_place, dn_place, *refs):
    refs, (w_up, w_dn, pre, up_sems, dn_sems) = refs[:-5], refs[-5:]
    refs, lows = refs[:-ways], refs[-ways:]
    *parts, gains, d, u0, u1, u2, u3, n0, n1, n2, n3, total, f, active, d_pre, keep = refs
    up_copies = fetch(up_place, (u0, u1, u2, u3), w_up, lead, up_sems)
    dn_copies = fetch(dn_place, (n0, n1, n2, n3), w_dn, lead // 2, dn_sems)
    add_norm(1, parts, gains, total, f)
    for copy in up_copies:
        copy.wait()
    up(f, w_up, pre, active)
    for copy in dn_copies:
        copy.wait()
    feed_back(d, pre, w_up, w_dn, d_pre, keep, lows)


def columns_of(place, value, lead):
    block = value.shape[1] // (4 * lead)
    parts = []
    for n in range(4):
        top = place[0] if n % 2 == 0 else 1 - place[0]
        core = place[1] if n < 2 else 1 - place[1]
        starts = [((top * lead + a) * 2 + core) * block for a in range(lead)]
        if block % 128 == 0:
            starts = [pl.multiple_of(at, 128) for at in starts]
        parts.append(jnp.concatenate([value[:, pl.ds(at, block)] for at in starts], 1))
    return parts


def weight_grad_kernel(lead, aligned, place, left, right, *outs):
    place = place if aligned else (0, 0)
    for part, out in zip(columns_of(place, left, lead), outs):
        out[...] = t_dot(part, right[...]).astype(bf16)


def attend_grad_kernel(lead, aligned, place, left, mixed, d_qkv, d, *outs):
    width = d_qkv.shape[1]
    third = width // 3
    place = place if aligned else (0, 0)
    block = left.shape[1] // (4 * lead)
    lefts, inners = columns_of(place, left, lead), columns_of(place, mixed, lead // 2)
    for part, inner, out in zip(lefts, inners, outs):
        out[:, pl.ds(0, width)] = t_dot(part, d_qkv[...]).astype(bf16)
        value = t_dot(inner, d[...]).astype(bf16)
        for h in range(inner.shape[1] // block):
            for k in range(2):
                out[pl.ds((2 * h + k) * block, block), pl.ds(width, third)] = value[
                    h * block : (h + 1) * block, k * third : (k + 1) * third
                ]


def turn(sl, value, lead):
    tokens, width = value.shape
    value = value.reshape(tokens, 2, lead, 2, width // (4 * lead))
    value = jnp.stack(split(value, sl.high[0], 1), 1)
    return jnp.stack(split(value, CORE, 3), 3).reshape(tokens, width)


def finish_kernel(span, chunk, side, keep, other, out, *refs):
    grad, new_m, step = refs[-3:]
    third = out.shape[-1]
    total = grad.shape[-1] - 8 * third
    pieces, (m, v) = [], refs[:2]
    base, filled = 8 * third, 0
    while 2 * filled < total:
        one, two, *refs = refs
        (m, v) = refs[:2]
        pieces.append((one, two, base + 2 * filled, chunk))
        filled += one.shape[1]
    for one, two, base, width in [(keep, other, 0, span)] + pieces:
        for source, x in ((one, side[0]), (two, 1 - side[0])):
            for n in range(source.shape[1] // width):
                at = pl.multiple_of(base + (2 * n + x) * width, 128)
                grad[0, :, pl.ds(at, width)] = source[:, pl.ds(n * width, width)]
    for k in range(2):
        grad[0, :, pl.ds((6 + k) * third, third)] = out[k]
    for n in range(grad.shape[2] // 1024):
        cols = pl.ds(n * 1024, 1024)
        new_m[0, :, cols], step[0, :, cols] = adam_update(m[0, :, cols], v[0, :, cols], grad[0, :, cols])


def finish_down_kernel(value, m, v, *refs):
    grad, new_m, step = refs[-3:]
    grad[0] = value[...]
    new_m[0], step[0] = adam_update(m[0], v[0], value[...])


def update(kernel, layer, shape, parts, specs, moments, before, name):
    one = pl.BlockSpec((1, *shape[1:]), lambda i: (layer, 0, 0))
    count = len(parts) + 2
    return pl.pallas_call(
        kernel,
        grid=(1,),
        out_shape=[jax.ShapeDtypeStruct(shape, f32)] * 3,
        in_specs=[*specs, one, one, *len(before) * [ANY]],
        out_specs=[one] * 3,
        input_output_aliases={count + n: n for n in range(len(before))},
        compiler_params=pltpu.CompilerParams(vmem_limit_bytes=20 << 20),
        name=name,
    )(*parts, *moments, *before)


def adam_update(moment, square, gradient):
    moment = beta_one * moment + (1.0 - beta_one) * gradient
    square = beta_two * square + (1.0 - beta_two) * gradient * gradient
    update = moment / first_fix / (jnp.sqrt(square / second_fix) + 1e-08)
    return (moment, update)


def dma(count):
    return pltpu.SemaphoreType.DMA((count,))


def body(
    dp,
    fsdp,
    inputs,
    cotangent,
    segment_ids,
    section_ids,
    w_big,
    w_down,
    norm_table,
    m_big,
    m_down,
    m_table,
    v_big,
    v_down,
    v_table,
):
    sl = Slice(dp, fsdp)
    length, width = inputs.shape[1:]
    rows = w_big.shape[1]
    feeds = w_down.shape[1]
    feed = w_big.shape[2] - 4 * width
    high = dp // 4
    lead = high
    half, part = width // 2, 3 * width // 2
    block = fsdp * rows
    count = norm_table.shape[0]
    size = (width // HEADS) ** -0.5
    two_f, two_b = ((2 * length, width), f32), ((2 * length, width), bf16)
    wide_b = ((2 * length, feed // 2), bf16)

    def lows(ways):
        return ways * [((2 // ways * length, width), bf16)]

    quarter = ((width // 4, 2 * width), bf16)
    gain_row = ((1, width), f32)
    place = jnp.stack([mine(sl.high[0]), mine(CORE)])
    w_attn = pltpu.VMEM((width, 2 * width), bf16)
    w_upper = pltpu.VMEM((width, feed // 2), bf16)
    w_lower = pltpu.VMEM((feed // 2, width), bf16)

    def qkv_sides(layer):
        value = w_big[layer, :, : 3 * width].reshape(rows, 3, high, 2, 2 * block)
        return [v.reshape(rows, part) for v in split(value, SIDE, 3)]

    def up_sides(layer):
        value = w_big[layer, :, 4 * width :].reshape(rows, high, 2, 2 * fsdp * feeds)
        return [v.reshape(rows, feed // 2) for v in split(value, SIDE, 2)]

    def prepare(table_part):
        shapes = 2 * [(rows, part + 128)] + 2 * [(rows, feed // 2)] + 2 * [(rows, part + feed // 2)]
        shapes.append((2, 2, rows, half))
        if rows % 16 == 0:
            return call(
                prepare_kernel,
                [(shape, bf16) for shape in shapes],
                [mine(SIDE)[None], w_big, table_part],
                [SMEM, ANY, ANY],
                [dma(2 * (6 * high + 6) + 2)],
                name="prepare",
            )
        first = [jnp.concatenate([v, table_part], -1) for v in qkv_sides(0)]
        after = [jnp.concatenate([a, b], -1) for a, b in zip(qkv_sides(1), up_sides(1))]
        out = w_big[:, :, 3 * width : 4 * width].reshape(2, rows, 2, half)
        return [*first, *up_sides(0), *after, jnp.swapaxes(out, 1, 2)]

    def place_sides(kernel, shape, keep, other, out, name):
        return call(
            kernel,
            [(shape, bf16)],
            [mine(SIDE)[None], keep, other, out],
            [SMEM, VMEM, VMEM, VMEM],
            name=name,
        )[0]

    live = Live()
    downs = [live.flow(Gather(sl, w_down[n], 1, n == 1)) for n in range(2)]

    downs[0].start()
    downs[1].start()
    table_part = norm_table.reshape(-1)
    table_part = jnp.pad(table_part, (0, rows * 128 - table_part.shape[0])).reshape(rows, 128)
    first, first_sent, up0, up0_sent, after, after_sent, out_proj = prepare(table_part)
    live.put(
        first=[first, sl.flip(first_sent, SIDE)],
        up=[up0, up0_sent],
        after=[after, after_sent],
        out=out_proj,
    )
    live.seal(downs[0], downs[1])

    own = place_sides(
        place_first_kernel, (2, rows, 2 * width + 128), *live.first, live.out[0], "place_first"
    )
    attns = [live.flow(Gather(sl, own.reshape(2 * rows, -1), 2))]
    attns[0].start()
    downs[0].start()
    extra = jnp.zeros((16, width), bf16)
    extra = extra.at[0, :length].set(segment_ids[0].astype(bf16))
    extra = extra.at[1, 0].set(section_ids[0].astype(bf16))
    pack = jnp.concatenate([inputs[0], cotangent[0], extra], 0)
    live.put(
        up=[live.up[0], sl.flip(live.up[1], SIDE)],
        after=[live.after[0], sl.flip(live.after[1], SIDE)],
        pack=[pack, sl.flip(pack, SIDE)],
    )
    live.drop("first")
    live.seal(attns[0], downs[0])

    ups = [live.flow(Gather(sl, interleave(*live.up, SIDE, 1)[0], 2))]
    downs[0].start()
    attns[0].start()
    ups[0].start()
    own = place_sides(
        place_next_kernel, (4, rows, 2 * width), *live.after, live.out[1], "place_next"
    )
    live.put(own=own)
    live.drop("up", "after", "out")
    packed = jnp.stack(live.pack)
    extras = packed[:, 2 * length :]
    segments = extras[:, 0, :length].astype(f32)
    same = segments[:, :, None] == segments[:, None, :]
    position = jnp.arange(length)
    live.put(
        hidden=packed[:, :length].reshape(2 * length, width).astype(f32),
        d_low=packed[:, length : 2 * length].reshape(2 * length, width),
        sections=extras[:, 1, 0].astype(jnp.int32),
        allows=[
            (same & (position[:, None] >= position[None, :])).astype(f32),
            same.astype(f32),
        ],
    )
    live.drop("pack")
    live.seal(attns[0], ups[0], downs[0])

    twins = live.flow(Gather(sl, live.own.reshape(4 * rows, -1), 2, twins=True))
    live.drop("own")
    attns[0].start()
    twins.start()
    ups[0].start()
    downs[0].finish()
    live.seal(attns[0], ups[0], twins)

    def gains_of(quarters, sections):
        wide = norm_table.shape[1]
        if wide == 128:
            return call(
                partial(gains_kernel, lead, count, rows),
                2 * [((2, 4 * width), f32)],
                [place, sections, *quarters],
                [SMEM, SMEM] + [ANY] * 4,
                [
                    pltpu.VMEM((4, width // 4, 128), bf16),
                    pltpu.VMEM((4, width // 4, 128), f32),
                    dma(4),
                ],
                name="gains",
            )
        parts = jnp.stack([q[:, 2 * width :] for q in quarters])
        parts = parts.reshape(4, lead // 2, 2, fsdp, rows * 128)[..., : count * wide]
        parts = parts.reshape(4, lead // 2, 2, fsdp, count, wide)
        pick = jnp.concatenate([jnp.zeros((2,), jnp.int32), 1 + sections])
        pick = (pick[:, None] == jnp.arange(count)[None, :]).astype(bf16)
        picked = jnp.einsum("sr,qhxdrj->qshxdj", pick, parts, preferred_element_type=f32)
        own, top, core, both = picked
        both = merge(merge(own, core, CORE, 3), merge(top, both, CORE, 3), sl.high[0], 1)
        return list(both.reshape(2, 2, 4 * width))

    def cross():
        live.put(other=[sl.flip(row, SIDE) for row in live.low])

    def shares():
        return [live.keep, *live.other]

    def attend(layer, base, ways=2):
        parts = [base] if layer == 0 else [base, *shares()]
        total, first, qkv, mixed, keep, *low = call(
            partial(attend_kernel, ways, size, lead, 2 * block),
            [two_f, two_b, ((2 * length, part), bf16), ((2 * length, half), bf16), two_f, *lows(ways)],
            [
                attns[layer].place,
                *parts,
                live.gains[layer],
                *attns[layer].quarters,
                live.allows[layer],
            ],
            [SMEM] + [VMEM] * (len(parts) + 1) + [ANY] * 4 + [VMEM],
            [w_attn, dma(4 * lead)],
            name="attend",
        )
        hidden = base if layer == 0 else total
        live.put(**{f"attn{layer}": (hidden, first, qkv, mixed)}, keep=keep, low=low)

    def feed_forward(layer, ways=2):
        attended, second, pre, active, keep, *low = call(
            partial(feed_kernel, ways, lead),
            [two_f, two_b, (wide_b[0], f32), wide_b, two_f, *lows(ways)],
            [
                ups[layer].place,
                downs[layer].place,
                live.values[f"attn{layer}"][0],
                *shares(),
                live.gains[layer],
                *ups[layer].quarters,
                *downs[layer].quarters,
            ],
            [SMEM, SMEM] + [VMEM] * (3 + len(live.other)) + [ANY] * 8,
            [w_upper, w_lower, dma(4 * lead), dma(2 * lead)],
            name="feed",
        )
        live.put(**{f"feed{layer}": (attended, second, pre, active)}, keep=keep, low=low)

    def feed_turn(layer, ways=2):
        attended, second, active, d_pre, keep, *low = call(
            partial(feed_turn_kernel, ways, lead),
            [two_f, two_b, wide_b, wide_b, two_f, *lows(ways)],
            [
                ups[layer].place,
                downs[layer].place,
                live.values[f"attn{layer}"][0],
                *shares(),
                live.gains[layer],
                live.d_low,
                *ups[layer].quarters,
                *downs[layer].quarters,
            ],
            [SMEM, SMEM] + [VMEM] * (4 + len(live.other)) + [ANY] * 8,
            [w_upper, w_lower, pltpu.VMEM(wide_b[0], f32), dma(4 * lead), dma(2 * lead)],
            name="feed_turn",
        )
        live.put(**{f"feed{layer}": (attended, second, None, active)}, d_pre=d_pre, keep=keep, low=low)

    def feed_down(layer):
        keep, *low = call(
            partial(down_kernel, lead // 2),
            [two_f, *lows(1)],
            [downs[layer].place, live.values[f"feed{layer}"][3], *downs[layer].quarters],
            [SMEM, VMEM, ANY, ANY, ANY, ANY],
            [w_lower, dma(2 * lead)],
            name="down",
        )
        live.put(keep=keep, low=low)

    def feed_back(layer, ways=1):
        grad, d_low, d_gain, d_shift, d_pre, keep, *low = call(
            partial(feed_back_kernel, ways, lead),
            [two_f, two_b, gain_row, gain_row, wide_b, two_f, *lows(ways)],
            [
                ups[layer].place,
                downs[layer].place,
                live.grad,
                *shares(),
                live.values[f"attn{layer + 1}"][0],
                live.gains[layer + 1],
                live.values[f"feed{layer}"][2],
                *ups[layer].quarters,
                *downs[layer].quarters,
            ],
            [SMEM, SMEM] + [VMEM] * (5 + len(live.other)) + [ANY] * 8,
            [w_upper, w_lower, dma(4 * lead), dma(2 * lead)],
            name="feed_back",
        )
        live.put(grad=grad, d_low=d_low, d_pre=d_pre, keep=keep, low=low)
        live.put(**{f"gains{layer + 1}0": jnp.concatenate([d_gain, d_shift], 1)})

    def down_grad(layer, top_last=False):
        aligned = feed // 4 // lead % 128 == 0
        active = live.values[f"feed{layer}"][3]
        parts = call(
            partial(weight_grad_kernel, lead // 2, aligned),
            [((feed // 8, width), bf16)] * 4,
            [place, active if aligned else turn(sl, active, lead // 2), live.d_low],
            [SMEM, VMEM, VMEM],
            name="down_grad",
        )
        return live.flow(Scatter(sl, parts, 1, top_last))

    def up_grad(layer, piece=None):
        aligned = block % 128 == 0
        second, right = live.values[f"feed{layer}"][1], live.d_pre
        columns = feed // 2
        if piece is not None:
            columns = feed // 4
            right = right[:, piece * columns : (piece + 1) * columns]
        parts = call(
            partial(weight_grad_kernel, lead, aligned),
            [((width // 4, columns), bf16)] * 4,
            [place, second if aligned else turn(sl, second, lead), right],
            [SMEM, VMEM, VMEM],
            name="up_grad",
        )
        return live.flow(Scatter(sl, parts, 2, piece == 1))

    def norm_back(which, layer, hidden):
        grad, d_low, d_gain, d_shift = call(
            partial(norm_back_kernel, which),
            [two_f, two_b, gain_row, gain_row],
            [live.grad, *shares(), hidden, live.gains[layer]],
            [VMEM] * (4 + len(live.other)),
            name="norm_back",
        )
        live.put(grad=grad, d_low=d_low)
        live.put(**{f"gains{layer}{which}": jnp.concatenate([d_gain, d_shift], 1)})

    def attend_back(layer, ways=1):
        grad, d_low, d_gain, d_shift, d_qkv, keep, *low = call(
            partial(attend_back_kernel, ways, size, lead, 2 * block),
            [two_f, two_b, gain_row, gain_row, ((2 * length, part), bf16), two_f, *lows(ways)],
            [
                attns[layer].place,
                live.grad,
                *shares(),
                live.values[f"feed{layer}"][0],
                live.gains[layer],
                *attns[layer].quarters,
                live.allows[layer],
                live.values[f"attn{layer}"][2],
            ],
            [SMEM] + [VMEM] * (4 + len(live.other)) + [ANY] * 4 + [VMEM] * 2,
            [w_attn, pltpu.VMEM((2 * length, half), bf16), dma(4 * lead)],
            name="attend_back",
        )
        live.put(grad=grad, d_low=d_low, d_qkv=d_qkv, keep=keep, low=low)
        live.put(**{f"gains{layer}1": jnp.concatenate([d_gain, d_shift], 1)})

    def attend_grad(layer):
        hidden, first, qkv, mixed = live.values[f"attn{layer}"]
        aligned = block % 128 == 0
        if not aligned:
            first, mixed = turn(sl, first, lead), turn(sl, mixed, lead // 2)
        parts = call(
            partial(attend_grad_kernel, lead, aligned),
            [quarter] * 4,
            [place, first, mixed, live.d_qkv, live.d_low],
            [SMEM] + [VMEM] * 4,
            name="attend_grad",
        )
        return live.flow(Scatter(sl, parts, 2))

    def sides(flow, wide, columns):
        value = flow.value.reshape(2, rows, wide)
        keep, send = split(value[..., :columns], SIDE, 0)
        return keep, sl.flip(send, SIDE), value[..., columns:]

    def finish(layer, g_attn, g_ups, before):
        keep, other, out = g_attn
        return update(
            partial(finish_kernel, 2 * block, 2 * fsdp * feeds),
            layer,
            w_big.shape,
            [mine(SIDE)[None], keep, other, out, *itertools.chain(*g_ups)],
            [SMEM] + [VMEM] * (3 + 2 * len(g_ups)),
            [m_big, v_big],
            before,
            "finish",
        )

    def finish_down(layer, flow, before):
        return update(
            finish_down_kernel,
            layer,
            w_down.shape,
            [flow.value],
            [VMEM],
            [m_down, v_down],
            before,
            "finish_down",
        )

    def table_terms():
        first, second = [
            jnp.concatenate([live.values[f"gains{n}0"], live.values[f"gains{n}1"]], 1) for n in range(2)
        ]
        hit = jnp.arange(count - 1) == section_ids[0]
        terms = jnp.concatenate([first, jnp.where(hit[:, None], second, 0.0)], 0)
        terms = terms.reshape(count, high, 2, 2, fsdp, norm_table.shape[1])
        return jnp.moveaxis(terms, 0, 4)

    def table_step(pos, bits):
        value = live.table
        for bit in bits:
            keep, send = split(value, bit, pos)
            value = keep + sl.flip(send, bit)
        live.put(table=value)

    ups[0].start()
    twins.start()
    attns[0].finish()
    live.put(gains=gains_of(attns[0].quarters, live.sections))
    attend(0, live.hidden)
    cross()
    live.seal(ups[0], twins)

    attns.append(live.flow(twins.part(0)))
    ups.append(live.flow(twins.part(1)))
    live.flows.remove(twins)
    attns[1].start()
    downs[1].start()
    ups[0].finish()
    feed_forward(0)
    cross()
    live.seal(attns[1], downs[1])

    ups[1].start()
    downs[1].start()
    attns[1].finish()
    attend(1, live.feed0[0])
    cross()
    live.seal(ups[1], downs[1])

    ups[1].finish()
    downs[1].finish()
    live.put(grad=live.d_low.astype(f32))
    feed_turn(1)
    g_down1 = down_grad(1, True)
    g_down1.cross()
    g_down1.start()
    live.seal()

    g_up1 = up_grad(1)
    g_up1.cross()
    g_up1.start()
    cross()
    attend_back(1)
    live.seal(g_down1, g_up1)

    g_down1.start()
    g_up1.start()
    g_attn1 = attend_grad(1)
    g_attn1.cross()
    g_attn1.start()
    cross()
    feed_back(0)
    g_down0 = down_grad(0)
    live.seal(g_down1, g_up1, g_attn1)

    cross()
    g_down0.cross()
    g_down0.start()
    g_down1.start()
    g_up1.start()
    g_attn1.start()
    g_up0b = up_grad(0, 1)
    g_up0b.cross()
    attend_back(0)
    live.seal(g_down0, g_down1, g_up1, g_attn1)

    cross()
    g_attn0 = attend_grad(0)
    g_attn0.cross()
    g_attn0.start()
    g_up0b.start()
    g_attn1.start()
    g_down0.start()
    g_up0a = up_grad(0, 0)
    norm_back(0, 0, live.attn0[0])
    live.put(down=finish_down(1, g_down1, []), up1=sides(g_up1, feed // 2, feed // 2)[:2])
    live.seal(g_attn0, g_attn1, g_down0, g_up0b)

    g_up0a.cross()
    g_up0a.start()
    g_attn0.start()
    g_up0b.start()
    g_down0.start()
    live.put(table=table_terms())
    table_step(2, [CORE])
    table_step(1, [SIDE])
    table = live.table.reshape(*(len(sl.high) + len(sl.deep)) * [2], count, -1)
    live.put(table=table)
    attn1 = sides(g_attn1, 2 * width, part)
    live.put(big=finish(1, attn1, [live.up1], []))
    feed_down(1)
    live.seal(g_up0a, g_attn0, g_up0b, g_down0)

    g_up0a.start()
    g_attn0.start()
    g_up0b.start()
    cross()
    out_act = live.feed1[0][:length] + (live.keep[:length] + live.other[0][length:].astype(f32))
    table_step(0, sl.high)
    table_step(-3, sl.deep[-1:])
    live.put(out_act=out_act.astype(bf16), down=finish_down(0, g_down0, live.down))
    live.seal(g_up0a, g_attn0, g_up0b)

    g_up0a.start()
    live.put(attn0=sides(g_attn0, 2 * width, part), up0b=sides(g_up0b, feed // 4, feed // 4)[:2])
    live.seal(g_up0a)

    table_step(0, sl.deep[:-1])
    up0a = sides(g_up0a, feed // 4, feed // 4)[:2]
    grad_big, new_m_big, step_big = finish(0, live.attn0, [up0a, live.up0b], live.big)
    grad_down, new_m_down, step_down = live.down
    grad_table = live.table
    new_m_table, step_table = adam_update(m_table, v_table, grad_table)
    return (
        live.out_act[None],
        live.d_low[:length][None],
        grad_big,
        grad_down,
        grad_table,
        new_m_big,
        new_m_down,
        new_m_table,
        step_big,
        step_down,
        step_table,
    )


def solution(mesh):
    both = ("dp", "fsdp")
    rows, middle, last = P(both, None, None), P(None, both, None), P(None, both)
    return jax.shard_map(
        partial(body, mesh.shape["dp"], mesh.shape["fsdp"]),
        mesh=mesh,
        in_specs=(rows, rows, P(both, None), P(both), middle, middle, last)
        + 2 * (middle, middle, last),
        out_specs=(rows, rows) + 3 * (middle, middle, last),
        check_vma=False,
    )
```

time: 490 us -> 429 us (0.88)
  waiting for transfers between devices: 261 us -> 192 us
  Pallas kernels: 92.6 us -> 99.6 us
    ppermute x84 -> x89, waiting for transfers between devices: 261 us -> 192 us  [flip(): lax.ppermute(value, axis, [(i, i ^ mask) for i in range(self.size[axis])])]
    unnamed x138 -> x207, local copies, waits for them, and re-layouts: 18.9 us -> 30 us
    pallas_call x54 -> x53, Pallas kernels: 85.1 us -> 92.1 us  [call(): pl.pallas_call(kernel, out_shape=[jax.ShapeDtypeStruct(shape, kind) for s...]
    slice x28 -> x6, local copies, waits for them, and re-layouts: 8.6 us -> 2.08 us  [the longest x2 1.05 us: sides(): keep, send = split(value[..., :columns], SIDE, 0)]
    ppermute x84 -> x89, starting transfers between devices: 82.1 us -> 83.3 us  [flip(): lax.ppermute(value, axis, [(i, i ^ mask) for i in range(self.size[axis])])]
  transfers between devices with their start and end apart: 84 -> 89, of which waited for: 43 -> 41; matrix products, arithmetic and copies ran while one was open for 4% -> 4% of each run, Pallas kernels for 17% -> 19%
where the time goes in v3:
time: 429 us; the launch traced here: 425 us
  waiting for transfers between devices  192 us (45%)
  Pallas kernels  99.6 us (23%)
  starting transfers between devices  83.3 us (19%)
  local copies, waits for them, and re-layouts  36.3 us (8%)
  other arithmetic  10.6 us (2%)
    ppermute x89, waiting for transfers between devices, flip(): lax.ppermute(value, axis, [(i, i ^ mask) for i in range(self.size[axis])])  192 us
    pallas_call x53, Pallas kernels, call(): pl.pallas_call(kernel, out_shape=[jax.ShapeDtypeStruct(shape, kind) for s...  92.1 us
    ppermute x89, starting transfers between devices, flip(): lax.ppermute(value, axis, [(i, i ^ mask) for i in range(self.size[axis])])  83.3 us
    unnamed x207, local copies, waits for them, and re-layouts  30 us
  transfers between devices with their start and end apart: 89, of which 41 were waited for; matrix products, arithmetic and copies ran while one was open for 4% of the time, Pallas kernels for 19%

profile of v3, /device:TPU:0, one launch (start us, length us, event | category | flops | bytes accessed | tf_op | source)
XLA Modules:
  0.0 424.5 jit_solution(14182622874351789220)
XLA Ops:
  1.9 4.1 collective-permute-start.1
  13.1 4.8 %collective-permute-done.1 = bf16[128,1024]{1,0:T(8,128)(2,1)S(1)} collective-permute-done((bf16[128,1024]{1,0:T(8,128)(2,1)S(1)}, bf16[128,1024]{1,0:T(8,128)(2,1)S(1)}, u32[]{:S(2)}, u32[]{:S(2)}) %collective-permute-start.1) | collective-permute-done | bytes 262176 | tf_op jit(solution)/shard_map/ppermute | solution.py:42
  18.7 3.4 collective-permute-start.6
  25.1 8.8 %collective-permute-done.5 = bf16[32,2048]{1,0:T(8,128)(2,1)S(1)} collective-permute-done((bf16[32,2048]{1,0:T(8,128)(2,1)S(1)}, bf16[32,2048]{1,0:T(8,128)(2,1)S(1)}, u32[]{:S(2)}, u32[]{:S(2)}) %collective-permute-start.5) | collective-permute-done | bytes 131104 | tf_op jit(solution)/shard_map/ppermute | solution.py:42
  33.9 2.1 collective-permute-done.6
  38.6 3.4 collective-permute-start.8
  44.7 2.1 fusion
  47.7 12.4 %collective-permute-done.9 = bf16[64,2048]{1,0:T(8,128)(2,1)S(1)} collective-permute-done((bf16[64,2048]{1,0:T(8,128)(2,1)S(1)}, bf16[64,2048]{1,0:T(8,128)(2,1)S(1)}, u32[]{:S(2)}, u32[]{:S(2)}) %collective-permute-start.9) | collective-permute-done | bytes 262176 | tf_op jit(solution)/shard_map/ppermute | solution.py:42
  63.5 4.5 %collective-permute-start.15 = (bf16[128,2048]{1,0:T(8,128)(2,1)S(1)}, bf16[128,2048]{1,0:T(8,128)(2,1)S(1)}, u32[]{:S(2)}, u32[]{:S(2)}) collective-permute-start(bf16[128,2048]{1,0:T(8,128)(2,1)S(1)} %bitcast.234), channel_id=1, source_target_pairs={{0,1},{1,0},{2,3},{3,2},{4,5},{5,4},{6,7},{7,6},{8,9},{9,8},{10,11... | collective-permute-start | bytes 1572872 | tf_op jit(solution)/shard_map/ppermute | solution.py:42
  69.4 20.5 %collective-permute-done.15 = bf16[128,2048]{1,0:T(8,128)(2,1)S(1)} collective-permute-done((bf16[128,2048]{1,0:T(8,128)(2,1)S(1)}, bf16[128,2048]{1,0:T(8,128)(2,1)S(1)}, u32[]{:S(2)}, u32[]{:S(2)}) %collective-permute-start.15) | collective-permute-done | bytes 524320 | tf_op jit(solution)/shard_map/ppermute | solution.py:42
  89.9 3.9 collective-permute-done.16
  101.5 9.2 %attend.2 = (f32[256,1024]{1,0:T(8,128)}, bf16[256,1024]{1,0:T(8,128)(2,1)S(1)}, bf16[256,1536]{1,0:T(8,128)(2,1)S(1)}, bf16[256,512]{1,0:T(8,128)(2,1)S(1)}, f3...) custom-call(s32[2]{0:T(128)S(1)} %pad_add_fusion.place.up_place.dn_place, ...), custom_call_target="tpu_custom_call" | custom-call | tf_op jit(solution)/shard_map/attend/pallas_call | solution.py:54
  112.9 9.8 %collective-permute-done.22 = bf16[256,2048]{1,0:T(8,128)(2,1)} collective-permute-done((bf16[256,2048]{1,0:T(8,128)(2,1)}, bf16[256,2048]{1,0:T(8,128)(2,1)}, u32[]{:S(2)}, u32[]{:S(2)}) %collective-permute-start.22) | collective-permute-done | bytes 1048608 | tf_op jit(solution)/shard_map/ppermute | solution.py:42
  129.2 5.5 %feed.1 = (f32[256,1024]{1,0:T(8,128)S(1)}, bf16[256,1024]{1,0:T(8,128)(2,1)S(1)}, f32[256,2048]{1,0:T(8,128)S(1)}, bf16[256,2048]{1,0:T(8,128)(2,1)S(1)}, f32[2...) custom-call(s32[2]{0:T(128)S(1)} %pad_add_fusion.place.up_place.dn_place, ...), custom_call_target="tpu_custom_call" | custom-call | tf_op jit(solution)/shard_map/feed/pallas_call | solution.py:54
  136.9 17.8 %collective-permute-done.28 = bf16[256,1024]{1,0:T(8,128)(2,1)S(1)} collective-permute-done((bf16[256,1024]{1,0:T(8,128)(2,1)S(1)}, bf16[256,1024]{1,0:T(8,128)(2,1)S(1)}, u32[]{:S(2)}, u32[]{:S(2)}) %collective-permute-start.28) | collective-permute-done | bytes 524320 | tf_op jit(solution)/shard_map/ppermute | solution.py:42
  157.5 8.2 %attend.3 = (f32[256,1024]{1,0:T(8,128)S(1)}, bf16[256,1024]{1,0:T(8,128)(2,1)S(1)}, bf16[256,1536]{1,0:T(8,128)(2,1)S(1)}, bf16[256,512]{1,0:T(8,128)(2,1)S(1)}...) custom-call(s32[2]{0:T(128)S(1)} %pad_add_fusion.place.up_place.dn_place, ...), custom_call_target="tpu_custom_call" | custom-call | tf_op jit(solution)/shard_map/attend/pallas_call | solution.py:54
  167.8 12.7 %collective-permute-done.34 = bf16[512,1024]{1,0:T(8,128)(2,1)S(1)} collective-permute-done((bf16[512,1024]{1,0:T(8,128)(2,1)S(1)}, bf16[512,1024]{1,0:T(8,128)(2,1)S(1)}, u32[]{:S(2)}, u32[]{:S(2)}) %collective-permute-start.34) | collective-permute-done | bytes 1048608 | tf_op jit(solution)/shard_map/ppermute | solution.py:42
  181.5 2.0 collective-permute-done.36.refs_12_.q2
  186.5 6.8 %feed_turn.1 = (f32[256,1024]{1,0:T(8,128)S(1)}, bf16[256,1024]{1,0:T(8,128)(2,1)S(1)}, bf16[256,2048]{1,0:T(8,128)(2,1)S(1)}, bf16[256,2048]{1,0:T(8,128)(2,1)S...) custom-call(s32[2]{0:T(128)S(1)} %pad_add_fusion.place.up_place.dn_place, ...), custom_call_target="tpu_custom_call" | custom-call | tf_op jit(solution)/shard_map/feed_turn/pallas_call | solution.py:54
  193.3 1.8 down_grad.2
  195.9 2.0 collective-permute-done.38
  199.9 1.8 up_grad.3
  207.6 7.2 %collective-permute-done.40.refs_0_ = bf16[128,1024]{1,0:T(8,128)(2,1)S(1)} collective-permute-done((bf16[128,1024]{1,0:T(8,128)(2,1)S(1)}, bf16[128,1024]{1,0:T(8,128)(2,1)S(1)}, u32[]{:S(2)}, u32[]{:S(2)}) %collective-permute-start.40) | collective-permute-done | bytes 262176 | tf_op jit(solution)/shard_map/ppermute | solution.py:42
  214.8 4.5 %collective-permute-done.41.refs_1_ = bf16[128,1024]{1,0:T(8,128)(2,1)S(1)} collective-permute-done((bf16[128,1024]{1,0:T(8,128)(2,1)S(1)}, bf16[128,1024]{1,0:T(8,128)(2,1)S(1)}, u32[]{:S(2)}, u32[]{:S(2)}) %collective-permute-start.41) | collective-permute-done | bytes 262176 | tf_op jit(solution)/shard_map/ppermute | solution.py:42
  219.3 10.2 %attend_back.2 = (f32[256,1024]{1,0:T(8,128)S(1)}, bf16[256,1024]{1,0:T(8,128)(2,1)S(1)}, f32[1,1024]{1,0:T(1,128)S(1)}, f32[1,1024]{1,0:T(1,128)S(1)}, bf16[256...) custom-call(s32[2]{0:T(128)S(1)} %pad_add_fusion.place.up_place.dn_place, ...), custom_call_target="tpu_custom_call" | custom-call | tf_op jit(solution)/shard_map/attend_back/pallas_call | solution.py:54
  232.5 2.1 collective-permute-done.48.two
  240.2 9.2 %collective-permute-done.46.refs_0_ = bf16[256,1024]{1,0:T(8,128)(2,1)S(1)} collective-permute-done((bf16[256,1024]{1,0:T(8,128)(2,1)S(1)}, bf16[256,1024]{1,0:T(8,128)(2,1)S(1)}, u32[]{:S(2)}, u32[]{:S(2)}) %collective-permute-start.46) | collective-permute-done | bytes 524320 | tf_op jit(solution)/shard_map/ppermute | solution.py:42
  249.3 6.1 %feed_back.1 = (f32[256,1024]{1,0:T(8,128)S(1)}, bf16[256,1024]{1,0:T(8,128)(2,1)S(1)}, f32[1,1024]{1,0:T(1,128)S(1)}, f32[1,1024]{1,0:T(1,128)S(1)}, bf16[256,2...) custom-call(s32[2]{0:T(128)S(1)} %pad_add_fusion.place.up_place.dn_place, ...), custom_call_target="tpu_custom_call" | custom-call | tf_op jit(solution)/shard_map/feed_back/pallas_call | solution.py:54
  258.2 2.8 collective-permute-done.50
  261.0 3.9 collective-permute-done.49
  271.2 2.2 collective-permute-start.59
  273.4 10.1 %collective-permute-done.52.refs_0_ = bf16[256,1024]{1,0:T(8,128)(2,1)S(1)} collective-permute-done((bf16[256,1024]{1,0:T(8,128)(2,1)S(1)}, bf16[256,1024]{1,0:T(8,128)(2,1)S(1)}, u32[]{:S(2)}, u32[]{:S(2)}) %collective-permute-start.52) | collective-permute-done | bytes 524320 | tf_op jit(solution)/shard_map/ppermute | solution.py:42
  286.1 10.9 %attend_back.3 = (f32[256,1024]{1,0:T(8,128)S(1)}, bf16[256,1024]{1,0:T(8,128)(2,1)S(1)}, f32[1,1024]{1,0:T(1,128)S(1)}, f32[1,1024]{1,0:T(1,128)S(1)}, bf16[256...) custom-call(s32[2]{0:T(128)S(1)} %pad_add_fusion.place.up_place.dn_place, ...), custom_call_target="tpu_custom_call" | custom-call | tf_op jit(solution)/shard_map/attend_back/pallas_call | solution.py:54
  300.8 2.8 attend_grad.3
  314.9 12.7 %collective-permute-done.66 = bf16[64,2048]{1,0:T(8,128)(2,1)S(1)} collective-permute-done((bf16[64,2048]{1,0:T(8,128)(2,1)S(1)}, bf16[64,2048]{1,0:T(8,128)(2,1)S(1)}, u32[]{:S(2)}, u32[]{:S(2)}) %collective-permute-start.66) | collective-permute-done | bytes 262176 | tf_op jit(solution)/shard_map/ppermute | solution.py:42
  327.6 2.7 collective-permute-start.68
  331.4 2.0 up_grad.5
  338.1 3.9 collective-permute-done.68
  362.6 2.4 down.1
  366.9 2.4 finish.2
  369.3 6.4 %collective-permute-done.76 = bf16[128,1024]{1,0:T(8,128)(2,1)} collective-permute-done((bf16[128,1024]{1,0:T(8,128)(2,1)}, bf16[128,1024]{1,0:T(8,128)(2,1)}, u32[]{:S(2)}, u32[]{:S(2)}) %collective-permute-start.76) | collective-permute-done | bytes 262176 | tf_op jit(solution)/shard_map/ppermute | solution.py:42
  375.7 4.2 collective-permute-done.77
  384.3 2.8 collective-permute-start.82
  393.6 6.7 %collective-permute-done.78 = bf16[256,1024]{1,0:T(8,128)(2,1)S(1)} collective-permute-done((bf16[256,1024]{1,0:T(8,128)(2,1)S(1)}, bf16[256,1024]{1,0:T(8,128)(2,1)S(1)}, u32[]{:S(2)}, u32[]{:S(2)}) %collective-permute-start.78) | collective-permute-done | bytes 524320 | tf_op jit(solution)/shard_map/ppermute | solution.py:42
  408.4 3.2 collective-permute-done.85.refs_3_
  411.7 2.6 collective-permute-start.88
  417.6 2.6 collective-permute-done.87.refs_1_
  421.9 2.4 finish.3
  (450 shorter events, 144.7 us)
Async XLA Ops:
  1.9 16.0 %collective-permute-start.1 = (bf16[128,1024]{1,0:T(8,128)(2,1)S(1)}, bf16[128,1024]{1,0:T(8,128)(2,1)S(1)}, u32[]{:S(2)}, u32[]{:S(2)}) collective-permute-start(bf16[128,1024]{1,0:T(8,128)(2,1)S(1)} %get-tuple-element.574), channel_id=1, source_target_pairs={{0,2},{1,3},{2,0},{3,1},{4,6},{5,7},{6,4},{7,5},{8,10},{9,11},{10,... | collective-permute-start | bytes 786440 | tf_op jit(solution)/shard_map/ppermute | solution.py:42
  12.4 23.6 %collective-permute-start.4 = (bf16[272,1024]{1,0:T(8,128)(2,1)}, bf16[272,1024]{1,0:T(8,128)(2,1)}, u32[]{:S(2)}, u32[]{:S(2)}) collective-permute-start(bf16[272,1024]{1,0:T(8,128)(2,1)} %pad_maximum_fusion), channel_id=1, source_target_pairs={{0,8},{4,12},{8,0},{12,4},{16,24},{20,28},{24,16},{28,20},{1,9},{5... | collective-permute-start | bytes 1671176 | tf_op jit(solution)/shard_map/ppermute | solution.py:42
  17.9 19.1 %collective-permute-start.7 = (bf16[256,1024]{1,0:T(8,128)(2,1)S(1)}, bf16[256,1024]{1,0:T(8,128)(2,1)S(1)}, u32[]{:S(2)}, u32[]{:S(2)}) collective-permute-start(bf16[256,1024]{1,0:T(8,128)(2,1)S(1)} %bitcast.231), channel_id=1, source_target_pairs={{0,1},{1,0},{2,3},{3,2},{4,5},{5,4},{6,7},{7,6},{8,9},{9,8},{10,11... | collective-permute-start | bytes 1572872 | tf_op jit(solution)/shard_map/ppermute | solution.py:42
  18.7 17.3 %collective-permute-start.6 = (bf16[64,2176]{1,0:T(8,128)(2,1)S(1)}, bf16[64,2176]{1,0:T(8,128)(2,1)S(1)}, u32[]{:S(2)}, u32[]{:S(2)}) collective-permute-start(bf16[64,2176]{1,0:T(8,128)(2,1)S(1)} %bitcast.236), channel_id=1, source_target_pairs={{0,2},{1,3},{2,0},{3,1},{4,6},{5,7},{6,4},{7,5},{8,10},{9,11},{10,... | collective-permute-start | bytes 835592 | tf_op jit(solution)/shard_map/ppermute | solution.py:42
  37.1 23.7 %collective-permute-start.10 = (bf16[512,1024]{1,0:T(8,128)(2,1)S(1)}, bf16[512,1024]{1,0:T(8,128)(2,1)S(1)}, u32[]{:S(2)}, u32[]{:S(2)}) collective-permute-start(bf16[512,1024]{1,0:T(8,128)(2,1)S(1)} %bitcast.208), channel_id=1, source_target_pairs={{0,16},{4,20},{8,24},{12,28},{16,0},{20,4},{24,8},{28,12},{1,17},{... | collective-permute-start | bytes 3145736 | tf_op jit(solution)/shard_map/ppermute | solution.py:42
  38.5 22.4 %collective-permute-start.11 = (bf16[512,1024]{1,0:T(8,128)(2,1)S(1)}, bf16[512,1024]{1,0:T(8,128)(2,1)S(1)}, u32[]{:S(2)}, u32[]{:S(2)}) collective-permute-start(bf16[512,1024]{1,0:T(8,128)(2,1)S(1)} %bitcast.209), channel_id=1, source_target_pairs={{0,4},{4,0},{8,12},{12,8},{16,20},{20,16},{24,28},{28,24},{1,5},{5... | collective-permute-start | bytes 3145736 | tf_op jit(solution)/shard_map/ppermute | solution.py:42
  38.6 22.3 %collective-permute-start.8 = (bf16[128,2176]{1,0:T(8,128)(2,1)S(1)}, bf16[128,2176]{1,0:T(8,128)(2,1)S(1)}, u32[]{:S(2)}, u32[]{:S(2)}) collective-permute-start(bf16[128,2176]{1,0:T(8,128)(2,1)S(1)} %bitcast.227), channel_id=1, source_target_pairs={{0,1},{1,0},{2,3},{3,2},{4,5},{5,4},{6,7},{7,6},{8,9},{9,8},{10,11... | collective-permute-start | bytes 1671176 | tf_op jit(solution)/shard_map/ppermute | solution.py:42
  42.0 18.2 %collective-permute-start.9 = (bf16[64,2048]{1,0:T(8,128)(2,1)S(1)}, bf16[64,2048]{1,0:T(8,128)(2,1)S(1)}, u32[]{:S(2)}, u32[]{:S(2)}) collective-permute-start(bf16[64,2048]{1,0:T(8,128)(2,1)S(1)} %bitcast.258), channel_id=1, source_target_pairs={{0,2},{1,3},{2,0},{3,1},{4,6},{5,7},{6,4},{7,5},{8,10},{9,11},{10,... | collective-permute-start | bytes 786440 | tf_op jit(solution)/shard_map/ppermute | solution.py:42
  61.9 32.8 %collective-permute-start.13 = (bf16[256,2176]{1,0:T(8,128)(2,1)S(1)}, bf16[256,2176]{1,0:T(8,128)(2,1)S(1)}, u32[]{:S(2)}, u32[]{:S(2)}) collective-permute-start(bf16[256,2176]{1,0:T(8,128)(2,1)S(1)} %bitcast.203), channel_id=1, source_target_pairs={{0,16},{4,20},{8,24},{12,28},{16,0},{20,4},{24,8},{28,12},{1,17},{... | collective-permute-start | bytes 3342344 | tf_op jit(solution)/shard_map/ppermute | solution.py:42
  63.0 31.8 %collective-permute-start.14 = (bf16[256,2176]{1,0:T(8,128)(2,1)S(1)}, bf16[256,2176]{1,0:T(8,128)(2,1)S(1)}, u32[]{:S(2)}, u32[]{:S(2)}) collective-permute-start(bf16[256,2176]{1,0:T(8,128)(2,1)S(1)} %bitcast.204), channel_id=1, source_target_pairs={{0,4},{4,0},{8,12},{12,8},{16,20},{20,16},{24,28},{28,24},{1,5},{5... | collective-permute-start | bytes 3342344 | tf_op jit(solution)/shard_map/ppermute | solution.py:42
  63.0 30.8 %collective-permute-start.12 = (bf16[512,1024]{1,0:T(8,128)(2,1)S(1)}, bf16[512,1024]{1,0:T(8,128)(2,1)S(1)}, u32[]{:S(2)}, u32[]{:S(2)}) collective-permute-start(bf16[512,1024]{1,0:T(8,128)(2,1)S(1)} %collective-permute-done.10.refs_10_.refs_9_), channel_id=1, source_target_pairs={{0,4},{4,0},{8,12},{12,8},{16,20},{20,16},{24,28},{28,24},{1,5},{5... | collective-permute-start | bytes 3145736 | tf_op jit(solution)/shard_map/ppermute | solution.py:42
  63.5 26.4 %collective-permute-start.15 = (bf16[128,2048]{1,0:T(8,128)(2,1)S(1)}, bf16[128,2048]{1,0:T(8,128)(2,1)S(1)}, u32[]{:S(2)}, u32[]{:S(2)}) collective-permute-start(bf16[128,2048]{1,0:T(8,128)(2,1)S(1)} %bitcast.234), channel_id=1, source_target_pairs={{0,1},{1,0},{2,3},{3,2},{4,5},{5,4},{6,7},{7,6},{8,9},{9,8},{10,11... | collective-permute-start | bytes 1572872 | tf_op jit(solution)/shard_map/ppermute | solution.py:42
  68.0 25.7 %collective-permute-start.16 = (bf16[128,2048]{1,0:T(8,128)(2,1)S(1)}, bf16[128,2048]{1,0:T(8,128)(2,1)S(1)}, u32[]{:S(2)}, u32[]{:S(2)}) collective-permute-start(bf16[128,2048]{1,0:T(8,128)(2,1)S(1)} %bitcast.233), channel_id=1, source_target_pairs={{0,2},{1,3},{2,0},{3,1},{4,6},{5,7},{6,4},{7,5},{8,10},{9,11},{10,... | collective-permute-start | bytes 1572872 | tf_op jit(solution)/shard_map/ppermute | solution.py:42
  96.8 25.9 %collective-permute-start.22 = (bf16[256,2048]{1,0:T(8,128)(2,1)}, bf16[256,2048]{1,0:T(8,128)(2,1)}, u32[]{:S(2)}, u32[]{:S(2)}) collective-permute-start(bf16[256,2048]{1,0:T(8,128)(2,1)} %bitcast.48), channel_id=1, source_target_pairs={{0,1},{1,0},{2,3},{3,2},{4,5},{5,4},{6,7},{7,6},{8,9},{9,8},{10,11... | collective-permute-start | bytes 3145736 | tf_op jit(solution)/shard_map/ppermute | solution.py:42
  97.9 25.9 %collective-permute-start.20 = (bf16[256,2048]{1,0:T(8,128)(2,1)}, bf16[256,2048]{1,0:T(8,128)(2,1)}, u32[]{:S(2)}, u32[]{:S(2)}) collective-permute-start(bf16[256,2048]{1,0:T(8,128)(2,1)} %bitcast.45.refs_5_.refs_4_), channel_id=1, source_target_pairs={{0,16},{4,20},{8,24},{12,28},{16,0},{20,4},{24,8},{28,12},{1,17},{... | collective-permute-start | bytes 3145736 | tf_op jit(solution)/shard_map/ppermute | solution.py:42
  98.4 25.4 %collective-permute-start.21 = (bf16[256,2048]{1,0:T(8,128)(2,1)}, bf16[256,2048]{1,0:T(8,128)(2,1)}, u32[]{:S(2)}, u32[]{:S(2)}) collective-permute-start(bf16[256,2048]{1,0:T(8,128)(2,1)} %bitcast.45.refs_5_.refs_4_), channel_id=1, source_target_pairs={{0,4},{4,0},{8,12},{12,8},{16,20},{20,16},{24,28},{28,24},{1,5},{5... | collective-permute-start | bytes 3145736 | tf_op jit(solution)/shard_map/ppermute | solution.py:42
  126.6 28.1 %collective-permute-start.26 = (bf16[256,2048]{1,0:T(8,128)(2,1)S(1)}, bf16[256,2048]{1,0:T(8,128)(2,1)S(1)}, u32[]{:S(2)}, u32[]{:S(2)}) collective-permute-start(bf16[256,2048]{1,0:T(8,128)(2,1)S(1)} %bitcast.223), channel_id=1, source_target_pairs={{0,16},{4,20},{8,24},{12,28},{16,0},{20,4},{24,8},{28,12},{1,17},{... | collective-permute-start | bytes 3145736 | tf_op jit(solution)/shard_map/ppermute | solution.py:42
  128.2 26.5 %collective-permute-start.27 = (bf16[256,2048]{1,0:T(8,128)(2,1)S(1)}, bf16[256,2048]{1,0:T(8,128)(2,1)S(1)}, u32[]{:S(2)}, u32[]{:S(2)}) collective-permute-start(bf16[256,2048]{1,0:T(8,128)(2,1)S(1)} %bitcast.224), channel_id=1, source_target_pairs={{0,4},{4,0},{8,12},{12,8},{16,20},{20,16},{24,28},{28,24},{1,5},{5... | collective-permute-start | bytes 3145736 | tf_op jit(solution)/shard_map/ppermute | solution.py:42
  128.5 26.2 %collective-permute-start.28 = (bf16[256,1024]{1,0:T(8,128)(2,1)S(1)}, bf16[256,1024]{1,0:T(8,128)(2,1)S(1)}, u32[]{:S(2)}, u32[]{:S(2)}) collective-permute-start(bf16[256,1024]{1,0:T(8,128)(2,1)S(1)} %bitcast.229), channel_id=1, source_target_pairs={{0,2},{1,3},{2,0},{3,1},{4,6},{5,7},{6,4},{7,5},{8,10},{9,11},{10,... | collective-permute-start | bytes 1572872 | tf_op jit(solution)/shard_map/ppermute | solution.py:42
  134.8 19.9 %collective-permute-start.24 = (bf16[128,1024]{1,0:T(8,128)(2,1)S(1)}, bf16[128,1024]{1,0:T(8,128)(2,1)S(1)}, u32[]{:S(2)}, u32[]{:S(2)}) collective-permute-start(bf16[128,1024]{1,0:T(8,128)(2,1)S(1)} %get-tuple-element.655), channel_id=1, source_target_pairs={{0,8},{4,12},{8,0},{12,4},{16,24},{20,28},{24,16},{28,20},{1,9},{5... | collective-permute-start | bytes 786440 | tf_op jit(solution)/shard_map/ppermute | solution.py:42
  136.4 18.3 %collective-permute-start.25 = (bf16[128,1024]{1,0:T(8,128)(2,1)S(1)}, bf16[128,1024]{1,0:T(8,128)(2,1)S(1)}, u32[]{:S(2)}, u32[]{:S(2)}) collective-permute-start(bf16[128,1024]{1,0:T(8,128)(2,1)S(1)} %get-tuple-element.656), channel_id=1, source_target_pairs={{0,8},{4,12},{8,0},{12,4},{16,24},{20,28},{24,16},{28,20},{1,9},{5... | collective-permute-start | bytes 786440 | tf_op jit(solution)/shard_map/ppermute | solution.py:42
  154.9 25.6 %collective-permute-start.34 = (bf16[512,1024]{1,0:T(8,128)(2,1)S(1)}, bf16[512,1024]{1,0:T(8,128)(2,1)S(1)}, u32[]{:S(2)}, u32[]{:S(2)}) collective-permute-start(bf16[512,1024]{1,0:T(8,128)(2,1)S(1)} %bitcast.215), channel_id=1, source_target_pairs={{0,1},{1,0},{2,3},{3,2},{4,5},{5,4},{6,7},{7,6},{8,9},{9,8},{10,11... | collective-permute-start | bytes 3145736 | tf_op jit(solution)/shard_map/ppermute | solution.py:42
  155.0 25.6 %collective-permute-start.32 = (bf16[256,2048]{1,0:T(8,128)(2,1)S(1)}, bf16[256,2048]{1,0:T(8,128)(2,1)S(1)}, u32[]{:S(2)}, u32[]{:S(2)}) collective-permute-start(bf16[256,2048]{1,0:T(8,128)(2,1)S(1)} %bitcast.237), channel_id=1, source_target_pairs={{0,16},{4,20},{8,24},{12,28},{16,0},{20,4},{24,8},{28,12},{1,17},{... | collective-permute-start | bytes 3145736 | tf_op jit(solution)/shard_map/ppermute | solution.py:42
  156.1 24.5 %collective-permute-start.33 = (bf16[256,2048]{1,0:T(8,128)(2,1)S(1)}, bf16[256,2048]{1,0:T(8,128)(2,1)S(1)}, u32[]{:S(2)}, u32[]{:S(2)}) collective-permute-start(bf16[256,2048]{1,0:T(8,128)(2,1)S(1)} %bitcast.238), channel_id=1, source_target_pairs={{0,4},{4,0},{8,12},{12,8},{16,20},{20,16},{24,28},{28,24},{1,5},{5... | collective-permute-start | bytes 3145736 | tf_op jit(solution)/shard_map/ppermute | solution.py:42
  202.0 27.5 %collective-permute-start.44 = (bf16[512,1024]{1,0:T(8,128)(2,1)S(1)}, bf16[512,1024]{1,0:T(8,128)(2,1)S(1)}, u32[]{:S(2)}, u32[]{:S(2)}) collective-permute-start(bf16[512,1024]{1,0:T(8,128)(2,1)S(1)} %bitcast.299), channel_id=1, source_target_pairs={{0,1},{1,0},{2,3},{3,2},{4,5},{5,4},{6,7},{7,6},{8,9},{9,8},{10,11... | collective-permute-start | bytes 3145736 | tf_op jit(solution)/shard_map/ppermute | solution.py:42
  203.6 25.8 %collective-permute-start.42 = (bf16[256,2048]{1,0:T(8,128)(2,1)S(1)}, bf16[256,2048]{1,0:T(8,128)(2,1)S(1)}, u32[]{:S(2)}, u32[]{:S(2)}) collective-permute-start(bf16[256,2048]{1,0:T(8,128)(2,1)S(1)} %get-tuple-element.816), channel_id=1, source_target_pairs={{0,4},{4,0},{8,12},{12,8},{16,20},{20,16},{24,28},{28,24},{1,5},{5... | collective-permute-start | bytes 3145736 | tf_op jit(solution)/shard_map/ppermute | solution.py:42
  204.7 25.3 %collective-permute-start.45 = (bf16[256,2048]{1,0:T(8,128)(2,1)S(1)}, bf16[256,2048]{1,0:T(8,128)(2,1)S(1)}, u32[]{:S(2)}, u32[]{:S(2)}) collective-permute-start(bf16[256,2048]{1,0:T(8,128)(2,1)S(1)} %add_low.5), channel_id=1, source_target_pairs={{0,16},{4,20},{8,24},{12,28},{16,0},{20,4},{24,8},{28,12},{1,17},{... | collective-permute-start | bytes 3145736 | tf_op jit(solution)/shard_map/ppermute | solution.py:42
  232.0 33.0 %collective-permute-start.47 = (bf16[256,2048]{1,0:T(8,128)(2,1)S(1)}, bf16[256,2048]{1,0:T(8,128)(2,1)S(1)}, u32[]{:S(2)}, u32[]{:S(2)}) collective-permute-start(bf16[256,2048]{1,0:T(8,128)(2,1)S(1)} %get-tuple-element.874), channel_id=1, source_target_pairs={{0,4},{4,0},{8,12},{12,8},{16,20},{20,16},{24,28},{28,24},{1,5},{5... | collective-permute-start | bytes 3145736 | tf_op jit(solution)/shard_map/ppermute | solution.py:42
  234.8 30.1 %collective-permute-start.51 = (bf16[256,2048]{1,0:T(8,128)(2,1)S(1)}, bf16[256,2048]{1,0:T(8,128)(2,1)S(1)}, u32[]{:S(2)}, u32[]{:S(2)}) collective-permute-start(bf16[256,2048]{1,0:T(8,128)(2,1)S(1)} %add_low.6), channel_id=1, source_target_pairs={{0,16},{4,20},{8,24},{12,28},{16,0},{20,4},{24,8},{28,12},{1,17},{... | collective-permute-start | bytes 3145736 | tf_op jit(solution)/shard_map/ppermute | solution.py:42
  237.6 23.5 %collective-permute-start.50 = (bf16[128,2048]{1,0:T(8,128)(2,1)S(1)}, bf16[128,2048]{1,0:T(8,128)(2,1)S(1)}, u32[]{:S(2)}, u32[]{:S(2)}) collective-permute-start(bf16[128,2048]{1,0:T(8,128)(2,1)S(1)} %bitcast.303), channel_id=1, source_target_pairs={{0,1},{1,0},{2,3},{3,2},{4,5},{5,4},{6,7},{7,6},{8,9},{9,8},{10,11... | collective-permute-start | bytes 1572872 | tf_op jit(solution)/shard_map/ppermute | solution.py:42
  239.5 25.4 %collective-permute-start.49 = (bf16[256,1024]{1,0:T(8,128)(2,1)S(1)}, bf16[256,1024]{1,0:T(8,128)(2,1)S(1)}, u32[]{:S(2)}, u32[]{:S(2)}) collective-permute-start(bf16[256,1024]{1,0:T(8,128)(2,1)S(1)} %bitcast.304), channel_id=1, source_target_pairs={{0,2},{1,3},{2,0},{3,1},{4,6},{5,7},{6,4},{7,5},{8,10},{9,11},{10,... | collective-permute-start | bytes 1572872 | tf_op jit(solution)/shard_map/ppermute | solution.py:42
  266.9 33.9 %collective-permute-start.53 = (bf16[512,1024]{1,0:T(8,128)(2,1)S(1)}, bf16[512,1024]{1,0:T(8,128)(2,1)S(1)}, u32[]{:S(2)}, u32[]{:S(2)}) collective-permute-start(bf16[512,1024]{1,0:T(8,128)(2,1)S(1)} %get-tuple-element.926), channel_id=1, source_target_pairs={{0,4},{4,0},{8,12},{12,8},{16,20},{20,16},{24,28},{28,24},{1,5},{5... | collective-permute-start | bytes 3145736 | tf_op jit(solution)/shard_map/ppermute | solution.py:42
  267.8 33.0 %collective-permute-start.57 = (bf16[512,1024]{1,0:T(8,128)(2,1)S(1)}, bf16[512,1024]{1,0:T(8,128)(2,1)S(1)}, u32[]{:S(2)}, u32[]{:S(2)}) collective-permute-start(bf16[512,1024]{1,0:T(8,128)(2,1)S(1)} %add_low.7), channel_id=1, source_target_pairs={{0,16},{4,20},{8,24},{12,28},{16,0},{20,4},{24,8},{28,12},{1,17},{... | collective-permute-start | bytes 3145736 | tf_op jit(solution)/shard_map/ppermute | solution.py:42
  270.1 29.8 %collective-permute-start.60 = (bf16[128,2048]{1,0:T(8,128)(2,1)S(1)}, bf16[128,2048]{1,0:T(8,128)(2,1)S(1)}, u32[]{:S(2)}, u32[]{:S(2)}) collective-permute-start(bf16[128,2048]{1,0:T(8,128)(2,1)S(1)} %bitcast.302), channel_id=1, source_target_pairs={{0,1},{1,0},{2,3},{3,2},{4,5},{5,4},{6,7},{7,6},{8,9},{9,8},{10,11... | collective-permute-start | bytes 1572872 | tf_op jit(solution)/shard_map/ppermute | solution.py:42
  271.2 28.7 %collective-permute-start.59 = (bf16[64,2048]{1,0:T(8,128)(2,1)S(1)}, bf16[64,2048]{1,0:T(8,128)(2,1)S(1)}, u32[]{:S(2)}, u32[]{:S(2)}) collective-permute-start(bf16[64,2048]{1,0:T(8,128)(2,1)S(1)} %bitcast.307), channel_id=1, source_target_pairs={{0,2},{1,3},{2,0},{3,1},{4,6},{5,7},{6,4},{7,5},{8,10},{9,11},{10,... | collective-permute-start | bytes 786440 | tf_op jit(solution)/shard_map/ppermute | solution.py:42
  283.5 16.4 %collective-permute-start.58 = (bf16[128,1024]{1,0:T(8,128)(2,1)S(1)}, bf16[128,1024]{1,0:T(8,128)(2,1)S(1)}, u32[]{:S(2)}, u32[]{:S(2)}) collective-permute-start(bf16[128,1024]{1,0:T(8,128)(2,1)S(1)} %bitcast.308), channel_id=1, source_target_pairs={{0,16},{4,20},{8,24},{12,28},{16,0},{20,4},{24,8},{28,12},{1,17},{... | collective-permute-start | bytes 786440 | tf_op jit(solution)/shard_map/ppermute | solution.py:42
  305.7 36.3 %collective-permute-start.63 = (bf16[256,2048]{1,0:T(8,128)(2,1)}, bf16[256,2048]{1,0:T(8,128)(2,1)S(1)}, u32[]{:S(2)}, u32[]{:S(2)}) collective-permute-start(bf16[256,2048]{1,0:T(8,128)(2,1)} %copy-done.85), channel_id=1, source_target_pairs={{0,4},{4,0},{8,12},{12,8},{16,20},{20,16},{24,28},{28,24},{1,5},{5... | collective-permute-start | bytes 3145736 | tf_op jit(solution)/shard_map/ppermute | solution.py:42
  310.2 27.9 %collective-permute-start.67 = (bf16[256,1024]{1,0:T(8,128)(2,1)S(1)}, bf16[256,1024]{1,0:T(8,128)(2,1)S(1)}, u32[]{:S(2)}, u32[]{:S(2)}) collective-permute-start(bf16[256,1024]{1,0:T(8,128)(2,1)S(1)} %bitcast.301), channel_id=1, source_target_pairs={{0,1},{1,0},{2,3},{3,2},{4,5},{5,4},{6,7},{7,6},{8,9},{9,8},{10,11... | collective-permute-start | bytes 1572872 | tf_op jit(solution)/shard_map/ppermute | solution.py:42
  311.1 16.5 %collective-permute-start.66 = (bf16[64,2048]{1,0:T(8,128)(2,1)S(1)}, bf16[64,2048]{1,0:T(8,128)(2,1)S(1)}, u32[]{:S(2)}, u32[]{:S(2)}) collective-permute-start(bf16[64,2048]{1,0:T(8,128)(2,1)S(1)} %bitcast.309), channel_id=1, source_target_pairs={{0,2},{1,3},{2,0},{3,1},{4,6},{5,7},{6,4},{7,5},{8,10},{9,11},{10,... | collective-permute-start | bytes 786440 | tf_op jit(solution)/shard_map/ppermute | solution.py:42
  312.7 17.7 %collective-permute-start.61 = (bf16[256,1024]{1,0:T(8,128)(2,1)S(1)}, bf16[256,1024]{1,0:T(8,128)(2,1)S(1)}, u32[]{:S(2)}, u32[]{:S(2)}) collective-permute-start(bf16[256,1024]{1,0:T(8,128)(2,1)S(1)} %copy-done.91), channel_id=1, source_target_pairs={{0,8},{4,12},{8,0},{12,4},{16,24},{20,28},{24,16},{28,20},{1,9},{5... | collective-permute-start | bytes 1572872 | tf_op jit(solution)/shard_map/ppermute | solution.py:42
  313.5 28.5 %collective-permute-start.65 = (bf16[256,2048]{1,0:T(8,128)(2,1)S(1)}, bf16[256,2048]{1,0:T(8,128)(2,1)S(1)}, u32[]{:S(2)}, u32[]{:S(2)}) collective-permute-start(bf16[256,2048]{1,0:T(8,128)(2,1)S(1)} %add_low.8), channel_id=1, source_target_pairs={{0,16},{4,20},{8,24},{12,28},{16,0},{20,4},{24,8},{28,12},{1,17},{... | collective-permute-start | bytes 3145736 | tf_op jit(solution)/shard_map/ppermute | solution.py:42
  343.1 36.8 %collective-permute-start.75 = (bf16[128,2048]{1,0:T(8,128)(2,1)}, bf16[128,2048]{1,0:T(8,128)(2,1)}, u32[]{:S(2)}, u32[]{:S(2)}) collective-permute-start(bf16[128,2048]{1,0:T(8,128)(2,1)} %bitcast.130), channel_id=1, source_target_pairs={{0,1},{1,0},{2,3},{3,2},{4,5},{5,4},{6,7},{7,6},{8,9},{9,8},{10,11... | collective-permute-start | bytes 1572872 | tf_op jit(solution)/shard_map/ppermute | solution.py:42
  346.7 33.3 %collective-permute-start.72 = (bf16[256,1024]{1,0:T(8,128)(2,1)}, bf16[256,1024]{1,0:T(8,128)(2,1)}, u32[]{:S(2)}, u32[]{:S(2)}) collective-permute-start(bf16[256,1024]{1,0:T(8,128)(2,1)} %get-tuple-element.1021), channel_id=1, source_target_pairs={{0,4},{4,0},{8,12},{12,8},{16,20},{20,16},{24,28},{28,24},{1,5},{5... | collective-permute-start | bytes 1572872 | tf_op jit(solution)/shard_map/ppermute | solution.py:42
  347.7 32.3 %collective-permute-start.74 = (bf16[256,1024]{1,0:T(8,128)(2,1)}, bf16[256,1024]{1,0:T(8,128)(2,1)}, u32[]{:S(2)}, u32[]{:S(2)}) collective-permute-start(bf16[256,1024]{1,0:T(8,128)(2,1)} %add_low.9), channel_id=1, source_target_pairs={{0,16},{4,20},{8,24},{12,28},{16,0},{20,4},{24,8},{28,12},{1,17},{... | collective-permute-start | bytes 1572872 | tf_op jit(solution)/shard_map/ppermute | solution.py:42
  354.0 21.7 %collective-permute-start.76 = (bf16[128,1024]{1,0:T(8,128)(2,1)}, bf16[128,1024]{1,0:T(8,128)(2,1)}, u32[]{:S(2)}, u32[]{:S(2)}) collective-permute-start(bf16[128,1024]{1,0:T(8,128)(2,1)} %bitcast.125), channel_id=1, source_target_pairs={{0,2},{1,3},{2,0},{3,1},{4,6},{5,7},{6,4},{7,5},{8,10},{9,11},{10,... | collective-permute-start | bytes 786440 | tf_op jit(solution)/shard_map/ppermute | solution.py:42
  355.9 24.1 %collective-permute-start.77 = (bf16[128,1024]{1,0:T(8,128)(2,1)}, bf16[128,1024]{1,0:T(8,128)(2,1)}, u32[]{:S(2)}, u32[]{:S(2)}) collective-permute-start(bf16[128,1024]{1,0:T(8,128)(2,1)} %bitcast.121), channel_id=1, source_target_pairs={{0,2},{1,3},{2,0},{3,1},{4,6},{5,7},{6,4},{7,5},{8,10},{9,11},{10,... | collective-permute-start | bytes 786440 | tf_op jit(solution)/shard_map/ppermute | solution.py:42
  382.8 18.3 %collective-permute-start.81 = (bf16[128,1024]{1,0:T(8,128)(2,1)S(1)}, bf16[128,1024]{1,0:T(8,128)(2,1)S(1)}, u32[]{:S(2)}, u32[]{:S(2)}) collective-permute-start(bf16[128,1024]{1,0:T(8,128)(2,1)S(1)} %bitcast.305), channel_id=1, source_target_pairs={{0,1},{1,0},{2,3},{3,2},{4,5},{5,4},{6,7},{7,6},{8,9},{9,8},{10,11... | collective-permute-start | bytes 786440 | tf_op jit(solution)/shard_map/ppermute | solution.py:42
  384.3 16.9 %collective-permute-start.82 = (bf16[64,2048]{1,0:T(8,128)(2,1)S(1)}, bf16[64,2048]{1,0:T(8,128)(2,1)S(1)}, u32[]{:S(2)}, u32[]{:S(2)}) collective-permute-start(bf16[64,2048]{1,0:T(8,128)(2,1)S(1)} %bitcast.306), channel_id=1, source_target_pairs={{0,2},{1,3},{2,0},{3,1},{4,6},{5,7},{6,4},{7,5},{8,10},{9,11},{10,... | collective-permute-start | bytes 786440 | tf_op jit(solution)/shard_map/ppermute | solution.py:42
  (144 other events, 1362.5 us)

commit v4 on v3

--- a/solution.py
+++ b/solution.py
@@ -57,7 +57,7 @@
         in_specs=specs,
         out_specs=[VMEM] * len(outs),
         scratch_shapes=list(scratch),
-        compiler_params=pltpu.CompilerParams(vmem_limit_bytes=held + (8 << 20)),
+        compiler_params=pltpu.CompilerParams(vmem_limit_bytes=held + (3 << 20)),
         name=name,
     )(*operands)
 
@@ -74,23 +74,26 @@
     return keep, send
 
 
-def interleave_kernel(side, own, other, *outs):
-    each = own.shape[0] // len(outs)
-    for n, out in enumerate(outs):
-        part = pl.ds(n * each, each)
-        out[:, pl.ds(side[0], 1)] = own[part][:, None]
-        out[:, pl.ds(1 - side[0], 1)] = other[part][:, None]
-
-
-def interleave(own, other, bit, before, outs=1):
-    rows, n = own.shape
+def interleave_kernel(count, side, *refs):
+    owns, others, outs = refs[:count], refs[count : 2 * count], refs[2 * count :]
+    each = count * owns[0].shape[0] // len(outs)
+    for n, (own, other) in enumerate(zip(owns, others)):
+        for m in range(own.shape[0]):
+            out, at = outs[(n * own.shape[0] + m) // each], (n * own.shape[0] + m) % each
+            out[pl.ds(at, 1), pl.ds(side[0], 1)] = own[pl.ds(m, 1)][:, None]
+            out[pl.ds(at, 1), pl.ds(1 - side[0], 1)] = other[pl.ds(m, 1)][:, None]
+
+
+def interleave(owns, others, bit, before, outs=1):
+    rows, n = owns[0].shape
+    count = len(owns)
     shape = (before, rows // before, n)
-    whole = (before // outs, 2, rows // before, n)
+    whole = (count * before // outs, 2, rows // before, n)
     result = call(
-        interleave_kernel,
-        outs * [(whole, own.dtype)],
-        [mine(bit)[None], own.reshape(shape), other.reshape(shape)],
-        [SMEM, VMEM, VMEM],
+        partial(interleave_kernel, count),
+        outs * [(whole, owns[0].dtype)],
+        [mine(bit)[None], *(v.reshape(shape) for v in (*owns, *others))],
+        [SMEM] + [VMEM] * (2 * count),
         name="interleave",
     )
     return [part.reshape(-1, n) for part in result]
@@ -163,7 +166,7 @@
         *others, self.bit = self.steps.pop(0)
         for bit in others:
             other = self.sl.flip(self.value, bit)
-            self.value = interleave(self.value, other, bit, self.before(bit))[0]
+            self.value = interleave([self.value], [other], bit, self.before(bit))[0]
             self.have.append(bit)
         self.air = self.sl.flip(self.value, self.bit)
 
@@ -173,7 +176,7 @@
             self.quarters, self.value = [self.value, *air], None
             return
         last = (self.top_first or self.twins) and not self.steps
-        halves = interleave(self.value, air, self.bit, self.before(self.bit), 1 + last)
+        halves = interleave([self.value], [air], self.bit, self.before(self.bit), 1 + last)
         self.have.append(self.bit)
         if last and self.twins:
             self.value = halves
@@ -182,6 +185,13 @@
             self.value = None
         else:
             self.value = halves[0]
+
+    def join(self, other):
+        made = Gather(self.sl, None, self.lead, twins=True)
+        airs = self.air, other.air
+        made.value = interleave([self.value, other.value], airs, self.bit, self.before(self.bit))[0]
+        made.have, made.steps = self.have + [self.bit], self.steps
+        return made
 
     def part(self, n):
         made = Gather(self.sl, self.value[n], self.lead)
@@ -233,6 +243,7 @@
     def cross(self):
         own, top, core, both = self.quarters
         top_other = self.sl.flip(both, CORE)
+        core, _ = lax.optimization_barrier((core, top_other))
         core_other = self.sl.flip(core, CORE)
         rows, n = top.shape
         if not self.top_last:
@@ -306,7 +317,8 @@
         for name in names:
             del self.values[name]
 
-    def seal(self, *landing):
+    def seal(self, *landing, keep=()):
+        landing = [*keep, *landing]
         kept = (
             self.values,
             [(made.value, made.quarters) for made in self.flows],
@@ -315,8 +327,9 @@
         self.values, flown, airs = lax.optimization_barrier(kept)
         for made, (made.value, made.quarters) in zip(self.flows, flown):
             pass
-        for made, made.air in zip(landing, airs):
-            made.land()
+        for n, (made, made.air) in enumerate(zip(landing, airs)):
+            if n >= len(keep):
+                made.land()
 
 
 def dot(left, right):
@@ -652,22 +665,20 @@
     return jnp.stack(split(value, CORE, 3), 3).reshape(tokens, width)
 
 
-def finish_kernel(span, chunk, side, keep, other, out, *refs):
+def finish_kernel(span, chunk, part, side, keep, other, out, *refs):
     grad, new_m, step = refs[-3:]
     third = out.shape[-1]
-    total = grad.shape[-1] - 8 * third
-    pieces, (m, v) = [], refs[:2]
-    base, filled = 8 * third, 0
-    while 2 * filled < total:
-        one, two, *refs = refs
-        (m, v) = refs[:2]
-        pieces.append((one, two, base + 2 * filled, chunk))
-        filled += one.shape[1]
-    for one, two, base, width in [(keep, other, 0, span)] + pieces:
+    total = (grad.shape[-1] - 8 * third) // 2
+    late = total - (keep.shape[1] - part)
+    m, v = refs[2:4] if late else refs[:2]
+    pieces = [(keep, other, 0, 0, part, span), (keep, other, part, 8 * third + 2 * late, total - late, chunk)]
+    if late:
+        pieces.append((refs[0], refs[1], 0, 8 * third, late, chunk))
+    for one, two, first, base, count, width in pieces:
         for source, x in ((one, side[0]), (two, 1 - side[0])):
-            for n in range(source.shape[1] // width):
+            for n in range(count // width):
                 at = pl.multiple_of(base + (2 * n + x) * width, 128)
-                grad[0, :, pl.ds(at, width)] = source[:, pl.ds(n * width, width)]
+                grad[0, :, pl.ds(at, width)] = source[:, pl.ds(first + n * width, width)]
     for k in range(2):
         grad[0, :, pl.ds((6 + k) * third, third)] = out[k]
     for n in range(grad.shape[2] // 1024):
@@ -816,7 +827,7 @@
     live.drop("first")
     live.seal(attns[0], downs[0])
 
-    ups = [live.flow(Gather(sl, interleave(*live.up, SIDE, 1)[0], 2))]
+    ups = [live.flow(Gather(sl, interleave(live.up[:1], live.up[1:], SIDE, 1)[0], 2))]
     downs[0].start()
     attns[0].start()
     ups[0].start()
@@ -842,13 +853,22 @@
     live.drop("pack")
     live.seal(attns[0], ups[0], downs[0])
 
-    twins = live.flow(Gather(sl, live.own.reshape(4 * rows, -1), 2, twins=True))
+    own = live.own.reshape(2, 2 * rows, -1)
+    attns.append(live.flow(Gather(sl, own[0], 2)))
+    ups.append(live.flow(Gather(sl, own[1], 2)))
     live.drop("own")
     attns[0].start()
-    twins.start()
+    attns[1].start()
     ups[0].start()
     downs[0].finish()
-    live.seal(attns[0], ups[0], twins)
+    live.seal(attns[0], ups[0], attns[1])
+
+    def gate(*made):
+        airs = [flow.air for flow in made]
+        other, airs = lax.optimization_barrier((live.other, airs))
+        live.put(other=other)
+        for flow, flow.air in zip(made, airs):
+            pass
 
     def gains_of(quarters, sections):
         wide = norm_table.shape[1]
@@ -1046,19 +1066,21 @@
         )
         return live.flow(Scatter(sl, parts, 2))
 
-    def sides(flow, wide, columns):
-        value = flow.value.reshape(2, rows, wide)
-        keep, send = split(value[..., :columns], SIDE, 0)
-        return keep, sl.flip(send, SIDE), value[..., columns:]
-
-    def finish(layer, g_attn, g_ups, before):
-        keep, other, out = g_attn
+    def two_sides(flows, wides, counts):
+        values = [flow.value.reshape(2, rows, wide) for flow, wide in zip(flows, wides)]
+        both = jnp.concatenate([v[..., :n] for v, n in zip(values, counts)], -1)
+        keep, send = split(both, SIDE, 0)
+        return keep, sl.flip(send, SIDE), values[0][..., counts[0] :]
+
+    def finish(layer, big, before, more=None):
+        keep, other, out = big
+        more = [] if more is None else list(more[:2])
         return update(
-            partial(finish_kernel, 2 * block, 2 * fsdp * feeds),
+            partial(finish_kernel, 2 * block, 2 * fsdp * feeds, part),
             layer,
             w_big.shape,
-            [mine(SIDE)[None], keep, other, out, *itertools.chain(*g_ups)],
-            [SMEM] + [VMEM] * (3 + 2 * len(g_ups)),
+            [mine(SIDE)[None], keep, other, out, *more],
+            [SMEM] + [VMEM] * (3 + len(more)),
             [m_big, v_big],
             before,
             "finish",
@@ -1093,22 +1115,21 @@
         live.put(table=value)
 
     ups[0].start()
-    twins.start()
+    attns[1].start()
+    ups[1].start()
     attns[0].finish()
     live.put(gains=gains_of(attns[0].quarters, live.sections))
-    attend(0, live.hidden)
+    attend(0, live.hidden, 1)
     cross()
-    live.seal(ups[0], twins)
-
-    attns.append(live.flow(twins.part(0)))
-    ups.append(live.flow(twins.part(1)))
-    live.flows.remove(twins)
+    live.seal(ups[0], attns[1], ups[1])
+
     attns[1].start()
+    ups[1].start()
     downs[1].start()
     ups[0].finish()
-    feed_forward(0)
+    feed_forward(0, 1)
     cross()
-    live.seal(attns[1], downs[1])
+    live.seal(attns[1], ups[1], downs[1])
 
     ups[1].start()
     downs[1].start()
@@ -1121,15 +1142,15 @@
     downs[1].finish()
     live.put(grad=live.d_low.astype(f32))
     feed_turn(1)
+    live.seal()
+
+    cross()
+    g_up1 = up_grad(1)
+    g_up1.cross()
+    g_up1.start()
     g_down1 = down_grad(1, True)
     g_down1.cross()
     g_down1.start()
-    live.seal()
-
-    g_up1 = up_grad(1)
-    g_up1.cross()
-    g_up1.start()
-    cross()
     attend_back(1)
     live.seal(g_down1, g_up1)
 
@@ -1146,13 +1167,13 @@
     cross()
     g_down0.cross()
     g_down0.start()
-    g_down1.start()
+    g_up0b = up_grad(0, 1)
+    g_up0b.cross()
+    g_up0b.start()
     g_up1.start()
     g_attn1.start()
-    g_up0b = up_grad(0, 1)
-    g_up0b.cross()
     attend_back(0)
-    live.seal(g_down0, g_down1, g_up1, g_attn1)
+    live.seal(g_down0, g_up1, g_attn1, g_up0b)
 
     cross()
     g_attn0 = attend_grad(0)
@@ -1161,43 +1182,43 @@
     g_up0b.start()
     g_attn1.start()
     g_down0.start()
+    gate(g_up0b, g_attn1, g_down0)
+    norm_back(0, 0, live.attn0[0])
+    live.seal(g_attn0, g_attn1, g_down0, g_up0b)
+
     g_up0a = up_grad(0, 0)
-    norm_back(0, 0, live.attn0[0])
-    live.put(down=finish_down(1, g_down1, []), up1=sides(g_up1, feed // 2, feed // 2)[:2])
-    live.seal(g_attn0, g_attn1, g_down0, g_up0b)
-
     g_up0a.cross()
     g_up0a.start()
     g_attn0.start()
+    g_down0.start()
     g_up0b.start()
-    g_down0.start()
+    feed_down(1)
+    big1 = two_sides([g_attn1, g_up1], [2 * width, feed // 2], [part, feed // 2])
+    live.put(big=finish(1, big1, []))
     live.put(table=table_terms())
+    live.seal(g_up0a, g_attn0, g_down0, g_up0b)
+
+    g_up0a.start()
+    g_attn0.start()
+    g_down1.start()
+    cross()
     table_step(2, [CORE])
     table_step(1, [SIDE])
     table = live.table.reshape(*(len(sl.high) + len(sl.deep)) * [2], count, -1)
-    live.put(table=table)
-    attn1 = sides(g_attn1, 2 * width, part)
-    live.put(big=finish(1, attn1, [live.up1], []))
-    feed_down(1)
-    live.seal(g_up0a, g_attn0, g_up0b, g_down0)
+    live.put(table=table, down=finish_down(0, g_down0, []))
+    live.seal(g_up0a, g_attn0, g_down1)
 
     g_up0a.start()
-    g_attn0.start()
-    g_up0b.start()
-    cross()
     out_act = live.feed1[0][:length] + (live.keep[:length] + live.other[0][length:].astype(f32))
+    big0 = two_sides([g_attn0, g_up0b], [2 * width, feed // 4], [part, feed // 4])
     table_step(0, sl.high)
     table_step(-3, sl.deep[-1:])
-    live.put(out_act=out_act.astype(bf16), down=finish_down(0, g_down0, live.down))
-    live.seal(g_up0a, g_attn0, g_up0b)
-
-    g_up0a.start()
-    live.put(attn0=sides(g_attn0, 2 * width, part), up0b=sides(g_up0b, feed // 4, feed // 4)[:2])
+    live.put(out_act=out_act.astype(bf16), down=finish_down(1, g_down1, live.down), big0=big0)
     live.seal(g_up0a)
 
     table_step(0, sl.deep[:-1])
-    up0a = sides(g_up0a, feed // 4, feed // 4)[:2]
-    grad_big, new_m_big, step_big = finish(0, live.attn0, [up0a, live.up0b], live.big)
+    up0a = two_sides([g_up0a], [feed // 4], [feed // 4])
+    grad_big, new_m_big, step_big = finish(0, live.big0, live.big, up0a)
     grad_down, new_m_down, step_down = live.down
     grad_table = live.table
     new_m_table, step_table = adam_update(m_table, v_table, grad_table)

time: 429 us -> 409 us (0.953)
  local copies, waits for them, and re-layouts: 36.3 us -> 13.7 us
  waiting for transfers between devices: 192 us -> 202 us
    unnamed x207 -> x125, local copies, waits for them, and re-layouts: 30 us -> 10.7 us
    ppermute x89 -> x87, waiting for transfers between devices: 192 us -> 202 us  [flip(): lax.ppermute(value, axis, [(i, i ^ mask) for i in range(self.size[axis])])]
    ppermute x89 -> x87, starting transfers between devices: 83.3 us -> 79.9 us  [flip(): lax.ppermute(value, axis, [(i, i ^ mask) for i in range(self.size[axis])])]
    pallas_call x53 -> x55, Pallas kernels: 92.1 us -> 89.9 us  [call(): pl.pallas_call(kernel, out_shape=[jax.ShapeDtypeStruct(shape, kind) for s...]
  transfers between devices with their start and end apart: 89 -> 87, of which waited for: 41 -> 44; matrix products, arithmetic and copies ran while one was open for 4% -> 3% of each run, Pallas kernels for 19% -> 20%
where the time goes in v4:
time: 409 us; the launch traced here: 405 us
  waiting for transfers between devices  202 us (49%)
  Pallas kernels  97.4 us (24%)
  starting transfers between devices  79.9 us (20%)
  local copies, waits for them, and re-layouts  13.7 us (3%)
  other arithmetic  9.12 us (2%)
    ppermute x87, waiting for transfers between devices, flip(): lax.ppermute(value, axis, [(i, i ^ mask) for i in range(self.size[axis])])  202 us
    pallas_call x55, Pallas kernels, call(): pl.pallas_call(kernel, out_shape=[jax.ShapeDtypeStruct(shape, kind) for s...  89.9 us
    ppermute x87, starting transfers between devices, flip(): lax.ppermute(value, axis, [(i, i ^ mask) for i in range(self.size[axis])])  79.9 us
    unnamed x125, local copies, waits for them, and re-layouts  10.7 us
  transfers between devices with their start and end apart: 87, of which 44 were waited for; matrix products, arithmetic and copies ran while one was open for 3% of the time, Pallas kernels for 20%

profile of v4, /device:TPU:0, one launch (start us, length us, event | category | flops | bytes accessed | tf_op | source)
XLA Modules:
  0.0 405.0 jit_solution(7774444614624617107)
XLA Ops:
  1.9 3.0 collective-permute-start.2
  4.9 2.6 collective-permute-start.1
  13.1 6.1 %collective-permute-done.1 = bf16[128,1024]{1,0:T(8,128)(2,1)S(1)} collective-permute-done((bf16[128,1024]{1,0:T(8,128)(2,1)S(1)}, bf16[128,1024]{1,0:T(8,128)(2,1)S(1)}, u32[]{:S(2)}, u32[]{:S(2)}) %collective-permute-start.1) | collective-permute-done | bytes 262176 | tf_op jit(solution)/shard_map/ppermute | solution.py:42
  20.0 3.4 collective-permute-start.6
  26.3 7.6 %collective-permute-done.5 = bf16[32,2048]{1,0:T(8,128)(2,1)S(1)} collective-permute-done((bf16[32,2048]{1,0:T(8,128)(2,1)S(1)}, bf16[32,2048]{1,0:T(8,128)(2,1)S(1)}, u32[]{:S(2)}, u32[]{:S(2)}) %collective-permute-start.5) | collective-permute-done | bytes 131104 | tf_op jit(solution)/shard_map/ppermute | solution.py:42
  33.9 3.4 collective-permute-done.6
  38.8 2.7 collective-permute-start.9
  41.6 2.5 collective-permute-start.8
  48.0 5.8 %collective-permute-done.9 = bf16[64,2048]{1,0:T(8,128)(2,1)S(1)} collective-permute-done((bf16[64,2048]{1,0:T(8,128)(2,1)S(1)}, bf16[64,2048]{1,0:T(8,128)(2,1)S(1)}, u32[]{:S(2)}, u32[]{:S(2)}) %collective-permute-start.9) | collective-permute-done | bytes 262176 | tf_op jit(solution)/shard_map/ppermute | solution.py:42
  53.9 6.2 %collective-permute-done.8 = bf16[128,2176]{1,0:T(8,128)(2,1)S(1)} collective-permute-done((bf16[128,2176]{1,0:T(8,128)(2,1)S(1)}, bf16[128,2176]{1,0:T(8,128)(2,1)S(1)}, u32[]{:S(2)}, u32[]{:S(2)}) %collective-permute-start.8) | collective-permute-done | bytes 557088 | tf_op jit(solution)/shard_map/ppermute | solution.py:42
  60.1 3.7 collective-permute-done.10.refs_9_
  64.8 3.5 collective-permute-start.15
  71.4 14.3 %collective-permute-done.16 = bf16[64,2048]{1,0:T(8,128)(2,1)S(1)} collective-permute-done((bf16[64,2048]{1,0:T(8,128)(2,1)S(1)}, bf16[64,2048]{1,0:T(8,128)(2,1)S(1)}, u32[]{:S(2)}, u32[]{:S(2)}) %collective-permute-start.16) | collective-permute-done | bytes 262176 | tf_op jit(solution)/shard_map/ppermute | solution.py:42
  87.4 3.6 collective-permute-done.13.q1.refs_3_.refs_4_
  95.1 3.5 collective-permute-start.21
  100.1 9.3 %attend.2 = (f32[256,1024]{1,0:T(8,128)}, bf16[256,1024]{1,0:T(8,128)(2,1)S(1)}, bf16[256,1536]{1,0:T(8,128)(2,1)S(1)}, bf16[256,512]{1,0:T(8,128)(2,1)S(1)}, f3...) custom-call(s32[2]{0:T(128)S(1)} %pad_add_fusion.place.up_place.dn_place, ...), custom_call_target="tpu_custom_call" | custom-call | tf_op jit(solution)/shard_map/attend/pallas_call | solution.py:54
  112.8 11.9 %collective-permute-done.22 = bf16[64,2048]{1,0:T(8,128)(2,1)S(1)} collective-permute-done((bf16[64,2048]{1,0:T(8,128)(2,1)S(1)}, bf16[64,2048]{1,0:T(8,128)(2,1)S(1)}, u32[]{:S(2)}, u32[]{:S(2)}) %collective-permute-start.22) | collective-permute-done | bytes 262176 | tf_op jit(solution)/shard_map/ppermute | solution.py:42
  127.1 2.3 collective-permute-start.28
  129.4 5.5 %feed.1 = (f32[256,1024]{1,0:T(8,128)S(1)}, bf16[256,1024]{1,0:T(8,128)(2,1)S(1)}, f32[256,2048]{1,0:T(8,128)S(1)}, bf16[256,2048]{1,0:T(8,128)(2,1)S(1)}, f32[2...) custom-call(s32[2]{0:T(128)S(1)} %pad_add_fusion.place.up_place.dn_place, s32[2]{0:T(128)S(1)} %pad_add_fusion.place.up_place.dn_place, ...), custom_call_target="tpu_custom_call" | custom-call | tf_op jit(solution)/shard_map/feed/pallas_call | solution.py:54
  135.5 15.5 %collective-permute-done.27 = bf16[128,2048]{1,0:T(8,128)(2,1)S(1)} collective-permute-done((bf16[128,2048]{1,0:T(8,128)(2,1)S(1)}, bf16[128,2048]{1,0:T(8,128)(2,1)S(1)}, u32[]{:S(2)}, u32[]{:S(2)}) %collective-permute-start.27) | collective-permute-done | bytes 524320 | tf_op jit(solution)/shard_map/ppermute | solution.py:42
  155.7 8.1 %attend.3 = (f32[256,1024]{1,0:T(8,128)S(1)}, bf16[256,1024]{1,0:T(8,128)(2,1)S(1)}, bf16[256,1536]{1,0:T(8,128)(2,1)S(1)}, bf16[256,512]{1,0:T(8,128)(2,1)S(1)}...) custom-call(s32[2]{0:T(128)S(1)} %pad_add_fusion.place.up_place.dn_place, ...), custom_call_target="tpu_custom_call" | custom-call | tf_op jit(solution)/shard_map/attend/pallas_call | solution.py:54
  166.0 12.8 %collective-permute-done.32.refs_7_ = bf16[256,2048]{1,0:T(8,128)(2,1)S(1)} collective-permute-done((bf16[256,2048]{1,0:T(8,128)(2,1)S(1)}, bf16[256,2048]{1,0:T(8,128)(2,1)S(1)}, u32[]{:S(2)}, u32[]{:S(2)}) %collective-permute-start.32) | collective-permute-done | bytes 1048608 | tf_op jit(solution)/shard_map/ppermute | solution.py:42
  184.8 6.7 %feed_turn.1 = (f32[256,1024]{1,0:T(8,128)S(1)}, bf16[256,1024]{1,0:T(8,128)(2,1)S(1)}, bf16[256,2048]{1,0:T(8,128)(2,1)S(1)}, bf16[256,2048]{1,0:T(8,128)(2,1)S...) custom-call(s32[2]{0:T(128)S(1)} %pad_add_fusion.place.up_place.dn_place, ...), custom_call_target="tpu_custom_call" | custom-call | tf_op jit(solution)/shard_map/feed_turn/pallas_call | solution.py:54
  203.2 7.2 %collective-permute-done.38.refs_0_ = bf16[128,1024]{1,0:T(8,128)(2,1)S(1)} collective-permute-done((bf16[128,1024]{1,0:T(8,128)(2,1)S(1)}, bf16[128,1024]{1,0:T(8,128)(2,1)S(1)}, u32[]{:S(2)}, u32[]{:S(2)}) %collective-permute-start.38) | collective-permute-done | bytes 262176 | tf_op jit(solution)/shard_map/ppermute | solution.py:42
  210.4 4.3 %collective-permute-done.39.refs_1_ = bf16[128,1024]{1,0:T(8,128)(2,1)S(1)} collective-permute-done((bf16[128,1024]{1,0:T(8,128)(2,1)S(1)}, bf16[128,1024]{1,0:T(8,128)(2,1)S(1)}, u32[]{:S(2)}, u32[]{:S(2)}) %collective-permute-start.39) | collective-permute-done | bytes 262176 | tf_op jit(solution)/shard_map/ppermute | solution.py:42
  214.7 10.1 %attend_back.2 = (f32[256,1024]{1,0:T(8,128)S(1)}, bf16[256,1024]{1,0:T(8,128)(2,1)S(1)}, f32[1,1024]{1,0:T(1,128)S(1)}, f32[1,1024]{1,0:T(1,128)S(1)}, bf16[256...) custom-call(s32[2]{0:T(128)S(1)} %pad_add_fusion.place.up_place.dn_place, ...), custom_call_target="tpu_custom_call" | custom-call | tf_op jit(solution)/shard_map/attend_back/pallas_call | solution.py:54
  227.8 2.6 collective-permute-done.47.two
  235.9 10.2 %collective-permute-done.46.refs_0_ = bf16[256,1024]{1,0:T(8,128)(2,1)S(1)} collective-permute-done((bf16[256,1024]{1,0:T(8,128)(2,1)S(1)}, bf16[256,1024]{1,0:T(8,128)(2,1)S(1)}, u32[]{:S(2)}, u32[]{:S(2)}) %collective-permute-start.46) | collective-permute-done | bytes 524320 | tf_op jit(solution)/shard_map/ppermute | solution.py:42
  246.1 6.0 %feed_back.1 = (f32[256,1024]{1,0:T(8,128)S(1)}, bf16[256,1024]{1,0:T(8,128)(2,1)S(1)}, f32[1,1024]{1,0:T(1,128)S(1)}, f32[1,1024]{1,0:T(1,128)S(1)}, bf16[256,2...) custom-call(s32[2]{0:T(128)S(1)} %pad_add_fusion.place.up_place.dn_place, ...), custom_call_target="tpu_custom_call" | custom-call | tf_op jit(solution)/shard_map/feed_back/pallas_call | solution.py:54
  254.0 3.0 collective-permute-done.50
  257.0 2.7 collective-permute-done.49
  269.8 8.8 %collective-permute-done.52.refs_0_ = bf16[256,1024]{1,0:T(8,128)(2,1)S(1)} collective-permute-done((bf16[256,1024]{1,0:T(8,128)(2,1)S(1)}, bf16[256,1024]{1,0:T(8,128)(2,1)S(1)}, u32[]{:S(2)}, u32[]{:S(2)}) %collective-permute-start.52) | collective-permute-done | bytes 524320 | tf_op jit(solution)/shard_map/ppermute | solution.py:42
  278.8 11.7 %attend_back.3 = (f32[256,1024]{1,0:T(8,128)S(1)}, bf16[256,1024]{1,0:T(8,128)(2,1)S(1)}, f32[1,1024]{1,0:T(1,128)S(1)}, f32[1,1024]{1,0:T(1,128)S(1)}, bf16[256...) custom-call(s32[2]{0:T(128)S(1)} %pad_add_fusion.place.up_place.dn_place, ...), custom_call_target="tpu_custom_call" | custom-call | tf_op jit(solution)/shard_map/attend_back/pallas_call | solution.py:54
  290.6 4.4 %collective-permute-done.58 = bf16[64,2048]{1,0:T(8,128)(2,1)S(1)} collective-permute-done((bf16[64,2048]{1,0:T(8,128)(2,1)S(1)}, bf16[64,2048]{1,0:T(8,128)(2,1)S(1)}, u32[]{:S(2)}, u32[]{:S(2)}) %collective-permute-start.58) | collective-permute-done | bytes 262176 | tf_op jit(solution)/shard_map/ppermute | solution.py:42
  294.9 2.2 collective-permute-done.60
  297.1 2.5 attend_grad.3
  299.7 2.7 collective-permute-done.65.two
  313.0 8.2 %collective-permute-done.62 = bf16[128,1024]{1,0:T(8,128)(2,1)} collective-permute-done((bf16[128,1024]{1,0:T(8,128)(2,1)}, bf16[128,1024]{1,0:T(8,128)(2,1)}, u32[]{:S(2)}, u32[]{:S(2)}) %collective-permute-start.62) | collective-permute-done | bytes 262176 | tf_op jit(solution)/shard_map/ppermute | solution.py:42
  322.2 13.6 %collective-permute-done.63 = bf16[64,2048]{1,0:T(8,128)(2,1)S(1)} collective-permute-done((bf16[64,2048]{1,0:T(8,128)(2,1)S(1)}, bf16[64,2048]{1,0:T(8,128)(2,1)S(1)}, u32[]{:S(2)}, u32[]{:S(2)}) %collective-permute-start.63) | collective-permute-done | bytes 262176 | tf_op jit(solution)/shard_map/ppermute | solution.py:42
  335.9 2.8 norm_back.1
  349.7 2.4 down.1
  355.0 2.4 finish.2
  357.4 7.5 %collective-permute-done.74 = bf16[64,1024]{1,0:T(8,128)(2,1)S(1)} collective-permute-done((bf16[64,1024]{1,0:T(8,128)(2,1)S(1)}, bf16[64,1024]{1,0:T(8,128)(2,1)S(1)}, u32[]{:S(2)}, u32[]{:S(2)}) %collective-permute-start.74) | collective-permute-done | bytes 131104 | tf_op jit(solution)/shard_map/ppermute | solution.py:42
  366.8 2.9 collective-permute-start.79
  373.4 10.6 %collective-permute-done.77 = f32[2,4,9,128]{3,1,2,0:T(4,128)S(1)} collective-permute-done((f32[2,4,9,128]{3,1,2,0:T(4,128)S(1)}, f32[2,4,9,128]{3,1,2,0:T(4,128)S(1)}, u32[]{:S(2)}, u32[]{:S(2)}) %collective-permute-start.77) | collective-permute-done | bytes 36896 | tf_op jit(solution)/shard_map/ppermute | solution.py:42
  394.3 2.3 collective-permute-start.86
  399.5 2.9 collective-permute-done.85.refs_1_
  402.4 2.4 finish.3
  (366 shorter events, 121.8 us)
Async XLA Ops:
  12.4 24.8 %collective-permute-start.4 = (bf16[272,1024]{1,0:T(8,128)(2,1)}, bf16[272,1024]{1,0:T(8,128)(2,1)}, u32[]{:S(2)}, u32[]{:S(2)}) collective-permute-start(bf16[272,1024]{1,0:T(8,128)(2,1)} %pad_maximum_fusion), channel_id=1, source_target_pairs={{0,8},{4,12},{8,0},{12,4},{16,24},{20,28},{24,16},{28,20},{1,9},{5... | collective-permute-start | bytes 1671176 | tf_op jit(solution)/shard_map/ppermute | solution.py:42
  19.2 18.8 %collective-permute-start.7 = (bf16[256,1024]{1,0:T(8,128)(2,1)S(1)}, bf16[256,1024]{1,0:T(8,128)(2,1)S(1)}, u32[]{:S(2)}, u32[]{:S(2)}) collective-permute-start(bf16[256,1024]{1,0:T(8,128)(2,1)S(1)} %bitcast.228), channel_id=1, source_target_pairs={{0,1},{1,0},{2,3},{3,2},{4,5},{5,4},{6,7},{7,6},{8,9},{9,8},{10,11... | collective-permute-start | bytes 1572872 | tf_op jit(solution)/shard_map/ppermute | solution.py:42
  20.0 17.3 %collective-permute-start.6 = (bf16[64,2176]{1,0:T(8,128)(2,1)S(1)}, bf16[64,2176]{1,0:T(8,128)(2,1)S(1)}, u32[]{:S(2)}, u32[]{:S(2)}) collective-permute-start(bf16[64,2176]{1,0:T(8,128)(2,1)S(1)} %bitcast.236), channel_id=1, source_target_pairs={{0,2},{1,3},{2,0},{3,1},{4,6},{5,7},{6,4},{7,5},{8,10},{9,11},{10,... | collective-permute-start | bytes 835592 | tf_op jit(solution)/shard_map/ppermute | solution.py:42
  38.1 22.0 %collective-permute-start.11 = (bf16[512,1024]{1,0:T(8,128)(2,1)S(1)}, bf16[512,1024]{1,0:T(8,128)(2,1)S(1)}, u32[]{:S(2)}, u32[]{:S(2)}) collective-permute-start(bf16[512,1024]{1,0:T(8,128)(2,1)S(1)} %bitcast.202), channel_id=1, source_target_pairs={{0,4},{4,0},{8,12},{12,8},{16,20},{20,16},{24,28},{28,24},{1,5},{5... | collective-permute-start | bytes 3145736 | tf_op jit(solution)/shard_map/ppermute | solution.py:42
  38.2 25.6 %collective-permute-start.10 = (bf16[512,1024]{1,0:T(8,128)(2,1)S(1)}, bf16[512,1024]{1,0:T(8,128)(2,1)S(1)}, u32[]{:S(2)}, u32[]{:S(2)}) collective-permute-start(bf16[512,1024]{1,0:T(8,128)(2,1)S(1)} %bitcast.203), channel_id=1, source_target_pairs={{0,16},{4,20},{8,24},{12,28},{16,0},{20,4},{24,8},{28,12},{1,17},{... | collective-permute-start | bytes 3145736 | tf_op jit(solution)/shard_map/ppermute | solution.py:42
  38.8 15.1 %collective-permute-start.9 = (bf16[64,2048]{1,0:T(8,128)(2,1)S(1)}, bf16[64,2048]{1,0:T(8,128)(2,1)S(1)}, u32[]{:S(2)}, u32[]{:S(2)}) collective-permute-start(bf16[64,2048]{1,0:T(8,128)(2,1)S(1)} %bitcast.253), channel_id=1, source_target_pairs={{0,2},{1,3},{2,0},{3,1},{4,6},{5,7},{6,4},{7,5},{8,10},{9,11},{10,... | collective-permute-start | bytes 786440 | tf_op jit(solution)/shard_map/ppermute | solution.py:42
  41.6 18.5 %collective-permute-start.8 = (bf16[128,2176]{1,0:T(8,128)(2,1)S(1)}, bf16[128,2176]{1,0:T(8,128)(2,1)S(1)}, u32[]{:S(2)}, u32[]{:S(2)}) collective-permute-start(bf16[128,2176]{1,0:T(8,128)(2,1)S(1)} %bitcast.224), channel_id=1, source_target_pairs={{0,1},{1,0},{2,3},{3,2},{4,5},{5,4},{6,7},{7,6},{8,9},{9,8},{10,11... | collective-permute-start | bytes 1671176 | tf_op jit(solution)/shard_map/ppermute | solution.py:42
  63.9 23.6 %collective-permute-start.14 = (bf16[256,2176]{1,0:T(8,128)(2,1)S(1)}, bf16[256,2176]{1,0:T(8,128)(2,1)S(1)}, u32[]{:S(2)}, u32[]{:S(2)}) collective-permute-start(bf16[256,2176]{1,0:T(8,128)(2,1)S(1)} %bitcast.197), channel_id=1, source_target_pairs={{0,4},{4,0},{8,12},{12,8},{16,20},{20,16},{24,28},{28,24},{1,5},{5... | collective-permute-start | bytes 3342344 | tf_op jit(solution)/shard_map/ppermute | solution.py:42
  63.9 27.1 %collective-permute-start.13 = (bf16[256,2176]{1,0:T(8,128)(2,1)S(1)}, bf16[256,2176]{1,0:T(8,128)(2,1)}, u32[]{:S(2)}, u32[]{:S(2)}) collective-permute-start(bf16[256,2176]{1,0:T(8,128)(2,1)S(1)} %bitcast.198), channel_id=1, source_target_pairs={{0,16},{4,20},{8,24},{12,28},{16,0},{20,4},{24,8},{28,12},{1,17},{... | collective-permute-start | bytes 3342344 | tf_op jit(solution)/shard_map/ppermute | solution.py:42
  64.7 21.7 %collective-permute-start.12 = (bf16[512,1024]{1,0:T(8,128)(2,1)S(1)}, bf16[512,1024]{1,0:T(8,128)(2,1)S(1)}, u32[]{:S(2)}, u32[]{:S(2)}) collective-permute-start(bf16[512,1024]{1,0:T(8,128)(2,1)S(1)} %collective-permute-done.10.refs_9_), channel_id=1, source_target_pairs={{0,4},{4,0},{8,12},{12,8},{16,20},{20,16},{24,28},{28,24},{1,5},{5... | collective-permute-start | bytes 3145736 | tf_op jit(solution)/shard_map/ppermute | solution.py:42
  64.8 21.7 %collective-permute-start.15 = (bf16[128,2048]{1,0:T(8,128)(2,1)S(1)}, bf16[128,2048]{1,0:T(8,128)(2,1)S(1)}, u32[]{:S(2)}, u32[]{:S(2)}) collective-permute-start(bf16[128,2048]{1,0:T(8,128)(2,1)S(1)} %bitcast.234), channel_id=1, source_target_pairs={{0,1},{1,0},{2,3},{3,2},{4,5},{5,4},{6,7},{7,6},{8,9},{9,8},{10,11... | collective-permute-start | bytes 1572872 | tf_op jit(solution)/shard_map/ppermute | solution.py:42
  69.0 16.7 %collective-permute-start.16 = (bf16[64,2048]{1,0:T(8,128)(2,1)S(1)}, bf16[64,2048]{1,0:T(8,128)(2,1)S(1)}, u32[]{:S(2)}, u32[]{:S(2)}) collective-permute-start(bf16[64,2048]{1,0:T(8,128)(2,1)S(1)} %bitcast.258), channel_id=1, source_target_pairs={{0,2},{1,3},{2,0},{3,1},{4,6},{5,7},{6,4},{7,5},{8,10},{9,11},{10,... | collective-permute-start | bytes 786440 | tf_op jit(solution)/shard_map/ppermute | solution.py:42
  92.1 32.6 %collective-permute-start.20 = (bf16[256,2048]{1,0:T(8,128)(2,1)}, bf16[256,2048]{1,0:T(8,128)(2,1)}, u32[]{:S(2)}, u32[]{:S(2)}) collective-permute-start(bf16[256,2048]{1,0:T(8,128)(2,1)} %bitcast.46.refs_4_), channel_id=1, source_target_pairs={{0,4},{4,0},{8,12},{12,8},{16,20},{20,16},{24,28},{28,24},{1,5},{5... | collective-permute-start | bytes 3145736 | tf_op jit(solution)/shard_map/ppermute | solution.py:42
  92.6 32.1 %collective-permute-start.19 = (bf16[256,2048]{1,0:T(8,128)(2,1)}, bf16[256,2048]{1,0:T(8,128)(2,1)}, u32[]{:S(2)}, u32[]{:S(2)}) collective-permute-start(bf16[256,2048]{1,0:T(8,128)(2,1)} %bitcast.46.refs_4_), channel_id=1, source_target_pairs={{0,16},{4,20},{8,24},{12,28},{16,0},{20,4},{24,8},{28,12},{1,17},{... | collective-permute-start | bytes 3145736 | tf_op jit(solution)/shard_map/ppermute | solution.py:42
  95.1 29.6 %collective-permute-start.21 = (bf16[128,2048]{1,0:T(8,128)(2,1)S(1)}, bf16[128,2048]{1,0:T(8,128)(2,1)S(1)}, u32[]{:S(2)}, u32[]{:S(2)}) collective-permute-start(bf16[128,2048]{1,0:T(8,128)(2,1)S(1)} %bitcast.230), channel_id=1, source_target_pairs={{0,1},{1,0},{2,3},{3,2},{4,5},{5,4},{6,7},{7,6},{8,9},{9,8},{10,11... | collective-permute-start | bytes 1572872 | tf_op jit(solution)/shard_map/ppermute | solution.py:42
  109.5 15.2 %collective-permute-start.18 = (bf16[256,1024]{1,0:T(8,128)(2,1)S(1)}, bf16[256,1024]{1,0:T(8,128)(2,1)S(1)}, u32[]{:S(2)}, u32[]{:S(2)}) collective-permute-start(bf16[256,1024]{1,0:T(8,128)(2,1)S(1)} %get-tuple-element.625), channel_id=1, source_target_pairs={{0,8},{4,12},{8,0},{12,4},{16,24},{20,28},{24,16},{28,20},{1,9},{5... | collective-permute-start | bytes 1572872 | tf_op jit(solution)/shard_map/ppermute | solution.py:42
  124.9 28.0 %collective-permute-start.26 = (bf16[256,2048]{1,0:T(8,128)(2,1)S(1)}, bf16[256,2048]{1,0:T(8,128)(2,1)S(1)}, u32[]{:S(2)}, u32[]{:S(2)}) collective-permute-start(bf16[256,2048]{1,0:T(8,128)(2,1)S(1)} %bitcast.206), channel_id=1, source_target_pairs={{0,4},{4,0},{8,12},{12,8},{16,20},{20,16},{24,28},{28,24},{1,5},{5... | collective-permute-start | bytes 3145736 | tf_op jit(solution)/shard_map/ppermute | solution.py:42
  125.4 27.5 %collective-permute-start.25 = (bf16[256,2048]{1,0:T(8,128)(2,1)S(1)}, bf16[256,2048]{1,0:T(8,128)(2,1)S(1)}, u32[]{:S(2)}, u32[]{:S(2)}) collective-permute-start(bf16[256,2048]{1,0:T(8,128)(2,1)S(1)} %bitcast.207), channel_id=1, source_target_pairs={{0,16},{4,20},{8,24},{12,28},{16,0},{20,4},{24,8},{28,12},{1,17},{... | collective-permute-start | bytes 3145736 | tf_op jit(solution)/shard_map/ppermute | solution.py:42
  127.0 24.0 %collective-permute-start.27 = (bf16[128,2048]{1,0:T(8,128)(2,1)S(1)}, bf16[128,2048]{1,0:T(8,128)(2,1)S(1)}, u32[]{:S(2)}, u32[]{:S(2)}) collective-permute-start(bf16[128,2048]{1,0:T(8,128)(2,1)S(1)} %bitcast.232), channel_id=1, source_target_pairs={{0,1},{1,0},{2,3},{3,2},{4,5},{5,4},{6,7},{7,6},{8,9},{9,8},{10,11... | collective-permute-start | bytes 1572872 | tf_op jit(solution)/shard_map/ppermute | solution.py:42
  127.1 25.9 %collective-permute-start.28 = (bf16[256,1024]{1,0:T(8,128)(2,1)S(1)}, bf16[256,1024]{1,0:T(8,128)(2,1)S(1)}, u32[]{:S(2)}, u32[]{:S(2)}) collective-permute-start(bf16[256,1024]{1,0:T(8,128)(2,1)S(1)} %bitcast.226), channel_id=1, source_target_pairs={{0,2},{1,3},{2,0},{3,1},{4,6},{5,7},{6,4},{7,5},{8,10},{9,11},{10,... | collective-permute-start | bytes 1572872 | tf_op jit(solution)/shard_map/ppermute | solution.py:42
  134.9 18.1 %collective-permute-start.24 = (bf16[256,1024]{1,0:T(8,128)(2,1)S(1)}, bf16[256,1024]{1,0:T(8,128)(2,1)S(1)}, u32[]{:S(2)}, u32[]{:S(2)}) collective-permute-start(bf16[256,1024]{1,0:T(8,128)(2,1)S(1)} %get-tuple-element.659), channel_id=1, source_target_pairs={{0,8},{4,12},{8,0},{12,4},{16,24},{20,28},{24,16},{28,20},{1,9},{5... | collective-permute-start | bytes 1572872 | tf_op jit(solution)/shard_map/ppermute | solution.py:42
  153.7 25.1 %collective-permute-start.32 = (bf16[256,2048]{1,0:T(8,128)(2,1)S(1)}, bf16[256,2048]{1,0:T(8,128)(2,1)S(1)}, u32[]{:S(2)}, u32[]{:S(2)}) collective-permute-start(bf16[256,2048]{1,0:T(8,128)(2,1)S(1)} %bitcast.214), channel_id=1, source_target_pairs={{0,16},{4,20},{8,24},{12,28},{16,0},{20,4},{24,8},{28,12},{1,17},{... | collective-permute-start | bytes 3145736 | tf_op jit(solution)/shard_map/ppermute | solution.py:42
  154.3 24.9 %collective-permute-start.34 = (bf16[512,1024]{1,0:T(8,128)(2,1)S(1)}, bf16[512,1024]{1,0:T(8,128)(2,1)S(1)}, u32[]{:S(2)}, u32[]{:S(2)}) collective-permute-start(bf16[512,1024]{1,0:T(8,128)(2,1)S(1)} %bitcast.216), channel_id=1, source_target_pairs={{0,1},{1,0},{2,3},{3,2},{4,5},{5,4},{6,7},{7,6},{8,9},{9,8},{10,11... | collective-permute-start | bytes 3145736 | tf_op jit(solution)/shard_map/ppermute | solution.py:42
  163.8 15.3 %collective-permute-start.30 = (bf16[128,1024]{1,0:T(8,128)(2,1)S(1)}, bf16[128,1024]{1,0:T(8,128)(2,1)S(1)}, u32[]{:S(2)}, u32[]{:S(2)}) collective-permute-start(bf16[128,1024]{1,0:T(8,128)(2,1)S(1)} %get-tuple-element.692), channel_id=1, source_target_pairs={{0,8},{4,12},{8,0},{12,4},{16,24},{20,28},{24,16},{28,20},{1,9},{5... | collective-permute-start | bytes 786440 | tf_op jit(solution)/shard_map/ppermute | solution.py:42
  198.2 26.6 %collective-permute-start.41 = (bf16[256,2048]{1,0:T(8,128)(2,1)S(1)}, bf16[256,2048]{1,0:T(8,128)(2,1)S(1)}, u32[]{:S(2)}, u32[]{:S(2)}) collective-permute-start(bf16[256,2048]{1,0:T(8,128)(2,1)S(1)} %get-tuple-element.814), channel_id=1, source_target_pairs={{0,4},{4,0},{8,12},{12,8},{16,20},{20,16},{24,28},{28,24},{1,5},{5... | collective-permute-start | bytes 3145736 | tf_op jit(solution)/shard_map/ppermute | solution.py:42
  198.8 26.0 %collective-permute-start.45 = (bf16[256,2048]{1,0:T(8,128)(2,1)S(1)}, bf16[256,2048]{1,0:T(8,128)(2,1)S(1)}, u32[]{:S(2)}, u32[]{:S(2)}) collective-permute-start(bf16[256,2048]{1,0:T(8,128)(2,1)S(1)} %add_low.5), channel_id=1, source_target_pairs={{0,16},{4,20},{8,24},{12,28},{16,0},{20,4},{24,8},{28,12},{1,17},{... | collective-permute-start | bytes 3145736 | tf_op jit(solution)/shard_map/ppermute | solution.py:42
  200.9 25.0 %collective-permute-start.44 = (bf16[512,1024]{1,0:T(8,128)(2,1)S(1)}, bf16[512,1024]{1,0:T(8,128)(2,1)S(1)}, u32[]{:S(2)}, u32[]{:S(2)}) collective-permute-start(bf16[512,1024]{1,0:T(8,128)(2,1)S(1)} %bitcast.301), channel_id=1, source_target_pairs={{0,1},{1,0},{2,3},{3,2},{4,5},{5,4},{6,7},{7,6},{8,9},{9,8},{10,11... | collective-permute-start | bytes 3145736 | tf_op jit(solution)/shard_map/ppermute | solution.py:42
  230.4 29.3 %collective-permute-start.48 = (bf16[256,2048]{1,0:T(8,128)(2,1)S(1)}, bf16[256,2048]{1,0:T(8,128)(2,1)S(1)}, u32[]{:S(2)}, u32[]{:S(2)}) collective-permute-start(bf16[256,2048]{1,0:T(8,128)(2,1)S(1)} %get-tuple-element.881), channel_id=1, source_target_pairs={{0,4},{4,0},{8,12},{12,8},{16,20},{20,16},{24,28},{28,24},{1,5},{5... | collective-permute-start | bytes 3145736 | tf_op jit(solution)/shard_map/ppermute | solution.py:42
  230.8 28.9 %collective-permute-start.51 = (bf16[256,2048]{1,0:T(8,128)(2,1)S(1)}, bf16[256,2048]{1,0:T(8,128)(2,1)S(1)}, u32[]{:S(2)}, u32[]{:S(2)}) collective-permute-start(bf16[256,2048]{1,0:T(8,128)(2,1)S(1)} %add_low.6), channel_id=1, source_target_pairs={{0,16},{4,20},{8,24},{12,28},{16,0},{20,4},{24,8},{28,12},{1,17},{... | collective-permute-start | bytes 3145736 | tf_op jit(solution)/shard_map/ppermute | solution.py:42
  233.1 23.9 %collective-permute-start.50 = (bf16[128,2048]{1,0:T(8,128)(2,1)S(1)}, bf16[128,2048]{1,0:T(8,128)(2,1)S(1)}, u32[]{:S(2)}, u32[]{:S(2)}) collective-permute-start(bf16[128,2048]{1,0:T(8,128)(2,1)S(1)} %bitcast.305), channel_id=1, source_target_pairs={{0,1},{1,0},{2,3},{3,2},{4,5},{5,4},{6,7},{7,6},{8,9},{9,8},{10,11... | collective-permute-start | bytes 1572872 | tf_op jit(solution)/shard_map/ppermute | solution.py:42
  234.1 25.6 %collective-permute-start.49 = (bf16[256,1024]{1,0:T(8,128)(2,1)S(1)}, bf16[256,1024]{1,0:T(8,128)(2,1)S(1)}, u32[]{:S(2)}, u32[]{:S(2)}) collective-permute-start(bf16[256,1024]{1,0:T(8,128)(2,1)S(1)} %bitcast.306), channel_id=1, source_target_pairs={{0,2},{1,3},{2,0},{3,1},{4,6},{5,7},{6,4},{7,5},{8,10},{9,11},{10,... | collective-permute-start | bytes 1572872 | tf_op jit(solution)/shard_map/ppermute | solution.py:42
  263.6 33.6 %collective-permute-start.54 = (bf16[512,1024]{1,0:T(8,128)(2,1)S(1)}, bf16[512,1024]{1,0:T(8,128)(2,1)S(1)}, u32[]{:S(2)}, u32[]{:S(2)}) collective-permute-start(bf16[512,1024]{1,0:T(8,128)(2,1)S(1)} %get-tuple-element.934), channel_id=1, source_target_pairs={{0,4},{4,0},{8,12},{12,8},{16,20},{20,16},{24,28},{28,24},{1,5},{5... | collective-permute-start | bytes 3145736 | tf_op jit(solution)/shard_map/ppermute | solution.py:42
  263.9 33.2 %collective-permute-start.57 = (bf16[512,1024]{1,0:T(8,128)(2,1)S(1)}, bf16[512,1024]{1,0:T(8,128)(2,1)S(1)}, u32[]{:S(2)}, u32[]{:S(2)}) collective-permute-start(bf16[512,1024]{1,0:T(8,128)(2,1)S(1)} %add_low.7), channel_id=1, source_target_pairs={{0,16},{4,20},{8,24},{12,28},{16,0},{20,4},{24,8},{28,12},{1,17},{... | collective-permute-start | bytes 3145736 | tf_op jit(solution)/shard_map/ppermute | solution.py:42
  266.6 28.4 %collective-permute-start.59 = (bf16[128,2048]{1,0:T(8,128)(2,1)S(1)}, bf16[128,2048]{1,0:T(8,128)(2,1)S(1)}, u32[]{:S(2)}, u32[]{:S(2)}) collective-permute-start(bf16[128,2048]{1,0:T(8,128)(2,1)S(1)} %bitcast.303), channel_id=1, source_target_pairs={{0,1},{1,0},{2,3},{3,2},{4,5},{5,4},{6,7},{7,6},{8,9},{9,8},{10,11... | collective-permute-start | bytes 1572872 | tf_op jit(solution)/shard_map/ppermute | solution.py:42
  266.9 30.2 %collective-permute-start.60 = (bf16[256,1024]{1,0:T(8,128)(2,1)S(1)}, bf16[256,1024]{1,0:T(8,128)(2,1)S(1)}, u32[]{:S(2)}, u32[]{:S(2)}) collective-permute-start(bf16[256,1024]{1,0:T(8,128)(2,1)S(1)} %bitcast.304), channel_id=1, source_target_pairs={{0,1},{1,0},{2,3},{3,2},{4,5},{5,4},{6,7},{7,6},{8,9},{9,8},{10,11... | collective-permute-start | bytes 1572872 | tf_op jit(solution)/shard_map/ppermute | solution.py:42
  278.6 16.3 %collective-permute-start.58 = (bf16[64,2048]{1,0:T(8,128)(2,1)S(1)}, bf16[64,2048]{1,0:T(8,128)(2,1)S(1)}, u32[]{:S(2)}, u32[]{:S(2)}) collective-permute-start(bf16[64,2048]{1,0:T(8,128)(2,1)S(1)} %bitcast.311), channel_id=1, source_target_pairs={{0,2},{1,3},{2,0},{3,1},{4,6},{5,7},{6,4},{7,5},{8,10},{9,11},{10,... | collective-permute-start | bytes 786440 | tf_op jit(solution)/shard_map/ppermute | solution.py:42
  302.4 36.4 %collective-permute-start.66 = (bf16[256,2048]{1,0:T(8,128)(2,1)}, bf16[256,2048]{1,0:T(8,128)(2,1)}, u32[]{:S(2)}, u32[]{:S(2)}) collective-permute-start(bf16[256,2048]{1,0:T(8,128)(2,1)} %get-tuple-element.987), channel_id=1, source_target_pairs={{0,4},{4,0},{8,12},{12,8},{16,20},{20,16},{24,28},{28,24},{1,5},{5... | collective-permute-start | bytes 3145736 | tf_op jit(solution)/shard_map/ppermute | solution.py:42
  303.7 35.0 %collective-permute-start.67 = (bf16[256,2048]{1,0:T(8,128)(2,1)}, bf16[256,2048]{1,0:T(8,128)(2,1)}, u32[]{:S(2)}, u32[]{:S(2)}) collective-permute-start(bf16[256,2048]{1,0:T(8,128)(2,1)} %add_low.8), channel_id=1, source_target_pairs={{0,16},{4,20},{8,24},{12,28},{16,0},{20,4},{24,8},{28,12},{1,17},{... | collective-permute-start | bytes 3145736 | tf_op jit(solution)/shard_map/ppermute | solution.py:42
  305.9 15.2 %collective-permute-start.62 = (bf16[128,1024]{1,0:T(8,128)(2,1)}, bf16[128,1024]{1,0:T(8,128)(2,1)}, u32[]{:S(2)}, u32[]{:S(2)}) collective-permute-start(bf16[128,1024]{1,0:T(8,128)(2,1)} %bitcast.102), channel_id=1, source_target_pairs={{0,2},{1,3},{2,0},{3,1},{4,6},{5,7},{6,4},{7,5},{8,10},{9,11},{10,... | collective-permute-start | bytes 786440 | tf_op jit(solution)/shard_map/ppermute | solution.py:42
  307.1 28.7 %collective-permute-start.61 = (bf16[256,1024]{1,0:T(8,128)(2,1)}, bf16[256,1024]{1,0:T(8,128)(2,1)}, u32[]{:S(2)}, u32[]{:S(2)}) collective-permute-start(bf16[256,1024]{1,0:T(8,128)(2,1)} %get-tuple-element.948), channel_id=1, source_target_pairs={{0,8},{4,12},{8,0},{12,4},{16,24},{20,28},{24,16},{28,20},{1,9},{5... | collective-permute-start | bytes 1572872 | tf_op jit(solution)/shard_map/ppermute | solution.py:42
  309.6 26.3 %collective-permute-start.64 = (bf16[256,1024]{1,0:T(8,128)(2,1)}, bf16[256,1024]{1,0:T(8,128)(2,1)}, u32[]{:S(2)}, u32[]{:S(2)}) collective-permute-start(bf16[256,1024]{1,0:T(8,128)(2,1)} %bitcast.109), channel_id=1, source_target_pairs={{0,1},{1,0},{2,3},{3,2},{4,5},{5,4},{6,7},{7,6},{8,9},{9,8},{10,11... | collective-permute-start | bytes 1572872 | tf_op jit(solution)/shard_map/ppermute | solution.py:42
  343.4 21.5 %collective-permute-start.73 = (bf16[128,1024]{1,0:T(8,128)(2,1)S(1)}, bf16[128,1024]{1,0:T(8,128)(2,1)S(1)}, u32[]{:S(2)}, u32[]{:S(2)}) collective-permute-start(bf16[128,1024]{1,0:T(8,128)(2,1)S(1)} %bitcast.308), channel_id=1, source_target_pairs={{0,2},{1,3},{2,0},{3,1},{4,6},{5,7},{6,4},{7,5},{8,10},{9,11},{10,... | collective-permute-start | bytes 786440 | tf_op jit(solution)/shard_map/ppermute | solution.py:42
  345.6 19.9 %collective-permute-start.72 = (bf16[128,2048]{1,0:T(8,128)(2,1)S(1)}, bf16[128,2048]{1,0:T(8,128)(2,1)S(1)}, u32[]{:S(2)}, u32[]{:S(2)}) collective-permute-start(bf16[128,2048]{1,0:T(8,128)(2,1)S(1)} %bitcast.302), channel_id=1, source_target_pairs={{0,1},{1,0},{2,3},{3,2},{4,5},{5,4},{6,7},{7,6},{8,9},{9,8},{10,11... | collective-permute-start | bytes 1572872 | tf_op jit(solution)/shard_map/ppermute | solution.py:42
  347.6 18.0 %collective-permute-start.70 = (bf16[256,1024]{1,0:T(8,128)(2,1)S(1)}, bf16[256,1024]{1,0:T(8,128)(2,1)S(1)}, u32[]{:S(2)}, u32[]{:S(2)}) collective-permute-start(bf16[256,1024]{1,0:T(8,128)(2,1)S(1)} %get-tuple-element.1031), channel_id=1, source_target_pairs={{0,4},{4,0},{8,12},{12,8},{16,20},{20,16},{24,28},{28,24},{1,5},{5... | collective-permute-start | bytes 1572872 | tf_op jit(solution)/shard_map/ppermute | solution.py:42
  347.7 17.8 %collective-permute-start.71 = (bf16[256,1024]{1,0:T(8,128)(2,1)S(1)}, bf16[256,1024]{1,0:T(8,128)(2,1)S(1)}, u32[]{:S(2)}, u32[]{:S(2)}) collective-permute-start(bf16[256,1024]{1,0:T(8,128)(2,1)S(1)} %add_low.9), channel_id=1, source_target_pairs={{0,16},{4,20},{8,24},{12,28},{16,0},{20,4},{24,8},{28,12},{1,17},{... | collective-permute-start | bytes 1572872 | tf_op jit(solution)/shard_map/ppermute | solution.py:42
  365.6 18.3 %collective-permute-start.80 = (bf16[128,1024]{1,0:T(8,128)(2,1)S(1)}, bf16[128,1024]{1,0:T(8,128)(2,1)S(1)}, u32[]{:S(2)}, u32[]{:S(2)}) collective-permute-start(bf16[128,1024]{1,0:T(8,128)(2,1)S(1)} %bitcast.307), channel_id=1, source_target_pairs={{0,16},{4,20},{8,24},{12,28},{16,0},{20,4},{24,8},{28,12},{1,17},{... | collective-permute-start | bytes 786440 | tf_op jit(solution)/shard_map/ppermute | solution.py:42
  366.6 17.4 %collective-permute-start.78 = (bf16[128,1024]{1,0:T(8,128)(2,1)S(1)}, bf16[128,1024]{1,0:T(8,128)(2,1)S(1)}, u32[]{:S(2)}, u32[]{:S(2)}) collective-permute-start(bf16[128,1024]{1,0:T(8,128)(2,1)S(1)} %bitcast.309), channel_id=1, source_target_pairs={{0,1},{1,0},{2,3},{3,2},{4,5},{5,4},{6,7},{7,6},{8,9},{9,8},{10,11... | collective-permute-start | bytes 786440 | tf_op jit(solution)/shard_map/ppermute | solution.py:42
  366.8 17.2 %collective-permute-start.79 = (bf16[64,2048]{1,0:T(8,128)(2,1)S(1)}, bf16[64,2048]{1,0:T(8,128)(2,1)S(1)}, u32[]{:S(2)}, u32[]{:S(2)}) collective-permute-start(bf16[64,2048]{1,0:T(8,128)(2,1)S(1)} %bitcast.310), channel_id=1, source_target_pairs={{0,2},{1,3},{2,0},{3,1},{4,6},{5,7},{6,4},{7,5},{8,10},{9,11},{10,... | collective-permute-start | bytes 786440 | tf_op jit(solution)/shard_map/ppermute | solution.py:42
  (101 other events, 1084.3 us)

commit v5 on v4

--- a/solution.py
+++ b/solution.py
@@ -496,8 +496,13 @@
         put_rows(lows, cols, value)
 
 
-def attend_back_kernel(ways, size, lead, block, place, d_out, part, *refs):
+def attend_back_kernel(ways, size, lead, block, grads, place, *refs):
+    if grads:
+        (first, mixed), refs = refs[:2], refs[2:]
+    (d_out, part), refs = refs[:2], refs[2:]
     refs, (weight, d_mixed, sems) = refs[:-3], refs[-3:]
+    if grads:
+        refs, outs = refs[:-4], refs[-4:]
     refs, lows = refs[:-ways], refs[-ways:]
     *others, attended, gains, q0, q1, q2, q3, allow, qkv, total, d, d_gain, d_shift, d_qkv, keep = refs
     copies = fetch(place, (q0, q1, q2, q3), weight, lead, sems)
@@ -540,6 +545,8 @@
         value = dot_t(d_qkv[...], weight[cols, pl.ds(0, 3 * third)])
         keep[:, cols] = value
         put_rows(lows, cols, value)
+    if grads:
+        attend_grad(lead, place, first, mixed, d_qkv, d, outs)
 
 
 def up(f, weight, pre, active):
@@ -608,8 +615,10 @@
     feed_back(d, pre, w_up, w_dn, d_pre, keep, lows)
 
 
-def feed_turn_kernel(ways, lead, up_place, dn_place, *refs):
+def feed_turn_kernel(ways, lead, grads, place, up_place, dn_place, *refs):
     refs, (w_up, w_dn, pre, up_sems, dn_sems) = refs[:-5], refs[-5:]
+    if grads:
+        refs, up_outs, dn_outs = refs[:-8], refs[-8:-4], refs[-4:]
     refs, lows = refs[:-ways], refs[-ways:]
     *parts, gains, d, u0, u1, u2, u3, n0, n1, n2, n3, total, f, active, d_pre, keep = refs
     up_copies = fetch(up_place, (u0, u1, u2, u3), w_up, lead, up_sems)
@@ -621,6 +630,9 @@
     for copy in dn_copies:
         copy.wait()
     feed_back(d, pre, w_up, w_dn, d_pre, keep, lows)
+    if grads:
+        weight_grad(lead, place, f, d_pre, up_outs)
+        weight_grad(lead // 2, place, active, d, dn_outs)
 
 
 def columns_of(place, value, lead):
@@ -636,16 +648,22 @@
     return parts
 
 
-def weight_grad_kernel(lead, aligned, place, left, right, *outs):
-    place = place if aligned else (0, 0)
+def weight_grad(lead, place, left, right, outs):
     for part, out in zip(columns_of(place, left, lead), outs):
         out[...] = t_dot(part, right[...]).astype(bf16)
 
 
+def weight_grad_kernel(lead, aligned, place, left, right, *outs):
+    weight_grad(lead, place if aligned else (0, 0), left, right, outs)
+
+
 def attend_grad_kernel(lead, aligned, place, left, mixed, d_qkv, d, *outs):
+    attend_grad(lead, place if aligned else (0, 0), left, mixed, d_qkv, d, outs)
+
+
+def attend_grad(lead, place, left, mixed, d_qkv, d, outs):
     width = d_qkv.shape[1]
     third = width // 3
-    place = place if aligned else (0, 0)
     block = left.shape[1] // (4 * lead)
     lefts, inners = columns_of(place, left, lead), columns_of(place, mixed, lead // 2)
     for part, inner, out in zip(lefts, inners, outs):
@@ -863,6 +881,10 @@
     downs[0].finish()
     live.seal(attns[0], ups[0], attns[1])
 
+    def after(made, value):
+        (keep, send), _ = lax.optimization_barrier((made.quarters, value))
+        made.quarters = [keep, send]
+
     def gate(*made):
         airs = [flow.air for flow in made]
         other, airs = lax.optimization_barrier((live.other, airs))
@@ -940,10 +962,13 @@
         live.put(**{f"feed{layer}": (attended, second, pre, active)}, keep=keep, low=low)
 
     def feed_turn(layer, ways=2):
+        grads = False
+        quarters = 4 * [quarter] + 4 * [((feed // 8, width), bf16)]
         attended, second, active, d_pre, keep, *low = call(
-            partial(feed_turn_kernel, ways, lead),
-            [two_f, two_b, wide_b, wide_b, two_f, *lows(ways)],
+            partial(feed_turn_kernel, ways, lead, grads),
+            [two_f, two_b, wide_b, wide_b, two_f, *lows(ways), *(quarters if grads else [])],
             [
+                place,
                 ups[layer].place,
                 downs[layer].place,
                 live.values[f"attn{layer}"][0],
@@ -953,7 +978,7 @@
                 *ups[layer].quarters,
                 *downs[layer].quarters,
             ],
-            [SMEM, SMEM] + [VMEM] * (4 + len(live.other)) + [ANY] * 8,
+            [SMEM] * 3 + [VMEM] * (4 + len(live.other)) + [ANY] * 8,
             [w_upper, w_lower, pltpu.VMEM(wide_b[0], f32), dma(4 * lead), dma(2 * lead)],
             name="feed_turn",
         )
@@ -1032,11 +1057,17 @@
         live.put(**{f"gains{layer}{which}": jnp.concatenate([d_gain, d_shift], 1)})
 
     def attend_back(layer, ways=1):
+        grads = block % 128 == 0
+        hidden, first, qkv, mixed = live.values[f"attn{layer}"]
         grad, d_low, d_gain, d_shift, d_qkv, keep, *low = call(
-            partial(attend_back_kernel, ways, size, lead, 2 * block),
-            [two_f, two_b, gain_row, gain_row, ((2 * length, part), bf16), two_f, *lows(ways)],
+            partial(attend_back_kernel, ways, size, lead, 2 * block, grads),
+            [
+                *(two_f, two_b, gain_row, gain_row, ((2 * length, part), bf16), two_f, *lows(ways)),
+                *(4 * [quarter] if grads else []),
+            ],
             [
                 attns[layer].place,
+                *([first, mixed] if grads else []),
                 live.grad,
                 *shares(),
                 live.values[f"feed{layer}"][0],
@@ -1045,12 +1076,14 @@
                 live.allows[layer],
                 live.values[f"attn{layer}"][2],
             ],
-            [SMEM] + [VMEM] * (4 + len(live.other)) + [ANY] * 4 + [VMEM] * 2,
+            [SMEM] + [VMEM] * (4 + 2 * grads + len(live.other)) + [ANY] * 4 + [VMEM] * 2,
             [w_attn, pltpu.VMEM((2 * length, half), bf16), dma(4 * lead)],
             name="attend_back",
         )
+        low, made = low[:ways], low[ways:]
         live.put(grad=grad, d_low=d_low, d_qkv=d_qkv, keep=keep, low=low)
         live.put(**{f"gains{layer}1": jnp.concatenate([d_gain, d_shift], 1)})
+        return live.flow(Scatter(sl, made, 2)) if grads else attend_grad(layer)
 
     def attend_grad(layer):
         hidden, first, qkv, mixed = live.values[f"attn{layer}"]
@@ -1151,44 +1184,46 @@
     g_down1 = down_grad(1, True)
     g_down1.cross()
     g_down1.start()
-    attend_back(1)
+    g_attn1 = attend_back(1)
     live.seal(g_down1, g_up1)
 
     g_down1.start()
     g_up1.start()
-    g_attn1 = attend_grad(1)
     g_attn1.cross()
     g_attn1.start()
     cross()
     feed_back(0)
-    g_down0 = down_grad(0)
+    g_down0, g_up0b, g_up0a = down_grad(0), up_grad(0, 1), up_grad(0, 0)
     live.seal(g_down1, g_up1, g_attn1)
 
     cross()
     g_down0.cross()
     g_down0.start()
-    g_up0b = up_grad(0, 1)
     g_up0b.cross()
     g_up0b.start()
+    g_up0a.cross()
+    after(g_up1, g_down0.quarters[0][1])
     g_up1.start()
     g_attn1.start()
-    attend_back(0)
+    g_attn0 = attend_back(0)
     live.seal(g_down0, g_up1, g_attn1, g_up0b)
 
     cross()
-    g_attn0 = attend_grad(0)
     g_attn0.cross()
     g_attn0.start()
     g_up0b.start()
+    g_down0.start()
+    after(g_attn1, g_attn0.quarters[0][1])
     g_attn1.start()
-    g_down0.start()
     gate(g_up0b, g_attn1, g_down0)
     norm_back(0, 0, live.attn0[0])
     live.seal(g_attn0, g_attn1, g_down0, g_up0b)
 
-    g_up0a = up_grad(0, 0)
-    g_up0a.cross()
     g_up0a.start()
+    after(g_down0, g_attn0.quarters[1])
+    (g_attn1.value, g_up1.value), g_attn0.quarters[1] = lax.optimization_barrier(
+        ((g_attn1.value, g_up1.value), g_attn0.quarters[1])
+    )
     g_attn0.start()
     g_down0.start()
     g_up0b.start()

time: 409 us -> 398 us (0.973)
  waiting for transfers between devices: 202 us -> 189 us
  local copies, waits for them, and re-layouts: 13.7 us -> 21.6 us
    ppermute x87, waiting for transfers between devices: 202 us -> 189 us  [flip(): lax.ppermute(value, axis, [(i, i ^ mask) for i in range(self.size[axis])])]
    unnamed x125 -> x151, local copies, waits for them, and re-layouts: 10.7 us -> 18.7 us
    pallas_call x55 -> x53, Pallas kernels: 89.9 us -> 86.5 us  [call(): pl.pallas_call(kernel, out_shape=[jax.ShapeDtypeStruct(shape, kind) for s...]
  transfers between devices with their start and end apart: 87 -> 87, of which waited for: 44 -> 44; matrix products, arithmetic and copies ran while one was open for 3% -> 2% of each run, Pallas kernels for 20% -> 21%
where the time goes in v5:
time: 398 us; the launch traced here: 395 us
  waiting for transfers between devices  189 us (47%)
  Pallas kernels  94 us (24%)
  starting transfers between devices  79.5 us (20%)
  local copies, waits for them, and re-layouts  21.6 us (5%)
  other arithmetic  8.08 us (2%)
    ppermute x87, waiting for transfers between devices, flip(): lax.ppermute(value, axis, [(i, i ^ mask) for i in range(self.size[axis])])  189 us
    pallas_call x53, Pallas kernels, call(): pl.pallas_call(kernel, out_shape=[jax.ShapeDtypeStruct(shape, kind) for s...  86.5 us
    ppermute x87, starting transfers between devices, flip(): lax.ppermute(value, axis, [(i, i ^ mask) for i in range(self.size[axis])])  79.5 us
    unnamed x151, local copies, waits for them, and re-layouts  18.7 us
  transfers between devices with their start and end apart: 87, of which 44 were waited for; matrix products, arithmetic and copies ran while one was open for 2% of the time, Pallas kernels for 21%

profile of v5, /device:TPU:0, one launch (start us, length us, event | category | flops | bytes accessed | tf_op | source)
XLA Modules:
  0.0 394.8 jit_solution(18150850474035650453)
XLA Ops:
  1.9 4.1 %collective-permute-start.1 = (bf16[128,1024]{1,0:T(8,128)(2,1)S(1)}, bf16[128,1024]{1,0:T(8,128)(2,1)S(1)}, u32[]{:S(2)}, u32[]{:S(2)}) collective-permute-start(bf16[128,1024]{1,0:T(8,128)(2,1)S(1)} %get-tuple-element.592), channel_id=1, source_target_pairs={{0,2},{1,3},{2,0},{3,1},{4,6},{5,7},{6,4},{7,5},{8,10},{9,11},{10,... | collective-permute-start | bytes 786440 | tf_op jit(solution)/shard_map/ppermute | solution.py:42
  13.1 4.8 %collective-permute-done.1 = bf16[128,1024]{1,0:T(8,128)(2,1)S(1)} collective-permute-done((bf16[128,1024]{1,0:T(8,128)(2,1)S(1)}, bf16[128,1024]{1,0:T(8,128)(2,1)S(1)}, u32[]{:S(2)}, u32[]{:S(2)}) %collective-permute-start.1) | collective-permute-done | bytes 262176 | tf_op jit(solution)/shard_map/ppermute | solution.py:42
  18.7 3.4 collective-permute-start.6
  25.1 8.8 %collective-permute-done.5 = bf16[32,2048]{1,0:T(8,128)(2,1)S(1)} collective-permute-done((bf16[32,2048]{1,0:T(8,128)(2,1)S(1)}, bf16[32,2048]{1,0:T(8,128)(2,1)S(1)}, u32[]{:S(2)}, u32[]{:S(2)}) %collective-permute-start.5) | collective-permute-done | bytes 131104 | tf_op jit(solution)/shard_map/ppermute | solution.py:42
  33.9 2.2 collective-permute-done.6
  38.6 3.4 collective-permute-start.8
  44.7 2.1 fusion
  47.7 12.4 %collective-permute-done.9 = bf16[64,2048]{1,0:T(8,128)(2,1)S(1)} collective-permute-done((bf16[64,2048]{1,0:T(8,128)(2,1)S(1)}, bf16[64,2048]{1,0:T(8,128)(2,1)S(1)}, u32[]{:S(2)}, u32[]{:S(2)}) %collective-permute-start.9) | collective-permute-done | bytes 262176 | tf_op jit(solution)/shard_map/ppermute | solution.py:42
  63.5 4.5 %collective-permute-start.15 = (bf16[128,2048]{1,0:T(8,128)(2,1)S(1)}, bf16[128,2048]{1,0:T(8,128)(2,1)S(1)}, u32[]{:S(2)}, u32[]{:S(2)}) collective-permute-start(bf16[128,2048]{1,0:T(8,128)(2,1)S(1)} %bitcast.234), channel_id=1, source_target_pairs={{0,1},{1,0},{2,3},{3,2},{4,5},{5,4},{6,7},{7,6},{8,9},{9,8},{10,11... | collective-permute-start | bytes 1572872 | tf_op jit(solution)/shard_map/ppermute | solution.py:42
  70.9 14.1 %collective-permute-done.16 = bf16[64,2048]{1,0:T(8,128)(2,1)S(1)} collective-permute-done((bf16[64,2048]{1,0:T(8,128)(2,1)S(1)}, bf16[64,2048]{1,0:T(8,128)(2,1)S(1)}, u32[]{:S(2)}, u32[]{:S(2)}) %collective-permute-start.16) | collective-permute-done | bytes 262176 | tf_op jit(solution)/shard_map/ppermute | solution.py:42
  93.1 3.7 collective-permute-start.21
  99.6 9.5 %attend.2 = (f32[256,1024]{1,0:T(8,128)}, bf16[256,1024]{1,0:T(8,128)(2,1)S(1)}, bf16[256,1536]{1,0:T(8,128)(2,1)S(1)}, bf16[256,512]{1,0:T(8,128)(2,1)S(1)}, f3...) custom-call(s32[2]{0:T(128)S(1)} %pad_add_fusion.place.up_place.dn_place, ...), custom_call_target="tpu_custom_call" | custom-call | tf_op jit(solution)/shard_map/attend/pallas_call | solution.py:54
  111.7 13.1 %collective-permute-done.22 = bf16[64,2048]{1,0:T(8,128)(2,1)S(1)} collective-permute-done((bf16[64,2048]{1,0:T(8,128)(2,1)S(1)}, bf16[64,2048]{1,0:T(8,128)(2,1)S(1)}, u32[]{:S(2)}, u32[]{:S(2)}) %collective-permute-start.22) | collective-permute-done | bytes 262176 | tf_op jit(solution)/shard_map/ppermute | solution.py:42
  125.9 2.1 collective-permute-start.28
  128.1 5.5 %feed.1 = (f32[256,1024]{1,0:T(8,128)S(1)}, bf16[256,1024]{1,0:T(8,128)(2,1)S(1)}, f32[256,2048]{1,0:T(8,128)S(1)}, bf16[256,2048]{1,0:T(8,128)(2,1)S(1)}, f32[2...) custom-call(s32[2]{0:T(128)S(1)} %pad_add_fusion.place.up_place.dn_place, s32[2]{0:T(128)S(1)} %pad_add_fusion.place.up_place.dn_place, ...), custom_call_target="tpu_custom_call" | custom-call | tf_op jit(solution)/shard_map/feed/pallas_call | solution.py:54
  134.2 16.0 %collective-permute-done.27 = bf16[128,2048]{1,0:T(8,128)(2,1)S(1)} collective-permute-done((bf16[128,2048]{1,0:T(8,128)(2,1)S(1)}, bf16[128,2048]{1,0:T(8,128)(2,1)S(1)}, u32[]{:S(2)}, u32[]{:S(2)}) %collective-permute-start.27) | collective-permute-done | bytes 524320 | tf_op jit(solution)/shard_map/ppermute | solution.py:42
  150.2 2.1 collective-permute-done.28
  155.1 8.2 %attend.3 = (f32[256,1024]{1,0:T(8,128)S(1)}, bf16[256,1024]{1,0:T(8,128)(2,1)S(1)}, bf16[256,1536]{1,0:T(8,128)(2,1)S(1)}, bf16[256,512]{1,0:T(8,128)(2,1)S(1)}...) custom-call(s32[2]{0:T(128)S(1)} %pad_add_fusion.place.up_place.dn_place, ...), custom_call_target="tpu_custom_call" | custom-call | tf_op jit(solution)/shard_map/attend/pallas_call | solution.py:54
  166.2 12.0 %collective-permute-done.32.refs_7_ = bf16[256,2048]{1,0:T(8,128)(2,1)S(1)} collective-permute-done((bf16[256,2048]{1,0:T(8,128)(2,1)S(1)}, bf16[256,2048]{1,0:T(8,128)(2,1)S(1)}, u32[]{:S(2)}, u32[]{:S(2)}) %collective-permute-start.32) | collective-permute-done | bytes 1048608 | tf_op jit(solution)/shard_map/ppermute | solution.py:42
  185.5 6.5 %feed_turn.1 = (f32[256,1024]{1,0:T(8,128)S(1)}, bf16[256,1024]{1,0:T(8,128)(2,1)S(1)}, bf16[256,2048]{1,0:T(8,128)(2,1)S(1)}, bf16[256,2048]{1,0:T(8,128)(2,1)S...) custom-call(s32[2]{0:T(128)S(1)} %pad_add_fusion.place.up_place.dn_place, ...), custom_call_target="tpu_custom_call" | custom-call | tf_op jit(solution)/shard_map/feed_turn/pallas_call | solution.py:54
  192.1 1.8 down_grad.2
  196.8 1.9 collective-permute-done.40.two
  203.1 7.1 %collective-permute-done.38.refs_4_ = bf16[128,1024]{1,0:T(8,128)(2,1)S(1)} collective-permute-done((bf16[128,1024]{1,0:T(8,128)(2,1)S(1)}, bf16[128,1024]{1,0:T(8,128)(2,1)S(1)}, u32[]{:S(2)}, u32[]{:S(2)}) %collective-permute-start.38) | collective-permute-done | bytes 262176 | tf_op jit(solution)/shard_map/ppermute | solution.py:42
  210.2 4.8 %collective-permute-done.39.refs_5_ = bf16[128,1024]{1,0:T(8,128)(2,1)S(1)} collective-permute-done((bf16[128,1024]{1,0:T(8,128)(2,1)S(1)}, bf16[128,1024]{1,0:T(8,128)(2,1)S(1)}, u32[]{:S(2)}, u32[]{:S(2)}) %collective-permute-start.39) | collective-permute-done | bytes 262176 | tf_op jit(solution)/shard_map/ppermute | solution.py:42
  215.0 12.1 %attend_back.2 = (f32[256,1024]{1,0:T(8,128)S(1)}, bf16[256,1024]{1,0:T(8,128)(2,1)}, f32[1,1024]{1,0:T(1,128)S(1)}, f32[1,1024]{1,0:T(1,128)S(1)}, bf16[256,153...) custom-call(s32[2]{0:T(128)S(1)} %pad_add_fusion.place.up_place.dn_p, ...), custom_call_target="tpu_custom_call" | custom-call | tf_op jit(solution)/shard_map/attend_back/pallas_call | solution.py:54
  227.3 2.6 collective-permute-done.47.two
  234.3 10.7 %collective-permute-done.46.refs_0_ = bf16[256,1024]{1,0:T(8,128)(2,1)S(1)} collective-permute-done((bf16[256,1024]{1,0:T(8,128)(2,1)S(1)}, bf16[256,1024]{1,0:T(8,128)(2,1)S(1)}, u32[]{:S(2)}, u32[]{:S(2)}) %collective-permute-start.46) | collective-permute-done | bytes 524320 | tf_op jit(solution)/shard_map/ppermute | solution.py:42
  245.0 6.1 %feed_back.1 = (f32[256,1024]{1,0:T(8,128)S(1)}, bf16[256,1024]{1,0:T(8,128)(2,1)S(1)}, f32[1,1024]{1,0:T(1,128)S(1)}, f32[1,1024]{1,0:T(1,128)S(1)}, bf16[256,2...) custom-call(s32[2]{0:T(128)S(1)} %pad_add_fusion.place.up_place.dn_place, ...), custom_call_target="tpu_custom_call" | custom-call | tf_op jit(solution)/shard_map/feed_back/pallas_call | solution.py:54
  255.6 2.1 collective-permute-done.49
  258.3 2.1 collective-permute-done.53.two
  267.4 9.4 %collective-permute-done.52.refs_4_ = bf16[256,1024]{1,0:T(8,128)(2,1)S(1)} collective-permute-done((bf16[256,1024]{1,0:T(8,128)(2,1)S(1)}, bf16[256,1024]{1,0:T(8,128)(2,1)S(1)}, u32[]{:S(2)}, u32[]{:S(2)}) %collective-permute-start.52) | collective-permute-done | bytes 524320 | tf_op jit(solution)/shard_map/ppermute | solution.py:42
  280.2 13.1 %attend_back.3 = (f32[256,1024]{1,0:T(8,128)S(1)}, bf16[256,1024]{1,0:T(8,128)(2,1)}, f32[1,1024]{1,0:T(1,128)S(1)}, f32[1,1024]{1,0:T(1,128)S(1)}, bf16[256,153...) custom-call(s32[2]{0:T(128)S(1)} %pad_add_fusion.place.up_place.dn_p, ...), custom_call_target="tpu_custom_call" | custom-call | tf_op jit(solution)/shard_map/attend_back/pallas_call | solution.py:54
  296.3 2.6 collective-permute-done.65.two
  311.1 11.6 %collective-permute-done.64 = bf16[128,1024]{1,0:T(8,128)(2,1)S(1)} collective-permute-done((bf16[128,1024]{1,0:T(8,128)(2,1)S(1)}, bf16[128,1024]{1,0:T(8,128)(2,1)S(1)}, u32[]{:S(2)}, u32[]{:S(2)}) %collective-permute-start.64) | collective-permute-done | bytes 262176 | tf_op jit(solution)/shard_map/ppermute | solution.py:42
  322.8 3.1 collective-permute-done.68
  325.8 6.6 %collective-permute-done.67 = bf16[64,2048]{1,0:T(8,128)(2,1)S(1)} collective-permute-done((bf16[64,2048]{1,0:T(8,128)(2,1)S(1)}, bf16[64,2048]{1,0:T(8,128)(2,1)S(1)}, u32[]{:S(2)}, u32[]{:S(2)}) %collective-permute-start.67) | collective-permute-done | bytes 262176 | tf_op jit(solution)/shard_map/ppermute | solution.py:42
  332.4 2.8 norm_back.1
  341.9 2.4 collective-permute-start.73
  345.3 2.3 down.1
  349.5 2.4 finish.2
  351.9 3.6 collective-permute-done.74
  357.1 2.2 collective-permute-done.72
  366.5 6.4 %collective-permute-done.77 = f32[2,4,9,128]{3,1,2,0:T(4,128)S(1)} collective-permute-done((f32[2,4,9,128]{3,1,2,0:T(4,128)S(1)}, f32[2,4,9,128]{3,1,2,0:T(4,128)S(1)}, u32[]{:S(2)}, u32[]{:S(2)}) %collective-permute-start.77) | collective-permute-done | bytes 36896 | tf_op jit(solution)/shard_map/ppermute | solution.py:42
  374.4 2.3 collective-permute-done.79
  379.6 2.0 collective-permute-done.82
  383.6 2.5 collective-permute-done.83
  388.4 3.1 collective-permute-done.86
  392.2 2.4 finish.3
  (389 shorter events, 121.2 us)
Async XLA Ops:
  1.9 16.0 %collective-permute-start.1 = (bf16[128,1024]{1,0:T(8,128)(2,1)S(1)}, bf16[128,1024]{1,0:T(8,128)(2,1)S(1)}, u32[]{:S(2)}, u32[]{:S(2)}) collective-permute-start(bf16[128,1024]{1,0:T(8,128)(2,1)S(1)} %get-tuple-element.592), channel_id=1, source_target_pairs={{0,2},{1,3},{2,0},{3,1},{4,6},{5,7},{6,4},{7,5},{8,10},{9,11},{10,... | collective-permute-start | bytes 786440 | tf_op jit(solution)/shard_map/ppermute | solution.py:42
  12.4 23.6 %collective-permute-start.4 = (bf16[272,1024]{1,0:T(8,128)(2,1)}, bf16[272,1024]{1,0:T(8,128)(2,1)}, u32[]{:S(2)}, u32[]{:S(2)}) collective-permute-start(bf16[272,1024]{1,0:T(8,128)(2,1)} %pad_maximum_fusion), channel_id=1, source_target_pairs={{0,8},{4,12},{8,0},{12,4},{16,24},{20,28},{24,16},{28,20},{1,9},{5... | collective-permute-start | bytes 1671176 | tf_op jit(solution)/shard_map/ppermute | solution.py:42
  17.9 19.1 %collective-permute-start.7 = (bf16[256,1024]{1,0:T(8,128)(2,1)S(1)}, bf16[256,1024]{1,0:T(8,128)(2,1)S(1)}, u32[]{:S(2)}, u32[]{:S(2)}) collective-permute-start(bf16[256,1024]{1,0:T(8,128)(2,1)S(1)} %bitcast.228), channel_id=1, source_target_pairs={{0,1},{1,0},{2,3},{3,2},{4,5},{5,4},{6,7},{7,6},{8,9},{9,8},{10,11... | collective-permute-start | bytes 1572872 | tf_op jit(solution)/shard_map/ppermute | solution.py:42
  18.7 17.3 %collective-permute-start.6 = (bf16[64,2176]{1,0:T(8,128)(2,1)S(1)}, bf16[64,2176]{1,0:T(8,128)(2,1)S(1)}, u32[]{:S(2)}, u32[]{:S(2)}) collective-permute-start(bf16[64,2176]{1,0:T(8,128)(2,1)S(1)} %bitcast.236), channel_id=1, source_target_pairs={{0,2},{1,3},{2,0},{3,1},{4,6},{5,7},{6,4},{7,5},{8,10},{9,11},{10,... | collective-permute-start | bytes 835592 | tf_op jit(solution)/shard_map/ppermute | solution.py:42
  37.1 23.7 %collective-permute-start.10 = (bf16[512,1024]{1,0:T(8,128)(2,1)S(1)}, bf16[512,1024]{1,0:T(8,128)(2,1)S(1)}, u32[]{:S(2)}, u32[]{:S(2)}) collective-permute-start(bf16[512,1024]{1,0:T(8,128)(2,1)S(1)} %bitcast.202), channel_id=1, source_target_pairs={{0,16},{4,20},{8,24},{12,28},{16,0},{20,4},{24,8},{28,12},{1,17},{... | collective-permute-start | bytes 3145736 | tf_op jit(solution)/shard_map/ppermute | solution.py:42
  38.5 22.4 %collective-permute-start.11 = (bf16[512,1024]{1,0:T(8,128)(2,1)S(1)}, bf16[512,1024]{1,0:T(8,128)(2,1)S(1)}, u32[]{:S(2)}, u32[]{:S(2)}) collective-permute-start(bf16[512,1024]{1,0:T(8,128)(2,1)S(1)} %bitcast.203), channel_id=1, source_target_pairs={{0,4},{4,0},{8,12},{12,8},{16,20},{20,16},{24,28},{28,24},{1,5},{5... | collective-permute-start | bytes 3145736 | tf_op jit(solution)/shard_map/ppermute | solution.py:42
  38.6 22.3 %collective-permute-start.8 = (bf16[128,2176]{1,0:T(8,128)(2,1)S(1)}, bf16[128,2176]{1,0:T(8,128)(2,1)S(1)}, u32[]{:S(2)}, u32[]{:S(2)}) collective-permute-start(bf16[128,2176]{1,0:T(8,128)(2,1)S(1)} %bitcast.224), channel_id=1, source_target_pairs={{0,1},{1,0},{2,3},{3,2},{4,5},{5,4},{6,7},{7,6},{8,9},{9,8},{10,11... | collective-permute-start | bytes 1671176 | tf_op jit(solution)/shard_map/ppermute | solution.py:42
  42.0 18.2 %collective-permute-start.9 = (bf16[64,2048]{1,0:T(8,128)(2,1)S(1)}, bf16[64,2048]{1,0:T(8,128)(2,1)S(1)}, u32[]{:S(2)}, u32[]{:S(2)}) collective-permute-start(bf16[64,2048]{1,0:T(8,128)(2,1)S(1)} %bitcast.254), channel_id=1, source_target_pairs={{0,2},{1,3},{2,0},{3,1},{4,6},{5,7},{6,4},{7,5},{8,10},{9,11},{10,... | collective-permute-start | bytes 786440 | tf_op jit(solution)/shard_map/ppermute | solution.py:42
  61.9 26.4 %collective-permute-start.13 = (bf16[256,2176]{1,0:T(8,128)(2,1)S(1)}, bf16[256,2176]{1,0:T(8,128)(2,1)S(1)}, u32[]{:S(2)}, u32[]{:S(2)}) collective-permute-start(bf16[256,2176]{1,0:T(8,128)(2,1)S(1)} %bitcast.197), channel_id=1, source_target_pairs={{0,16},{4,20},{8,24},{12,28},{16,0},{20,4},{24,8},{28,12},{1,17},{... | collective-permute-start | bytes 3342344 | tf_op jit(solution)/shard_map/ppermute | solution.py:42
  63.0 25.3 %collective-permute-start.14 = (bf16[256,2176]{1,0:T(8,128)(2,1)S(1)}, bf16[256,2176]{1,0:T(8,128)(2,1)S(1)}, u32[]{:S(2)}, u32[]{:S(2)}) collective-permute-start(bf16[256,2176]{1,0:T(8,128)(2,1)S(1)} %bitcast.198), channel_id=1, source_target_pairs={{0,4},{4,0},{8,12},{12,8},{16,20},{20,16},{24,28},{28,24},{1,5},{5... | collective-permute-start | bytes 3342344 | tf_op jit(solution)/shard_map/ppermute | solution.py:42
  63.0 22.8 %collective-permute-start.12 = (bf16[512,1024]{1,0:T(8,128)(2,1)S(1)}, bf16[512,1024]{1,0:T(8,128)(2,1)S(1)}, u32[]{:S(2)}, u32[]{:S(2)}) collective-permute-start(bf16[512,1024]{1,0:T(8,128)(2,1)S(1)} %collective-permute-done.10.refs_9_), channel_id=1, source_target_pairs={{0,4},{4,0},{8,12},{12,8},{16,20},{20,16},{24,28},{28,24},{1,5},{5... | collective-permute-start | bytes 3145736 | tf_op jit(solution)/shard_map/ppermute | solution.py:42
  63.5 22.2 %collective-permute-start.15 = (bf16[128,2048]{1,0:T(8,128)(2,1)S(1)}, bf16[128,2048]{1,0:T(8,128)(2,1)S(1)}, u32[]{:S(2)}, u32[]{:S(2)}) collective-permute-start(bf16[128,2048]{1,0:T(8,128)(2,1)S(1)} %bitcast.234), channel_id=1, source_target_pairs={{0,1},{1,0},{2,3},{3,2},{4,5},{5,4},{6,7},{7,6},{8,9},{9,8},{10,11... | collective-permute-start | bytes 1572872 | tf_op jit(solution)/shard_map/ppermute | solution.py:42
  68.8 16.2 %collective-permute-start.16 = (bf16[64,2048]{1,0:T(8,128)(2,1)S(1)}, bf16[64,2048]{1,0:T(8,128)(2,1)S(1)}, u32[]{:S(2)}, u32[]{:S(2)}) collective-permute-start(bf16[64,2048]{1,0:T(8,128)(2,1)S(1)} %bitcast.259), channel_id=1, source_target_pairs={{0,2},{1,3},{2,0},{3,1},{4,6},{5,7},{6,4},{7,5},{8,10},{9,11},{10,... | collective-permute-start | bytes 786440 | tf_op jit(solution)/shard_map/ppermute | solution.py:42
  90.3 34.5 %collective-permute-start.19 = (bf16[256,2048]{1,0:T(8,128)(2,1)}, bf16[256,2048]{1,0:T(8,128)(2,1)}, u32[]{:S(2)}, u32[]{:S(2)}) collective-permute-start(bf16[256,2048]{1,0:T(8,128)(2,1)} %bitcast.46.refs_4_), channel_id=1, source_target_pairs={{0,16},{4,20},{8,24},{12,28},{16,0},{20,4},{24,8},{28,12},{1,17},{... | collective-permute-start | bytes 3145736 | tf_op jit(solution)/shard_map/ppermute | solution.py:42
  90.8 34.0 %collective-permute-start.20 = (bf16[256,2048]{1,0:T(8,128)(2,1)}, bf16[256,2048]{1,0:T(8,128)(2,1)}, u32[]{:S(2)}, u32[]{:S(2)}) collective-permute-start(bf16[256,2048]{1,0:T(8,128)(2,1)} %bitcast.46.refs_4_), channel_id=1, source_target_pairs={{0,4},{4,0},{8,12},{12,8},{16,20},{20,16},{24,28},{28,24},{1,5},{5... | collective-permute-start | bytes 3145736 | tf_op jit(solution)/shard_map/ppermute | solution.py:42
  93.1 31.8 %collective-permute-start.21 = (bf16[128,2048]{1,0:T(8,128)(2,1)S(1)}, bf16[128,2048]{1,0:T(8,128)(2,1)S(1)}, u32[]{:S(2)}, u32[]{:S(2)}) collective-permute-start(bf16[128,2048]{1,0:T(8,128)(2,1)S(1)} %bitcast.230), channel_id=1, source_target_pairs={{0,1},{1,0},{2,3},{3,2},{4,5},{5,4},{6,7},{7,6},{8,9},{9,8},{10,11... | collective-permute-start | bytes 1572872 | tf_op jit(solution)/shard_map/ppermute | solution.py:42
  109.1 15.8 %collective-permute-start.18 = (bf16[256,1024]{1,0:T(8,128)(2,1)S(1)}, bf16[256,1024]{1,0:T(8,128)(2,1)S(1)}, u32[]{:S(2)}, u32[]{:S(2)}) collective-permute-start(bf16[256,1024]{1,0:T(8,128)(2,1)S(1)} %get-tuple-element.638), channel_id=1, source_target_pairs={{0,8},{4,12},{8,0},{12,4},{16,24},{20,28},{24,16},{28,20},{1,9},{5... | collective-permute-start | bytes 1572872 | tf_op jit(solution)/shard_map/ppermute | solution.py:42
  125.1 27.3 %collective-permute-start.25 = (bf16[256,2048]{1,0:T(8,128)(2,1)S(1)}, bf16[256,2048]{1,0:T(8,128)(2,1)S(1)}, u32[]{:S(2)}, u32[]{:S(2)}) collective-permute-start(bf16[256,2048]{1,0:T(8,128)(2,1)S(1)} %bitcast.206), channel_id=1, source_target_pairs={{0,16},{4,20},{8,24},{12,28},{16,0},{20,4},{24,8},{28,12},{1,17},{... | collective-permute-start | bytes 3145736 | tf_op jit(solution)/shard_map/ppermute | solution.py:42
  125.6 26.7 %collective-permute-start.26 = (bf16[256,2048]{1,0:T(8,128)(2,1)S(1)}, bf16[256,2048]{1,0:T(8,128)(2,1)S(1)}, u32[]{:S(2)}, u32[]{:S(2)}) collective-permute-start(bf16[256,2048]{1,0:T(8,128)(2,1)S(1)} %bitcast.207), channel_id=1, source_target_pairs={{0,4},{4,0},{8,12},{12,8},{16,20},{20,16},{24,28},{28,24},{1,5},{5... | collective-permute-start | bytes 3145736 | tf_op jit(solution)/shard_map/ppermute | solution.py:42
  125.8 24.3 %collective-permute-start.27 = (bf16[128,2048]{1,0:T(8,128)(2,1)S(1)}, bf16[128,2048]{1,0:T(8,128)(2,1)S(1)}, u32[]{:S(2)}, u32[]{:S(2)}) collective-permute-start(bf16[128,2048]{1,0:T(8,128)(2,1)S(1)} %bitcast.232), channel_id=1, source_target_pairs={{0,1},{1,0},{2,3},{3,2},{4,5},{5,4},{6,7},{7,6},{8,9},{9,8},{10,11... | collective-permute-start | bytes 1572872 | tf_op jit(solution)/shard_map/ppermute | solution.py:42
  125.9 26.4 %collective-permute-start.28 = (bf16[256,1024]{1,0:T(8,128)(2,1)S(1)}, bf16[256,1024]{1,0:T(8,128)(2,1)S(1)}, u32[]{:S(2)}, u32[]{:S(2)}) collective-permute-start(bf16[256,1024]{1,0:T(8,128)(2,1)S(1)} %bitcast.226), channel_id=1, source_target_pairs={{0,2},{1,3},{2,0},{3,1},{4,6},{5,7},{6,4},{7,5},{8,10},{9,11},{10,... | collective-permute-start | bytes 1572872 | tf_op jit(solution)/shard_map/ppermute | solution.py:42
  133.6 18.7 %collective-permute-start.24 = (bf16[256,1024]{1,0:T(8,128)(2,1)S(1)}, bf16[256,1024]{1,0:T(8,128)(2,1)S(1)}, u32[]{:S(2)}, u32[]{:S(2)}) collective-permute-start(bf16[256,1024]{1,0:T(8,128)(2,1)S(1)} %get-tuple-element.672), channel_id=1, source_target_pairs={{0,8},{4,12},{8,0},{12,4},{16,24},{20,28},{24,16},{28,20},{1,9},{5... | collective-permute-start | bytes 1572872 | tf_op jit(solution)/shard_map/ppermute | solution.py:42
  152.5 25.6 %collective-permute-start.32 = (bf16[256,2048]{1,0:T(8,128)(2,1)S(1)}, bf16[256,2048]{1,0:T(8,128)(2,1)S(1)}, u32[]{:S(2)}, u32[]{:S(2)}) collective-permute-start(bf16[256,2048]{1,0:T(8,128)(2,1)S(1)} %bitcast.213), channel_id=1, source_target_pairs={{0,16},{4,20},{8,24},{12,28},{16,0},{20,4},{24,8},{28,12},{1,17},{... | collective-permute-start | bytes 3145736 | tf_op jit(solution)/shard_map/ppermute | solution.py:42
  154.1 24.0 %collective-permute-start.33 = (bf16[256,2048]{1,0:T(8,128)(2,1)S(1)}, bf16[256,2048]{1,0:T(8,128)(2,1)S(1)}, u32[]{:S(2)}, u32[]{:S(2)}) collective-permute-start(bf16[256,2048]{1,0:T(8,128)(2,1)S(1)} %bitcast.214), channel_id=1, source_target_pairs={{0,4},{4,0},{8,12},{12,8},{16,20},{20,16},{24,28},{28,24},{1,5},{5... | collective-permute-start | bytes 3145736 | tf_op jit(solution)/shard_map/ppermute | solution.py:42
  154.4 25.4 %collective-permute-start.34 = (bf16[512,1024]{1,0:T(8,128)(2,1)S(1)}, bf16[512,1024]{1,0:T(8,128)(2,1)S(1)}, u32[]{:S(2)}, u32[]{:S(2)}) collective-permute-start(bf16[512,1024]{1,0:T(8,128)(2,1)S(1)} %bitcast.216), channel_id=1, source_target_pairs={{0,1},{1,0},{2,3},{3,2},{4,5},{5,4},{6,7},{7,6},{8,9},{9,8},{10,11... | collective-permute-start | bytes 3145736 | tf_op jit(solution)/shard_map/ppermute | solution.py:42
  164.1 15.7 %collective-permute-start.30 = (bf16[128,1024]{1,0:T(8,128)(2,1)S(1)}, bf16[128,1024]{1,0:T(8,128)(2,1)S(1)}, u32[]{:S(2)}, u32[]{:S(2)}) collective-permute-start(bf16[128,1024]{1,0:T(8,128)(2,1)S(1)} %get-tuple-element.705), channel_id=1, source_target_pairs={{0,8},{4,12},{8,0},{12,4},{16,24},{20,28},{24,16},{28,20},{1,9},{5... | collective-permute-start | bytes 786440 | tf_op jit(solution)/shard_map/ppermute | solution.py:42
  164.7 15.2 %collective-permute-start.31 = (bf16[128,1024]{1,0:T(8,128)(2,1)S(1)}, bf16[128,1024]{1,0:T(8,128)(2,1)S(1)}, u32[]{:S(2)}, u32[]{:S(2)}) collective-permute-start(bf16[128,1024]{1,0:T(8,128)(2,1)S(1)} %get-tuple-element.706), channel_id=1, source_target_pairs={{0,8},{4,12},{8,0},{12,4},{16,24},{20,28},{24,16},{28,20},{1,9},{5... | collective-permute-start | bytes 786440 | tf_op jit(solution)/shard_map/ppermute | solution.py:42
  198.7 28.5 %collective-permute-start.41 = (bf16[256,2048]{1,0:T(8,128)(2,1)S(1)}, bf16[256,2048]{1,0:T(8,128)(2,1)S(1)}, u32[]{:S(2)}, u32[]{:S(2)}) collective-permute-start(bf16[256,2048]{1,0:T(8,128)(2,1)S(1)} %get-tuple-element.825), channel_id=1, source_target_pairs={{0,4},{4,0},{8,12},{12,8},{16,20},{20,16},{24,28},{28,24},{1,5},{5... | collective-permute-start | bytes 3145736 | tf_op jit(solution)/shard_map/ppermute | solution.py:42
  199.3 27.8 %collective-permute-start.45 = (bf16[256,2048]{1,0:T(8,128)(2,1)S(1)}, bf16[256,2048]{1,0:T(8,128)(2,1)S(1)}, u32[]{:S(2)}, u32[]{:S(2)}) collective-permute-start(bf16[256,2048]{1,0:T(8,128)(2,1)S(1)} %add_low.5), channel_id=1, source_target_pairs={{0,16},{4,20},{8,24},{12,28},{16,0},{20,4},{24,8},{28,12},{1,17},{... | collective-permute-start | bytes 3145736 | tf_op jit(solution)/shard_map/ppermute | solution.py:42
  200.7 26.5 %collective-permute-start.44 = (bf16[512,1024]{1,0:T(8,128)(2,1)S(1)}, bf16[512,1024]{1,0:T(8,128)(2,1)S(1)}, u32[]{:S(2)}, u32[]{:S(2)}) collective-permute-start(bf16[512,1024]{1,0:T(8,128)(2,1)S(1)} %bitcast.303), channel_id=1, source_target_pairs={{0,1},{1,0},{2,3},{3,2},{4,5},{5,4},{6,7},{7,6},{8,9},{9,8},{10,11... | collective-permute-start | bytes 3145736 | tf_op jit(solution)/shard_map/ppermute | solution.py:42
  229.9 27.8 %collective-permute-start.48 = (bf16[256,2048]{1,0:T(8,128)(2,1)}, bf16[256,2048]{1,0:T(8,128)(2,1)S(1)}, u32[]{:S(2)}, u32[]{:S(2)}) collective-permute-start(bf16[256,2048]{1,0:T(8,128)(2,1)} %get-tuple-element.892), channel_id=1, source_target_pairs={{0,4},{4,0},{8,12},{12,8},{16,20},{20,16},{24,28},{28,24},{1,5},{5... | collective-permute-start | bytes 3145736 | tf_op jit(solution)/shard_map/ppermute | solution.py:42
  230.3 27.4 %collective-permute-start.51 = (bf16[256,2048]{1,0:T(8,128)(2,1)S(1)}, bf16[256,2048]{1,0:T(8,128)(2,1)S(1)}, u32[]{:S(2)}, u32[]{:S(2)}) collective-permute-start(bf16[256,2048]{1,0:T(8,128)(2,1)S(1)} %add_low.6), channel_id=1, source_target_pairs={{0,16},{4,20},{8,24},{12,28},{16,0},{20,4},{24,8},{28,12},{1,17},{... | collective-permute-start | bytes 3145736 | tf_op jit(solution)/shard_map/ppermute | solution.py:42
  231.8 25.8 %collective-permute-start.49 = (bf16[256,1024]{1,0:T(8,128)(2,1)S(1)}, bf16[256,1024]{1,0:T(8,128)(2,1)S(1)}, u32[]{:S(2)}, u32[]{:S(2)}) collective-permute-start(bf16[256,1024]{1,0:T(8,128)(2,1)S(1)} %bitcast.307), channel_id=1, source_target_pairs={{0,2},{1,3},{2,0},{3,1},{4,6},{5,7},{6,4},{7,5},{8,10},{9,11},{10,... | collective-permute-start | bytes 1572872 | tf_op jit(solution)/shard_map/ppermute | solution.py:42
  233.9 23.8 %collective-permute-start.50 = (bf16[128,2048]{1,0:T(8,128)(2,1)S(1)}, bf16[128,2048]{1,0:T(8,128)(2,1)S(1)}, u32[]{:S(2)}, u32[]{:S(2)}) collective-permute-start(bf16[128,2048]{1,0:T(8,128)(2,1)S(1)} %bitcast.308), channel_id=1, source_target_pairs={{0,1},{1,0},{2,3},{3,2},{4,5},{5,4},{6,7},{7,6},{8,9},{9,8},{10,11... | collective-permute-start | bytes 1572872 | tf_op jit(solution)/shard_map/ppermute | solution.py:42
  261.6 34.7 %collective-permute-start.59 = (bf16[512,1024]{1,0:T(8,128)(2,1)S(1)}, bf16[512,1024]{1,0:T(8,128)(2,1)S(1)}, u32[]{:S(2)}, u32[]{:S(2)}) collective-permute-start(bf16[512,1024]{1,0:T(8,128)(2,1)S(1)} %add_low.7), channel_id=1, source_target_pairs={{0,16},{4,20},{8,24},{12,28},{16,0},{20,4},{24,8},{28,12},{1,17},{... | collective-permute-start | bytes 3145736 | tf_op jit(solution)/shard_map/ppermute | solution.py:42
  264.9 28.5 %collective-permute-start.61 = (bf16[128,2048]{1,0:T(8,128)(2,1)S(1)}, bf16[128,2048]{1,0:T(8,128)(2,1)S(1)}, u32[]{:S(2)}, u32[]{:S(2)}) collective-permute-start(bf16[128,2048]{1,0:T(8,128)(2,1)S(1)} %bitcast.305), channel_id=1, source_target_pairs={{0,1},{1,0},{2,3},{3,2},{4,5},{5,4},{6,7},{7,6},{8,9},{9,8},{10,11... | collective-permute-start | bytes 1572872 | tf_op jit(solution)/shard_map/ppermute | solution.py:42
  265.6 28.7 %collective-permute-start.58 = (bf16[256,1024]{1,0:T(8,128)(2,1)S(1)}, bf16[256,1024]{1,0:T(8,128)(2,1)S(1)}, u32[]{:S(2)}, u32[]{:S(2)}) collective-permute-start(bf16[256,1024]{1,0:T(8,128)(2,1)S(1)} %get-tuple-element.963), channel_id=1, source_target_pairs={{0,4},{4,0},{8,12},{12,8},{16,20},{20,16},{24,28},{28,24},{1,5},{5... | collective-permute-start | bytes 1572872 | tf_op jit(solution)/shard_map/ppermute | solution.py:42
  265.8 29.6 %collective-permute-start.62 = (bf16[256,1024]{1,0:T(8,128)(2,1)S(1)}, bf16[256,1024]{1,0:T(8,128)(2,1)S(1)}, u32[]{:S(2)}, u32[]{:S(2)}) collective-permute-start(bf16[256,1024]{1,0:T(8,128)(2,1)S(1)} %bitcast.306), channel_id=1, source_target_pairs={{0,1},{1,0},{2,3},{3,2},{4,5},{5,4},{6,7},{7,6},{8,9},{9,8},{10,11... | collective-permute-start | bytes 1572872 | tf_op jit(solution)/shard_map/ppermute | solution.py:42
  276.9 19.4 %collective-permute-start.60 = (bf16[64,2048]{1,0:T(8,128)(2,1)S(1)}, bf16[64,2048]{1,0:T(8,128)(2,1)S(1)}, u32[]{:S(2)}, u32[]{:S(2)}) collective-permute-start(bf16[64,2048]{1,0:T(8,128)(2,1)S(1)} %bitcast.311), channel_id=1, source_target_pairs={{0,2},{1,3},{2,0},{3,1},{4,6},{5,7},{6,4},{7,5},{8,10},{9,11},{10,... | collective-permute-start | bytes 786440 | tf_op jit(solution)/shard_map/ppermute | solution.py:42
  299.4 35.8 %collective-permute-start.69 = (bf16[256,2048]{1,0:T(8,128)(2,1)S(1)}, bf16[256,2048]{1,0:T(8,128)(2,1)}, u32[]{:S(2)}, u32[]{:S(2)}) collective-permute-start(bf16[256,2048]{1,0:T(8,128)(2,1)S(1)} %add_low.9), channel_id=1, source_target_pairs={{0,16},{4,20},{8,24},{12,28},{16,0},{20,4},{24,8},{28,12},{1,17},{... | collective-permute-start | bytes 3145736 | tf_op jit(solution)/shard_map/ppermute | solution.py:42
  300.2 22.6 %collective-permute-start.63 = (bf16[256,1024]{1,0:T(8,128)(2,1)}, bf16[256,1024]{1,0:T(8,128)(2,1)}, u32[]{:S(2)}, u32[]{:S(2)}) collective-permute-start(bf16[256,1024]{1,0:T(8,128)(2,1)} %get-tuple-element.972), channel_id=1, source_target_pairs={{0,8},{4,12},{8,0},{12,4},{16,24},{20,28},{24,16},{28,20},{1,9},{5... | collective-permute-start | bytes 1572872 | tf_op jit(solution)/shard_map/ppermute | solution.py:42
  303.6 22.2 %collective-permute-start.68 = (bf16[256,1024]{1,0:T(8,128)(2,1)}, bf16[256,1024]{1,0:T(8,128)(2,1)}, u32[]{:S(2)}, u32[]{:S(2)}) collective-permute-start(bf16[256,1024]{1,0:T(8,128)(2,1)} %bitcast.110), channel_id=1, source_target_pairs={{0,1},{1,0},{2,3},{3,2},{4,5},{5,4},{6,7},{7,6},{8,9},{9,8},{10,11... | collective-permute-start | bytes 1572872 | tf_op jit(solution)/shard_map/ppermute | solution.py:42
  306.8 15.9 %collective-permute-start.64 = (bf16[128,1024]{1,0:T(8,128)(2,1)S(1)}, bf16[128,1024]{1,0:T(8,128)(2,1)S(1)}, u32[]{:S(2)}, u32[]{:S(2)}) collective-permute-start(bf16[128,1024]{1,0:T(8,128)(2,1)S(1)} %bitcast.315), channel_id=1, source_target_pairs={{0,2},{1,3},{2,0},{3,1},{4,6},{5,7},{6,4},{7,5},{8,10},{9,11},{10,... | collective-permute-start | bytes 786440 | tf_op jit(solution)/shard_map/ppermute | solution.py:42
  309.6 22.9 %collective-permute-start.67 = (bf16[64,2048]{1,0:T(8,128)(2,1)S(1)}, bf16[64,2048]{1,0:T(8,128)(2,1)S(1)}, u32[]{:S(2)}, u32[]{:S(2)}) collective-permute-start(bf16[64,2048]{1,0:T(8,128)(2,1)S(1)} %bitcast.314), channel_id=1, source_target_pairs={{0,2},{1,3},{2,0},{3,1},{4,6},{5,7},{6,4},{7,5},{8,10},{9,11},{10,... | collective-permute-start | bytes 786440 | tf_op jit(solution)/shard_map/ppermute | solution.py:42
  340.5 16.6 %collective-permute-start.71 = (bf16[256,1024]{1,0:T(8,128)(2,1)S(1)}, bf16[256,1024]{1,0:T(8,128)(2,1)S(1)}, u32[]{:S(2)}, u32[]{:S(2)}) collective-permute-start(bf16[256,1024]{1,0:T(8,128)(2,1)S(1)} %copy-done.43), channel_id=1, source_target_pairs={{0,16},{4,20},{8,24},{12,28},{16,0},{20,4},{24,8},{28,12},{1,17},{... | collective-permute-start | bytes 1572872 | tf_op jit(solution)/shard_map/ppermute | solution.py:42
  341.9 17.4 %collective-permute-start.72 = (bf16[128,2048]{1,0:T(8,128)(2,1)S(1)}, bf16[128,2048]{1,0:T(8,128)(2,1)S(1)}, u32[]{:S(2)}, u32[]{:S(2)}) collective-permute-start(bf16[128,2048]{1,0:T(8,128)(2,1)S(1)} %bitcast.304), channel_id=1, source_target_pairs={{0,1},{1,0},{2,3},{3,2},{4,5},{5,4},{6,7},{7,6},{8,9},{9,8},{10,11... | collective-permute-start | bytes 1572872 | tf_op jit(solution)/shard_map/ppermute | solution.py:42
  341.9 15.2 %collective-permute-start.73 = (bf16[128,1024]{1,0:T(8,128)(2,1)S(1)}, bf16[128,1024]{1,0:T(8,128)(2,1)S(1)}, u32[]{:S(2)}, u32[]{:S(2)}) collective-permute-start(bf16[128,1024]{1,0:T(8,128)(2,1)S(1)} %bitcast.310), channel_id=1, source_target_pairs={{0,2},{1,3},{2,0},{3,1},{4,6},{5,7},{6,4},{7,5},{8,10},{9,11},{10,... | collective-permute-start | bytes 786440 | tf_op jit(solution)/shard_map/ppermute | solution.py:42
  359.3 17.4 %collective-permute-start.75 = (bf16[256,1024]{1,0:T(8,128)(2,1)S(1)}, bf16[256,1024]{1,0:T(8,128)(2,1)S(1)}, u32[]{:S(2)}, u32[]{:S(2)}) collective-permute-start(bf16[256,1024]{1,0:T(8,128)(2,1)S(1)} %get-tuple-element.1070), channel_id=1, source_target_pairs={{0,8},{4,12},{8,0},{12,4},{16,24},{20,28},{24,16},{28,20},{1,9},{5... | collective-permute-start | bytes 1572872 | tf_op jit(solution)/shard_map/ppermute | solution.py:42
  (114 other events, 972.4 us)

commit v6 on v5

--- a/solution.py
+++ b/solution.py
@@ -99,9 +99,8 @@
     return [part.reshape(-1, n) for part in result]
 
 
-def prepare_kernel(side, big, table, first, first_sent, up0, up0_sent, after, after_sent, out, sems):
+def prepare_kernel(span, chunk, side, big, table, first, first_sent, up0, up0_sent, after, after_sent, out, sems):
     width = out.shape[-1] * 2
-    span, chunk = first.shape[1] // 6 // 128 * 128, up0.shape[1] // 2
     third = 3 * width
     copies = []
     for layer, qkv, up in ((0, (first, first_sent), (up0, up0_sent)), (1, (after, after_sent), (after, after_sent))):
@@ -110,7 +109,7 @@
                 at = pl.multiple_of((2 * n + x) * span, 128)
                 copies.append((big.at[layer, :, pl.ds(at, span)], target.at[:, pl.ds(n * span, span)]))
             base = 0 if layer == 0 else third // 2
-            for n in range(2):
+            for n in range(up0.shape[1] // chunk):
                 at = pl.multiple_of(4 * width + (2 * n + x) * chunk, 128)
                 copies.append((big.at[layer, :, pl.ds(at, chunk)], upper.at[:, pl.ds(base + n * chunk, chunk)]))
         for k in range(2):
@@ -689,14 +688,16 @@
     total = (grad.shape[-1] - 8 * third) // 2
     late = total - (keep.shape[1] - part)
     m, v = refs[2:4] if late else refs[:2]
-    pieces = [(keep, other, 0, 0, part, span), (keep, other, part, 8 * third + 2 * late, total - late, chunk)]
+    pieces = [(keep, other, 0, 0, 0, part, span), (keep, other, part, 8 * third, late, total - late, chunk)]
     if late:
-        pieces.append((refs[0], refs[1], 0, 8 * third, late, chunk))
-    for one, two, first, base, count, width in pieces:
+        pieces.append((refs[0], refs[1], 0, 8 * third, 0, late, chunk))
+    for one, two, first, base, start, count, width in pieces:
+        each = math.gcd(math.gcd(width, start), count)
         for source, x in ((one, side[0]), (two, 1 - side[0])):
-            for n in range(count // width):
-                at = pl.multiple_of(base + (2 * n + x) * width, 128)
-                grad[0, :, pl.ds(at, width)] = source[:, pl.ds(first + n * width, width)]
+            for n in range(count // each):
+                block, inside = divmod(start + n * each, width)
+                at = pl.multiple_of(base + (2 * block + x) * width + inside, 128)
+                grad[0, :, pl.ds(at, each)] = source[:, pl.ds(first + n * each, each)]
     for k in range(2):
         grad[0, :, pl.ds((6 + k) * third, third)] = out[k]
     for n in range(grad.shape[2] // 1024):
@@ -772,6 +773,7 @@
 
     quarter = ((width // 4, 2 * width), bf16)
     gain_row = ((1, width), f32)
+    up_first = feed // 2 - feed // 8
     place = jnp.stack([mine(sl.high[0]), mine(CORE)])
     w_attn = pltpu.VMEM((width, 2 * width), bf16)
     w_upper = pltpu.VMEM((width, feed // 2), bf16)
@@ -790,11 +792,11 @@
         shapes.append((2, 2, rows, half))
         if rows % 16 == 0:
             return call(
-                prepare_kernel,
+                partial(prepare_kernel, 2 * block, 2 * fsdp * feeds),
                 [(shape, bf16) for shape in shapes],
                 [mine(SIDE)[None], w_big, table_part],
                 [SMEM, ANY, ANY],
-                [dma(2 * (6 * high + 6) + 2)],
+                [dma(2 * (2 * 3 * high + 2 * high + 2) + 2)],
                 name="prepare",
             )
         first = [jnp.concatenate([v, table_part], -1) for v in qkv_sides(0)]
@@ -892,13 +894,13 @@
         for flow, flow.air in zip(made, airs):
             pass
 
-    def gains_of(quarters, sections):
+    def gains_of(flow, sections):
         wide = norm_table.shape[1]
         if wide == 128:
             return call(
                 partial(gains_kernel, lead, count, rows),
                 2 * [((2, 4 * width), f32)],
-                [place, sections, *quarters],
+                [place, sections, *pinned(flow)],
                 [SMEM, SMEM] + [ANY] * 4,
                 [
                     pltpu.VMEM((4, width // 4, 128), bf16),
@@ -907,7 +909,7 @@
                 ],
                 name="gains",
             )
-        parts = jnp.stack([q[:, 2 * width :] for q in quarters])
+        parts = jnp.stack([q[:, 2 * width :] for q in flow.quarters])
         parts = parts.reshape(4, lead // 2, 2, fsdp, rows * 128)[..., : count * wide]
         parts = parts.reshape(4, lead // 2, 2, fsdp, count, wide)
         pick = jnp.concatenate([jnp.zeros((2,), jnp.int32), 1 + sections])
@@ -916,6 +918,12 @@
         own, top, core, both = picked
         both = merge(merge(own, core, CORE, 3), merge(top, both, CORE, 3), sl.high[0], 1)
         return list(both.reshape(2, 2, 4 * width))
+
+    def pinned(flow):
+        own, top, core, both = flow.quarters
+        if flow is downs[0]:
+            both = pltpu.with_memory_space_constraint(both, pltpu.HBM)
+        return [own, top, pltpu.with_memory_space_constraint(core, pltpu.HBM), both]
 
     def cross():
         live.put(other=[sl.flip(row, SIDE) for row in live.low])
@@ -932,7 +940,7 @@
                 attns[layer].place,
                 *parts,
                 live.gains[layer],
-                *attns[layer].quarters,
+                *pinned(attns[layer]),
                 live.allows[layer],
             ],
             [SMEM] + [VMEM] * (len(parts) + 1) + [ANY] * 4 + [VMEM],
@@ -952,8 +960,8 @@
                 live.values[f"attn{layer}"][0],
                 *shares(),
                 live.gains[layer],
-                *ups[layer].quarters,
-                *downs[layer].quarters,
+                *pinned(ups[layer]),
+                *pinned(downs[layer]),
             ],
             [SMEM, SMEM] + [VMEM] * (3 + len(live.other)) + [ANY] * 8,
             [w_upper, w_lower, dma(4 * lead), dma(2 * lead)],
@@ -975,8 +983,8 @@
                 *shares(),
                 live.gains[layer],
                 live.d_low,
-                *ups[layer].quarters,
-                *downs[layer].quarters,
+                *pinned(ups[layer]),
+                *pinned(downs[layer]),
             ],
             [SMEM] * 3 + [VMEM] * (4 + len(live.other)) + [ANY] * 8,
             [w_upper, w_lower, pltpu.VMEM(wide_b[0], f32), dma(4 * lead), dma(2 * lead)],
@@ -988,7 +996,7 @@
         keep, *low = call(
             partial(down_kernel, lead // 2),
             [two_f, *lows(1)],
-            [downs[layer].place, live.values[f"feed{layer}"][3], *downs[layer].quarters],
+            [downs[layer].place, live.values[f"feed{layer}"][3], *pinned(downs[layer])],
             [SMEM, VMEM, ANY, ANY, ANY, ANY],
             [w_lower, dma(2 * lead)],
             name="down",
@@ -1007,8 +1015,8 @@
                 live.values[f"attn{layer + 1}"][0],
                 live.gains[layer + 1],
                 live.values[f"feed{layer}"][2],
-                *ups[layer].quarters,
-                *downs[layer].quarters,
+                *pinned(ups[layer]),
+                *pinned(downs[layer]),
             ],
             [SMEM, SMEM] + [VMEM] * (5 + len(live.other)) + [ANY] * 8,
             [w_upper, w_lower, dma(4 * lead), dma(2 * lead)],
@@ -1034,8 +1042,8 @@
         second, right = live.values[f"feed{layer}"][1], live.d_pre
         columns = feed // 2
         if piece is not None:
-            columns = feed // 4
-            right = right[:, piece * columns : (piece + 1) * columns]
+            right = right[:, :up_first] if piece == 0 else right[:, up_first:]
+            columns = right.shape[1]
         parts = call(
             partial(weight_grad_kernel, lead, aligned),
             [((width // 4, columns), bf16)] * 4,
@@ -1072,7 +1080,7 @@
                 *shares(),
                 live.values[f"feed{layer}"][0],
                 live.gains[layer],
-                *attns[layer].quarters,
+                *pinned(attns[layer]),
                 live.allows[layer],
                 live.values[f"attn{layer}"][2],
             ],
@@ -1151,7 +1159,7 @@
     attns[1].start()
     ups[1].start()
     attns[0].finish()
-    live.put(gains=gains_of(attns[0].quarters, live.sections))
+    live.put(gains=gains_of(attns[0], live.sections))
     attend(0, live.hidden, 1)
     cross()
     live.seal(ups[0], attns[1], ups[1])
@@ -1245,14 +1253,15 @@
 
     g_up0a.start()
     out_act = live.feed1[0][:length] + (live.keep[:length] + live.other[0][length:].astype(f32))
-    big0 = two_sides([g_attn0, g_up0b], [2 * width, feed // 4], [part, feed // 4])
+    rest = feed // 2 - up_first
+    big0 = two_sides([g_attn0, g_up0b], [2 * width, rest], [part, rest])
     table_step(0, sl.high)
     table_step(-3, sl.deep[-1:])
     live.put(out_act=out_act.astype(bf16), down=finish_down(1, g_down1, live.down), big0=big0)
     live.seal(g_up0a)
 
     table_step(0, sl.deep[:-1])
-    up0a = two_sides([g_up0a], [feed // 4], [feed // 4])
+    up0a = two_sides([g_up0a], [up_first], [up_first])
     grad_big, new_m_big, step_big = finish(0, live.big0, live.big, up0a)
     grad_down, new_m_down, step_down = live.down
     grad_table = live.table

time: 398 us -> 395 us (level)
  local copies, waits for them, and re-layouts: 21.6 us -> 15 us
  waiting for transfers between devices: 189 us -> 185 us
    unnamed x151 -> x139, local copies, waits for them, and re-layouts: 18.7 us -> 12 us
  transfers between devices with their start and end apart: 87 -> 87, of which waited for: 44 -> 42; matrix products, arithmetic and copies ran while one was open for 2% -> 3% of each run, Pallas kernels for 21% -> 22%
where the time goes in v6:
time: 395 us; the launch traced here: 392 us
  waiting for transfers between devices  185 us (47%)
  Pallas kernels  96.9 us (25%)
  starting transfers between devices  82.8 us (21%)
  local copies, waits for them, and re-layouts  15 us (4%)
  other arithmetic  9.03 us (2%)
    ppermute x87, waiting for transfers between devices, flip(): lax.ppermute(value, axis, [(i, i ^ mask) for i in range(self.size[axis])])  185 us
    pallas_call x53, Pallas kernels, call(): pl.pallas_call(kernel, out_shape=[jax.ShapeDtypeStruct(shape, kind) for s...  89.4 us
    ppermute x87, starting transfers between devices, flip(): lax.ppermute(value, axis, [(i, i ^ mask) for i in range(self.size[axis])])  82.8 us
    unnamed x139, local copies, waits for them, and re-layouts  12 us
  transfers between devices with their start and end apart: 87, of which 42 were waited for; matrix products, arithmetic and copies ran while one was open for 3% of the time, Pallas kernels for 22%

profile of v6, /device:TPU:0, one launch (start us, length us, event | category | flops | bytes accessed | tf_op | source)
XLA Modules:
  0.0 391.7 jit_solution(6228217371563383106)
XLA Ops:
  1.9 4.1 %collective-permute-start.1 = (bf16[128,1024]{1,0:T(8,128)(2,1)S(1)}, bf16[128,1024]{1,0:T(8,128)(2,1)S(1)}, u32[]{:S(2)}, u32[]{:S(2)}) collective-permute-start(bf16[128,1024]{1,0:T(8,128)(2,1)S(1)} %get-tuple-element.592), channel_id=1, source_target_pairs={{0,2},{1,3},{2,0},{3,1},{4,6},{5,7},{6,4},{7,5},{8,10},{9,11},{10,... | collective-permute-start | bytes 786440 | tf_op jit(solution)/shard_map/ppermute | solution.py:42
  13.1 4.8 %collective-permute-done.1 = bf16[128,1024]{1,0:T(8,128)(2,1)S(1)} collective-permute-done((bf16[128,1024]{1,0:T(8,128)(2,1)S(1)}, bf16[128,1024]{1,0:T(8,128)(2,1)S(1)}, u32[]{:S(2)}, u32[]{:S(2)}) %collective-permute-start.1) | collective-permute-done | bytes 262176 | tf_op jit(solution)/shard_map/ppermute | solution.py:42
  18.7 3.4 collective-permute-start.6
  25.0 8.8 %collective-permute-done.5 = bf16[32,2048]{1,0:T(8,128)(2,1)S(1)} collective-permute-done((bf16[32,2048]{1,0:T(8,128)(2,1)S(1)}, bf16[32,2048]{1,0:T(8,128)(2,1)S(1)}, u32[]{:S(2)}, u32[]{:S(2)}) %collective-permute-start.5) | collective-permute-done | bytes 131104 | tf_op jit(solution)/shard_map/ppermute | solution.py:42
  33.9 2.2 collective-permute-done.6
  38.6 3.4 collective-permute-start.8
  44.7 2.1 fusion
  47.7 12.4 %collective-permute-done.9 = bf16[64,2048]{1,0:T(8,128)(2,1)S(1)} collective-permute-done((bf16[64,2048]{1,0:T(8,128)(2,1)S(1)}, bf16[64,2048]{1,0:T(8,128)(2,1)S(1)}, u32[]{:S(2)}, u32[]{:S(2)}) %collective-permute-start.9) | collective-permute-done | bytes 262176 | tf_op jit(solution)/shard_map/ppermute | solution.py:42
  63.5 4.5 %collective-permute-start.15 = (bf16[128,2048]{1,0:T(8,128)(2,1)S(1)}, bf16[128,2048]{1,0:T(8,128)(2,1)S(1)}, u32[]{:S(2)}, u32[]{:S(2)}) collective-permute-start(bf16[128,2048]{1,0:T(8,128)(2,1)S(1)} %bitcast.234), channel_id=1, source_target_pairs={{0,1},{1,0},{2,3},{3,2},{4,5},{5,4},{6,7},{7,6},{8,9},{9,8},{10,11... | collective-permute-start | bytes 1572872 | tf_op jit(solution)/shard_map/ppermute | solution.py:42
  70.2 14.8 %collective-permute-done.16 = bf16[64,2048]{1,0:T(8,128)(2,1)S(1)} collective-permute-done((bf16[64,2048]{1,0:T(8,128)(2,1)S(1)}, bf16[64,2048]{1,0:T(8,128)(2,1)S(1)}, u32[]{:S(2)}, u32[]{:S(2)}) %collective-permute-start.16) | collective-permute-done | bytes 262176 | tf_op jit(solution)/shard_map/ppermute | solution.py:42
  85.7 2.6 collective-permute-done.13.q1.refs_3_.refs_8_
  92.1 3.7 collective-permute-start.21
  97.4 9.9 %attend.2 = (f32[256,1024]{1,0:T(8,128)}, bf16[256,1024]{1,0:T(8,128)(2,1)S(1)}, bf16[256,1536]{1,0:T(8,128)(2,1)S(1)}, bf16[256,512]{1,0:T(8,128)(2,1)S(1)}, f3...) custom-call(s32[2]{0:T(128)S(1)} %pad_add_fusion.place.up_place.dn_place, ...), custom_call_target="tpu_custom_call" | custom-call | tf_op jit(solution)/shard_map/attend/pallas_call | solution.py:54
  109.9 13.2 %collective-permute-done.22 = bf16[64,2048]{1,0:T(8,128)(2,1)S(1)} collective-permute-done((bf16[64,2048]{1,0:T(8,128)(2,1)S(1)}, bf16[64,2048]{1,0:T(8,128)(2,1)S(1)}, u32[]{:S(2)}, u32[]{:S(2)}) %collective-permute-start.22) | collective-permute-done | bytes 262176 | tf_op jit(solution)/shard_map/ppermute | solution.py:42
  124.2 2.1 collective-permute-start.28
  126.3 5.5 %feed.1 = (f32[256,1024]{1,0:T(8,128)S(1)}, bf16[256,1024]{1,0:T(8,128)(2,1)S(1)}, f32[256,2048]{1,0:T(8,128)S(1)}, bf16[256,2048]{1,0:T(8,128)(2,1)S(1)}, f32[2...) custom-call(s32[2]{0:T(128)S(1)} %pad_add_fusion.place.up_place.dn_place, s32[2]{0:T(128)S(1)} %pad_add_fusion.place.up_place.dn_place, ...), custom_call_target="tpu_custom_call" | custom-call | tf_op jit(solution)/shard_map/feed/pallas_call | solution.py:54
  132.4 15.9 %collective-permute-done.27 = bf16[128,2048]{1,0:T(8,128)(2,1)S(1)} collective-permute-done((bf16[128,2048]{1,0:T(8,128)(2,1)S(1)}, bf16[128,2048]{1,0:T(8,128)(2,1)S(1)}, u32[]{:S(2)}, u32[]{:S(2)}) %collective-permute-start.27) | collective-permute-done | bytes 524320 | tf_op jit(solution)/shard_map/ppermute | solution.py:42
  148.3 2.5 collective-permute-done.28
  153.5 8.8 %attend.3 = (f32[256,1024]{1,0:T(8,128)S(1)}, bf16[256,1024]{1,0:T(8,128)(2,1)S(1)}, bf16[256,1536]{1,0:T(8,128)(2,1)S(1)}, bf16[256,512]{1,0:T(8,128)(2,1)S(1)}...) custom-call(s32[2]{0:T(128)S(1)} %pad_add_fusion.place.up_place.dn_place, ...), custom_call_target="tpu_custom_call" | custom-call | tf_op jit(solution)/shard_map/attend/pallas_call | solution.py:54
  164.4 12.1 %collective-permute-done.32.refs_7_ = bf16[256,2048]{1,0:T(8,128)(2,1)S(1)} collective-permute-done((bf16[256,2048]{1,0:T(8,128)(2,1)S(1)}, bf16[256,2048]{1,0:T(8,128)(2,1)S(1)}, u32[]{:S(2)}, u32[]{:S(2)}) %collective-permute-start.32) | collective-permute-done | bytes 1048608 | tf_op jit(solution)/shard_map/ppermute | solution.py:42
  183.8 6.5 %feed_turn.1 = (f32[256,1024]{1,0:T(8,128)S(1)}, bf16[256,1024]{1,0:T(8,128)(2,1)S(1)}, bf16[256,2048]{1,0:T(8,128)(2,1)S(1)}, bf16[256,2048]{1,0:T(8,128)(2,1)S...) custom-call(s32[2]{0:T(128)S(1)} %pad_add_fusion.place.up_place.dn_place, ...), custom_call_target="tpu_custom_call" | custom-call | tf_op jit(solution)/shard_map/feed_turn/pallas_call | solution.py:54
  190.4 1.8 down_grad.2
  192.4 1.8 up_grad.3
  195.1 1.9 collective-permute-done.40.two
  201.4 7.1 %collective-permute-done.38.refs_4_ = bf16[128,1024]{1,0:T(8,128)(2,1)S(1)} collective-permute-done((bf16[128,1024]{1,0:T(8,128)(2,1)S(1)}, bf16[128,1024]{1,0:T(8,128)(2,1)S(1)}, u32[]{:S(2)}, u32[]{:S(2)}) %collective-permute-start.38) | collective-permute-done | bytes 262176 | tf_op jit(solution)/shard_map/ppermute | solution.py:42
  208.5 4.8 %collective-permute-done.39.refs_5_ = bf16[128,1024]{1,0:T(8,128)(2,1)S(1)} collective-permute-done((bf16[128,1024]{1,0:T(8,128)(2,1)S(1)}, bf16[128,1024]{1,0:T(8,128)(2,1)S(1)}, u32[]{:S(2)}, u32[]{:S(2)}) %collective-permute-start.39) | collective-permute-done | bytes 262176 | tf_op jit(solution)/shard_map/ppermute | solution.py:42
  213.3 12.0 %attend_back.2 = (f32[256,1024]{1,0:T(8,128)S(1)}, bf16[256,1024]{1,0:T(8,128)(2,1)}, f32[1,1024]{1,0:T(1,128)S(1)}, f32[1,1024]{1,0:T(1,128)S(1)}, bf16[256,153...) custom-call(s32[2]{0:T(128)S(1)} %pad_add_fusion.place.up_place.dn_p, ...), custom_call_target="tpu_custom_call" | custom-call | tf_op jit(solution)/shard_map/attend_back/pallas_call | solution.py:54
  225.5 2.6 collective-permute-done.47.two
  232.5 10.7 %collective-permute-done.46.refs_0_ = bf16[256,1024]{1,0:T(8,128)(2,1)S(1)} collective-permute-done((bf16[256,1024]{1,0:T(8,128)(2,1)S(1)}, bf16[256,1024]{1,0:T(8,128)(2,1)S(1)}, u32[]{:S(2)}, u32[]{:S(2)}) %collective-permute-start.46) | collective-permute-done | bytes 524320 | tf_op jit(solution)/shard_map/ppermute | solution.py:42
  243.2 6.5 %feed_back.1 = (f32[256,1024]{1,0:T(8,128)S(1)}, bf16[256,1024]{1,0:T(8,128)(2,1)S(1)}, f32[1,1024]{1,0:T(1,128)S(1)}, f32[1,1024]{1,0:T(1,128)S(1)}, bf16[256,2...) custom-call(s32[2]{0:T(128)S(1)} %pad_add_fusion.place.up_place.dn_place, ...), custom_call_target="tpu_custom_call" | custom-call | tf_op jit(solution)/shard_map/feed_back/pallas_call | solution.py:54
  252.4 1.8 down_grad.3
  256.5 2.1 collective-permute-done.53.two
  266.8 7.7 %collective-permute-done.52.refs_4_ = bf16[256,1024]{1,0:T(8,128)(2,1)S(1)} collective-permute-done((bf16[256,1024]{1,0:T(8,128)(2,1)S(1)}, bf16[256,1024]{1,0:T(8,128)(2,1)S(1)}, u32[]{:S(2)}, u32[]{:S(2)}) %collective-permute-start.52) | collective-permute-done | bytes 524320 | tf_op jit(solution)/shard_map/ppermute | solution.py:42
  276.3 13.5 %attend_back.3 = (f32[256,1024]{1,0:T(8,128)S(1)}, bf16[256,1024]{1,0:T(8,128)(2,1)}, f32[1,1024]{1,0:T(1,128)S(1)}, f32[1,1024]{1,0:T(1,128)S(1)}, bf16[256,153...) custom-call(s32[2]{0:T(128)S(1)} %pad_add_fusion.place.up_place.dn_p, ...), custom_call_target="tpu_custom_call" | custom-call | tf_op jit(solution)/shard_map/attend_back/pallas_call | solution.py:54
  292.2 2.6 collective-permute-done.65.two
  304.7 2.0 collective-permute-start.67
  307.8 8.0 %collective-permute-done.64 = bf16[128,512]{1,0:T(8,128)(2,1)S(1)} collective-permute-done((bf16[128,512]{1,0:T(8,128)(2,1)S(1)}, bf16[128,512]{1,0:T(8,128)(2,1)S(1)}, u32[]{:S(2)}, u32[]{:S(2)}) %collective-permute-start.64) | collective-permute-done | bytes 131104 | tf_op jit(solution)/shard_map/ppermute | solution.py:42
  315.8 6.0 %collective-permute-done.68 = bf16[256,1024]{1,0:T(8,128)(2,1)} collective-permute-done((bf16[256,1024]{1,0:T(8,128)(2,1)}, bf16[256,1024]{1,0:T(8,128)(2,1)}, u32[]{:S(2)}, u32[]{:S(2)}) %collective-permute-start.68) | collective-permute-done | bytes 524320 | tf_op jit(solution)/shard_map/ppermute | solution.py:42
  321.9 2.8 norm_back.1
  334.5 3.6 down.1
  339.1 2.4 finish.2
  341.5 8.5 %collective-permute-done.74 = bf16[64,512]{1,0:T(8,128)(2,1)S(1)} collective-permute-done((bf16[64,512]{1,0:T(8,128)(2,1)S(1)}, bf16[64,512]{1,0:T(8,128)(2,1)S(1)}, u32[]{:S(2)}, u32[]{:S(2)}) %collective-permute-start.74) | collective-permute-done | bytes 65568 | tf_op jit(solution)/shard_map/ppermute | solution.py:42
  357.6 5.1 %collective-permute-done.77 = f32[2,4,9,128]{3,1,2,0:T(4,128)S(1)} collective-permute-done((f32[2,4,9,128]{3,1,2,0:T(4,128)S(1)}, f32[2,4,9,128]{3,1,2,0:T(4,128)S(1)}, u32[]{:S(2)}, u32[]{:S(2)}) %collective-permute-start.77) | collective-permute-done | bytes 36896 | tf_op jit(solution)/shard_map/ppermute | solution.py:42
  362.7 4.3 %collective-permute-done.79 = bf16[64,2048]{1,0:T(8,128)(2,1)S(1)} collective-permute-done((bf16[64,2048]{1,0:T(8,128)(2,1)S(1)}, bf16[64,2048]{1,0:T(8,128)(2,1)S(1)}, u32[]{:S(2)}, u32[]{:S(2)}) %collective-permute-start.79) | collective-permute-done | bytes 262176 | tf_op jit(solution)/shard_map/ppermute | solution.py:42
  371.3 2.1 collective-permute-start.84
  378.1 4.3 %collective-permute-done.84 = bf16[64,1536]{1,0:T(8,128)(2,1)S(1)} collective-permute-done((bf16[64,1536]{1,0:T(8,128)(2,1)S(1)}, bf16[64,1536]{1,0:T(8,128)(2,1)S(1)}, u32[]{:S(2)}, u32[]{:S(2)}) %collective-permute-start.84) | collective-permute-done | bytes 196640 | tf_op jit(solution)/shard_map/ppermute | solution.py:42
  384.0 3.8 collective-permute-done.86
  389.1 2.4 finish.3
  (378 shorter events, 113.1 us)
Async XLA Ops:
  1.9 16.0 %collective-permute-start.1 = (bf16[128,1024]{1,0:T(8,128)(2,1)S(1)}, bf16[128,1024]{1,0:T(8,128)(2,1)S(1)}, u32[]{:S(2)}, u32[]{:S(2)}) collective-permute-start(bf16[128,1024]{1,0:T(8,128)(2,1)S(1)} %get-tuple-element.592), channel_id=1, source_target_pairs={{0,2},{1,3},{2,0},{3,1},{4,6},{5,7},{6,4},{7,5},{8,10},{9,11},{10,... | collective-permute-start | bytes 786440 | tf_op jit(solution)/shard_map/ppermute | solution.py:42
  12.4 23.6 %collective-permute-start.4 = (bf16[272,1024]{1,0:T(8,128)(2,1)}, bf16[272,1024]{1,0:T(8,128)(2,1)}, u32[]{:S(2)}, u32[]{:S(2)}) collective-permute-start(bf16[272,1024]{1,0:T(8,128)(2,1)} %pad_maximum_fusion), channel_id=1, source_target_pairs={{0,8},{4,12},{8,0},{12,4},{16,24},{20,28},{24,16},{28,20},{1,9},{5... | collective-permute-start | bytes 1671176 | tf_op jit(solution)/shard_map/ppermute | solution.py:42
  17.9 19.1 %collective-permute-start.7 = (bf16[256,1024]{1,0:T(8,128)(2,1)S(1)}, bf16[256,1024]{1,0:T(8,128)(2,1)S(1)}, u32[]{:S(2)}, u32[]{:S(2)}) collective-permute-start(bf16[256,1024]{1,0:T(8,128)(2,1)S(1)} %bitcast.228), channel_id=1, source_target_pairs={{0,1},{1,0},{2,3},{3,2},{4,5},{5,4},{6,7},{7,6},{8,9},{9,8},{10,11... | collective-permute-start | bytes 1572872 | tf_op jit(solution)/shard_map/ppermute | solution.py:42
  18.7 17.3 %collective-permute-start.6 = (bf16[64,2176]{1,0:T(8,128)(2,1)S(1)}, bf16[64,2176]{1,0:T(8,128)(2,1)S(1)}, u32[]{:S(2)}, u32[]{:S(2)}) collective-permute-start(bf16[64,2176]{1,0:T(8,128)(2,1)S(1)} %bitcast.236), channel_id=1, source_target_pairs={{0,2},{1,3},{2,0},{3,1},{4,6},{5,7},{6,4},{7,5},{8,10},{9,11},{10,... | collective-permute-start | bytes 835592 | tf_op jit(solution)/shard_map/ppermute | solution.py:42
  37.2 23.7 %collective-permute-start.10 = (bf16[512,1024]{1,0:T(8,128)(2,1)S(1)}, bf16[512,1024]{1,0:T(8,128)(2,1)S(1)}, u32[]{:S(2)}, u32[]{:S(2)}) collective-permute-start(bf16[512,1024]{1,0:T(8,128)(2,1)S(1)} %bitcast.202), channel_id=1, source_target_pairs={{0,16},{4,20},{8,24},{12,28},{16,0},{20,4},{24,8},{28,12},{1,17},{... | collective-permute-start | bytes 3145736 | tf_op jit(solution)/shard_map/ppermute | solution.py:42
  38.5 22.4 %collective-permute-start.11 = (bf16[512,1024]{1,0:T(8,128)(2,1)S(1)}, bf16[512,1024]{1,0:T(8,128)(2,1)S(1)}, u32[]{:S(2)}, u32[]{:S(2)}) collective-permute-start(bf16[512,1024]{1,0:T(8,128)(2,1)S(1)} %bitcast.203), channel_id=1, source_target_pairs={{0,4},{4,0},{8,12},{12,8},{16,20},{20,16},{24,28},{28,24},{1,5},{5... | collective-permute-start | bytes 3145736 | tf_op jit(solution)/shard_map/ppermute | solution.py:42
  38.6 22.3 %collective-permute-start.8 = (bf16[128,2176]{1,0:T(8,128)(2,1)S(1)}, bf16[128,2176]{1,0:T(8,128)(2,1)S(1)}, u32[]{:S(2)}, u32[]{:S(2)}) collective-permute-start(bf16[128,2176]{1,0:T(8,128)(2,1)S(1)} %bitcast.224), channel_id=1, source_target_pairs={{0,1},{1,0},{2,3},{3,2},{4,5},{5,4},{6,7},{7,6},{8,9},{9,8},{10,11... | collective-permute-start | bytes 1671176 | tf_op jit(solution)/shard_map/ppermute | solution.py:42
  42.0 18.2 %collective-permute-start.9 = (bf16[64,2048]{1,0:T(8,128)(2,1)S(1)}, bf16[64,2048]{1,0:T(8,128)(2,1)S(1)}, u32[]{:S(2)}, u32[]{:S(2)}) collective-permute-start(bf16[64,2048]{1,0:T(8,128)(2,1)S(1)} %bitcast.254), channel_id=1, source_target_pairs={{0,2},{1,3},{2,0},{3,1},{4,6},{5,7},{6,4},{7,5},{8,10},{9,11},{10,... | collective-permute-start | bytes 786440 | tf_op jit(solution)/shard_map/ppermute | solution.py:42
  61.9 26.4 %collective-permute-start.13 = (bf16[256,2176]{1,0:T(8,128)(2,1)S(1)}, bf16[256,2176]{1,0:T(8,128)(2,1)S(1)}, u32[]{:S(2)}, u32[]{:S(2)}) collective-permute-start(bf16[256,2176]{1,0:T(8,128)(2,1)S(1)} %bitcast.197), channel_id=1, source_target_pairs={{0,16},{4,20},{8,24},{12,28},{16,0},{20,4},{24,8},{28,12},{1,17},{... | collective-permute-start | bytes 3342344 | tf_op jit(solution)/shard_map/ppermute | solution.py:42
  63.0 25.3 %collective-permute-start.14 = (bf16[256,2176]{1,0:T(8,128)(2,1)S(1)}, bf16[256,2176]{1,0:T(8,128)(2,1)S(1)}, u32[]{:S(2)}, u32[]{:S(2)}) collective-permute-start(bf16[256,2176]{1,0:T(8,128)(2,1)S(1)} %bitcast.198), channel_id=1, source_target_pairs={{0,4},{4,0},{8,12},{12,8},{16,20},{20,16},{24,28},{28,24},{1,5},{5... | collective-permute-start | bytes 3342344 | tf_op jit(solution)/shard_map/ppermute | solution.py:42
  63.0 22.8 %collective-permute-start.12 = (bf16[512,1024]{1,0:T(8,128)(2,1)S(1)}, bf16[512,1024]{1,0:T(8,128)(2,1)S(1)}, u32[]{:S(2)}, u32[]{:S(2)}) collective-permute-start(bf16[512,1024]{1,0:T(8,128)(2,1)S(1)} %collective-permute-done.10.refs_9_), channel_id=1, source_target_pairs={{0,4},{4,0},{8,12},{12,8},{16,20},{20,16},{24,28},{28,24},{1,5},{5... | collective-permute-start | bytes 3145736 | tf_op jit(solution)/shard_map/ppermute | solution.py:42
  63.5 22.2 %collective-permute-start.15 = (bf16[128,2048]{1,0:T(8,128)(2,1)S(1)}, bf16[128,2048]{1,0:T(8,128)(2,1)S(1)}, u32[]{:S(2)}, u32[]{:S(2)}) collective-permute-start(bf16[128,2048]{1,0:T(8,128)(2,1)S(1)} %bitcast.234), channel_id=1, source_target_pairs={{0,1},{1,0},{2,3},{3,2},{4,5},{5,4},{6,7},{7,6},{8,9},{9,8},{10,11... | collective-permute-start | bytes 1572872 | tf_op jit(solution)/shard_map/ppermute | solution.py:42
  68.8 16.2 %collective-permute-start.16 = (bf16[64,2048]{1,0:T(8,128)(2,1)S(1)}, bf16[64,2048]{1,0:T(8,128)(2,1)S(1)}, u32[]{:S(2)}, u32[]{:S(2)}) collective-permute-start(bf16[64,2048]{1,0:T(8,128)(2,1)S(1)} %bitcast.259), channel_id=1, source_target_pairs={{0,2},{1,3},{2,0},{3,1},{4,6},{5,7},{6,4},{7,5},{8,10},{9,11},{10,... | collective-permute-start | bytes 786440 | tf_op jit(solution)/shard_map/ppermute | solution.py:42
  89.4 33.7 %collective-permute-start.19 = (bf16[256,2048]{1,0:T(8,128)(2,1)}, bf16[256,2048]{1,0:T(8,128)(2,1)}, u32[]{:S(2)}, u32[]{:S(2)}) collective-permute-start(bf16[256,2048]{1,0:T(8,128)(2,1)} %bitcast.46.refs_4_), channel_id=1, source_target_pairs={{0,16},{4,20},{8,24},{12,28},{16,0},{20,4},{24,8},{28,12},{1,17},{... | collective-permute-start | bytes 3145736 | tf_op jit(solution)/shard_map/ppermute | solution.py:42
  90.0 33.2 %collective-permute-start.20 = (bf16[256,2048]{1,0:T(8,128)(2,1)}, bf16[256,2048]{1,0:T(8,128)(2,1)}, u32[]{:S(2)}, u32[]{:S(2)}) collective-permute-start(bf16[256,2048]{1,0:T(8,128)(2,1)} %bitcast.46.refs_4_), channel_id=1, source_target_pairs={{0,4},{4,0},{8,12},{12,8},{16,20},{20,16},{24,28},{28,24},{1,5},{5... | collective-permute-start | bytes 3145736 | tf_op jit(solution)/shard_map/ppermute | solution.py:42
  92.1 31.0 %collective-permute-start.21 = (bf16[128,2048]{1,0:T(8,128)(2,1)S(1)}, bf16[128,2048]{1,0:T(8,128)(2,1)S(1)}, u32[]{:S(2)}, u32[]{:S(2)}) collective-permute-start(bf16[128,2048]{1,0:T(8,128)(2,1)S(1)} %bitcast.230), channel_id=1, source_target_pairs={{0,1},{1,0},{2,3},{3,2},{4,5},{5,4},{6,7},{7,6},{8,9},{9,8},{10,11... | collective-permute-start | bytes 1572872 | tf_op jit(solution)/shard_map/ppermute | solution.py:42
  107.3 15.8 %collective-permute-start.18 = (bf16[256,1024]{1,0:T(8,128)(2,1)S(1)}, bf16[256,1024]{1,0:T(8,128)(2,1)S(1)}, u32[]{:S(2)}, u32[]{:S(2)}) collective-permute-start(bf16[256,1024]{1,0:T(8,128)(2,1)S(1)} %get-tuple-element.638), channel_id=1, source_target_pairs={{0,8},{4,12},{8,0},{12,4},{16,24},{20,28},{24,16},{28,20},{1,9},{5... | collective-permute-start | bytes 1572872 | tf_op jit(solution)/shard_map/ppermute | solution.py:42
  123.3 27.4 %collective-permute-start.25 = (bf16[256,2048]{1,0:T(8,128)(2,1)S(1)}, bf16[256,2048]{1,0:T(8,128)(2,1)S(1)}, u32[]{:S(2)}, u32[]{:S(2)}) collective-permute-start(bf16[256,2048]{1,0:T(8,128)(2,1)S(1)} %bitcast.206), channel_id=1, source_target_pairs={{0,16},{4,20},{8,24},{12,28},{16,0},{20,4},{24,8},{28,12},{1,17},{... | collective-permute-start | bytes 3145736 | tf_op jit(solution)/shard_map/ppermute | solution.py:42
  123.9 26.9 %collective-permute-start.26 = (bf16[256,2048]{1,0:T(8,128)(2,1)S(1)}, bf16[256,2048]{1,0:T(8,128)(2,1)S(1)}, u32[]{:S(2)}, u32[]{:S(2)}) collective-permute-start(bf16[256,2048]{1,0:T(8,128)(2,1)S(1)} %bitcast.207), channel_id=1, source_target_pairs={{0,4},{4,0},{8,12},{12,8},{16,20},{20,16},{24,28},{28,24},{1,5},{5... | collective-permute-start | bytes 3145736 | tf_op jit(solution)/shard_map/ppermute | solution.py:42
  124.1 24.2 %collective-permute-start.27 = (bf16[128,2048]{1,0:T(8,128)(2,1)S(1)}, bf16[128,2048]{1,0:T(8,128)(2,1)S(1)}, u32[]{:S(2)}, u32[]{:S(2)}) collective-permute-start(bf16[128,2048]{1,0:T(8,128)(2,1)S(1)} %bitcast.232), channel_id=1, source_target_pairs={{0,1},{1,0},{2,3},{3,2},{4,5},{5,4},{6,7},{7,6},{8,9},{9,8},{10,11... | collective-permute-start | bytes 1572872 | tf_op jit(solution)/shard_map/ppermute | solution.py:42
  124.2 26.5 %collective-permute-start.28 = (bf16[256,1024]{1,0:T(8,128)(2,1)S(1)}, bf16[256,1024]{1,0:T(8,128)(2,1)S(1)}, u32[]{:S(2)}, u32[]{:S(2)}) collective-permute-start(bf16[256,1024]{1,0:T(8,128)(2,1)S(1)} %bitcast.226), channel_id=1, source_target_pairs={{0,2},{1,3},{2,0},{3,1},{4,6},{5,7},{6,4},{7,5},{8,10},{9,11},{10,... | collective-permute-start | bytes 1572872 | tf_op jit(solution)/shard_map/ppermute | solution.py:42
  131.8 18.9 %collective-permute-start.24 = (bf16[256,1024]{1,0:T(8,128)(2,1)S(1)}, bf16[256,1024]{1,0:T(8,128)(2,1)S(1)}, u32[]{:S(2)}, u32[]{:S(2)}) collective-permute-start(bf16[256,1024]{1,0:T(8,128)(2,1)S(1)} %get-tuple-element.672), channel_id=1, source_target_pairs={{0,8},{4,12},{8,0},{12,4},{16,24},{20,28},{24,16},{28,20},{1,9},{5... | collective-permute-start | bytes 1572872 | tf_op jit(solution)/shard_map/ppermute | solution.py:42
  150.9 25.6 %collective-permute-start.32 = (bf16[256,2048]{1,0:T(8,128)(2,1)S(1)}, bf16[256,2048]{1,0:T(8,128)(2,1)S(1)}, u32[]{:S(2)}, u32[]{:S(2)}) collective-permute-start(bf16[256,2048]{1,0:T(8,128)(2,1)S(1)} %bitcast.213), channel_id=1, source_target_pairs={{0,16},{4,20},{8,24},{12,28},{16,0},{20,4},{24,8},{28,12},{1,17},{... | collective-permute-start | bytes 3145736 | tf_op jit(solution)/shard_map/ppermute | solution.py:42
  152.4 24.2 %collective-permute-start.33 = (bf16[256,2048]{1,0:T(8,128)(2,1)S(1)}, bf16[256,2048]{1,0:T(8,128)(2,1)S(1)}, u32[]{:S(2)}, u32[]{:S(2)}) collective-permute-start(bf16[256,2048]{1,0:T(8,128)(2,1)S(1)} %bitcast.214), channel_id=1, source_target_pairs={{0,4},{4,0},{8,12},{12,8},{16,20},{20,16},{24,28},{28,24},{1,5},{5... | collective-permute-start | bytes 3145736 | tf_op jit(solution)/shard_map/ppermute | solution.py:42
  152.7 25.4 %collective-permute-start.34 = (bf16[512,1024]{1,0:T(8,128)(2,1)S(1)}, bf16[512,1024]{1,0:T(8,128)(2,1)S(1)}, u32[]{:S(2)}, u32[]{:S(2)}) collective-permute-start(bf16[512,1024]{1,0:T(8,128)(2,1)S(1)} %bitcast.216), channel_id=1, source_target_pairs={{0,1},{1,0},{2,3},{3,2},{4,5},{5,4},{6,7},{7,6},{8,9},{9,8},{10,11... | collective-permute-start | bytes 3145736 | tf_op jit(solution)/shard_map/ppermute | solution.py:42
  162.3 15.8 %collective-permute-start.30 = (bf16[128,1024]{1,0:T(8,128)(2,1)S(1)}, bf16[128,1024]{1,0:T(8,128)(2,1)S(1)}, u32[]{:S(2)}, u32[]{:S(2)}) collective-permute-start(bf16[128,1024]{1,0:T(8,128)(2,1)S(1)} %get-tuple-element.705), channel_id=1, source_target_pairs={{0,8},{4,12},{8,0},{12,4},{16,24},{20,28},{24,16},{28,20},{1,9},{5... | collective-permute-start | bytes 786440 | tf_op jit(solution)/shard_map/ppermute | solution.py:42
  197.0 28.3 %collective-permute-start.41 = (bf16[256,2048]{1,0:T(8,128)(2,1)S(1)}, bf16[256,2048]{1,0:T(8,128)(2,1)S(1)}, u32[]{:S(2)}, u32[]{:S(2)}) collective-permute-start(bf16[256,2048]{1,0:T(8,128)(2,1)S(1)} %get-tuple-element.825), channel_id=1, source_target_pairs={{0,4},{4,0},{8,12},{12,8},{16,20},{20,16},{24,28},{28,24},{1,5},{5... | collective-permute-start | bytes 3145736 | tf_op jit(solution)/shard_map/ppermute | solution.py:42
  197.6 27.7 %collective-permute-start.45 = (bf16[256,2048]{1,0:T(8,128)(2,1)S(1)}, bf16[256,2048]{1,0:T(8,128)(2,1)S(1)}, u32[]{:S(2)}, u32[]{:S(2)}) collective-permute-start(bf16[256,2048]{1,0:T(8,128)(2,1)S(1)} %add_low.5), channel_id=1, source_target_pairs={{0,16},{4,20},{8,24},{12,28},{16,0},{20,4},{24,8},{28,12},{1,17},{... | collective-permute-start | bytes 3145736 | tf_op jit(solution)/shard_map/ppermute | solution.py:42
  199.0 26.4 %collective-permute-start.44 = (bf16[512,1024]{1,0:T(8,128)(2,1)S(1)}, bf16[512,1024]{1,0:T(8,128)(2,1)S(1)}, u32[]{:S(2)}, u32[]{:S(2)}) collective-permute-start(bf16[512,1024]{1,0:T(8,128)(2,1)S(1)} %bitcast.303), channel_id=1, source_target_pairs={{0,1},{1,0},{2,3},{3,2},{4,5},{5,4},{6,7},{7,6},{8,9},{9,8},{10,11... | collective-permute-start | bytes 3145736 | tf_op jit(solution)/shard_map/ppermute | solution.py:42
  228.1 27.8 %collective-permute-start.48 = (bf16[256,2048]{1,0:T(8,128)(2,1)S(1)}, bf16[256,2048]{1,0:T(8,128)(2,1)S(1)}, u32[]{:S(2)}, u32[]{:S(2)}) collective-permute-start(bf16[256,2048]{1,0:T(8,128)(2,1)S(1)} %get-tuple-element.892), channel_id=1, source_target_pairs={{0,4},{4,0},{8,12},{12,8},{16,20},{20,16},{24,28},{28,24},{1,5},{5... | collective-permute-start | bytes 3145736 | tf_op jit(solution)/shard_map/ppermute | solution.py:42
  228.5 27.4 %collective-permute-start.51 = (bf16[256,2048]{1,0:T(8,128)(2,1)S(1)}, bf16[256,2048]{1,0:T(8,128)(2,1)S(1)}, u32[]{:S(2)}, u32[]{:S(2)}) collective-permute-start(bf16[256,2048]{1,0:T(8,128)(2,1)S(1)} %add_low.6), channel_id=1, source_target_pairs={{0,16},{4,20},{8,24},{12,28},{16,0},{20,4},{24,8},{28,12},{1,17},{... | collective-permute-start | bytes 3145736 | tf_op jit(solution)/shard_map/ppermute | solution.py:42
  230.1 25.8 %collective-permute-start.49 = (bf16[256,1024]{1,0:T(8,128)(2,1)S(1)}, bf16[256,1024]{1,0:T(8,128)(2,1)S(1)}, u32[]{:S(2)}, u32[]{:S(2)}) collective-permute-start(bf16[256,1024]{1,0:T(8,128)(2,1)S(1)} %bitcast.306), channel_id=1, source_target_pairs={{0,2},{1,3},{2,0},{3,1},{4,6},{5,7},{6,4},{7,5},{8,10},{9,11},{10,... | collective-permute-start | bytes 1572872 | tf_op jit(solution)/shard_map/ppermute | solution.py:42
  232.1 23.8 %collective-permute-start.50 = (bf16[128,2048]{1,0:T(8,128)(2,1)S(1)}, bf16[128,2048]{1,0:T(8,128)(2,1)S(1)}, u32[]{:S(2)}, u32[]{:S(2)}) collective-permute-start(bf16[128,2048]{1,0:T(8,128)(2,1)S(1)} %bitcast.307), channel_id=1, source_target_pairs={{0,1},{1,0},{2,3},{3,2},{4,5},{5,4},{6,7},{7,6},{8,9},{9,8},{10,11... | collective-permute-start | bytes 1572872 | tf_op jit(solution)/shard_map/ppermute | solution.py:42
  259.4 32.7 %collective-permute-start.59 = (bf16[512,1024]{1,0:T(8,128)(2,1)S(1)}, bf16[512,1024]{1,0:T(8,128)(2,1)S(1)}, u32[]{:S(2)}, u32[]{:S(2)}) collective-permute-start(bf16[512,1024]{1,0:T(8,128)(2,1)S(1)} %add_low.7), channel_id=1, source_target_pairs={{0,16},{4,20},{8,24},{12,28},{16,0},{20,4},{24,8},{28,12},{1,17},{... | collective-permute-start | bytes 3145736 | tf_op jit(solution)/shard_map/ppermute | solution.py:42
  262.3 29.8 %collective-permute-start.58 = (bf16[256,1536]{1,0:T(8,128)(2,1)S(1)}, bf16[256,1536]{1,0:T(8,128)(2,1)S(1)}, u32[]{:S(2)}, u32[]{:S(2)}) collective-permute-start(bf16[256,1536]{1,0:T(8,128)(2,1)S(1)} %get-tuple-element.963), channel_id=1, source_target_pairs={{0,4},{4,0},{8,12},{12,8},{16,20},{20,16},{24,28},{28,24},{1,5},{5... | collective-permute-start | bytes 2359304 | tf_op jit(solution)/shard_map/ppermute | solution.py:42
  263.8 28.3 %collective-permute-start.61 = (bf16[128,2048]{1,0:T(8,128)(2,1)S(1)}, bf16[128,2048]{1,0:T(8,128)(2,1)S(1)}, u32[]{:S(2)}, u32[]{:S(2)}) collective-permute-start(bf16[128,2048]{1,0:T(8,128)(2,1)S(1)} %bitcast.305), channel_id=1, source_target_pairs={{0,1},{1,0},{2,3},{3,2},{4,5},{5,4},{6,7},{7,6},{8,9},{9,8},{10,11... | collective-permute-start | bytes 1572872 | tf_op jit(solution)/shard_map/ppermute | solution.py:42
  265.4 26.6 %collective-permute-start.62 = (bf16[256,512]{1,0:T(8,128)(2,1)S(1)}, bf16[256,512]{1,0:T(8,128)(2,1)S(1)}, u32[]{:S(2)}, u32[]{:S(2)}) collective-permute-start(bf16[256,512]{1,0:T(8,128)(2,1)S(1)} %bitcast.312), channel_id=1, source_target_pairs={{0,1},{1,0},{2,3},{3,2},{4,5},{5,4},{6,7},{7,6},{8,9},{9,8},{10,11... | collective-permute-start | bytes 786440 | tf_op jit(solution)/shard_map/ppermute | solution.py:42
  274.5 17.7 %collective-permute-start.60 = (bf16[64,2048]{1,0:T(8,128)(2,1)S(1)}, bf16[64,2048]{1,0:T(8,128)(2,1)S(1)}, u32[]{:S(2)}, u32[]{:S(2)}) collective-permute-start(bf16[64,2048]{1,0:T(8,128)(2,1)S(1)} %bitcast.310), channel_id=1, source_target_pairs={{0,2},{1,3},{2,0},{3,1},{4,6},{5,7},{6,4},{7,5},{8,10},{9,11},{10,... | collective-permute-start | bytes 786440 | tf_op jit(solution)/shard_map/ppermute | solution.py:42
  295.3 29.4 %collective-permute-start.69 = (bf16[256,2048]{1,0:T(8,128)(2,1)S(1)}, bf16[256,2048]{1,0:T(8,128)(2,1)}, u32[]{:S(2)}, u32[]{:S(2)}) collective-permute-start(bf16[256,2048]{1,0:T(8,128)(2,1)S(1)} %add_low.9), channel_id=1, source_target_pairs={{0,16},{4,20},{8,24},{12,28},{16,0},{20,4},{24,8},{28,12},{1,17},{... | collective-permute-start | bytes 3145736 | tf_op jit(solution)/shard_map/ppermute | solution.py:42
  296.1 19.7 %collective-permute-start.63 = (bf16[256,1024]{1,0:T(8,128)(2,1)}, bf16[256,1024]{1,0:T(8,128)(2,1)}, u32[]{:S(2)}, u32[]{:S(2)}) collective-permute-start(bf16[256,1024]{1,0:T(8,128)(2,1)} %get-tuple-element.972), channel_id=1, source_target_pairs={{0,8},{4,12},{8,0},{12,4},{16,24},{20,28},{24,16},{28,20},{1,9},{5... | collective-permute-start | bytes 1572872 | tf_op jit(solution)/shard_map/ppermute | solution.py:42
  299.5 22.4 %collective-permute-start.68 = (bf16[256,1024]{1,0:T(8,128)(2,1)}, bf16[256,1024]{1,0:T(8,128)(2,1)}, u32[]{:S(2)}, u32[]{:S(2)}) collective-permute-start(bf16[256,1024]{1,0:T(8,128)(2,1)} %bitcast.110), channel_id=1, source_target_pairs={{0,1},{1,0},{2,3},{3,2},{4,5},{5,4},{6,7},{7,6},{8,9},{9,8},{10,11... | collective-permute-start | bytes 1572872 | tf_op jit(solution)/shard_map/ppermute | solution.py:42
  304.7 17.1 %collective-permute-start.67 = (bf16[64,2048]{1,0:T(8,128)(2,1)S(1)}, bf16[64,2048]{1,0:T(8,128)(2,1)S(1)}, u32[]{:S(2)}, u32[]{:S(2)}) collective-permute-start(bf16[64,2048]{1,0:T(8,128)(2,1)S(1)} %bitcast.314), channel_id=1, source_target_pairs={{0,2},{1,3},{2,0},{3,1},{4,6},{5,7},{6,4},{7,5},{8,10},{9,11},{10,... | collective-permute-start | bytes 786440 | tf_op jit(solution)/shard_map/ppermute | solution.py:42
  330.1 19.8 %collective-permute-start.71 = (bf16[256,1536]{1,0:T(8,128)(2,1)S(1)}, bf16[256,1536]{1,0:T(8,128)(2,1)S(1)}, u32[]{:S(2)}, u32[]{:S(2)}) collective-permute-start(bf16[256,1536]{1,0:T(8,128)(2,1)S(1)} %copy-done.36), channel_id=1, source_target_pairs={{0,16},{4,20},{8,24},{12,28},{16,0},{20,4},{24,8},{28,12},{1,17},{... | collective-permute-start | bytes 2359304 | tf_op jit(solution)/shard_map/ppermute | solution.py:42
  331.5 18.5 %collective-permute-start.72 = (bf16[128,2048]{1,0:T(8,128)(2,1)S(1)}, bf16[128,2048]{1,0:T(8,128)(2,1)S(1)}, u32[]{:S(2)}, u32[]{:S(2)}) collective-permute-start(bf16[128,2048]{1,0:T(8,128)(2,1)S(1)} %bitcast.304), channel_id=1, source_target_pairs={{0,1},{1,0},{2,3},{3,2},{4,5},{5,4},{6,7},{7,6},{8,9},{9,8},{10,11... | collective-permute-start | bytes 1572872 | tf_op jit(solution)/shard_map/ppermute | solution.py:42
  332.7 17.3 %collective-permute-start.73 = (bf16[128,1024]{1,0:T(8,128)(2,1)S(1)}, bf16[128,1024]{1,0:T(8,128)(2,1)S(1)}, u32[]{:S(2)}, u32[]{:S(2)}) collective-permute-start(bf16[128,1024]{1,0:T(8,128)(2,1)S(1)} %bitcast.311), channel_id=1, source_target_pairs={{0,2},{1,3},{2,0},{3,1},{4,6},{5,7},{6,4},{7,5},{8,10},{9,11},{10,... | collective-permute-start | bytes 786440 | tf_op jit(solution)/shard_map/ppermute | solution.py:42
  333.5 16.5 %collective-permute-start.74 = (bf16[64,512]{1,0:T(8,128)(2,1)S(1)}, bf16[64,512]{1,0:T(8,128)(2,1)S(1)}, u32[]{:S(2)}, u32[]{:S(2)}) collective-permute-start(bf16[64,512]{1,0:T(8,128)(2,1)S(1)} %bitcast.317), channel_id=1, source_target_pairs={{0,16},{4,20},{8,24},{12,28},{16,0},{20,4},{24,8},{28,12},{1,17},{... | collective-permute-start | bytes 196616 | tf_op jit(solution)/shard_map/ppermute | solution.py:42
  350.0 18.1 %collective-permute-start.75 = (bf16[256,1024]{1,0:T(8,128)(2,1)S(1)}, bf16[256,1024]{1,0:T(8,128)(2,1)S(1)}, u32[]{:S(2)}, u32[]{:S(2)}) collective-permute-start(bf16[256,1024]{1,0:T(8,128)(2,1)S(1)} %get-tuple-element.1070), channel_id=1, source_target_pairs={{0,8},{4,12},{8,0},{12,4},{16,24},{20,28},{24,16},{28,20},{1,9},{5... | collective-permute-start | bytes 1572872 | tf_op jit(solution)/shard_map/ppermute | solution.py:42
  351.0 17.2 %collective-permute-start.78 = (bf16[128,1536]{1,0:T(8,128)(2,1)S(1)}, bf16[128,1536]{1,0:T(8,128)(2,1)S(1)}, u32[]{:S(2)}, u32[]{:S(2)}) collective-permute-start(bf16[128,1536]{1,0:T(8,128)(2,1)S(1)} %bitcast.308), channel_id=1, source_target_pairs={{0,1},{1,0},{2,3},{3,2},{4,5},{5,4},{6,7},{7,6},{8,9},{9,8},{10,11... | collective-permute-start | bytes 1179656 | tf_op jit(solution)/shard_map/ppermute | solution.py:42
  (108 other events, 915.0 us)

commit v7 on v6

--- a/solution.py
+++ b/solution.py
@@ -682,24 +682,36 @@
     return jnp.stack(split(value, CORE, 3), 3).reshape(tokens, width)
 
 
-def finish_kernel(span, chunk, part, side, keep, other, out, *refs):
-    grad, new_m, step = refs[-3:]
+def finish_kernel(span, side, keep, other, out, m, v, *refs):
     third = out.shape[-1]
-    total = (grad.shape[-1] - 8 * third) // 2
-    late = total - (keep.shape[1] - part)
+    place_sides([(keep, other, 0, 0, 3 * third, span)], side, refs[-3])
+    for k in range(2):
+        refs[-3][0, :, pl.ds((6 + k) * third, third)] = out[k]
+    adam_columns(m, v, *refs[-3:])
+
+
+def finish_up_kernel(chunk, first, side, keep, other, *refs):
+    grad = refs[-3]
+    late = grad.shape[-1] // 2 - (keep.shape[1] - first)
+    pieces = [(keep, other, first, late, keep.shape[1] - first, chunk)]
+    if late:
+        pieces.append((refs[0], refs[1], 0, 0, late, chunk))
+    place_sides(pieces, side, grad)
     m, v = refs[2:4] if late else refs[:2]
-    pieces = [(keep, other, 0, 0, 0, part, span), (keep, other, part, 8 * third, late, total - late, chunk)]
-    if late:
-        pieces.append((refs[0], refs[1], 0, 8 * third, 0, late, chunk))
-    for one, two, first, base, start, count, width in pieces:
+    adam_columns(m, v, *refs[-3:])
+
+
+def place_sides(pieces, side, grad):
+    for one, two, first, start, count, width in pieces:
         each = math.gcd(math.gcd(width, start), count)
         for source, x in ((one, side[0]), (two, 1 - side[0])):
             for n in range(count // each):
                 block, inside = divmod(start + n * each, width)
-                at = pl.multiple_of(base + (2 * block + x) * width + inside, 128)
+                at = pl.multiple_of((2 * block + x) * width + inside, 128)
                 grad[0, :, pl.ds(at, each)] = source[:, pl.ds(first + n * each, each)]
-    for k in range(2):
-        grad[0, :, pl.ds((6 + k) * third, third)] = out[k]
+
+
+def adam_columns(m, v, grad, new_m, step):
     for n in range(grad.shape[2] // 1024):
         cols = pl.ds(n * 1024, 1024)
         new_m[0, :, cols], step[0, :, cols] = adam_update(m[0, :, cols], v[0, :, cols], grad[0, :, cols])
@@ -711,8 +723,9 @@
     new_m[0], step[0] = adam_update(m[0], v[0], value[...])
 
 
-def update(kernel, layer, shape, parts, specs, moments, before, name):
-    one = pl.BlockSpec((1, *shape[1:]), lambda i: (layer, 0, 0))
+def update(kernel, layer, shape, parts, specs, moments, before, name, half=None):
+    wide = shape[2] if half is None else shape[2] // 2
+    one = pl.BlockSpec((1, shape[1], wide), lambda i: (layer, 0, half or 0))
     count = len(parts) + 2
     return pl.pallas_call(
         kernel,
@@ -1115,16 +1128,29 @@
 
     def finish(layer, big, before, more=None):
         keep, other, out = big
-        more = [] if more is None else list(more[:2])
-        return update(
-            partial(finish_kernel, 2 * block, 2 * fsdp * feeds, part),
+        side = mine(SIDE)[None]
+        before = update(
+            partial(finish_kernel, 2 * block),
             layer,
             w_big.shape,
-            [mine(SIDE)[None], keep, other, out, *more],
-            [SMEM] + [VMEM] * (3 + len(more)),
+            [side, keep, other, out],
+            [SMEM, VMEM, VMEM, VMEM],
             [m_big, v_big],
             before,
             "finish",
+            0,
+        )
+        more = [] if more is None else list(more[:2])
+        return update(
+            partial(finish_up_kernel, 2 * fsdp * feeds, part),
+            layer,
+            w_big.shape,
+            [side, keep, other, *more],
+            [SMEM] + [VMEM] * (2 + len(more)),
+            [m_big, v_big],
+            before,
+            "finish_up",
+            1,
         )
 
     def finish_down(layer, flow, before):
@@ -1223,7 +1249,6 @@
     g_down0.start()
     after(g_attn1, g_attn0.quarters[0][1])
     g_attn1.start()
-    gate(g_up0b, g_attn1, g_down0)
     norm_back(0, 0, live.attn0[0])
     live.seal(g_attn0, g_attn1, g_down0, g_up0b)
 
@@ -1239,13 +1264,13 @@
     big1 = two_sides([g_attn1, g_up1], [2 * width, feed // 2], [part, feed // 2])
     live.put(big=finish(1, big1, []))
     live.put(table=table_terms())
+    table_step(2, [CORE])
     live.seal(g_up0a, g_attn0, g_down0, g_up0b)
 
     g_up0a.start()
     g_attn0.start()
     g_down1.start()
     cross()
-    table_step(2, [CORE])
     table_step(1, [SIDE])
     table = live.table.reshape(*(len(sl.high) + len(sl.deep)) * [2], count, -1)
     live.put(table=table, down=finish_down(0, g_down0, []))

time: 395 us -> 391 us (0.990)
  waiting for transfers between devices: 185 us -> 165 us
  Pallas kernels: 96.9 us -> 103 us
    ppermute x87, waiting for transfers between devices: 185 us -> 165 us  [flip(): lax.ppermute(value, axis, [(i, i ^ mask) for i in range(self.size[axis])])]
    pallas_call x4 -> x6, Pallas kernels: 7.47 us -> 10.4 us  [update(): pl.pallas_call(kernel, grid=(1,), out_shape=[jax.ShapeDtypeStruct(shape,...]
    unnamed x139 -> x181, local copies, waits for them, and re-layouts: 12 us -> 13.7 us
  transfers between devices with their start and end apart: 87 -> 87, of which waited for: 42 -> 41; matrix products, arithmetic and copies ran while one was open for 3% -> 3% of each run, Pallas kernels for 22% -> 23%
where the time goes in v7:
time: 391 us; the launch traced here: 387 us
  waiting for transfers between devices  165 us (42%)
  Pallas kernels  103 us (26%)
  starting transfers between devices  85.3 us (22%)
  local copies, waits for them, and re-layouts  18.1 us (5%)
  other arithmetic  11.8 us (3%)
    ppermute x87, waiting for transfers between devices, flip(): lax.ppermute(value, axis, [(i, i ^ mask) for i in range(self.size[axis])])  165 us
    pallas_call x53, Pallas kernels, call(): pl.pallas_call(kernel, out_shape=[jax.ShapeDtypeStruct(shape, kind) for s...  92.6 us
    ppermute x87, starting transfers between devices, flip(): lax.ppermute(value, axis, [(i, i ^ mask) for i in range(self.size[axis])])  85.3 us
    unnamed x181, local copies, waits for them, and re-layouts  13.7 us
    pallas_call x6, Pallas kernels, update(): pl.pallas_call(kernel, grid=(1,), out_shape=[jax.ShapeDtypeStruct(shape,...  10.4 us
  transfers between devices with their start and end apart: 87, of which 41 were waited for; matrix products, arithmetic and copies ran while one was open for 3% of the time, Pallas kernels for 23%

profile of v7, /device:TPU:0, one launch (start us, length us, event | category | flops | bytes accessed | tf_op | source)
XLA Modules:
  0.0 386.5 jit_solution(10838895121921468597)
XLA Ops:
  1.8 4.1 %collective-permute-start.1 = (bf16[128,1024]{1,0:T(8,128)(2,1)S(1)}, bf16[128,1024]{1,0:T(8,128)(2,1)S(1)}, u32[]{:S(2)}, u32[]{:S(2)}) collective-permute-start(bf16[128,1024]{1,0:T(8,128)(2,1)S(1)} %get-tuple-element.594), channel_id=1, source_target_pairs={{0,2},{1,3},{2,0},{3,1},{4,6},{5,7},{6,4},{7,5},{8,10},{9,11},{10,... | collective-permute-start | bytes 786440 | tf_op jit(solution)/shard_map/ppermute | solution.py:42
  14.9 2.9 collective-permute-done.1
  18.7 3.4 collective-permute-start.6
  25.0 9.7 %collective-permute-done.5 = bf16[32,2048]{1,0:T(8,128)(2,1)S(1)} collective-permute-done((bf16[32,2048]{1,0:T(8,128)(2,1)S(1)}, bf16[32,2048]{1,0:T(8,128)(2,1)S(1)}, u32[]{:S(2)}, u32[]{:S(2)}) %collective-permute-start.5) | collective-permute-done | bytes 131104 | tf_op jit(solution)/shard_map/ppermute | solution.py:42
  38.5 3.4 collective-permute-start.8
  41.9 1.8 collective-permute-start.9
  44.6 2.1 fusion
  47.6 12.5 %collective-permute-done.9 = bf16[64,2048]{1,0:T(8,128)(2,1)S(1)} collective-permute-done((bf16[64,2048]{1,0:T(8,128)(2,1)S(1)}, bf16[64,2048]{1,0:T(8,128)(2,1)S(1)}, u32[]{:S(2)}, u32[]{:S(2)}) %collective-permute-start.9) | collective-permute-done | bytes 262176 | tf_op jit(solution)/shard_map/ppermute | solution.py:42
  62.6 4.5 %collective-permute-start.15 = (bf16[128,2048]{1,0:T(8,128)(2,1)S(1)}, bf16[128,2048]{1,0:T(8,128)(2,1)S(1)}, u32[]{:S(2)}, u32[]{:S(2)}) collective-permute-start(bf16[128,2048]{1,0:T(8,128)(2,1)S(1)} %bitcast.238), channel_id=1, source_target_pairs={{0,1},{1,0},{2,3},{3,2},{4,5},{5,4},{6,7},{7,6},{8,9},{9,8},{10,11... | collective-permute-start | bytes 1572872 | tf_op jit(solution)/shard_map/ppermute | solution.py:42
  69.3 14.8 %collective-permute-done.16 = bf16[64,2048]{1,0:T(8,128)(2,1)S(1)} collective-permute-done((bf16[64,2048]{1,0:T(8,128)(2,1)S(1)}, bf16[64,2048]{1,0:T(8,128)(2,1)S(1)}, u32[]{:S(2)}, u32[]{:S(2)}) %collective-permute-start.16) | collective-permute-done | bytes 262176 | tf_op jit(solution)/shard_map/ppermute | solution.py:42
  84.8 2.6 collective-permute-done.13.q1.refs_3_.refs_8_
  91.2 3.7 collective-permute-start.21
  96.5 9.9 %attend.2 = (f32[256,1024]{1,0:T(8,128)}, bf16[256,1024]{1,0:T(8,128)(2,1)S(1)}, bf16[256,1536]{1,0:T(8,128)(2,1)S(1)}, bf16[256,512]{1,0:T(8,128)(2,1)S(1)}, f3...) custom-call(s32[2]{0:T(128)S(1)} %pad_add_fusion.place.up_place.dn_place, ...), custom_call_target="tpu_custom_call" | custom-call | tf_op jit(solution)/shard_map/attend/pallas_call | solution.py:54
  109.1 13.2 %collective-permute-done.22 = bf16[64,2048]{1,0:T(8,128)(2,1)S(1)} collective-permute-done((bf16[64,2048]{1,0:T(8,128)(2,1)S(1)}, bf16[64,2048]{1,0:T(8,128)(2,1)S(1)}, u32[]{:S(2)}, u32[]{:S(2)}) %collective-permute-start.22) | collective-permute-done | bytes 262176 | tf_op jit(solution)/shard_map/ppermute | solution.py:42
  123.4 2.1 collective-permute-start.28
  125.5 5.5 %feed.1 = (f32[256,1024]{1,0:T(8,128)S(1)}, bf16[256,1024]{1,0:T(8,128)(2,1)S(1)}, f32[256,2048]{1,0:T(8,128)S(1)}, bf16[256,2048]{1,0:T(8,128)(2,1)S(1)}, f32[2...) custom-call(s32[2]{0:T(128)S(1)} %pad_add_fusion.place.up_place.dn_place, s32[2]{0:T(128)S(1)} %pad_add_fusion.place.up_place.dn_place, ...), custom_call_target="tpu_custom_call" | custom-call | tf_op jit(solution)/shard_map/feed/pallas_call | solution.py:54
  131.7 16.0 %collective-permute-done.27 = bf16[128,2048]{1,0:T(8,128)(2,1)S(1)} collective-permute-done((bf16[128,2048]{1,0:T(8,128)(2,1)S(1)}, bf16[128,2048]{1,0:T(8,128)(2,1)S(1)}, u32[]{:S(2)}, u32[]{:S(2)}) %collective-permute-start.27) | collective-permute-done | bytes 524320 | tf_op jit(solution)/shard_map/ppermute | solution.py:42
  147.6 2.1 collective-permute-done.28
  152.5 8.8 %attend.3 = (f32[256,1024]{1,0:T(8,128)S(1)}, bf16[256,1024]{1,0:T(8,128)(2,1)S(1)}, bf16[256,1536]{1,0:T(8,128)(2,1)S(1)}, bf16[256,512]{1,0:T(8,128)(2,1)S(1)}...) custom-call(s32[2]{0:T(128)S(1)} %pad_add_fusion.place.up_place.dn_place, ...), custom_call_target="tpu_custom_call" | custom-call | tf_op jit(solution)/shard_map/attend/pallas_call | solution.py:54
  163.4 12.1 %collective-permute-done.32.refs_7_ = bf16[256,2048]{1,0:T(8,128)(2,1)S(1)} collective-permute-done((bf16[256,2048]{1,0:T(8,128)(2,1)S(1)}, bf16[256,2048]{1,0:T(8,128)(2,1)S(1)}, u32[]{:S(2)}, u32[]{:S(2)}) %collective-permute-start.32) | collective-permute-done | bytes 1048608 | tf_op jit(solution)/shard_map/ppermute | solution.py:42
  183.0 6.6 %feed_turn.1 = (f32[256,1024]{1,0:T(8,128)S(1)}, bf16[256,1024]{1,0:T(8,128)(2,1)S(1)}, bf16[256,2048]{1,0:T(8,128)(2,1)S(1)}, bf16[256,2048]{1,0:T(8,128)(2,1)S...) custom-call(s32[2]{0:T(128)S(1)} %pad_add_fusion.place.up_place.dn_place, ...), custom_call_target="tpu_custom_call" | custom-call | tf_op jit(solution)/shard_map/feed_turn/pallas_call | solution.py:54
  189.6 1.8 down_grad.2
  191.6 1.8 up_grad.3
  194.3 1.9 collective-permute-done.40.two
  200.6 7.1 %collective-permute-done.38.refs_4_ = bf16[128,1024]{1,0:T(8,128)(2,1)S(1)} collective-permute-done((bf16[128,1024]{1,0:T(8,128)(2,1)S(1)}, bf16[128,1024]{1,0:T(8,128)(2,1)S(1)}, u32[]{:S(2)}, u32[]{:S(2)}) %collective-permute-start.38) | collective-permute-done | bytes 262176 | tf_op jit(solution)/shard_map/ppermute | solution.py:42
  207.7 4.8 %collective-permute-done.39.refs_5_ = bf16[128,1024]{1,0:T(8,128)(2,1)S(1)} collective-permute-done((bf16[128,1024]{1,0:T(8,128)(2,1)S(1)}, bf16[128,1024]{1,0:T(8,128)(2,1)S(1)}, u32[]{:S(2)}, u32[]{:S(2)}) %collective-permute-start.39) | collective-permute-done | bytes 262176 | tf_op jit(solution)/shard_map/ppermute | solution.py:42
  212.5 11.9 %attend_back.2 = (f32[256,1024]{1,0:T(8,128)S(1)}, bf16[256,1024]{1,0:T(8,128)(2,1)}, f32[1,1024]{1,0:T(1,128)S(1)}, f32[1,1024]{1,0:T(1,128)S(1)}, bf16[256,153...) custom-call(s32[2]{0:T(128)S(1)} %pad_add_fusion.place.up_place.dn_p, ...), custom_call_target="tpu_custom_call" | custom-call | tf_op jit(solution)/shard_map/attend_back/pallas_call | solution.py:54
  224.6 2.6 collective-permute-done.47.two
  231.6 10.7 %collective-permute-done.46.refs_0_ = bf16[256,1024]{1,0:T(8,128)(2,1)S(1)} collective-permute-done((bf16[256,1024]{1,0:T(8,128)(2,1)S(1)}, bf16[256,1024]{1,0:T(8,128)(2,1)S(1)}, u32[]{:S(2)}, u32[]{:S(2)}) %collective-permute-start.46) | collective-permute-done | bytes 524320 | tf_op jit(solution)/shard_map/ppermute | solution.py:42
  242.3 6.5 %feed_back.1 = (f32[256,1024]{1,0:T(8,128)S(1)}, bf16[256,1024]{1,0:T(8,128)(2,1)S(1)}, f32[1,1024]{1,0:T(1,128)S(1)}, f32[1,1024]{1,0:T(1,128)S(1)}, bf16[256,2...) custom-call(s32[2]{0:T(128)S(1)} %pad_add_fusion.place.up_place.dn_place, ...), custom_call_target="tpu_custom_call" | custom-call | tf_op jit(solution)/shard_map/feed_back/pallas_call | solution.py:54
  251.6 1.8 down_grad.3
  255.6 2.1 collective-permute-done.53.two
  266.9 6.7 %collective-permute-done.52.refs_4_ = bf16[256,1024]{1,0:T(8,128)(2,1)S(1)} collective-permute-done((bf16[256,1024]{1,0:T(8,128)(2,1)S(1)}, bf16[256,1024]{1,0:T(8,128)(2,1)S(1)}, u32[]{:S(2)}, u32[]{:S(2)}) %collective-permute-start.52) | collective-permute-done | bytes 524320 | tf_op jit(solution)/shard_map/ppermute | solution.py:42
  275.4 13.5 %attend_back.3 = (f32[256,1024]{1,0:T(8,128)S(1)}, bf16[256,1024]{1,0:T(8,128)(2,1)}, f32[1,1024]{1,0:T(1,128)S(1)}, f32[1,1024]{1,0:T(1,128)S(1)}, bf16[256,153...) custom-call(s32[2]{0:T(128)S(1)} %pad_add_fusion.place.up_place.dn_p, ...), custom_call_target="tpu_custom_call" | custom-call | tf_op jit(solution)/shard_map/attend_back/pallas_call | solution.py:54
  291.7 2.6 collective-permute-done.64.two
  302.9 1.9 collective-permute-start.67
  304.9 4.8 %collective-permute-done.63.refs_0_ = bf16[256,1024]{1,0:T(8,128)(2,1)} collective-permute-done((bf16[256,1024]{1,0:T(8,128)(2,1)}, bf16[256,1024]{1,0:T(8,128)(2,1)}, u32[]{:S(2)}, u32[]{:S(2)}) %collective-permute-start.63) | collective-permute-done | bytes 524320 | tf_op jit(solution)/shard_map/ppermute | solution.py:42
  309.7 2.8 norm_back.1
  312.5 3.6 collective-permute-done.69
  316.1 5.9 %collective-permute-done.68 = bf16[256,1024]{1,0:T(8,128)(2,1)S(1)} collective-permute-done((bf16[256,1024]{1,0:T(8,128)(2,1)S(1)}, bf16[256,1024]{1,0:T(8,128)(2,1)S(1)}, u32[]{:S(2)}, u32[]{:S(2)}) %collective-permute-start.68) | collective-permute-done | bytes 524320 | tf_op jit(solution)/shard_map/ppermute | solution.py:42
  322.2 2.8 add_split.22
  336.5 3.6 down.1
  341.8 2.4 finish.2
  344.2 2.5 finish_up.2
  358.8 2.5 collective-permute-done.77
  361.3 3.5 collective-permute-done.79
  368.9 2.7 collective-permute-start.84
  376.2 1.8 collective-permute-done.84
  (421 shorter events, 124.9 us)
Async XLA Ops:
  1.8 16.0 %collective-permute-start.1 = (bf16[128,1024]{1,0:T(8,128)(2,1)S(1)}, bf16[128,1024]{1,0:T(8,128)(2,1)S(1)}, u32[]{:S(2)}, u32[]{:S(2)}) collective-permute-start(bf16[128,1024]{1,0:T(8,128)(2,1)S(1)} %get-tuple-element.594), channel_id=1, source_target_pairs={{0,2},{1,3},{2,0},{3,1},{4,6},{5,7},{6,4},{7,5},{8,10},{9,11},{10,... | collective-permute-start | bytes 786440 | tf_op jit(solution)/shard_map/ppermute | solution.py:42
  13.3 22.7 %collective-permute-start.4 = (bf16[272,1024]{1,0:T(8,128)(2,1)}, bf16[272,1024]{1,0:T(8,128)(2,1)}, u32[]{:S(2)}, u32[]{:S(2)}) collective-permute-start(bf16[272,1024]{1,0:T(8,128)(2,1)} %pad_maximum_fusion), channel_id=1, source_target_pairs={{0,8},{4,12},{8,0},{12,4},{16,24},{20,28},{24,16},{28,20},{1,9},{5... | collective-permute-start | bytes 1671176 | tf_op jit(solution)/shard_map/ppermute | solution.py:42
  17.9 19.1 %collective-permute-start.7 = (bf16[256,1024]{1,0:T(8,128)(2,1)S(1)}, bf16[256,1024]{1,0:T(8,128)(2,1)S(1)}, u32[]{:S(2)}, u32[]{:S(2)}) collective-permute-start(bf16[256,1024]{1,0:T(8,128)(2,1)S(1)} %bitcast.232), channel_id=1, source_target_pairs={{0,1},{1,0},{2,3},{3,2},{4,5},{5,4},{6,7},{7,6},{8,9},{9,8},{10,11... | collective-permute-start | bytes 1572872 | tf_op jit(solution)/shard_map/ppermute | solution.py:42
  18.7 17.3 %collective-permute-start.6 = (bf16[64,2176]{1,0:T(8,128)(2,1)S(1)}, bf16[64,2176]{1,0:T(8,128)(2,1)S(1)}, u32[]{:S(2)}, u32[]{:S(2)}) collective-permute-start(bf16[64,2176]{1,0:T(8,128)(2,1)S(1)} %bitcast.240), channel_id=1, source_target_pairs={{0,2},{1,3},{2,0},{3,1},{4,6},{5,7},{6,4},{7,5},{8,10},{9,11},{10,... | collective-permute-start | bytes 835592 | tf_op jit(solution)/shard_map/ppermute | solution.py:42
  37.1 23.7 %collective-permute-start.10 = (bf16[512,1024]{1,0:T(8,128)(2,1)S(1)}, bf16[512,1024]{1,0:T(8,128)(2,1)S(1)}, u32[]{:S(2)}, u32[]{:S(2)}) collective-permute-start(bf16[512,1024]{1,0:T(8,128)(2,1)S(1)} %bitcast.206), channel_id=1, source_target_pairs={{0,16},{4,20},{8,24},{12,28},{16,0},{20,4},{24,8},{28,12},{1,17},{... | collective-permute-start | bytes 3145736 | tf_op jit(solution)/shard_map/ppermute | solution.py:42
  38.4 22.4 %collective-permute-start.11 = (bf16[512,1024]{1,0:T(8,128)(2,1)S(1)}, bf16[512,1024]{1,0:T(8,128)(2,1)S(1)}, u32[]{:S(2)}, u32[]{:S(2)}) collective-permute-start(bf16[512,1024]{1,0:T(8,128)(2,1)S(1)} %bitcast.207), channel_id=1, source_target_pairs={{0,4},{4,0},{8,12},{12,8},{16,20},{20,16},{24,28},{28,24},{1,5},{5... | collective-permute-start | bytes 3145736 | tf_op jit(solution)/shard_map/ppermute | solution.py:42
  38.5 22.3 %collective-permute-start.8 = (bf16[128,2176]{1,0:T(8,128)(2,1)S(1)}, bf16[128,2176]{1,0:T(8,128)(2,1)S(1)}, u32[]{:S(2)}, u32[]{:S(2)}) collective-permute-start(bf16[128,2176]{1,0:T(8,128)(2,1)S(1)} %bitcast.228), channel_id=1, source_target_pairs={{0,1},{1,0},{2,3},{3,2},{4,5},{5,4},{6,7},{7,6},{8,9},{9,8},{10,11... | collective-permute-start | bytes 1671176 | tf_op jit(solution)/shard_map/ppermute | solution.py:42
  41.9 18.2 %collective-permute-start.9 = (bf16[64,2048]{1,0:T(8,128)(2,1)S(1)}, bf16[64,2048]{1,0:T(8,128)(2,1)S(1)}, u32[]{:S(2)}, u32[]{:S(2)}) collective-permute-start(bf16[64,2048]{1,0:T(8,128)(2,1)S(1)} %bitcast.257), channel_id=1, source_target_pairs={{0,2},{1,3},{2,0},{3,1},{4,6},{5,7},{6,4},{7,5},{8,10},{9,11},{10,... | collective-permute-start | bytes 786440 | tf_op jit(solution)/shard_map/ppermute | solution.py:42
  61.0 26.5 %collective-permute-start.13 = (bf16[256,2176]{1,0:T(8,128)(2,1)S(1)}, bf16[256,2176]{1,0:T(8,128)(2,1)S(1)}, u32[]{:S(2)}, u32[]{:S(2)}) collective-permute-start(bf16[256,2176]{1,0:T(8,128)(2,1)S(1)} %bitcast.201), channel_id=1, source_target_pairs={{0,16},{4,20},{8,24},{12,28},{16,0},{20,4},{24,8},{28,12},{1,17},{... | collective-permute-start | bytes 3342344 | tf_op jit(solution)/shard_map/ppermute | solution.py:42
  62.1 25.4 %collective-permute-start.14 = (bf16[256,2176]{1,0:T(8,128)(2,1)S(1)}, bf16[256,2176]{1,0:T(8,128)(2,1)S(1)}, u32[]{:S(2)}, u32[]{:S(2)}) collective-permute-start(bf16[256,2176]{1,0:T(8,128)(2,1)S(1)} %bitcast.202), channel_id=1, source_target_pairs={{0,4},{4,0},{8,12},{12,8},{16,20},{20,16},{24,28},{28,24},{1,5},{5... | collective-permute-start | bytes 3342344 | tf_op jit(solution)/shard_map/ppermute | solution.py:42
  62.1 22.8 %collective-permute-start.12 = (bf16[512,1024]{1,0:T(8,128)(2,1)S(1)}, bf16[512,1024]{1,0:T(8,128)(2,1)S(1)}, u32[]{:S(2)}, u32[]{:S(2)}) collective-permute-start(bf16[512,1024]{1,0:T(8,128)(2,1)S(1)} %collective-permute-done.10.refs_9_), channel_id=1, source_target_pairs={{0,4},{4,0},{8,12},{12,8},{16,20},{20,16},{24,28},{28,24},{1,5},{5... | collective-permute-start | bytes 3145736 | tf_op jit(solution)/shard_map/ppermute | solution.py:42
  62.6 22.2 %collective-permute-start.15 = (bf16[128,2048]{1,0:T(8,128)(2,1)S(1)}, bf16[128,2048]{1,0:T(8,128)(2,1)S(1)}, u32[]{:S(2)}, u32[]{:S(2)}) collective-permute-start(bf16[128,2048]{1,0:T(8,128)(2,1)S(1)} %bitcast.238), channel_id=1, source_target_pairs={{0,1},{1,0},{2,3},{3,2},{4,5},{5,4},{6,7},{7,6},{8,9},{9,8},{10,11... | collective-permute-start | bytes 1572872 | tf_op jit(solution)/shard_map/ppermute | solution.py:42
  67.9 16.2 %collective-permute-start.16 = (bf16[64,2048]{1,0:T(8,128)(2,1)S(1)}, bf16[64,2048]{1,0:T(8,128)(2,1)S(1)}, u32[]{:S(2)}, u32[]{:S(2)}) collective-permute-start(bf16[64,2048]{1,0:T(8,128)(2,1)S(1)} %bitcast.262), channel_id=1, source_target_pairs={{0,2},{1,3},{2,0},{3,1},{4,6},{5,7},{6,4},{7,5},{8,10},{9,11},{10,... | collective-permute-start | bytes 786440 | tf_op jit(solution)/shard_map/ppermute | solution.py:42
  88.6 33.7 %collective-permute-start.19 = (bf16[256,2048]{1,0:T(8,128)(2,1)}, bf16[256,2048]{1,0:T(8,128)(2,1)}, u32[]{:S(2)}, u32[]{:S(2)}) collective-permute-start(bf16[256,2048]{1,0:T(8,128)(2,1)} %bitcast.46.refs_4_), channel_id=1, source_target_pairs={{0,16},{4,20},{8,24},{12,28},{16,0},{20,4},{24,8},{28,12},{1,17},{... | collective-permute-start | bytes 3145736 | tf_op jit(solution)/shard_map/ppermute | solution.py:42
  89.1 33.2 %collective-permute-start.20 = (bf16[256,2048]{1,0:T(8,128)(2,1)}, bf16[256,2048]{1,0:T(8,128)(2,1)}, u32[]{:S(2)}, u32[]{:S(2)}) collective-permute-start(bf16[256,2048]{1,0:T(8,128)(2,1)} %bitcast.46.refs_4_), channel_id=1, source_target_pairs={{0,4},{4,0},{8,12},{12,8},{16,20},{20,16},{24,28},{28,24},{1,5},{5... | collective-permute-start | bytes 3145736 | tf_op jit(solution)/shard_map/ppermute | solution.py:42
  91.2 31.1 %collective-permute-start.21 = (bf16[128,2048]{1,0:T(8,128)(2,1)S(1)}, bf16[128,2048]{1,0:T(8,128)(2,1)S(1)}, u32[]{:S(2)}, u32[]{:S(2)}) collective-permute-start(bf16[128,2048]{1,0:T(8,128)(2,1)S(1)} %bitcast.234), channel_id=1, source_target_pairs={{0,1},{1,0},{2,3},{3,2},{4,5},{5,4},{6,7},{7,6},{8,9},{9,8},{10,11... | collective-permute-start | bytes 1572872 | tf_op jit(solution)/shard_map/ppermute | solution.py:42
  106.4 15.9 %collective-permute-start.18 = (bf16[256,1024]{1,0:T(8,128)(2,1)S(1)}, bf16[256,1024]{1,0:T(8,128)(2,1)S(1)}, u32[]{:S(2)}, u32[]{:S(2)}) collective-permute-start(bf16[256,1024]{1,0:T(8,128)(2,1)S(1)} %get-tuple-element.640), channel_id=1, source_target_pairs={{0,8},{4,12},{8,0},{12,4},{16,24},{20,28},{24,16},{28,20},{1,9},{5... | collective-permute-start | bytes 1572872 | tf_op jit(solution)/shard_map/ppermute | solution.py:42
  122.5 27.3 %collective-permute-start.25 = (bf16[256,2048]{1,0:T(8,128)(2,1)S(1)}, bf16[256,2048]{1,0:T(8,128)(2,1)S(1)}, u32[]{:S(2)}, u32[]{:S(2)}) collective-permute-start(bf16[256,2048]{1,0:T(8,128)(2,1)S(1)} %bitcast.210), channel_id=1, source_target_pairs={{0,16},{4,20},{8,24},{12,28},{16,0},{20,4},{24,8},{28,12},{1,17},{... | collective-permute-start | bytes 3145736 | tf_op jit(solution)/shard_map/ppermute | solution.py:42
  123.1 26.7 %collective-permute-start.26 = (bf16[256,2048]{1,0:T(8,128)(2,1)S(1)}, bf16[256,2048]{1,0:T(8,128)(2,1)S(1)}, u32[]{:S(2)}, u32[]{:S(2)}) collective-permute-start(bf16[256,2048]{1,0:T(8,128)(2,1)S(1)} %bitcast.211), channel_id=1, source_target_pairs={{0,4},{4,0},{8,12},{12,8},{16,20},{20,16},{24,28},{28,24},{1,5},{5... | collective-permute-start | bytes 3145736 | tf_op jit(solution)/shard_map/ppermute | solution.py:42
  123.3 24.3 %collective-permute-start.27 = (bf16[128,2048]{1,0:T(8,128)(2,1)S(1)}, bf16[128,2048]{1,0:T(8,128)(2,1)S(1)}, u32[]{:S(2)}, u32[]{:S(2)}) collective-permute-start(bf16[128,2048]{1,0:T(8,128)(2,1)S(1)} %bitcast.236), channel_id=1, source_target_pairs={{0,1},{1,0},{2,3},{3,2},{4,5},{5,4},{6,7},{7,6},{8,9},{9,8},{10,11... | collective-permute-start | bytes 1572872 | tf_op jit(solution)/shard_map/ppermute | solution.py:42
  123.4 26.4 %collective-permute-start.28 = (bf16[256,1024]{1,0:T(8,128)(2,1)S(1)}, bf16[256,1024]{1,0:T(8,128)(2,1)S(1)}, u32[]{:S(2)}, u32[]{:S(2)}) collective-permute-start(bf16[256,1024]{1,0:T(8,128)(2,1)S(1)} %bitcast.230), channel_id=1, source_target_pairs={{0,2},{1,3},{2,0},{3,1},{4,6},{5,7},{6,4},{7,5},{8,10},{9,11},{10,... | collective-permute-start | bytes 1572872 | tf_op jit(solution)/shard_map/ppermute | solution.py:42
  131.1 18.7 %collective-permute-start.24 = (bf16[256,1024]{1,0:T(8,128)(2,1)S(1)}, bf16[256,1024]{1,0:T(8,128)(2,1)S(1)}, u32[]{:S(2)}, u32[]{:S(2)}) collective-permute-start(bf16[256,1024]{1,0:T(8,128)(2,1)S(1)} %get-tuple-element.674), channel_id=1, source_target_pairs={{0,8},{4,12},{8,0},{12,4},{16,24},{20,28},{24,16},{28,20},{1,9},{5... | collective-permute-start | bytes 1572872 | tf_op jit(solution)/shard_map/ppermute | solution.py:42
  150.0 25.6 %collective-permute-start.32 = (bf16[256,2048]{1,0:T(8,128)(2,1)S(1)}, bf16[256,2048]{1,0:T(8,128)(2,1)S(1)}, u32[]{:S(2)}, u32[]{:S(2)}) collective-permute-start(bf16[256,2048]{1,0:T(8,128)(2,1)S(1)} %bitcast.217), channel_id=1, source_target_pairs={{0,16},{4,20},{8,24},{12,28},{16,0},{20,4},{24,8},{28,12},{1,17},{... | collective-permute-start | bytes 3145736 | tf_op jit(solution)/shard_map/ppermute | solution.py:42
  151.6 24.0 %collective-permute-start.33 = (bf16[256,2048]{1,0:T(8,128)(2,1)S(1)}, bf16[256,2048]{1,0:T(8,128)(2,1)S(1)}, u32[]{:S(2)}, u32[]{:S(2)}) collective-permute-start(bf16[256,2048]{1,0:T(8,128)(2,1)S(1)} %bitcast.218), channel_id=1, source_target_pairs={{0,4},{4,0},{8,12},{12,8},{16,20},{20,16},{24,28},{28,24},{1,5},{5... | collective-permute-start | bytes 3145736 | tf_op jit(solution)/shard_map/ppermute | solution.py:42
  151.8 25.4 %collective-permute-start.34 = (bf16[512,1024]{1,0:T(8,128)(2,1)S(1)}, bf16[512,1024]{1,0:T(8,128)(2,1)S(1)}, u32[]{:S(2)}, u32[]{:S(2)}) collective-permute-start(bf16[512,1024]{1,0:T(8,128)(2,1)S(1)} %bitcast.220), channel_id=1, source_target_pairs={{0,1},{1,0},{2,3},{3,2},{4,5},{5,4},{6,7},{7,6},{8,9},{9,8},{10,11... | collective-permute-start | bytes 3145736 | tf_op jit(solution)/shard_map/ppermute | solution.py:42
  161.4 15.9 %collective-permute-start.30 = (bf16[128,1024]{1,0:T(8,128)(2,1)S(1)}, bf16[128,1024]{1,0:T(8,128)(2,1)S(1)}, u32[]{:S(2)}, u32[]{:S(2)}) collective-permute-start(bf16[128,1024]{1,0:T(8,128)(2,1)S(1)} %get-tuple-element.707), channel_id=1, source_target_pairs={{0,8},{4,12},{8,0},{12,4},{16,24},{20,28},{24,16},{28,20},{1,9},{5... | collective-permute-start | bytes 786440 | tf_op jit(solution)/shard_map/ppermute | solution.py:42
  162.0 15.3 %collective-permute-start.31 = (bf16[128,1024]{1,0:T(8,128)(2,1)S(1)}, bf16[128,1024]{1,0:T(8,128)(2,1)S(1)}, u32[]{:S(2)}, u32[]{:S(2)}) collective-permute-start(bf16[128,1024]{1,0:T(8,128)(2,1)S(1)} %get-tuple-element.708), channel_id=1, source_target_pairs={{0,8},{4,12},{8,0},{12,4},{16,24},{20,28},{24,16},{28,20},{1,9},{5... | collective-permute-start | bytes 786440 | tf_op jit(solution)/shard_map/ppermute | solution.py:42
  196.2 28.3 %collective-permute-start.41 = (bf16[256,2048]{1,0:T(8,128)(2,1)S(1)}, bf16[256,2048]{1,0:T(8,128)(2,1)S(1)}, u32[]{:S(2)}, u32[]{:S(2)}) collective-permute-start(bf16[256,2048]{1,0:T(8,128)(2,1)S(1)} %get-tuple-element.827), channel_id=1, source_target_pairs={{0,4},{4,0},{8,12},{12,8},{16,20},{20,16},{24,28},{28,24},{1,5},{5... | collective-permute-start | bytes 3145736 | tf_op jit(solution)/shard_map/ppermute | solution.py:42
  196.8 27.7 %collective-permute-start.45 = (bf16[256,2048]{1,0:T(8,128)(2,1)S(1)}, bf16[256,2048]{1,0:T(8,128)(2,1)S(1)}, u32[]{:S(2)}, u32[]{:S(2)}) collective-permute-start(bf16[256,2048]{1,0:T(8,128)(2,1)S(1)} %add_low.5), channel_id=1, source_target_pairs={{0,16},{4,20},{8,24},{12,28},{16,0},{20,4},{24,8},{28,12},{1,17},{... | collective-permute-start | bytes 3145736 | tf_op jit(solution)/shard_map/ppermute | solution.py:42
  198.2 26.3 %collective-permute-start.44 = (bf16[512,1024]{1,0:T(8,128)(2,1)S(1)}, bf16[512,1024]{1,0:T(8,128)(2,1)S(1)}, u32[]{:S(2)}, u32[]{:S(2)}) collective-permute-start(bf16[512,1024]{1,0:T(8,128)(2,1)S(1)} %bitcast.305), channel_id=1, source_target_pairs={{0,1},{1,0},{2,3},{3,2},{4,5},{5,4},{6,7},{7,6},{8,9},{9,8},{10,11... | collective-permute-start | bytes 3145736 | tf_op jit(solution)/shard_map/ppermute | solution.py:42
  227.3 27.8 %collective-permute-start.48 = (bf16[256,2048]{1,0:T(8,128)(2,1)S(1)}, bf16[256,2048]{1,0:T(8,128)(2,1)S(1)}, u32[]{:S(2)}, u32[]{:S(2)}) collective-permute-start(bf16[256,2048]{1,0:T(8,128)(2,1)S(1)} %get-tuple-element.894), channel_id=1, source_target_pairs={{0,4},{4,0},{8,12},{12,8},{16,20},{20,16},{24,28},{28,24},{1,5},{5... | collective-permute-start | bytes 3145736 | tf_op jit(solution)/shard_map/ppermute | solution.py:42
  227.6 27.4 %collective-permute-start.51 = (bf16[256,2048]{1,0:T(8,128)(2,1)S(1)}, bf16[256,2048]{1,0:T(8,128)(2,1)S(1)}, u32[]{:S(2)}, u32[]{:S(2)}) collective-permute-start(bf16[256,2048]{1,0:T(8,128)(2,1)S(1)} %add_low.6), channel_id=1, source_target_pairs={{0,16},{4,20},{8,24},{12,28},{16,0},{20,4},{24,8},{28,12},{1,17},{... | collective-permute-start | bytes 3145736 | tf_op jit(solution)/shard_map/ppermute | solution.py:42
  229.2 25.8 %collective-permute-start.49 = (bf16[256,1024]{1,0:T(8,128)(2,1)S(1)}, bf16[256,1024]{1,0:T(8,128)(2,1)S(1)}, u32[]{:S(2)}, u32[]{:S(2)}) collective-permute-start(bf16[256,1024]{1,0:T(8,128)(2,1)S(1)} %bitcast.307), channel_id=1, source_target_pairs={{0,2},{1,3},{2,0},{3,1},{4,6},{5,7},{6,4},{7,5},{8,10},{9,11},{10,... | collective-permute-start | bytes 1572872 | tf_op jit(solution)/shard_map/ppermute | solution.py:42
  231.2 23.8 %collective-permute-start.50 = (bf16[128,2048]{1,0:T(8,128)(2,1)S(1)}, bf16[128,2048]{1,0:T(8,128)(2,1)S(1)}, u32[]{:S(2)}, u32[]{:S(2)}) collective-permute-start(bf16[128,2048]{1,0:T(8,128)(2,1)S(1)} %bitcast.308), channel_id=1, source_target_pairs={{0,1},{1,0},{2,3},{3,2},{4,5},{5,4},{6,7},{7,6},{8,9},{9,8},{10,11... | collective-permute-start | bytes 1572872 | tf_op jit(solution)/shard_map/ppermute | solution.py:42
  258.5 33.0 %collective-permute-start.59 = (bf16[512,1024]{1,0:T(8,128)(2,1)S(1)}, bf16[512,1024]{1,0:T(8,128)(2,1)S(1)}, u32[]{:S(2)}, u32[]{:S(2)}) collective-permute-start(bf16[512,1024]{1,0:T(8,128)(2,1)S(1)} %add_low.7), channel_id=1, source_target_pairs={{0,16},{4,20},{8,24},{12,28},{16,0},{20,4},{24,8},{28,12},{1,17},{... | collective-permute-start | bytes 3145736 | tf_op jit(solution)/shard_map/ppermute | solution.py:42
  261.4 30.1 %collective-permute-start.58 = (bf16[256,1536]{1,0:T(8,128)(2,1)S(1)}, bf16[256,1536]{1,0:T(8,128)(2,1)S(1)}, u32[]{:S(2)}, u32[]{:S(2)}) collective-permute-start(bf16[256,1536]{1,0:T(8,128)(2,1)S(1)} %get-tuple-element.965), channel_id=1, source_target_pairs={{0,4},{4,0},{8,12},{12,8},{16,20},{20,16},{24,28},{28,24},{1,5},{5... | collective-permute-start | bytes 2359304 | tf_op jit(solution)/shard_map/ppermute | solution.py:42
  262.9 27.9 %collective-permute-start.61 = (bf16[128,2048]{1,0:T(8,128)(2,1)S(1)}, bf16[128,2048]{1,0:T(8,128)(2,1)S(1)}, u32[]{:S(2)}, u32[]{:S(2)}) collective-permute-start(bf16[128,2048]{1,0:T(8,128)(2,1)S(1)} %bitcast.306), channel_id=1, source_target_pairs={{0,1},{1,0},{2,3},{3,2},{4,5},{5,4},{6,7},{7,6},{8,9},{9,8},{10,11... | collective-permute-start | bytes 1572872 | tf_op jit(solution)/shard_map/ppermute | solution.py:42
  266.0 24.9 %collective-permute-start.62 = (bf16[256,512]{1,0:T(8,128)(2,1)S(1)}, bf16[256,512]{1,0:T(8,128)(2,1)S(1)}, u32[]{:S(2)}, u32[]{:S(2)}) collective-permute-start(bf16[256,512]{1,0:T(8,128)(2,1)S(1)} %bitcast.313), channel_id=1, source_target_pairs={{0,1},{1,0},{2,3},{3,2},{4,5},{5,4},{6,7},{7,6},{8,9},{9,8},{10,11... | collective-permute-start | bytes 786440 | tf_op jit(solution)/shard_map/ppermute | solution.py:42
  273.6 18.0 %collective-permute-start.60 = (bf16[64,2048]{1,0:T(8,128)(2,1)S(1)}, bf16[64,2048]{1,0:T(8,128)(2,1)S(1)}, u32[]{:S(2)}, u32[]{:S(2)}) collective-permute-start(bf16[64,2048]{1,0:T(8,128)(2,1)S(1)} %bitcast.312), channel_id=1, source_target_pairs={{0,2},{1,3},{2,0},{3,1},{4,6},{5,7},{6,4},{7,5},{8,10},{9,11},{10,... | collective-permute-start | bytes 786440 | tf_op jit(solution)/shard_map/ppermute | solution.py:42
  294.7 27.4 %collective-permute-start.66 = (bf16[256,2048]{1,0:T(8,128)(2,1)S(1)}, bf16[256,2048]{1,0:T(8,128)(2,1)}, u32[]{:S(2)}, u32[]{:S(2)}) collective-permute-start(bf16[256,2048]{1,0:T(8,128)(2,1)S(1)} %add_low.9), channel_id=1, source_target_pairs={{0,16},{4,20},{8,24},{12,28},{16,0},{20,4},{24,8},{28,12},{1,17},{... | collective-permute-start | bytes 3145736 | tf_op jit(solution)/shard_map/ppermute | solution.py:42
  299.9 22.1 %collective-permute-start.68 = (bf16[256,1024]{1,0:T(8,128)(2,1)S(1)}, bf16[256,1024]{1,0:T(8,128)(2,1)S(1)}, u32[]{:S(2)}, u32[]{:S(2)}) collective-permute-start(bf16[256,1024]{1,0:T(8,128)(2,1)S(1)} %bitcast.309), channel_id=1, source_target_pairs={{0,1},{1,0},{2,3},{3,2},{4,5},{5,4},{6,7},{7,6},{8,9},{9,8},{10,11... | collective-permute-start | bytes 1572872 | tf_op jit(solution)/shard_map/ppermute | solution.py:42
  302.9 19.2 %collective-permute-start.67 = (bf16[64,2048]{1,0:T(8,128)(2,1)S(1)}, bf16[64,2048]{1,0:T(8,128)(2,1)S(1)}, u32[]{:S(2)}, u32[]{:S(2)}) collective-permute-start(bf16[64,2048]{1,0:T(8,128)(2,1)S(1)} %bitcast.314), channel_id=1, source_target_pairs={{0,2},{1,3},{2,0},{3,1},{4,6},{5,7},{6,4},{7,5},{8,10},{9,11},{10,... | collective-permute-start | bytes 786440 | tf_op jit(solution)/shard_map/ppermute | solution.py:42
  326.9 14.9 %collective-permute-start.70 = (f32[32,3584]{1,0:T(8,128)}, f32[32,3584]{1,0:T(8,128)}, u32[]{:S(2)}, u32[]{:S(2)}) collective-permute-start(f32[32,3584]{1,0:T(8,128)} %get-tuple-element.1134), channel_id=1, source_target_pairs={{0,8},{4,12},{8,0},{12,4},{16,24},{20,28},{24,16},{28,20},{1,9},{5... | collective-permute-start | bytes 1376264 | tf_op jit(solution)/shard_map/ppermute | solution.py:42
  327.4 19.8 %collective-permute-start.72 = (bf16[256,1536]{1,0:T(8,128)(2,1)}, bf16[256,1536]{1,0:T(8,128)(2,1)}, u32[]{:S(2)}, u32[]{:S(2)}) collective-permute-start(bf16[256,1536]{1,0:T(8,128)(2,1)} %add_low.8), channel_id=1, source_target_pairs={{0,16},{4,20},{8,24},{12,28},{16,0},{20,4},{24,8},{28,12},{1,17},{... | collective-permute-start | bytes 2359304 | tf_op jit(solution)/shard_map/ppermute | solution.py:42
  328.8 18.5 %collective-permute-start.73 = (bf16[128,2048]{1,0:T(8,128)(2,1)}, bf16[128,2048]{1,0:T(8,128)(2,1)}, u32[]{:S(2)}, u32[]{:S(2)}) collective-permute-start(bf16[128,2048]{1,0:T(8,128)(2,1)} %bitcast.116), channel_id=1, source_target_pairs={{0,1},{1,0},{2,3},{3,2},{4,5},{5,4},{6,7},{7,6},{8,9},{9,8},{10,11... | collective-permute-start | bytes 1572872 | tf_op jit(solution)/shard_map/ppermute | solution.py:42
  331.7 15.6 %collective-permute-start.74 = (bf16[128,1024]{1,0:T(8,128)(2,1)}, bf16[128,1024]{1,0:T(8,128)(2,1)}, u32[]{:S(2)}, u32[]{:S(2)}) collective-permute-start(bf16[128,1024]{1,0:T(8,128)(2,1)} %bitcast.130), channel_id=1, source_target_pairs={{0,2},{1,3},{2,0},{3,1},{4,6},{5,7},{6,4},{7,5},{8,10},{9,11},{10,... | collective-permute-start | bytes 786440 | tf_op jit(solution)/shard_map/ppermute | solution.py:42
  347.3 19.2 %collective-permute-start.76 = (bf16[256,1024]{1,0:T(8,128)(2,1)S(1)}, bf16[256,1024]{1,0:T(8,128)(2,1)S(1)}, u32[]{:S(2)}, u32[]{:S(2)}) collective-permute-start(bf16[256,1024]{1,0:T(8,128)(2,1)S(1)} %get-tuple-element.1071), channel_id=1, source_target_pairs={{0,8},{4,12},{8,0},{12,4},{16,24},{20,28},{24,16},{28,20},{1,9},{5... | collective-permute-start | bytes 1572872 | tf_op jit(solution)/shard_map/ppermute | solution.py:42
  350.9 15.5 %collective-permute-start.78 = (bf16[128,1536]{1,0:T(8,128)(2,1)S(1)}, bf16[128,1536]{1,0:T(8,128)(2,1)S(1)}, u32[]{:S(2)}, u32[]{:S(2)}) collective-permute-start(bf16[128,1536]{1,0:T(8,128)(2,1)S(1)} %bitcast.310), channel_id=1, source_target_pairs={{0,1},{1,0},{2,3},{3,2},{4,5},{5,4},{6,7},{7,6},{8,9},{9,8},{10,11... | collective-permute-start | bytes 1179656 | tf_op jit(solution)/shard_map/ppermute | solution.py:42
  (129 other events, 1097.4 us)

commit v8 on v7

--- a/solution.py
+++ b/solution.py
@@ -471,8 +471,8 @@
         cols = pl.ds(n * third, third)
         qkv[:, cols] = dot(f[...], weight[:, cols]).astype(bf16)
 
-    def one_row(r, carry):
-        at = pl.ds(pl.multiple_of(r * length, length), length)
+    def one_row(r):
+        at = pl.ds(r * length, length)
         allowed = allow[r] > 0
         for p in range(third // 128):
             q = qkv[at, pl.ds(p * 128, 128)]
@@ -485,9 +485,9 @@
             mixed[at, pl.ds(p * 128, 128)] = jnp.where(
                 lanes_of(0, q.shape), halves[0], halves[1]
             ).astype(bf16)
-        return carry
-
-    lax.fori_loop(0, f.shape[0] // length, one_row, 0)
+
+    for r in range(f.shape[0] // length):
+        one_row(r)
     for k in range(2):
         cols = pl.ds(k * third, third)
         value = dot(mixed[...], out_block(weight, k, block, 3 * third))
@@ -514,8 +514,8 @@
     value = value + dot_t(d[:, pl.ds(third, third)], out_block(weight, 1, block, 3 * third))
     d_mixed[...] = value.astype(bf16)
 
-    def one_row(r, carry):
-        at = pl.ds(pl.multiple_of(r * length, length), length)
+    def one_row(r):
+        at = pl.ds(r * length, length)
         allowed = allow[r] > 0
         for p in range(third // 128):
             q = qkv[at, pl.ds(p * 128, 128)]
@@ -536,9 +536,9 @@
             for n, (halves, scale) in enumerate(((d_q, size), (d_k, size), (d_v, 1.0))):
                 value = jnp.where(pick, halves[0], halves[1]) * scale
                 d_qkv[at, pl.ds(n * third + p * 128, 128)] = value.astype(bf16)
-        return carry
-
-    lax.fori_loop(0, d.shape[0] // length, one_row, 0)
+
+    for r in range(d.shape[0] // length):
+        one_row(r)
     for n in range(keep.shape[1] // 256):
         cols = pl.ds(n * 256, 256)
         value = dot_t(d_qkv[...], weight[cols, pl.ds(0, 3 * third)])

time: 391 us -> 390 us (level)
  no operation moved by 1% of the time
where the time goes in v8:
time: 390 us; the launch traced here: 385 us
  waiting for transfers between devices  166 us (43%)
  Pallas kernels  101 us (26%)
  starting transfers between devices  85.4 us (22%)
  local copies, waits for them, and re-layouts  18.1 us (5%)
  other arithmetic  11.8 us (3%)
    ppermute x87, waiting for transfers between devices, flip(): lax.ppermute(value, axis, [(i, i ^ mask) for i in range(self.size[axis])])  166 us
    pallas_call x53, Pallas kernels, call(): pl.pallas_call(kernel, out_shape=[jax.ShapeDtypeStruct(shape, kind) for s...  90.6 us
    ppermute x87, starting transfers between devices, flip(): lax.ppermute(value, axis, [(i, i ^ mask) for i in range(self.size[axis])])  85.4 us
    unnamed x181, local copies, waits for them, and re-layouts  13.7 us
    pallas_call x6, Pallas kernels, update(): pl.pallas_call(kernel, grid=(1,), out_shape=[jax.ShapeDtypeStruct(shape,...  10.4 us
  transfers between devices with their start and end apart: 87, of which 41 were waited for; matrix products, arithmetic and copies ran while one was open for 3% of the time, Pallas kernels for 23%

profile of v8, /device:TPU:0, one launch (start us, length us, event | category | flops | bytes accessed | tf_op | source)
XLA Modules:
  0.0 385.3 jit_solution(633617622946303416)
XLA Ops:
  1.8 4.1 %collective-permute-start.1 = (bf16[128,1024]{1,0:T(8,128)(2,1)S(1)}, bf16[128,1024]{1,0:T(8,128)(2,1)S(1)}, u32[]{:S(2)}, u32[]{:S(2)}) collective-permute-start(bf16[128,1024]{1,0:T(8,128)(2,1)S(1)} %get-tuple-element.594), channel_id=1, source_target_pairs={{0,2},{1,3},{2,0},{3,1},{4,6},{5,7},{6,4},{7,5},{8,10},{9,11},{10,... | collective-permute-start | bytes 786440 | tf_op jit(solution)/shard_map/ppermute | solution.py:42
  14.9 2.9 collective-permute-done.1
  18.7 3.4 collective-permute-start.6
  25.0 9.7 %collective-permute-done.5 = bf16[32,2048]{1,0:T(8,128)(2,1)S(1)} collective-permute-done((bf16[32,2048]{1,0:T(8,128)(2,1)S(1)}, bf16[32,2048]{1,0:T(8,128)(2,1)S(1)}, u32[]{:S(2)}, u32[]{:S(2)}) %collective-permute-start.5) | collective-permute-done | bytes 131104 | tf_op jit(solution)/shard_map/ppermute | solution.py:42
  38.5 3.4 collective-permute-start.8
  41.9 1.8 collective-permute-start.9
  44.6 2.1 fusion
  47.7 12.4 %collective-permute-done.9 = bf16[64,2048]{1,0:T(8,128)(2,1)S(1)} collective-permute-done((bf16[64,2048]{1,0:T(8,128)(2,1)S(1)}, bf16[64,2048]{1,0:T(8,128)(2,1)S(1)}, u32[]{:S(2)}, u32[]{:S(2)}) %collective-permute-start.9) | collective-permute-done | bytes 262176 | tf_op jit(solution)/shard_map/ppermute | solution.py:42
  62.6 4.5 %collective-permute-start.15 = (bf16[128,2048]{1,0:T(8,128)(2,1)S(1)}, bf16[128,2048]{1,0:T(8,128)(2,1)S(1)}, u32[]{:S(2)}, u32[]{:S(2)}) collective-permute-start(bf16[128,2048]{1,0:T(8,128)(2,1)S(1)} %bitcast.238), channel_id=1, source_target_pairs={{0,1},{1,0},{2,3},{3,2},{4,5},{5,4},{6,7},{7,6},{8,9},{9,8},{10,11... | collective-permute-start | bytes 1572872 | tf_op jit(solution)/shard_map/ppermute | solution.py:42
  69.3 14.8 %collective-permute-done.16 = bf16[64,2048]{1,0:T(8,128)(2,1)S(1)} collective-permute-done((bf16[64,2048]{1,0:T(8,128)(2,1)S(1)}, bf16[64,2048]{1,0:T(8,128)(2,1)S(1)}, u32[]{:S(2)}, u32[]{:S(2)}) %collective-permute-start.16) | collective-permute-done | bytes 262176 | tf_op jit(solution)/shard_map/ppermute | solution.py:42
  84.8 2.6 collective-permute-done.13.q1.refs_3_.refs_8_
  91.2 3.7 collective-permute-start.21
  96.5 9.7 %attend.2 = (f32[256,1024]{1,0:T(8,128)}, bf16[256,1024]{1,0:T(8,128)(2,1)S(1)}, bf16[256,1536]{1,0:T(8,128)(2,1)S(1)}, bf16[256,512]{1,0:T(8,128)(2,1)S(1)}, f3...) custom-call(s32[2]{0:T(128)S(1)} %pad_add_fusion.place.up_place.dn_place, ...), custom_call_target="tpu_custom_call" | custom-call | tf_op jit(solution)/shard_map/attend/pallas_call | solution.py:54
  108.9 13.2 %collective-permute-done.22 = bf16[64,2048]{1,0:T(8,128)(2,1)S(1)} collective-permute-done((bf16[64,2048]{1,0:T(8,128)(2,1)S(1)}, bf16[64,2048]{1,0:T(8,128)(2,1)S(1)}, u32[]{:S(2)}, u32[]{:S(2)}) %collective-permute-start.22) | collective-permute-done | bytes 262176 | tf_op jit(solution)/shard_map/ppermute | solution.py:42
  123.1 2.1 collective-permute-start.28
  125.2 5.5 %feed.1 = (f32[256,1024]{1,0:T(8,128)S(1)}, bf16[256,1024]{1,0:T(8,128)(2,1)S(1)}, f32[256,2048]{1,0:T(8,128)S(1)}, bf16[256,2048]{1,0:T(8,128)(2,1)S(1)}, f32[2...) custom-call(s32[2]{0:T(128)S(1)} %pad_add_fusion.place.up_place.dn_place, s32[2]{0:T(128)S(1)} %pad_add_fusion.place.up_place.dn_place, ...), custom_call_target="tpu_custom_call" | custom-call | tf_op jit(solution)/shard_map/feed/pallas_call | solution.py:54
  131.4 16.0 %collective-permute-done.27 = bf16[128,2048]{1,0:T(8,128)(2,1)S(1)} collective-permute-done((bf16[128,2048]{1,0:T(8,128)(2,1)S(1)}, bf16[128,2048]{1,0:T(8,128)(2,1)S(1)}, u32[]{:S(2)}, u32[]{:S(2)}) %collective-permute-start.27) | collective-permute-done | bytes 524320 | tf_op jit(solution)/shard_map/ppermute | solution.py:42
  147.4 2.1 collective-permute-done.28
  152.2 8.1 %attend.3 = (f32[256,1024]{1,0:T(8,128)S(1)}, bf16[256,1024]{1,0:T(8,128)(2,1)S(1)}, bf16[256,1536]{1,0:T(8,128)(2,1)S(1)}, bf16[256,512]{1,0:T(8,128)(2,1)S(1)}...) custom-call(s32[2]{0:T(128)S(1)} %pad_add_fusion.place.up_place.dn_place, ...), custom_call_target="tpu_custom_call" | custom-call | tf_op jit(solution)/shard_map/attend/pallas_call | solution.py:54
  162.5 12.8 %collective-permute-done.32.refs_7_ = bf16[256,2048]{1,0:T(8,128)(2,1)S(1)} collective-permute-done((bf16[256,2048]{1,0:T(8,128)(2,1)S(1)}, bf16[256,2048]{1,0:T(8,128)(2,1)S(1)}, u32[]{:S(2)}, u32[]{:S(2)}) %collective-permute-start.32) | collective-permute-done | bytes 1048608 | tf_op jit(solution)/shard_map/ppermute | solution.py:42
  182.7 6.6 %feed_turn.1 = (f32[256,1024]{1,0:T(8,128)S(1)}, bf16[256,1024]{1,0:T(8,128)(2,1)S(1)}, bf16[256,2048]{1,0:T(8,128)(2,1)S(1)}, bf16[256,2048]{1,0:T(8,128)(2,1)S...) custom-call(s32[2]{0:T(128)S(1)} %pad_add_fusion.place.up_place.dn_place, ...), custom_call_target="tpu_custom_call" | custom-call | tf_op jit(solution)/shard_map/feed_turn/pallas_call | solution.py:54
  189.3 1.8 down_grad.2
  191.3 1.8 up_grad.3
  194.0 1.9 collective-permute-done.40.two
  200.3 7.1 %collective-permute-done.38.refs_4_ = bf16[128,1024]{1,0:T(8,128)(2,1)S(1)} collective-permute-done((bf16[128,1024]{1,0:T(8,128)(2,1)S(1)}, bf16[128,1024]{1,0:T(8,128)(2,1)S(1)}, u32[]{:S(2)}, u32[]{:S(2)}) %collective-permute-start.38) | collective-permute-done | bytes 262176 | tf_op jit(solution)/shard_map/ppermute | solution.py:42
  207.4 4.8 %collective-permute-done.39.refs_5_ = bf16[128,1024]{1,0:T(8,128)(2,1)S(1)} collective-permute-done((bf16[128,1024]{1,0:T(8,128)(2,1)S(1)}, bf16[128,1024]{1,0:T(8,128)(2,1)S(1)}, u32[]{:S(2)}, u32[]{:S(2)}) %collective-permute-start.39) | collective-permute-done | bytes 262176 | tf_op jit(solution)/shard_map/ppermute | solution.py:42
  212.2 11.5 %attend_back.2 = (f32[256,1024]{1,0:T(8,128)S(1)}, bf16[256,1024]{1,0:T(8,128)(2,1)}, f32[1,1024]{1,0:T(1,128)S(1)}, f32[1,1024]{1,0:T(1,128)S(1)}, bf16[256,153...) custom-call(s32[2]{0:T(128)S(1)} %pad_add_fusion.place.up_place.dn_p, ...), custom_call_target="tpu_custom_call" | custom-call | tf_op jit(solution)/shard_map/attend_back/pallas_call | solution.py:54
  223.9 2.6 collective-permute-done.47.two
  230.9 10.7 %collective-permute-done.46.refs_0_ = bf16[256,1024]{1,0:T(8,128)(2,1)S(1)} collective-permute-done((bf16[256,1024]{1,0:T(8,128)(2,1)S(1)}, bf16[256,1024]{1,0:T(8,128)(2,1)S(1)}, u32[]{:S(2)}, u32[]{:S(2)}) %collective-permute-start.46) | collective-permute-done | bytes 524320 | tf_op jit(solution)/shard_map/ppermute | solution.py:42
  241.6 6.5 %feed_back.1 = (f32[256,1024]{1,0:T(8,128)S(1)}, bf16[256,1024]{1,0:T(8,128)(2,1)S(1)}, f32[1,1024]{1,0:T(1,128)S(1)}, f32[1,1024]{1,0:T(1,128)S(1)}, bf16[256,2...) custom-call(s32[2]{0:T(128)S(1)} %pad_add_fusion.place.up_place.dn_place, ...), custom_call_target="tpu_custom_call" | custom-call | tf_op jit(solution)/shard_map/feed_back/pallas_call | solution.py:54
  250.9 1.8 down_grad.3
  254.9 2.1 collective-permute-done.53.two
  266.2 6.7 %collective-permute-done.52.refs_4_ = bf16[256,1024]{1,0:T(8,128)(2,1)S(1)} collective-permute-done((bf16[256,1024]{1,0:T(8,128)(2,1)S(1)}, bf16[256,1024]{1,0:T(8,128)(2,1)S(1)}, u32[]{:S(2)}, u32[]{:S(2)}) %collective-permute-start.52) | collective-permute-done | bytes 524320 | tf_op jit(solution)/shard_map/ppermute | solution.py:42
  274.7 12.9 %attend_back.3 = (f32[256,1024]{1,0:T(8,128)S(1)}, bf16[256,1024]{1,0:T(8,128)(2,1)}, f32[1,1024]{1,0:T(1,128)S(1)}, f32[1,1024]{1,0:T(1,128)S(1)}, bf16[256,153...) custom-call(s32[2]{0:T(128)S(1)} %pad_add_fusion.place.up_place.dn_p, ...), custom_call_target="tpu_custom_call" | custom-call | tf_op jit(solution)/shard_map/attend_back/pallas_call | solution.py:54
  290.4 2.6 collective-permute-done.64.two
  301.6 1.9 collective-permute-start.67
  303.6 4.8 %collective-permute-done.63.refs_0_ = bf16[256,1024]{1,0:T(8,128)(2,1)} collective-permute-done((bf16[256,1024]{1,0:T(8,128)(2,1)}, bf16[256,1024]{1,0:T(8,128)(2,1)}, u32[]{:S(2)}, u32[]{:S(2)}) %collective-permute-start.63) | collective-permute-done | bytes 524320 | tf_op jit(solution)/shard_map/ppermute | solution.py:42
  308.4 2.8 norm_back.1
  311.2 3.6 collective-permute-done.69
  314.8 6.0 %collective-permute-done.68 = bf16[256,1024]{1,0:T(8,128)(2,1)S(1)} collective-permute-done((bf16[256,1024]{1,0:T(8,128)(2,1)S(1)}, bf16[256,1024]{1,0:T(8,128)(2,1)S(1)}, u32[]{:S(2)}, u32[]{:S(2)}) %collective-permute-start.68) | collective-permute-done | bytes 524320 | tf_op jit(solution)/shard_map/ppermute | solution.py:42
  320.9 2.8 add_split.22
  335.2 3.6 down.1
  340.5 2.4 finish.2
  342.9 2.5 finish_up.2
  357.5 2.5 collective-permute-done.77
  360.0 3.5 collective-permute-done.79
  367.6 2.7 collective-permute-start.84
  374.9 1.8 collective-permute-done.84
  (421 shorter events, 124.9 us)
Async XLA Ops:
  1.8 16.0 %collective-permute-start.1 = (bf16[128,1024]{1,0:T(8,128)(2,1)S(1)}, bf16[128,1024]{1,0:T(8,128)(2,1)S(1)}, u32[]{:S(2)}, u32[]{:S(2)}) collective-permute-start(bf16[128,1024]{1,0:T(8,128)(2,1)S(1)} %get-tuple-element.594), channel_id=1, source_target_pairs={{0,2},{1,3},{2,0},{3,1},{4,6},{5,7},{6,4},{7,5},{8,10},{9,11},{10,... | collective-permute-start | bytes 786440 | tf_op jit(solution)/shard_map/ppermute | solution.py:42
  13.3 22.7 %collective-permute-start.4 = (bf16[272,1024]{1,0:T(8,128)(2,1)}, bf16[272,1024]{1,0:T(8,128)(2,1)}, u32[]{:S(2)}, u32[]{:S(2)}) collective-permute-start(bf16[272,1024]{1,0:T(8,128)(2,1)} %pad_maximum_fusion), channel_id=1, source_target_pairs={{0,8},{4,12},{8,0},{12,4},{16,24},{20,28},{24,16},{28,20},{1,9},{5... | collective-permute-start | bytes 1671176 | tf_op jit(solution)/shard_map/ppermute | solution.py:42
  17.9 19.1 %collective-permute-start.7 = (bf16[256,1024]{1,0:T(8,128)(2,1)S(1)}, bf16[256,1024]{1,0:T(8,128)(2,1)S(1)}, u32[]{:S(2)}, u32[]{:S(2)}) collective-permute-start(bf16[256,1024]{1,0:T(8,128)(2,1)S(1)} %bitcast.232), channel_id=1, source_target_pairs={{0,1},{1,0},{2,3},{3,2},{4,5},{5,4},{6,7},{7,6},{8,9},{9,8},{10,11... | collective-permute-start | bytes 1572872 | tf_op jit(solution)/shard_map/ppermute | solution.py:42
  18.7 17.3 %collective-permute-start.6 = (bf16[64,2176]{1,0:T(8,128)(2,1)S(1)}, bf16[64,2176]{1,0:T(8,128)(2,1)S(1)}, u32[]{:S(2)}, u32[]{:S(2)}) collective-permute-start(bf16[64,2176]{1,0:T(8,128)(2,1)S(1)} %bitcast.240), channel_id=1, source_target_pairs={{0,2},{1,3},{2,0},{3,1},{4,6},{5,7},{6,4},{7,5},{8,10},{9,11},{10,... | collective-permute-start | bytes 835592 | tf_op jit(solution)/shard_map/ppermute | solution.py:42
  37.1 23.7 %collective-permute-start.10 = (bf16[512,1024]{1,0:T(8,128)(2,1)S(1)}, bf16[512,1024]{1,0:T(8,128)(2,1)S(1)}, u32[]{:S(2)}, u32[]{:S(2)}) collective-permute-start(bf16[512,1024]{1,0:T(8,128)(2,1)S(1)} %bitcast.206), channel_id=1, source_target_pairs={{0,16},{4,20},{8,24},{12,28},{16,0},{20,4},{24,8},{28,12},{1,17},{... | collective-permute-start | bytes 3145736 | tf_op jit(solution)/shard_map/ppermute | solution.py:42
  38.4 22.4 %collective-permute-start.11 = (bf16[512,1024]{1,0:T(8,128)(2,1)S(1)}, bf16[512,1024]{1,0:T(8,128)(2,1)S(1)}, u32[]{:S(2)}, u32[]{:S(2)}) collective-permute-start(bf16[512,1024]{1,0:T(8,128)(2,1)S(1)} %bitcast.207), channel_id=1, source_target_pairs={{0,4},{4,0},{8,12},{12,8},{16,20},{20,16},{24,28},{28,24},{1,5},{5... | collective-permute-start | bytes 3145736 | tf_op jit(solution)/shard_map/ppermute | solution.py:42
  38.5 22.3 %collective-permute-start.8 = (bf16[128,2176]{1,0:T(8,128)(2,1)S(1)}, bf16[128,2176]{1,0:T(8,128)(2,1)S(1)}, u32[]{:S(2)}, u32[]{:S(2)}) collective-permute-start(bf16[128,2176]{1,0:T(8,128)(2,1)S(1)} %bitcast.228), channel_id=1, source_target_pairs={{0,1},{1,0},{2,3},{3,2},{4,5},{5,4},{6,7},{7,6},{8,9},{9,8},{10,11... | collective-permute-start | bytes 1671176 | tf_op jit(solution)/shard_map/ppermute | solution.py:42
  41.9 18.2 %collective-permute-start.9 = (bf16[64,2048]{1,0:T(8,128)(2,1)S(1)}, bf16[64,2048]{1,0:T(8,128)(2,1)S(1)}, u32[]{:S(2)}, u32[]{:S(2)}) collective-permute-start(bf16[64,2048]{1,0:T(8,128)(2,1)S(1)} %bitcast.257), channel_id=1, source_target_pairs={{0,2},{1,3},{2,0},{3,1},{4,6},{5,7},{6,4},{7,5},{8,10},{9,11},{10,... | collective-permute-start | bytes 786440 | tf_op jit(solution)/shard_map/ppermute | solution.py:42
  61.0 26.5 %collective-permute-start.13 = (bf16[256,2176]{1,0:T(8,128)(2,1)S(1)}, bf16[256,2176]{1,0:T(8,128)(2,1)S(1)}, u32[]{:S(2)}, u32[]{:S(2)}) collective-permute-start(bf16[256,2176]{1,0:T(8,128)(2,1)S(1)} %bitcast.201), channel_id=1, source_target_pairs={{0,16},{4,20},{8,24},{12,28},{16,0},{20,4},{24,8},{28,12},{1,17},{... | collective-permute-start | bytes 3342344 | tf_op jit(solution)/shard_map/ppermute | solution.py:42
  62.1 25.4 %collective-permute-start.14 = (bf16[256,2176]{1,0:T(8,128)(2,1)S(1)}, bf16[256,2176]{1,0:T(8,128)(2,1)S(1)}, u32[]{:S(2)}, u32[]{:S(2)}) collective-permute-start(bf16[256,2176]{1,0:T(8,128)(2,1)S(1)} %bitcast.202), channel_id=1, source_target_pairs={{0,4},{4,0},{8,12},{12,8},{16,20},{20,16},{24,28},{28,24},{1,5},{5... | collective-permute-start | bytes 3342344 | tf_op jit(solution)/shard_map/ppermute | solution.py:42
  62.1 22.8 %collective-permute-start.12 = (bf16[512,1024]{1,0:T(8,128)(2,1)S(1)}, bf16[512,1024]{1,0:T(8,128)(2,1)S(1)}, u32[]{:S(2)}, u32[]{:S(2)}) collective-permute-start(bf16[512,1024]{1,0:T(8,128)(2,1)S(1)} %collective-permute-done.10.refs_9_), channel_id=1, source_target_pairs={{0,4},{4,0},{8,12},{12,8},{16,20},{20,16},{24,28},{28,24},{1,5},{5... | collective-permute-start | bytes 3145736 | tf_op jit(solution)/shard_map/ppermute | solution.py:42
  62.6 22.2 %collective-permute-start.15 = (bf16[128,2048]{1,0:T(8,128)(2,1)S(1)}, bf16[128,2048]{1,0:T(8,128)(2,1)S(1)}, u32[]{:S(2)}, u32[]{:S(2)}) collective-permute-start(bf16[128,2048]{1,0:T(8,128)(2,1)S(1)} %bitcast.238), channel_id=1, source_target_pairs={{0,1},{1,0},{2,3},{3,2},{4,5},{5,4},{6,7},{7,6},{8,9},{9,8},{10,11... | collective-permute-start | bytes 1572872 | tf_op jit(solution)/shard_map/ppermute | solution.py:42
  67.9 16.2 %collective-permute-start.16 = (bf16[64,2048]{1,0:T(8,128)(2,1)S(1)}, bf16[64,2048]{1,0:T(8,128)(2,1)S(1)}, u32[]{:S(2)}, u32[]{:S(2)}) collective-permute-start(bf16[64,2048]{1,0:T(8,128)(2,1)S(1)} %bitcast.262), channel_id=1, source_target_pairs={{0,2},{1,3},{2,0},{3,1},{4,6},{5,7},{6,4},{7,5},{8,10},{9,11},{10,... | collective-permute-start | bytes 786440 | tf_op jit(solution)/shard_map/ppermute | solution.py:42
  88.5 33.5 %collective-permute-start.19 = (bf16[256,2048]{1,0:T(8,128)(2,1)}, bf16[256,2048]{1,0:T(8,128)(2,1)}, u32[]{:S(2)}, u32[]{:S(2)}) collective-permute-start(bf16[256,2048]{1,0:T(8,128)(2,1)} %bitcast.46.refs_4_), channel_id=1, source_target_pairs={{0,16},{4,20},{8,24},{12,28},{16,0},{20,4},{24,8},{28,12},{1,17},{... | collective-permute-start | bytes 3145736 | tf_op jit(solution)/shard_map/ppermute | solution.py:42
  89.0 33.0 %collective-permute-start.20 = (bf16[256,2048]{1,0:T(8,128)(2,1)}, bf16[256,2048]{1,0:T(8,128)(2,1)}, u32[]{:S(2)}, u32[]{:S(2)}) collective-permute-start(bf16[256,2048]{1,0:T(8,128)(2,1)} %bitcast.46.refs_4_), channel_id=1, source_target_pairs={{0,4},{4,0},{8,12},{12,8},{16,20},{20,16},{24,28},{28,24},{1,5},{5... | collective-permute-start | bytes 3145736 | tf_op jit(solution)/shard_map/ppermute | solution.py:42
  91.2 30.8 %collective-permute-start.21 = (bf16[128,2048]{1,0:T(8,128)(2,1)S(1)}, bf16[128,2048]{1,0:T(8,128)(2,1)S(1)}, u32[]{:S(2)}, u32[]{:S(2)}) collective-permute-start(bf16[128,2048]{1,0:T(8,128)(2,1)S(1)} %bitcast.234), channel_id=1, source_target_pairs={{0,1},{1,0},{2,3},{3,2},{4,5},{5,4},{6,7},{7,6},{8,9},{9,8},{10,11... | collective-permute-start | bytes 1572872 | tf_op jit(solution)/shard_map/ppermute | solution.py:42
  106.2 15.8 %collective-permute-start.18 = (bf16[256,1024]{1,0:T(8,128)(2,1)S(1)}, bf16[256,1024]{1,0:T(8,128)(2,1)S(1)}, u32[]{:S(2)}, u32[]{:S(2)}) collective-permute-start(bf16[256,1024]{1,0:T(8,128)(2,1)S(1)} %get-tuple-element.640), channel_id=1, source_target_pairs={{0,8},{4,12},{8,0},{12,4},{16,24},{20,28},{24,16},{28,20},{1,9},{5... | collective-permute-start | bytes 1572872 | tf_op jit(solution)/shard_map/ppermute | solution.py:42
  122.2 27.3 %collective-permute-start.25 = (bf16[256,2048]{1,0:T(8,128)(2,1)S(1)}, bf16[256,2048]{1,0:T(8,128)(2,1)S(1)}, u32[]{:S(2)}, u32[]{:S(2)}) collective-permute-start(bf16[256,2048]{1,0:T(8,128)(2,1)S(1)} %bitcast.210), channel_id=1, source_target_pairs={{0,16},{4,20},{8,24},{12,28},{16,0},{20,4},{24,8},{28,12},{1,17},{... | collective-permute-start | bytes 3145736 | tf_op jit(solution)/shard_map/ppermute | solution.py:42
  122.8 26.7 %collective-permute-start.26 = (bf16[256,2048]{1,0:T(8,128)(2,1)S(1)}, bf16[256,2048]{1,0:T(8,128)(2,1)S(1)}, u32[]{:S(2)}, u32[]{:S(2)}) collective-permute-start(bf16[256,2048]{1,0:T(8,128)(2,1)S(1)} %bitcast.211), channel_id=1, source_target_pairs={{0,4},{4,0},{8,12},{12,8},{16,20},{20,16},{24,28},{28,24},{1,5},{5... | collective-permute-start | bytes 3145736 | tf_op jit(solution)/shard_map/ppermute | solution.py:42
  123.0 24.3 %collective-permute-start.27 = (bf16[128,2048]{1,0:T(8,128)(2,1)S(1)}, bf16[128,2048]{1,0:T(8,128)(2,1)S(1)}, u32[]{:S(2)}, u32[]{:S(2)}) collective-permute-start(bf16[128,2048]{1,0:T(8,128)(2,1)S(1)} %bitcast.236), channel_id=1, source_target_pairs={{0,1},{1,0},{2,3},{3,2},{4,5},{5,4},{6,7},{7,6},{8,9},{9,8},{10,11... | collective-permute-start | bytes 1572872 | tf_op jit(solution)/shard_map/ppermute | solution.py:42
  123.1 26.4 %collective-permute-start.28 = (bf16[256,1024]{1,0:T(8,128)(2,1)S(1)}, bf16[256,1024]{1,0:T(8,128)(2,1)S(1)}, u32[]{:S(2)}, u32[]{:S(2)}) collective-permute-start(bf16[256,1024]{1,0:T(8,128)(2,1)S(1)} %bitcast.230), channel_id=1, source_target_pairs={{0,2},{1,3},{2,0},{3,1},{4,6},{5,7},{6,4},{7,5},{8,10},{9,11},{10,... | collective-permute-start | bytes 1572872 | tf_op jit(solution)/shard_map/ppermute | solution.py:42
  130.8 18.7 %collective-permute-start.24 = (bf16[256,1024]{1,0:T(8,128)(2,1)S(1)}, bf16[256,1024]{1,0:T(8,128)(2,1)S(1)}, u32[]{:S(2)}, u32[]{:S(2)}) collective-permute-start(bf16[256,1024]{1,0:T(8,128)(2,1)S(1)} %get-tuple-element.674), channel_id=1, source_target_pairs={{0,8},{4,12},{8,0},{12,4},{16,24},{20,28},{24,16},{28,20},{1,9},{5... | collective-permute-start | bytes 1572872 | tf_op jit(solution)/shard_map/ppermute | solution.py:42
  149.7 25.6 %collective-permute-start.32 = (bf16[256,2048]{1,0:T(8,128)(2,1)S(1)}, bf16[256,2048]{1,0:T(8,128)(2,1)S(1)}, u32[]{:S(2)}, u32[]{:S(2)}) collective-permute-start(bf16[256,2048]{1,0:T(8,128)(2,1)S(1)} %bitcast.217), channel_id=1, source_target_pairs={{0,16},{4,20},{8,24},{12,28},{16,0},{20,4},{24,8},{28,12},{1,17},{... | collective-permute-start | bytes 3145736 | tf_op jit(solution)/shard_map/ppermute | solution.py:42
  151.3 24.0 %collective-permute-start.33 = (bf16[256,2048]{1,0:T(8,128)(2,1)S(1)}, bf16[256,2048]{1,0:T(8,128)(2,1)S(1)}, u32[]{:S(2)}, u32[]{:S(2)}) collective-permute-start(bf16[256,2048]{1,0:T(8,128)(2,1)S(1)} %bitcast.218), channel_id=1, source_target_pairs={{0,4},{4,0},{8,12},{12,8},{16,20},{20,16},{24,28},{28,24},{1,5},{5... | collective-permute-start | bytes 3145736 | tf_op jit(solution)/shard_map/ppermute | solution.py:42
  151.5 25.4 %collective-permute-start.34 = (bf16[512,1024]{1,0:T(8,128)(2,1)S(1)}, bf16[512,1024]{1,0:T(8,128)(2,1)S(1)}, u32[]{:S(2)}, u32[]{:S(2)}) collective-permute-start(bf16[512,1024]{1,0:T(8,128)(2,1)S(1)} %bitcast.220), channel_id=1, source_target_pairs={{0,1},{1,0},{2,3},{3,2},{4,5},{5,4},{6,7},{7,6},{8,9},{9,8},{10,11... | collective-permute-start | bytes 3145736 | tf_op jit(solution)/shard_map/ppermute | solution.py:42
  160.4 16.6 %collective-permute-start.30 = (bf16[128,1024]{1,0:T(8,128)(2,1)S(1)}, bf16[128,1024]{1,0:T(8,128)(2,1)S(1)}, u32[]{:S(2)}, u32[]{:S(2)}) collective-permute-start(bf16[128,1024]{1,0:T(8,128)(2,1)S(1)} %get-tuple-element.707), channel_id=1, source_target_pairs={{0,8},{4,12},{8,0},{12,4},{16,24},{20,28},{24,16},{28,20},{1,9},{5... | collective-permute-start | bytes 786440 | tf_op jit(solution)/shard_map/ppermute | solution.py:42
  161.0 16.0 %collective-permute-start.31 = (bf16[128,1024]{1,0:T(8,128)(2,1)S(1)}, bf16[128,1024]{1,0:T(8,128)(2,1)S(1)}, u32[]{:S(2)}, u32[]{:S(2)}) collective-permute-start(bf16[128,1024]{1,0:T(8,128)(2,1)S(1)} %get-tuple-element.708), channel_id=1, source_target_pairs={{0,8},{4,12},{8,0},{12,4},{16,24},{20,28},{24,16},{28,20},{1,9},{5... | collective-permute-start | bytes 786440 | tf_op jit(solution)/shard_map/ppermute | solution.py:42
  195.9 27.9 %collective-permute-start.41 = (bf16[256,2048]{1,0:T(8,128)(2,1)S(1)}, bf16[256,2048]{1,0:T(8,128)(2,1)S(1)}, u32[]{:S(2)}, u32[]{:S(2)}) collective-permute-start(bf16[256,2048]{1,0:T(8,128)(2,1)S(1)} %get-tuple-element.827), channel_id=1, source_target_pairs={{0,4},{4,0},{8,12},{12,8},{16,20},{20,16},{24,28},{28,24},{1,5},{5... | collective-permute-start | bytes 3145736 | tf_op jit(solution)/shard_map/ppermute | solution.py:42
  196.5 27.3 %collective-permute-start.45 = (bf16[256,2048]{1,0:T(8,128)(2,1)S(1)}, bf16[256,2048]{1,0:T(8,128)(2,1)S(1)}, u32[]{:S(2)}, u32[]{:S(2)}) collective-permute-start(bf16[256,2048]{1,0:T(8,128)(2,1)S(1)} %add_low.5), channel_id=1, source_target_pairs={{0,16},{4,20},{8,24},{12,28},{16,0},{20,4},{24,8},{28,12},{1,17},{... | collective-permute-start | bytes 3145736 | tf_op jit(solution)/shard_map/ppermute | solution.py:42
  197.9 25.9 %collective-permute-start.44 = (bf16[512,1024]{1,0:T(8,128)(2,1)S(1)}, bf16[512,1024]{1,0:T(8,128)(2,1)S(1)}, u32[]{:S(2)}, u32[]{:S(2)}) collective-permute-start(bf16[512,1024]{1,0:T(8,128)(2,1)S(1)} %bitcast.305), channel_id=1, source_target_pairs={{0,1},{1,0},{2,3},{3,2},{4,5},{5,4},{6,7},{7,6},{8,9},{9,8},{10,11... | collective-permute-start | bytes 3145736 | tf_op jit(solution)/shard_map/ppermute | solution.py:42
  226.6 27.8 %collective-permute-start.48 = (bf16[256,2048]{1,0:T(8,128)(2,1)S(1)}, bf16[256,2048]{1,0:T(8,128)(2,1)S(1)}, u32[]{:S(2)}, u32[]{:S(2)}) collective-permute-start(bf16[256,2048]{1,0:T(8,128)(2,1)S(1)} %get-tuple-element.894), channel_id=1, source_target_pairs={{0,4},{4,0},{8,12},{12,8},{16,20},{20,16},{24,28},{28,24},{1,5},{5... | collective-permute-start | bytes 3145736 | tf_op jit(solution)/shard_map/ppermute | solution.py:42
  226.9 27.4 %collective-permute-start.51 = (bf16[256,2048]{1,0:T(8,128)(2,1)S(1)}, bf16[256,2048]{1,0:T(8,128)(2,1)S(1)}, u32[]{:S(2)}, u32[]{:S(2)}) collective-permute-start(bf16[256,2048]{1,0:T(8,128)(2,1)S(1)} %add_low.6), channel_id=1, source_target_pairs={{0,16},{4,20},{8,24},{12,28},{16,0},{20,4},{24,8},{28,12},{1,17},{... | collective-permute-start | bytes 3145736 | tf_op jit(solution)/shard_map/ppermute | solution.py:42
  228.5 25.8 %collective-permute-start.49 = (bf16[256,1024]{1,0:T(8,128)(2,1)S(1)}, bf16[256,1024]{1,0:T(8,128)(2,1)S(1)}, u32[]{:S(2)}, u32[]{:S(2)}) collective-permute-start(bf16[256,1024]{1,0:T(8,128)(2,1)S(1)} %bitcast.307), channel_id=1, source_target_pairs={{0,2},{1,3},{2,0},{3,1},{4,6},{5,7},{6,4},{7,5},{8,10},{9,11},{10,... | collective-permute-start | bytes 1572872 | tf_op jit(solution)/shard_map/ppermute | solution.py:42
  230.5 23.8 %collective-permute-start.50 = (bf16[128,2048]{1,0:T(8,128)(2,1)S(1)}, bf16[128,2048]{1,0:T(8,128)(2,1)S(1)}, u32[]{:S(2)}, u32[]{:S(2)}) collective-permute-start(bf16[128,2048]{1,0:T(8,128)(2,1)S(1)} %bitcast.308), channel_id=1, source_target_pairs={{0,1},{1,0},{2,3},{3,2},{4,5},{5,4},{6,7},{7,6},{8,9},{9,8},{10,11... | collective-permute-start | bytes 1572872 | tf_op jit(solution)/shard_map/ppermute | solution.py:42
  257.8 32.4 %collective-permute-start.59 = (bf16[512,1024]{1,0:T(8,128)(2,1)S(1)}, bf16[512,1024]{1,0:T(8,128)(2,1)S(1)}, u32[]{:S(2)}, u32[]{:S(2)}) collective-permute-start(bf16[512,1024]{1,0:T(8,128)(2,1)S(1)} %add_low.7), channel_id=1, source_target_pairs={{0,16},{4,20},{8,24},{12,28},{16,0},{20,4},{24,8},{28,12},{1,17},{... | collective-permute-start | bytes 3145736 | tf_op jit(solution)/shard_map/ppermute | solution.py:42
  260.7 29.5 %collective-permute-start.58 = (bf16[256,1536]{1,0:T(8,128)(2,1)S(1)}, bf16[256,1536]{1,0:T(8,128)(2,1)S(1)}, u32[]{:S(2)}, u32[]{:S(2)}) collective-permute-start(bf16[256,1536]{1,0:T(8,128)(2,1)S(1)} %get-tuple-element.965), channel_id=1, source_target_pairs={{0,4},{4,0},{8,12},{12,8},{16,20},{20,16},{24,28},{28,24},{1,5},{5... | collective-permute-start | bytes 2359304 | tf_op jit(solution)/shard_map/ppermute | solution.py:42
  262.2 27.3 %collective-permute-start.61 = (bf16[128,2048]{1,0:T(8,128)(2,1)S(1)}, bf16[128,2048]{1,0:T(8,128)(2,1)S(1)}, u32[]{:S(2)}, u32[]{:S(2)}) collective-permute-start(bf16[128,2048]{1,0:T(8,128)(2,1)S(1)} %bitcast.306), channel_id=1, source_target_pairs={{0,1},{1,0},{2,3},{3,2},{4,5},{5,4},{6,7},{7,6},{8,9},{9,8},{10,11... | collective-permute-start | bytes 1572872 | tf_op jit(solution)/shard_map/ppermute | solution.py:42
  265.3 24.3 %collective-permute-start.62 = (bf16[256,512]{1,0:T(8,128)(2,1)S(1)}, bf16[256,512]{1,0:T(8,128)(2,1)S(1)}, u32[]{:S(2)}, u32[]{:S(2)}) collective-permute-start(bf16[256,512]{1,0:T(8,128)(2,1)S(1)} %bitcast.313), channel_id=1, source_target_pairs={{0,1},{1,0},{2,3},{3,2},{4,5},{5,4},{6,7},{7,6},{8,9},{9,8},{10,11... | collective-permute-start | bytes 786440 | tf_op jit(solution)/shard_map/ppermute | solution.py:42
  272.9 17.4 %collective-permute-start.60 = (bf16[64,2048]{1,0:T(8,128)(2,1)S(1)}, bf16[64,2048]{1,0:T(8,128)(2,1)S(1)}, u32[]{:S(2)}, u32[]{:S(2)}) collective-permute-start(bf16[64,2048]{1,0:T(8,128)(2,1)S(1)} %bitcast.312), channel_id=1, source_target_pairs={{0,2},{1,3},{2,0},{3,1},{4,6},{5,7},{6,4},{7,5},{8,10},{9,11},{10,... | collective-permute-start | bytes 786440 | tf_op jit(solution)/shard_map/ppermute | solution.py:42
  293.4 27.4 %collective-permute-start.66 = (bf16[256,2048]{1,0:T(8,128)(2,1)S(1)}, bf16[256,2048]{1,0:T(8,128)(2,1)}, u32[]{:S(2)}, u32[]{:S(2)}) collective-permute-start(bf16[256,2048]{1,0:T(8,128)(2,1)S(1)} %add_low.9), channel_id=1, source_target_pairs={{0,16},{4,20},{8,24},{12,28},{16,0},{20,4},{24,8},{28,12},{1,17},{... | collective-permute-start | bytes 3145736 | tf_op jit(solution)/shard_map/ppermute | solution.py:42
  298.7 22.1 %collective-permute-start.68 = (bf16[256,1024]{1,0:T(8,128)(2,1)S(1)}, bf16[256,1024]{1,0:T(8,128)(2,1)S(1)}, u32[]{:S(2)}, u32[]{:S(2)}) collective-permute-start(bf16[256,1024]{1,0:T(8,128)(2,1)S(1)} %bitcast.309), channel_id=1, source_target_pairs={{0,1},{1,0},{2,3},{3,2},{4,5},{5,4},{6,7},{7,6},{8,9},{9,8},{10,11... | collective-permute-start | bytes 1572872 | tf_op jit(solution)/shard_map/ppermute | solution.py:42
  301.6 19.2 %collective-permute-start.67 = (bf16[64,2048]{1,0:T(8,128)(2,1)S(1)}, bf16[64,2048]{1,0:T(8,128)(2,1)S(1)}, u32[]{:S(2)}, u32[]{:S(2)}) collective-permute-start(bf16[64,2048]{1,0:T(8,128)(2,1)S(1)} %bitcast.314), channel_id=1, source_target_pairs={{0,2},{1,3},{2,0},{3,1},{4,6},{5,7},{6,4},{7,5},{8,10},{9,11},{10,... | collective-permute-start | bytes 786440 | tf_op jit(solution)/shard_map/ppermute | solution.py:42
  325.6 14.9 %collective-permute-start.70 = (f32[32,3584]{1,0:T(8,128)}, f32[32,3584]{1,0:T(8,128)}, u32[]{:S(2)}, u32[]{:S(2)}) collective-permute-start(f32[32,3584]{1,0:T(8,128)} %get-tuple-element.1134), channel_id=1, source_target_pairs={{0,8},{4,12},{8,0},{12,4},{16,24},{20,28},{24,16},{28,20},{1,9},{5... | collective-permute-start | bytes 1376264 | tf_op jit(solution)/shard_map/ppermute | solution.py:42
  326.2 19.8 %collective-permute-start.72 = (bf16[256,1536]{1,0:T(8,128)(2,1)}, bf16[256,1536]{1,0:T(8,128)(2,1)}, u32[]{:S(2)}, u32[]{:S(2)}) collective-permute-start(bf16[256,1536]{1,0:T(8,128)(2,1)} %add_low.8), channel_id=1, source_target_pairs={{0,16},{4,20},{8,24},{12,28},{16,0},{20,4},{24,8},{28,12},{1,17},{... | collective-permute-start | bytes 2359304 | tf_op jit(solution)/shard_map/ppermute | solution.py:42
  327.5 18.5 %collective-permute-start.73 = (bf16[128,2048]{1,0:T(8,128)(2,1)}, bf16[128,2048]{1,0:T(8,128)(2,1)}, u32[]{:S(2)}, u32[]{:S(2)}) collective-permute-start(bf16[128,2048]{1,0:T(8,128)(2,1)} %bitcast.116), channel_id=1, source_target_pairs={{0,1},{1,0},{2,3},{3,2},{4,5},{5,4},{6,7},{7,6},{8,9},{9,8},{10,11... | collective-permute-start | bytes 1572872 | tf_op jit(solution)/shard_map/ppermute | solution.py:42
  330.4 15.6 %collective-permute-start.74 = (bf16[128,1024]{1,0:T(8,128)(2,1)}, bf16[128,1024]{1,0:T(8,128)(2,1)}, u32[]{:S(2)}, u32[]{:S(2)}) collective-permute-start(bf16[128,1024]{1,0:T(8,128)(2,1)} %bitcast.130), channel_id=1, source_target_pairs={{0,2},{1,3},{2,0},{3,1},{4,6},{5,7},{6,4},{7,5},{8,10},{9,11},{10,... | collective-permute-start | bytes 786440 | tf_op jit(solution)/shard_map/ppermute | solution.py:42
  346.0 19.2 %collective-permute-start.76 = (bf16[256,1024]{1,0:T(8,128)(2,1)S(1)}, bf16[256,1024]{1,0:T(8,128)(2,1)S(1)}, u32[]{:S(2)}, u32[]{:S(2)}) collective-permute-start(bf16[256,1024]{1,0:T(8,128)(2,1)S(1)} %get-tuple-element.1071), channel_id=1, source_target_pairs={{0,8},{4,12},{8,0},{12,4},{16,24},{20,28},{24,16},{28,20},{1,9},{5... | collective-permute-start | bytes 1572872 | tf_op jit(solution)/shard_map/ppermute | solution.py:42
  349.6 15.5 %collective-permute-start.78 = (bf16[128,1536]{1,0:T(8,128)(2,1)S(1)}, bf16[128,1536]{1,0:T(8,128)(2,1)S(1)}, u32[]{:S(2)}, u32[]{:S(2)}) collective-permute-start(bf16[128,1536]{1,0:T(8,128)(2,1)S(1)} %bitcast.310), channel_id=1, source_target_pairs={{0,1},{1,0},{2,3},{3,2},{4,5},{5,4},{6,7},{7,6},{8,9},{9,8},{10,11... | collective-permute-start | bytes 1179656 | tf_op jit(solution)/shard_map/ppermute | solution.py:42
  (129 other events, 1095.1 us)

commit v9 on v8

--- a/solution.py
+++ b/solution.py
@@ -443,7 +443,7 @@
 def score(q, k, allowed, size):
     scores = jnp.where(allowed, dot_t(q, k) * size, -1e30)
     exponent = jnp.exp(scores - jnp.max(scores, axis=-1, keepdims=True))
-    return exponent / jnp.sum(exponent, axis=-1, keepdims=True)
+    return exponent * (1.0 / jnp.sum(exponent, axis=-1, keepdims=True))
 
 
 def lanes_of(which, shape):
@@ -1274,21 +1274,21 @@
     table_step(1, [SIDE])
     table = live.table.reshape(*(len(sl.high) + len(sl.deep)) * [2], count, -1)
     live.put(table=table, down=finish_down(0, g_down0, []))
+    table_step(0, sl.high)
     live.seal(g_up0a, g_attn0, g_down1)
 
     g_up0a.start()
     out_act = live.feed1[0][:length] + (live.keep[:length] + live.other[0][length:].astype(f32))
     rest = feed // 2 - up_first
     big0 = two_sides([g_attn0, g_up0b], [2 * width, rest], [part, rest])
-    table_step(0, sl.high)
     table_step(-3, sl.deep[-1:])
-    live.put(out_act=out_act.astype(bf16), down=finish_down(1, g_down1, live.down), big0=big0)
+    live.put(out_act=out_act.astype(bf16), big0=big0)
     live.seal(g_up0a)
 
     table_step(0, sl.deep[:-1])
     up0a = two_sides([g_up0a], [up_first], [up_first])
     grad_big, new_m_big, step_big = finish(0, live.big0, live.big, up0a)
-    grad_down, new_m_down, step_down = live.down
+    grad_down, new_m_down, step_down = finish_down(1, g_down1, live.down)
     grad_table = live.table
     new_m_table, step_table = adam_update(m_table, v_table, grad_table)
     return (

time: 390 us -> 390 us (level)
  transfers between devices with their start and end apart: 87 -> 87, of which waited for: 41 -> 40; matrix products, arithmetic and copies ran while one was open for 3% -> 3% of each run, Pallas kernels for 23% -> 23%
where the time goes in v9:
time: 390 us; the launch traced here: 385 us
  waiting for transfers between devices  168 us (43%)
  Pallas kernels  101 us (26%)
  starting transfers between devices  83.7 us (21%)
  local copies, waits for them, and re-layouts  18.1 us (5%)
  other arithmetic  11.8 us (3%)
    ppermute x87, waiting for transfers between devices, flip(): lax.ppermute(value, axis, [(i, i ^ mask) for i in range(self.size[axis])])  168 us
    pallas_call x53, Pallas kernels, call(): pl.pallas_call(kernel, out_shape=[jax.ShapeDtypeStruct(shape, kind) for s...  90.6 us
    ppermute x87, starting transfers between devices, flip(): lax.ppermute(value, axis, [(i, i ^ mask) for i in range(self.size[axis])])  83.7 us
    unnamed x181, local copies, waits for them, and re-layouts  13.7 us
    pallas_call x6, Pallas kernels, update(): pl.pallas_call(kernel, grid=(1,), out_shape=[jax.ShapeDtypeStruct(shape,...  10.4 us
  transfers between devices with their start and end apart: 87, of which 40 were waited for; matrix products, arithmetic and copies ran while one was open for 3% of the time, Pallas kernels for 23%

profile of v9, /device:TPU:0, one launch (start us, length us, event | category | flops | bytes accessed | tf_op | source)
XLA Modules:
  0.0 385.3 jit_solution(16186293472558139808)
XLA Ops:
  1.8 4.1 %collective-permute-start.1 = (bf16[128,1024]{1,0:T(8,128)(2,1)S(1)}, bf16[128,1024]{1,0:T(8,128)(2,1)S(1)}, u32[]{:S(2)}, u32[]{:S(2)}) collective-permute-start(bf16[128,1024]{1,0:T(8,128)(2,1)S(1)} %get-tuple-element.595), channel_id=1, source_target_pairs={{0,2},{1,3},{2,0},{3,1},{4,6},{5,7},{6,4},{7,5},{8,10},{9,11},{10,... | collective-permute-start | bytes 786440 | tf_op jit(solution)/shard_map/ppermute | solution.py:42
  14.9 2.9 collective-permute-done.1
  18.7 3.4 collective-permute-start.6
  25.0 9.7 %collective-permute-done.5 = bf16[32,2048]{1,0:T(8,128)(2,1)S(1)} collective-permute-done((bf16[32,2048]{1,0:T(8,128)(2,1)S(1)}, bf16[32,2048]{1,0:T(8,128)(2,1)S(1)}, u32[]{:S(2)}, u32[]{:S(2)}) %collective-permute-start.5) | collective-permute-done | bytes 131104 | tf_op jit(solution)/shard_map/ppermute | solution.py:42
  38.5 3.4 collective-permute-start.8
  41.9 1.8 collective-permute-start.9
  44.6 2.1 fusion
  47.7 12.4 %collective-permute-done.9 = bf16[64,2048]{1,0:T(8,128)(2,1)S(1)} collective-permute-done((bf16[64,2048]{1,0:T(8,128)(2,1)S(1)}, bf16[64,2048]{1,0:T(8,128)(2,1)S(1)}, u32[]{:S(2)}, u32[]{:S(2)}) %collective-permute-start.9) | collective-permute-done | bytes 262176 | tf_op jit(solution)/shard_map/ppermute | solution.py:42
  62.6 4.5 %collective-permute-start.15 = (bf16[128,2048]{1,0:T(8,128)(2,1)S(1)}, bf16[128,2048]{1,0:T(8,128)(2,1)S(1)}, u32[]{:S(2)}, u32[]{:S(2)}) collective-permute-start(bf16[128,2048]{1,0:T(8,128)(2,1)S(1)} %bitcast.238), channel_id=1, source_target_pairs={{0,1},{1,0},{2,3},{3,2},{4,5},{5,4},{6,7},{7,6},{8,9},{9,8},{10,11... | collective-permute-start | bytes 1572872 | tf_op jit(solution)/shard_map/ppermute | solution.py:42
  69.3 14.8 %collective-permute-done.16 = bf16[64,2048]{1,0:T(8,128)(2,1)S(1)} collective-permute-done((bf16[64,2048]{1,0:T(8,128)(2,1)S(1)}, bf16[64,2048]{1,0:T(8,128)(2,1)S(1)}, u32[]{:S(2)}, u32[]{:S(2)}) %collective-permute-start.16) | collective-permute-done | bytes 262176 | tf_op jit(solution)/shard_map/ppermute | solution.py:42
  84.8 2.6 collective-permute-done.13.q1.refs_3_.refs_8_
  91.2 3.7 collective-permute-start.21
  96.5 9.7 %attend.2 = (f32[256,1024]{1,0:T(8,128)}, bf16[256,1024]{1,0:T(8,128)(2,1)S(1)}, bf16[256,1536]{1,0:T(8,128)(2,1)S(1)}, bf16[256,512]{1,0:T(8,128)(2,1)S(1)}, f3...) custom-call(s32[2]{0:T(128)S(1)} %pad_add_fusion.place.up_place.dn_place, ...), custom_call_target="tpu_custom_call" | custom-call | tf_op jit(solution)/shard_map/attend/pallas_call | solution.py:54
  108.9 13.2 %collective-permute-done.22 = bf16[64,2048]{1,0:T(8,128)(2,1)S(1)} collective-permute-done((bf16[64,2048]{1,0:T(8,128)(2,1)S(1)}, bf16[64,2048]{1,0:T(8,128)(2,1)S(1)}, u32[]{:S(2)}, u32[]{:S(2)}) %collective-permute-start.22) | collective-permute-done | bytes 262176 | tf_op jit(solution)/shard_map/ppermute | solution.py:42
  123.1 2.1 collective-permute-start.28
  125.2 5.5 %feed.1 = (f32[256,1024]{1,0:T(8,128)S(1)}, bf16[256,1024]{1,0:T(8,128)(2,1)S(1)}, f32[256,2048]{1,0:T(8,128)S(1)}, bf16[256,2048]{1,0:T(8,128)(2,1)S(1)}, f32[2...) custom-call(s32[2]{0:T(128)S(1)} %pad_add_fusion.place.up_place.dn_place, s32[2]{0:T(128)S(1)} %pad_add_fusion.place.up_place.dn_place, ...), custom_call_target="tpu_custom_call" | custom-call | tf_op jit(solution)/shard_map/feed/pallas_call | solution.py:54
  131.4 16.0 %collective-permute-done.27 = bf16[128,2048]{1,0:T(8,128)(2,1)S(1)} collective-permute-done((bf16[128,2048]{1,0:T(8,128)(2,1)S(1)}, bf16[128,2048]{1,0:T(8,128)(2,1)S(1)}, u32[]{:S(2)}, u32[]{:S(2)}) %collective-permute-start.27) | collective-permute-done | bytes 524320 | tf_op jit(solution)/shard_map/ppermute | solution.py:42
  147.4 2.1 collective-permute-done.28
  152.2 8.1 %attend.3 = (f32[256,1024]{1,0:T(8,128)S(1)}, bf16[256,1024]{1,0:T(8,128)(2,1)S(1)}, bf16[256,1536]{1,0:T(8,128)(2,1)S(1)}, bf16[256,512]{1,0:T(8,128)(2,1)S(1)}...) custom-call(s32[2]{0:T(128)S(1)} %pad_add_fusion.place.up_place.dn_place, ...), custom_call_target="tpu_custom_call" | custom-call | tf_op jit(solution)/shard_map/attend/pallas_call | solution.py:54
  162.5 12.8 %collective-permute-done.32.refs_7_ = bf16[256,2048]{1,0:T(8,128)(2,1)S(1)} collective-permute-done((bf16[256,2048]{1,0:T(8,128)(2,1)S(1)}, bf16[256,2048]{1,0:T(8,128)(2,1)S(1)}, u32[]{:S(2)}, u32[]{:S(2)}) %collective-permute-start.32) | collective-permute-done | bytes 1048608 | tf_op jit(solution)/shard_map/ppermute | solution.py:42
  175.3 1.7 collective-permute-done.34
  182.7 6.6 %feed_turn.1 = (f32[256,1024]{1,0:T(8,128)S(1)}, bf16[256,1024]{1,0:T(8,128)(2,1)S(1)}, bf16[256,2048]{1,0:T(8,128)(2,1)S(1)}, bf16[256,2048]{1,0:T(8,128)(2,1)S...) custom-call(s32[2]{0:T(128)S(1)} %pad_add_fusion.place.up_place.dn_place, ...), custom_call_target="tpu_custom_call" | custom-call | tf_op jit(solution)/shard_map/feed_turn/pallas_call | solution.py:54
  189.3 1.8 down_grad.2
  191.3 1.8 up_grad.3
  194.0 1.9 collective-permute-done.40.two
  200.3 7.1 %collective-permute-done.38.refs_4_ = bf16[128,1024]{1,0:T(8,128)(2,1)S(1)} collective-permute-done((bf16[128,1024]{1,0:T(8,128)(2,1)S(1)}, bf16[128,1024]{1,0:T(8,128)(2,1)S(1)}, u32[]{:S(2)}, u32[]{:S(2)}) %collective-permute-start.38) | collective-permute-done | bytes 262176 | tf_op jit(solution)/shard_map/ppermute | solution.py:42
  207.4 4.8 %collective-permute-done.39.refs_5_ = bf16[128,1024]{1,0:T(8,128)(2,1)S(1)} collective-permute-done((bf16[128,1024]{1,0:T(8,128)(2,1)S(1)}, bf16[128,1024]{1,0:T(8,128)(2,1)S(1)}, u32[]{:S(2)}, u32[]{:S(2)}) %collective-permute-start.39) | collective-permute-done | bytes 262176 | tf_op jit(solution)/shard_map/ppermute | solution.py:42
  212.2 11.5 %attend_back.2 = (f32[256,1024]{1,0:T(8,128)S(1)}, bf16[256,1024]{1,0:T(8,128)(2,1)}, f32[1,1024]{1,0:T(1,128)S(1)}, f32[1,1024]{1,0:T(1,128)S(1)}, bf16[256,153...) custom-call(s32[2]{0:T(128)S(1)} %pad_add_fusion.place.up_place.dn_p, ...), custom_call_target="tpu_custom_call" | custom-call | tf_op jit(solution)/shard_map/attend_back/pallas_call | solution.py:54
  223.9 2.6 collective-permute-done.47.two
  230.9 10.7 %collective-permute-done.46.refs_0_ = bf16[256,1024]{1,0:T(8,128)(2,1)S(1)} collective-permute-done((bf16[256,1024]{1,0:T(8,128)(2,1)S(1)}, bf16[256,1024]{1,0:T(8,128)(2,1)S(1)}, u32[]{:S(2)}, u32[]{:S(2)}) %collective-permute-start.46) | collective-permute-done | bytes 524320 | tf_op jit(solution)/shard_map/ppermute | solution.py:42
  241.6 6.5 %feed_back.1 = (f32[256,1024]{1,0:T(8,128)S(1)}, bf16[256,1024]{1,0:T(8,128)(2,1)S(1)}, f32[1,1024]{1,0:T(1,128)S(1)}, f32[1,1024]{1,0:T(1,128)S(1)}, bf16[256,2...) custom-call(s32[2]{0:T(128)S(1)} %pad_add_fusion.place.up_place.dn_place, ...), custom_call_target="tpu_custom_call" | custom-call | tf_op jit(solution)/shard_map/feed_back/pallas_call | solution.py:54
  250.9 1.8 down_grad.3
  254.9 2.1 collective-permute-done.53.two
  266.2 6.7 %collective-permute-done.52.refs_4_ = bf16[256,1024]{1,0:T(8,128)(2,1)S(1)} collective-permute-done((bf16[256,1024]{1,0:T(8,128)(2,1)S(1)}, bf16[256,1024]{1,0:T(8,128)(2,1)S(1)}, u32[]{:S(2)}, u32[]{:S(2)}) %collective-permute-start.52) | collective-permute-done | bytes 524320 | tf_op jit(solution)/shard_map/ppermute | solution.py:42
  274.7 12.9 %attend_back.3 = (f32[256,1024]{1,0:T(8,128)S(1)}, bf16[256,1024]{1,0:T(8,128)(2,1)}, f32[1,1024]{1,0:T(1,128)S(1)}, f32[1,1024]{1,0:T(1,128)S(1)}, bf16[256,153...) custom-call(s32[2]{0:T(128)S(1)} %pad_add_fusion.place.up_place.dn_p, ...), custom_call_target="tpu_custom_call" | custom-call | tf_op jit(solution)/shard_map/attend_back/pallas_call | solution.py:54
  290.4 2.6 collective-permute-done.64.two
  301.6 1.9 collective-permute-start.67
  303.6 4.8 %collective-permute-done.63.refs_0_ = bf16[256,1024]{1,0:T(8,128)(2,1)} collective-permute-done((bf16[256,1024]{1,0:T(8,128)(2,1)}, bf16[256,1024]{1,0:T(8,128)(2,1)}, u32[]{:S(2)}, u32[]{:S(2)}) %collective-permute-start.63) | collective-permute-done | bytes 524320 | tf_op jit(solution)/shard_map/ppermute | solution.py:42
  308.4 2.8 norm_back.1
  311.2 3.6 collective-permute-done.69
  314.8 6.0 %collective-permute-done.68 = bf16[256,1024]{1,0:T(8,128)(2,1)S(1)} collective-permute-done((bf16[256,1024]{1,0:T(8,128)(2,1)S(1)}, bf16[256,1024]{1,0:T(8,128)(2,1)S(1)}, u32[]{:S(2)}, u32[]{:S(2)}) %collective-permute-start.68) | collective-permute-done | bytes 524320 | tf_op jit(solution)/shard_map/ppermute | solution.py:42
  320.9 2.8 add_split.22
  335.2 3.6 down.1
  340.5 2.4 finish.2
  342.9 2.5 finish_up.2
  356.1 3.9 %collective-permute-done.77 = f32[2,4,9,128]{3,1,2,0:T(4,128)S(1)} collective-permute-done((f32[2,4,9,128]{3,1,2,0:T(4,128)S(1)}, f32[2,4,9,128]{3,1,2,0:T(4,128)S(1)}, u32[]{:S(2)}, u32[]{:S(2)}) %collective-permute-start.77) | collective-permute-done | bytes 36896 | tf_op jit(solution)/shard_map/ppermute | solution.py:42
  366.1 2.2 collective-permute-start.83
  370.1 6.8 %collective-permute-done.84 = bf16[64,1536]{1,0:T(8,128)(2,1)S(1)} collective-permute-done((bf16[64,1536]{1,0:T(8,128)(2,1)S(1)}, bf16[64,1536]{1,0:T(8,128)(2,1)S(1)}, u32[]{:S(2)}, u32[]{:S(2)}) %collective-permute-start.84) | collective-permute-done | bytes 196640 | tf_op jit(solution)/shard_map/ppermute | solution.py:42
  (421 shorter events, 120.8 us)
Async XLA Ops:
  1.8 16.0 %collective-permute-start.1 = (bf16[128,1024]{1,0:T(8,128)(2,1)S(1)}, bf16[128,1024]{1,0:T(8,128)(2,1)S(1)}, u32[]{:S(2)}, u32[]{:S(2)}) collective-permute-start(bf16[128,1024]{1,0:T(8,128)(2,1)S(1)} %get-tuple-element.595), channel_id=1, source_target_pairs={{0,2},{1,3},{2,0},{3,1},{4,6},{5,7},{6,4},{7,5},{8,10},{9,11},{10,... | collective-permute-start | bytes 786440 | tf_op jit(solution)/shard_map/ppermute | solution.py:42
  13.3 22.7 %collective-permute-start.4 = (bf16[272,1024]{1,0:T(8,128)(2,1)}, bf16[272,1024]{1,0:T(8,128)(2,1)}, u32[]{:S(2)}, u32[]{:S(2)}) collective-permute-start(bf16[272,1024]{1,0:T(8,128)(2,1)} %pad_maximum_fusion), channel_id=1, source_target_pairs={{0,8},{4,12},{8,0},{12,4},{16,24},{20,28},{24,16},{28,20},{1,9},{5... | collective-permute-start | bytes 1671176 | tf_op jit(solution)/shard_map/ppermute | solution.py:42
  17.9 19.1 %collective-permute-start.7 = (bf16[256,1024]{1,0:T(8,128)(2,1)S(1)}, bf16[256,1024]{1,0:T(8,128)(2,1)S(1)}, u32[]{:S(2)}, u32[]{:S(2)}) collective-permute-start(bf16[256,1024]{1,0:T(8,128)(2,1)S(1)} %bitcast.232), channel_id=1, source_target_pairs={{0,1},{1,0},{2,3},{3,2},{4,5},{5,4},{6,7},{7,6},{8,9},{9,8},{10,11... | collective-permute-start | bytes 1572872 | tf_op jit(solution)/shard_map/ppermute | solution.py:42
  18.7 17.3 %collective-permute-start.6 = (bf16[64,2176]{1,0:T(8,128)(2,1)S(1)}, bf16[64,2176]{1,0:T(8,128)(2,1)S(1)}, u32[]{:S(2)}, u32[]{:S(2)}) collective-permute-start(bf16[64,2176]{1,0:T(8,128)(2,1)S(1)} %bitcast.240), channel_id=1, source_target_pairs={{0,2},{1,3},{2,0},{3,1},{4,6},{5,7},{6,4},{7,5},{8,10},{9,11},{10,... | collective-permute-start | bytes 835592 | tf_op jit(solution)/shard_map/ppermute | solution.py:42
  37.1 23.7 %collective-permute-start.10 = (bf16[512,1024]{1,0:T(8,128)(2,1)S(1)}, bf16[512,1024]{1,0:T(8,128)(2,1)S(1)}, u32[]{:S(2)}, u32[]{:S(2)}) collective-permute-start(bf16[512,1024]{1,0:T(8,128)(2,1)S(1)} %bitcast.206), channel_id=1, source_target_pairs={{0,16},{4,20},{8,24},{12,28},{16,0},{20,4},{24,8},{28,12},{1,17},{... | collective-permute-start | bytes 3145736 | tf_op jit(solution)/shard_map/ppermute | solution.py:42
  38.4 22.4 %collective-permute-start.11 = (bf16[512,1024]{1,0:T(8,128)(2,1)S(1)}, bf16[512,1024]{1,0:T(8,128)(2,1)S(1)}, u32[]{:S(2)}, u32[]{:S(2)}) collective-permute-start(bf16[512,1024]{1,0:T(8,128)(2,1)S(1)} %bitcast.207), channel_id=1, source_target_pairs={{0,4},{4,0},{8,12},{12,8},{16,20},{20,16},{24,28},{28,24},{1,5},{5... | collective-permute-start | bytes 3145736 | tf_op jit(solution)/shard_map/ppermute | solution.py:42
  38.5 22.3 %collective-permute-start.8 = (bf16[128,2176]{1,0:T(8,128)(2,1)S(1)}, bf16[128,2176]{1,0:T(8,128)(2,1)S(1)}, u32[]{:S(2)}, u32[]{:S(2)}) collective-permute-start(bf16[128,2176]{1,0:T(8,128)(2,1)S(1)} %bitcast.228), channel_id=1, source_target_pairs={{0,1},{1,0},{2,3},{3,2},{4,5},{5,4},{6,7},{7,6},{8,9},{9,8},{10,11... | collective-permute-start | bytes 1671176 | tf_op jit(solution)/shard_map/ppermute | solution.py:42
  41.9 18.2 %collective-permute-start.9 = (bf16[64,2048]{1,0:T(8,128)(2,1)S(1)}, bf16[64,2048]{1,0:T(8,128)(2,1)S(1)}, u32[]{:S(2)}, u32[]{:S(2)}) collective-permute-start(bf16[64,2048]{1,0:T(8,128)(2,1)S(1)} %bitcast.257), channel_id=1, source_target_pairs={{0,2},{1,3},{2,0},{3,1},{4,6},{5,7},{6,4},{7,5},{8,10},{9,11},{10,... | collective-permute-start | bytes 786440 | tf_op jit(solution)/shard_map/ppermute | solution.py:42
  61.0 26.5 %collective-permute-start.13 = (bf16[256,2176]{1,0:T(8,128)(2,1)S(1)}, bf16[256,2176]{1,0:T(8,128)(2,1)S(1)}, u32[]{:S(2)}, u32[]{:S(2)}) collective-permute-start(bf16[256,2176]{1,0:T(8,128)(2,1)S(1)} %bitcast.201), channel_id=1, source_target_pairs={{0,16},{4,20},{8,24},{12,28},{16,0},{20,4},{24,8},{28,12},{1,17},{... | collective-permute-start | bytes 3342344 | tf_op jit(solution)/shard_map/ppermute | solution.py:42
  62.1 25.4 %collective-permute-start.14 = (bf16[256,2176]{1,0:T(8,128)(2,1)S(1)}, bf16[256,2176]{1,0:T(8,128)(2,1)S(1)}, u32[]{:S(2)}, u32[]{:S(2)}) collective-permute-start(bf16[256,2176]{1,0:T(8,128)(2,1)S(1)} %bitcast.202), channel_id=1, source_target_pairs={{0,4},{4,0},{8,12},{12,8},{16,20},{20,16},{24,28},{28,24},{1,5},{5... | collective-permute-start | bytes 3342344 | tf_op jit(solution)/shard_map/ppermute | solution.py:42
  62.1 22.8 %collective-permute-start.12 = (bf16[512,1024]{1,0:T(8,128)(2,1)S(1)}, bf16[512,1024]{1,0:T(8,128)(2,1)S(1)}, u32[]{:S(2)}, u32[]{:S(2)}) collective-permute-start(bf16[512,1024]{1,0:T(8,128)(2,1)S(1)} %collective-permute-done.10.refs_9_), channel_id=1, source_target_pairs={{0,4},{4,0},{8,12},{12,8},{16,20},{20,16},{24,28},{28,24},{1,5},{5... | collective-permute-start | bytes 3145736 | tf_op jit(solution)/shard_map/ppermute | solution.py:42
  62.6 22.2 %collective-permute-start.15 = (bf16[128,2048]{1,0:T(8,128)(2,1)S(1)}, bf16[128,2048]{1,0:T(8,128)(2,1)S(1)}, u32[]{:S(2)}, u32[]{:S(2)}) collective-permute-start(bf16[128,2048]{1,0:T(8,128)(2,1)S(1)} %bitcast.238), channel_id=1, source_target_pairs={{0,1},{1,0},{2,3},{3,2},{4,5},{5,4},{6,7},{7,6},{8,9},{9,8},{10,11... | collective-permute-start | bytes 1572872 | tf_op jit(solution)/shard_map/ppermute | solution.py:42
  67.9 16.2 %collective-permute-start.16 = (bf16[64,2048]{1,0:T(8,128)(2,1)S(1)}, bf16[64,2048]{1,0:T(8,128)(2,1)S(1)}, u32[]{:S(2)}, u32[]{:S(2)}) collective-permute-start(bf16[64,2048]{1,0:T(8,128)(2,1)S(1)} %bitcast.262), channel_id=1, source_target_pairs={{0,2},{1,3},{2,0},{3,1},{4,6},{5,7},{6,4},{7,5},{8,10},{9,11},{10,... | collective-permute-start | bytes 786440 | tf_op jit(solution)/shard_map/ppermute | solution.py:42
  88.5 33.5 %collective-permute-start.19 = (bf16[256,2048]{1,0:T(8,128)(2,1)}, bf16[256,2048]{1,0:T(8,128)(2,1)}, u32[]{:S(2)}, u32[]{:S(2)}) collective-permute-start(bf16[256,2048]{1,0:T(8,128)(2,1)} %bitcast.46.refs_4_), channel_id=1, source_target_pairs={{0,16},{4,20},{8,24},{12,28},{16,0},{20,4},{24,8},{28,12},{1,17},{... | collective-permute-start | bytes 3145736 | tf_op jit(solution)/shard_map/ppermute | solution.py:42
  89.0 33.0 %collective-permute-start.20 = (bf16[256,2048]{1,0:T(8,128)(2,1)}, bf16[256,2048]{1,0:T(8,128)(2,1)}, u32[]{:S(2)}, u32[]{:S(2)}) collective-permute-start(bf16[256,2048]{1,0:T(8,128)(2,1)} %bitcast.46.refs_4_), channel_id=1, source_target_pairs={{0,4},{4,0},{8,12},{12,8},{16,20},{20,16},{24,28},{28,24},{1,5},{5... | collective-permute-start | bytes 3145736 | tf_op jit(solution)/shard_map/ppermute | solution.py:42
  91.2 30.8 %collective-permute-start.21 = (bf16[128,2048]{1,0:T(8,128)(2,1)S(1)}, bf16[128,2048]{1,0:T(8,128)(2,1)S(1)}, u32[]{:S(2)}, u32[]{:S(2)}) collective-permute-start(bf16[128,2048]{1,0:T(8,128)(2,1)S(1)} %bitcast.234), channel_id=1, source_target_pairs={{0,1},{1,0},{2,3},{3,2},{4,5},{5,4},{6,7},{7,6},{8,9},{9,8},{10,11... | collective-permute-start | bytes 1572872 | tf_op jit(solution)/shard_map/ppermute | solution.py:42
  106.2 15.8 %collective-permute-start.18 = (bf16[256,1024]{1,0:T(8,128)(2,1)S(1)}, bf16[256,1024]{1,0:T(8,128)(2,1)S(1)}, u32[]{:S(2)}, u32[]{:S(2)}) collective-permute-start(bf16[256,1024]{1,0:T(8,128)(2,1)S(1)} %get-tuple-element.641), channel_id=1, source_target_pairs={{0,8},{4,12},{8,0},{12,4},{16,24},{20,28},{24,16},{28,20},{1,9},{5... | collective-permute-start | bytes 1572872 | tf_op jit(solution)/shard_map/ppermute | solution.py:42
  122.2 27.3 %collective-permute-start.25 = (bf16[256,2048]{1,0:T(8,128)(2,1)S(1)}, bf16[256,2048]{1,0:T(8,128)(2,1)S(1)}, u32[]{:S(2)}, u32[]{:S(2)}) collective-permute-start(bf16[256,2048]{1,0:T(8,128)(2,1)S(1)} %bitcast.210), channel_id=1, source_target_pairs={{0,16},{4,20},{8,24},{12,28},{16,0},{20,4},{24,8},{28,12},{1,17},{... | collective-permute-start | bytes 3145736 | tf_op jit(solution)/shard_map/ppermute | solution.py:42
  122.8 26.7 %collective-permute-start.26 = (bf16[256,2048]{1,0:T(8,128)(2,1)S(1)}, bf16[256,2048]{1,0:T(8,128)(2,1)S(1)}, u32[]{:S(2)}, u32[]{:S(2)}) collective-permute-start(bf16[256,2048]{1,0:T(8,128)(2,1)S(1)} %bitcast.211), channel_id=1, source_target_pairs={{0,4},{4,0},{8,12},{12,8},{16,20},{20,16},{24,28},{28,24},{1,5},{5... | collective-permute-start | bytes 3145736 | tf_op jit(solution)/shard_map/ppermute | solution.py:42
  123.0 24.3 %collective-permute-start.27 = (bf16[128,2048]{1,0:T(8,128)(2,1)S(1)}, bf16[128,2048]{1,0:T(8,128)(2,1)S(1)}, u32[]{:S(2)}, u32[]{:S(2)}) collective-permute-start(bf16[128,2048]{1,0:T(8,128)(2,1)S(1)} %bitcast.236), channel_id=1, source_target_pairs={{0,1},{1,0},{2,3},{3,2},{4,5},{5,4},{6,7},{7,6},{8,9},{9,8},{10,11... | collective-permute-start | bytes 1572872 | tf_op jit(solution)/shard_map/ppermute | solution.py:42
  123.1 26.4 %collective-permute-start.28 = (bf16[256,1024]{1,0:T(8,128)(2,1)S(1)}, bf16[256,1024]{1,0:T(8,128)(2,1)S(1)}, u32[]{:S(2)}, u32[]{:S(2)}) collective-permute-start(bf16[256,1024]{1,0:T(8,128)(2,1)S(1)} %bitcast.230), channel_id=1, source_target_pairs={{0,2},{1,3},{2,0},{3,1},{4,6},{5,7},{6,4},{7,5},{8,10},{9,11},{10,... | collective-permute-start | bytes 1572872 | tf_op jit(solution)/shard_map/ppermute | solution.py:42
  130.8 18.7 %collective-permute-start.24 = (bf16[256,1024]{1,0:T(8,128)(2,1)S(1)}, bf16[256,1024]{1,0:T(8,128)(2,1)S(1)}, u32[]{:S(2)}, u32[]{:S(2)}) collective-permute-start(bf16[256,1024]{1,0:T(8,128)(2,1)S(1)} %get-tuple-element.675), channel_id=1, source_target_pairs={{0,8},{4,12},{8,0},{12,4},{16,24},{20,28},{24,16},{28,20},{1,9},{5... | collective-permute-start | bytes 1572872 | tf_op jit(solution)/shard_map/ppermute | solution.py:42
  149.7 25.6 %collective-permute-start.32 = (bf16[256,2048]{1,0:T(8,128)(2,1)S(1)}, bf16[256,2048]{1,0:T(8,128)(2,1)S(1)}, u32[]{:S(2)}, u32[]{:S(2)}) collective-permute-start(bf16[256,2048]{1,0:T(8,128)(2,1)S(1)} %bitcast.217), channel_id=1, source_target_pairs={{0,16},{4,20},{8,24},{12,28},{16,0},{20,4},{24,8},{28,12},{1,17},{... | collective-permute-start | bytes 3145736 | tf_op jit(solution)/shard_map/ppermute | solution.py:42
  151.3 24.0 %collective-permute-start.33 = (bf16[256,2048]{1,0:T(8,128)(2,1)S(1)}, bf16[256,2048]{1,0:T(8,128)(2,1)S(1)}, u32[]{:S(2)}, u32[]{:S(2)}) collective-permute-start(bf16[256,2048]{1,0:T(8,128)(2,1)S(1)} %bitcast.218), channel_id=1, source_target_pairs={{0,4},{4,0},{8,12},{12,8},{16,20},{20,16},{24,28},{28,24},{1,5},{5... | collective-permute-start | bytes 3145736 | tf_op jit(solution)/shard_map/ppermute | solution.py:42
  151.5 25.4 %collective-permute-start.34 = (bf16[512,1024]{1,0:T(8,128)(2,1)S(1)}, bf16[512,1024]{1,0:T(8,128)(2,1)S(1)}, u32[]{:S(2)}, u32[]{:S(2)}) collective-permute-start(bf16[512,1024]{1,0:T(8,128)(2,1)S(1)} %bitcast.220), channel_id=1, source_target_pairs={{0,1},{1,0},{2,3},{3,2},{4,5},{5,4},{6,7},{7,6},{8,9},{9,8},{10,11... | collective-permute-start | bytes 3145736 | tf_op jit(solution)/shard_map/ppermute | solution.py:42
  160.4 16.6 %collective-permute-start.30 = (bf16[128,1024]{1,0:T(8,128)(2,1)S(1)}, bf16[128,1024]{1,0:T(8,128)(2,1)S(1)}, u32[]{:S(2)}, u32[]{:S(2)}) collective-permute-start(bf16[128,1024]{1,0:T(8,128)(2,1)S(1)} %get-tuple-element.708), channel_id=1, source_target_pairs={{0,8},{4,12},{8,0},{12,4},{16,24},{20,28},{24,16},{28,20},{1,9},{5... | collective-permute-start | bytes 786440 | tf_op jit(solution)/shard_map/ppermute | solution.py:42
  161.0 16.0 %collective-permute-start.31 = (bf16[128,1024]{1,0:T(8,128)(2,1)S(1)}, bf16[128,1024]{1,0:T(8,128)(2,1)S(1)}, u32[]{:S(2)}, u32[]{:S(2)}) collective-permute-start(bf16[128,1024]{1,0:T(8,128)(2,1)S(1)} %get-tuple-element.709), channel_id=1, source_target_pairs={{0,8},{4,12},{8,0},{12,4},{16,24},{20,28},{24,16},{28,20},{1,9},{5... | collective-permute-start | bytes 786440 | tf_op jit(solution)/shard_map/ppermute | solution.py:42
  195.9 27.9 %collective-permute-start.41 = (bf16[256,2048]{1,0:T(8,128)(2,1)S(1)}, bf16[256,2048]{1,0:T(8,128)(2,1)S(1)}, u32[]{:S(2)}, u32[]{:S(2)}) collective-permute-start(bf16[256,2048]{1,0:T(8,128)(2,1)S(1)} %get-tuple-element.828), channel_id=1, source_target_pairs={{0,4},{4,0},{8,12},{12,8},{16,20},{20,16},{24,28},{28,24},{1,5},{5... | collective-permute-start | bytes 3145736 | tf_op jit(solution)/shard_map/ppermute | solution.py:42
  196.5 27.3 %collective-permute-start.45 = (bf16[256,2048]{1,0:T(8,128)(2,1)S(1)}, bf16[256,2048]{1,0:T(8,128)(2,1)S(1)}, u32[]{:S(2)}, u32[]{:S(2)}) collective-permute-start(bf16[256,2048]{1,0:T(8,128)(2,1)S(1)} %add_low.5), channel_id=1, source_target_pairs={{0,16},{4,20},{8,24},{12,28},{16,0},{20,4},{24,8},{28,12},{1,17},{... | collective-permute-start | bytes 3145736 | tf_op jit(solution)/shard_map/ppermute | solution.py:42
  197.9 25.9 %collective-permute-start.44 = (bf16[512,1024]{1,0:T(8,128)(2,1)S(1)}, bf16[512,1024]{1,0:T(8,128)(2,1)S(1)}, u32[]{:S(2)}, u32[]{:S(2)}) collective-permute-start(bf16[512,1024]{1,0:T(8,128)(2,1)S(1)} %bitcast.305), channel_id=1, source_target_pairs={{0,1},{1,0},{2,3},{3,2},{4,5},{5,4},{6,7},{7,6},{8,9},{9,8},{10,11... | collective-permute-start | bytes 3145736 | tf_op jit(solution)/shard_map/ppermute | solution.py:42
  226.6 27.8 %collective-permute-start.48 = (bf16[256,2048]{1,0:T(8,128)(2,1)S(1)}, bf16[256,2048]{1,0:T(8,128)(2,1)S(1)}, u32[]{:S(2)}, u32[]{:S(2)}) collective-permute-start(bf16[256,2048]{1,0:T(8,128)(2,1)S(1)} %get-tuple-element.895), channel_id=1, source_target_pairs={{0,4},{4,0},{8,12},{12,8},{16,20},{20,16},{24,28},{28,24},{1,5},{5... | collective-permute-start | bytes 3145736 | tf_op jit(solution)/shard_map/ppermute | solution.py:42
  226.9 27.4 %collective-permute-start.51 = (bf16[256,2048]{1,0:T(8,128)(2,1)S(1)}, bf16[256,2048]{1,0:T(8,128)(2,1)S(1)}, u32[]{:S(2)}, u32[]{:S(2)}) collective-permute-start(bf16[256,2048]{1,0:T(8,128)(2,1)S(1)} %add_low.6), channel_id=1, source_target_pairs={{0,16},{4,20},{8,24},{12,28},{16,0},{20,4},{24,8},{28,12},{1,17},{... | collective-permute-start | bytes 3145736 | tf_op jit(solution)/shard_map/ppermute | solution.py:42
  228.5 25.8 %collective-permute-start.49 = (bf16[256,1024]{1,0:T(8,128)(2,1)S(1)}, bf16[256,1024]{1,0:T(8,128)(2,1)S(1)}, u32[]{:S(2)}, u32[]{:S(2)}) collective-permute-start(bf16[256,1024]{1,0:T(8,128)(2,1)S(1)} %bitcast.307), channel_id=1, source_target_pairs={{0,2},{1,3},{2,0},{3,1},{4,6},{5,7},{6,4},{7,5},{8,10},{9,11},{10,... | collective-permute-start | bytes 1572872 | tf_op jit(solution)/shard_map/ppermute | solution.py:42
  230.5 23.8 %collective-permute-start.50 = (bf16[128,2048]{1,0:T(8,128)(2,1)S(1)}, bf16[128,2048]{1,0:T(8,128)(2,1)S(1)}, u32[]{:S(2)}, u32[]{:S(2)}) collective-permute-start(bf16[128,2048]{1,0:T(8,128)(2,1)S(1)} %bitcast.308), channel_id=1, source_target_pairs={{0,1},{1,0},{2,3},{3,2},{4,5},{5,4},{6,7},{7,6},{8,9},{9,8},{10,11... | collective-permute-start | bytes 1572872 | tf_op jit(solution)/shard_map/ppermute | solution.py:42
  257.8 32.4 %collective-permute-start.59 = (bf16[512,1024]{1,0:T(8,128)(2,1)S(1)}, bf16[512,1024]{1,0:T(8,128)(2,1)S(1)}, u32[]{:S(2)}, u32[]{:S(2)}) collective-permute-start(bf16[512,1024]{1,0:T(8,128)(2,1)S(1)} %add_low.7), channel_id=1, source_target_pairs={{0,16},{4,20},{8,24},{12,28},{16,0},{20,4},{24,8},{28,12},{1,17},{... | collective-permute-start | bytes 3145736 | tf_op jit(solution)/shard_map/ppermute | solution.py:42
  260.7 29.5 %collective-permute-start.58 = (bf16[256,1536]{1,0:T(8,128)(2,1)S(1)}, bf16[256,1536]{1,0:T(8,128)(2,1)S(1)}, u32[]{:S(2)}, u32[]{:S(2)}) collective-permute-start(bf16[256,1536]{1,0:T(8,128)(2,1)S(1)} %get-tuple-element.966), channel_id=1, source_target_pairs={{0,4},{4,0},{8,12},{12,8},{16,20},{20,16},{24,28},{28,24},{1,5},{5... | collective-permute-start | bytes 2359304 | tf_op jit(solution)/shard_map/ppermute | solution.py:42
  262.2 27.3 %collective-permute-start.61 = (bf16[128,2048]{1,0:T(8,128)(2,1)S(1)}, bf16[128,2048]{1,0:T(8,128)(2,1)S(1)}, u32[]{:S(2)}, u32[]{:S(2)}) collective-permute-start(bf16[128,2048]{1,0:T(8,128)(2,1)S(1)} %bitcast.306), channel_id=1, source_target_pairs={{0,1},{1,0},{2,3},{3,2},{4,5},{5,4},{6,7},{7,6},{8,9},{9,8},{10,11... | collective-permute-start | bytes 1572872 | tf_op jit(solution)/shard_map/ppermute | solution.py:42
  265.3 24.3 %collective-permute-start.62 = (bf16[256,512]{1,0:T(8,128)(2,1)S(1)}, bf16[256,512]{1,0:T(8,128)(2,1)S(1)}, u32[]{:S(2)}, u32[]{:S(2)}) collective-permute-start(bf16[256,512]{1,0:T(8,128)(2,1)S(1)} %bitcast.313), channel_id=1, source_target_pairs={{0,1},{1,0},{2,3},{3,2},{4,5},{5,4},{6,7},{7,6},{8,9},{9,8},{10,11... | collective-permute-start | bytes 786440 | tf_op jit(solution)/shard_map/ppermute | solution.py:42
  272.9 17.4 %collective-permute-start.60 = (bf16[64,2048]{1,0:T(8,128)(2,1)S(1)}, bf16[64,2048]{1,0:T(8,128)(2,1)S(1)}, u32[]{:S(2)}, u32[]{:S(2)}) collective-permute-start(bf16[64,2048]{1,0:T(8,128)(2,1)S(1)} %bitcast.312), channel_id=1, source_target_pairs={{0,2},{1,3},{2,0},{3,1},{4,6},{5,7},{6,4},{7,5},{8,10},{9,11},{10,... | collective-permute-start | bytes 786440 | tf_op jit(solution)/shard_map/ppermute | solution.py:42
  293.4 27.4 %collective-permute-start.66 = (bf16[256,2048]{1,0:T(8,128)(2,1)S(1)}, bf16[256,2048]{1,0:T(8,128)(2,1)}, u32[]{:S(2)}, u32[]{:S(2)}) collective-permute-start(bf16[256,2048]{1,0:T(8,128)(2,1)S(1)} %add_low.9), channel_id=1, source_target_pairs={{0,16},{4,20},{8,24},{12,28},{16,0},{20,4},{24,8},{28,12},{1,17},{... | collective-permute-start | bytes 3145736 | tf_op jit(solution)/shard_map/ppermute | solution.py:42
  298.7 22.1 %collective-permute-start.68 = (bf16[256,1024]{1,0:T(8,128)(2,1)S(1)}, bf16[256,1024]{1,0:T(8,128)(2,1)S(1)}, u32[]{:S(2)}, u32[]{:S(2)}) collective-permute-start(bf16[256,1024]{1,0:T(8,128)(2,1)S(1)} %bitcast.309), channel_id=1, source_target_pairs={{0,1},{1,0},{2,3},{3,2},{4,5},{5,4},{6,7},{7,6},{8,9},{9,8},{10,11... | collective-permute-start | bytes 1572872 | tf_op jit(solution)/shard_map/ppermute | solution.py:42
  301.6 19.2 %collective-permute-start.67 = (bf16[64,2048]{1,0:T(8,128)(2,1)S(1)}, bf16[64,2048]{1,0:T(8,128)(2,1)S(1)}, u32[]{:S(2)}, u32[]{:S(2)}) collective-permute-start(bf16[64,2048]{1,0:T(8,128)(2,1)S(1)} %bitcast.315), channel_id=1, source_target_pairs={{0,2},{1,3},{2,0},{3,1},{4,6},{5,7},{6,4},{7,5},{8,10},{9,11},{10,... | collective-permute-start | bytes 786440 | tf_op jit(solution)/shard_map/ppermute | solution.py:42
  325.6 14.9 %collective-permute-start.70 = (f32[32,3584]{1,0:T(8,128)}, f32[32,3584]{1,0:T(8,128)}, u32[]{:S(2)}, u32[]{:S(2)}) collective-permute-start(f32[32,3584]{1,0:T(8,128)} %get-tuple-element.1136), channel_id=1, source_target_pairs={{0,8},{4,12},{8,0},{12,4},{16,24},{20,28},{24,16},{28,20},{1,9},{5... | collective-permute-start | bytes 1376264 | tf_op jit(solution)/shard_map/ppermute | solution.py:42
  326.2 19.8 %collective-permute-start.72 = (bf16[256,1536]{1,0:T(8,128)(2,1)}, bf16[256,1536]{1,0:T(8,128)(2,1)}, u32[]{:S(2)}, u32[]{:S(2)}) collective-permute-start(bf16[256,1536]{1,0:T(8,128)(2,1)} %add_low.8), channel_id=1, source_target_pairs={{0,16},{4,20},{8,24},{12,28},{16,0},{20,4},{24,8},{28,12},{1,17},{... | collective-permute-start | bytes 2359304 | tf_op jit(solution)/shard_map/ppermute | solution.py:42
  327.5 18.5 %collective-permute-start.73 = (bf16[128,2048]{1,0:T(8,128)(2,1)}, bf16[128,2048]{1,0:T(8,128)(2,1)}, u32[]{:S(2)}, u32[]{:S(2)}) collective-permute-start(bf16[128,2048]{1,0:T(8,128)(2,1)} %bitcast.116), channel_id=1, source_target_pairs={{0,1},{1,0},{2,3},{3,2},{4,5},{5,4},{6,7},{7,6},{8,9},{9,8},{10,11... | collective-permute-start | bytes 1572872 | tf_op jit(solution)/shard_map/ppermute | solution.py:42
  330.4 15.6 %collective-permute-start.74 = (bf16[128,1024]{1,0:T(8,128)(2,1)}, bf16[128,1024]{1,0:T(8,128)(2,1)}, u32[]{:S(2)}, u32[]{:S(2)}) collective-permute-start(bf16[128,1024]{1,0:T(8,128)(2,1)} %bitcast.130), channel_id=1, source_target_pairs={{0,2},{1,3},{2,0},{3,1},{4,6},{5,7},{6,4},{7,5},{8,10},{9,11},{10,... | collective-permute-start | bytes 786440 | tf_op jit(solution)/shard_map/ppermute | solution.py:42
  346.0 19.2 %collective-permute-start.76 = (bf16[256,1024]{1,0:T(8,128)(2,1)S(1)}, bf16[256,1024]{1,0:T(8,128)(2,1)S(1)}, u32[]{:S(2)}, u32[]{:S(2)}) collective-permute-start(bf16[256,1024]{1,0:T(8,128)(2,1)S(1)} %get-tuple-element.1072), channel_id=1, source_target_pairs={{0,8},{4,12},{8,0},{12,4},{16,24},{20,28},{24,16},{28,20},{1,9},{5... | collective-permute-start | bytes 1572872 | tf_op jit(solution)/shard_map/ppermute | solution.py:42
  349.6 15.5 %collective-permute-start.79 = (bf16[128,1536]{1,0:T(8,128)(2,1)S(1)}, bf16[128,1536]{1,0:T(8,128)(2,1)S(1)}, u32[]{:S(2)}, u32[]{:S(2)}) collective-permute-start(bf16[128,1536]{1,0:T(8,128)(2,1)S(1)} %bitcast.310), channel_id=1, source_target_pairs={{0,1},{1,0},{2,3},{3,2},{4,5},{5,4},{6,7},{7,6},{8,9},{9,8},{10,11... | collective-permute-start | bytes 1179656 | tf_op jit(solution)/shard_map/ppermute | solution.py:42
  (129 other events, 1099.7 us)
